TPU v7x, 128 devices: a whole 4x4x4 slice. The times are simulated.
128 devices in a mesh: rows: 32 (over z, y, core), vecs: 4 (over x).
Axes of the slice: x: 4, y: 4, z: 4, core: 2. Of those that a mesh axis runs over, the one named last changes fastest.
Arguments:
- vectors: bfloat16 [131072, 1024], P('rows', 'vecs'), may hold values from -6 to 6, as said below
- blocks: bfloat16 [1024, 5, 128, 128], P('rows'), may hold values from -0.25 to 0.25
- columns: int32 [1024, 5], P('rows'), may hold values from 0 to 1023, as said below
Outputs:
- basis: float32 [131072, 1024], P('rows', 'vecs')
Inputs may be any that keep to these rules, and one draw needn't show every extreme that they name: Each block row i names 5 block columns of the form i + d clipped to 0 .. 1023, with distinct d in -8 .. 8; near the grid's ends some may repeat. `vectors`: entries of order one.
All inputs are finite; a program needn't handle non-finite values.
Results may differ from a plain program's by a relative error of at most 0.0075.
Values may be sent and summed in bfloat16 or wider, within the bound.
No kernel may reach another device: no remote copies, remote signals or barrier semaphores. Data moves between devices by JAX's collectives and lax.ppermute only.
A program may use at most 128 MiB of HBM per device.

v0:
```python
import jax
import jax.numpy as jnp
from jax import lax
from jax.sharding import PartitionSpec as P

DEGREE = 4


filter_center = 0.25
filter_radius = 1.25


def with_halo(shard, sides, width):
    for axis, dim in sides:
        count, length = (lax.axis_size(axis), shard.shape[dim])
        up = [(i, (i + 1) % count) for i in range(count - 1)]
        down = [(j, i) for i, j in up]
        last = lax.slice_in_dim(shard, length - width, length, axis=dim)
        first = lax.slice_in_dim(shard, 0, width, axis=dim)
        before = lax.ppermute(last, axis, up)
        after = lax.ppermute(first, axis, down)
        shard = jnp.concatenate([before, shard, after], axis=dim)
    return shard


def product(vec_bf, blocks, local_index):
    block_rows = blocks.shape[0]
    size_b = blocks.shape[2]
    width = vec_bf.shape[1]
    reach = block_rows // 4
    padded = with_halo(vec_bf, (("rows", 0),), reach * size_b)
    stacked = padded.reshape(block_rows + 2 * reach, size_b, width)
    picked = stacked[local_index]
    result = jnp.einsum("rjab,rjbk->rak", blocks, picked, preferred_element_type=jnp.float32)
    return result.reshape(block_rows * size_b, width)


def split_apply(left_bf, factor):
    factor_high = factor.astype(jnp.bfloat16)
    factor_low = (factor - factor_high.astype(jnp.float32)).astype(jnp.bfloat16)
    first = jnp.dot(left_bf, factor_high.T, preferred_element_type=jnp.float32)
    second = jnp.dot(left_bf, factor_low.T, preferred_element_type=jnp.float32)
    return first + second


def shards(vectors, blocks, columns):
    block_rows = blocks.shape[0]
    reach = block_rows // 4
    first_row = lax.axis_index("rows") * block_rows
    local_index = columns - first_row + reach
    total_rows = vectors.shape[0] * lax.axis_size("rows")
    older = vectors.astype(jnp.float32)
    current = (product(vectors, blocks, local_index) - filter_center * older) / filter_radius
    for iteration in range(1, DEGREE):
        rounded = current.astype(jnp.bfloat16)
        newer = (
            2.0 * (product(rounded, blocks, local_index) - filter_center * current) / filter_radius
            - older
        )
        older = current
        current = newer
    final = current.astype(jnp.bfloat16)
    panel_width = final.shape[1]
    full_width = panel_width * lax.axis_size("vecs")
    identity = jnp.eye(full_width, dtype=jnp.float32)
    whole_block = lax.all_gather(final, "vecs", axis=1, tiled=True)
    panel = jnp.dot(final.T, whole_block, preferred_element_type=jnp.float32)
    summed = lax.psum(panel, "rows")
    gram_matrix = lax.all_gather(summed, "vecs", axis=0, tiled=True) / total_rows
    lower = jnp.linalg.cholesky(gram_matrix)
    inverse = lax.linalg.triangular_solve(lower, identity, left_side=True, lower=True)
    own_rows = lax.dynamic_slice_in_dim(
        inverse, lax.axis_index("vecs") * panel_width, panel_width, 0
    )
    return split_apply(whole_block, own_rows)


def solution(mesh):
    in_specs = (P("rows", "vecs"), P("rows", None, None, None), P("rows", None))
    out_specs = P("rows", "vecs")
    return jax.shard_map(shards, mesh=mesh, in_specs=in_specs, out_specs=out_specs, check_vma=False)
```

profile of v0, /device:TPU:1, one launch (start us, length us, event | category | flops | bytes accessed | tf_op | source)
XLA Modules:
  0.0 772.7 jit_solution(1005979501189157616)
XLA Ops:
  7.8 4.6 collective-permute-start
  15.3 3.3 collective-permute-done
  19.3 3.7 collective-permute-done.1
  25.1 7.6 gather_fusion
  32.7 7.5 fusion.88
  44.3 2.4 collective-permute-start.3
  46.7 3.7 collective-permute-done.2
  50.4 4.4 collective-permute-done.3
  56.7 9.5 %gather_fusion.1 = bf16[160,128,256]{2,1,0:T(8,128)(2,1)} fusion(bf16[48,128,256]{2,1,0:T(8,128)(2,1)} %bitcast.194, s32[1024]{0:T(1024)S(1)} %pad_clamp_fusion), kind=kCustom, calls=%fused_computation.1 | custom fusion | bytes 20972160 | tf_op jit(solution)/shard_map/gather | solution.py:33
  66.2 7.5 fusion.89
  77.8 2.9 collective-permute-start.5
  80.7 3.2 collective-permute-done.4
  83.9 4.4 collective-permute-done.5
  90.1 9.5 %gather_fusion.2 = bf16[160,128,256]{2,1,0:T(8,128)(2,1)} fusion(bf16[48,128,256]{2,1,0:T(8,128)(2,1)} %bitcast.195, s32[1024]{0:T(1024)S(1)} %pad_clamp_fusion), kind=kCustom, calls=%fused_computation.2 | custom fusion | bytes 20972160 | tf_op jit(solution)/shard_map/gather | solution.py:33
  99.6 7.5 fusion.90
  107.6 2.6 fusion.80
  112.2 2.4 collective-permute-start.7
  114.6 3.7 collective-permute-done.6
  118.3 6.0 collective-permute-done.7
  126.2 9.5 %gather_fusion.3 = bf16[160,128,256]{2,1,0:T(8,128)(2,1)} fusion(bf16[48,128,256]{2,1,0:T(8,128)(2,1)} %bitcast.193, s32[1024]{0:T(1024)S(1)} %pad_clamp_fusion), kind=kCustom, calls=%fused_computation.3 | custom fusion | bytes 20972160 | tf_op jit(solution)/shard_map/gather | solution.py:33
  135.7 7.5 fusion.91
  144.9 4.4 fusion.3
  149.4 94.6 %all-gather.3.cloned.1.call-done = bf16[4096,1024]{1,0:T(8,128)(2,1)} async-done(((bf16[4096,256]{1,0:T(8,128)(2,1)}), bf16[4096,1024]{1,0:T(8,128)(2,1)}) %all-gather.3.cloned.1.call-update) | async-done | bytes 8388624 | tf_op jit(solution)/shard_map/all_gather | solution.py:66
  244.0 8.4 %fusion.87 = f32[256,1024]{0,1:T(8,128)} fusion(bf16[4096,256]{1,0:T(8,128)(2,1)} %fusion.3, bf16[4096,1024]{1,0:T(8,128)(2,1)} %all-gather.3.cloned.1.call-done), kind=kOutput, calls=%fused_computation.195 | convolution fusion | flops 2147483648 | bytes 11534336 | tf_op jit(solution)/shard_map/dot_general | solution.py:67
  252.5 106.3 %all-reduce.3.cloned.1.call-done = f32[256,1024]{0,1:T(8,128)} async-done(((f32[256,1024]{0,1:T(8,128)}), f32[256,1024]{0,1:T(8,128)}) %all-reduce.3.cloned.1.call-update) | async-done | bytes 1048592 | tf_op jit(solution)/shard_map/psum | solution.py:68
  359.2 2.5 fusion.28
  361.7 46.9 %all-gather.5.cloned.1.call-done = f32[1024,1024]{0,1:T(8,128)} async-done(((f32[256,1024]{0,1:T(8,128)}), f32[1024,1024]{0,1:T(8,128)}) %all-gather.5.cloned.1.call-update) | async-done | bytes 4194320 | tf_op jit(solution)/shard_map/all_gather | solution.py:69
  408.6 5.0 broadcast_multiply_fusion
  413.6 5.5 copy.8
  419.1 4.4 fusion.7
  425.5 11.7 %cholesky.223 = f32[128,128]{1,0:T(8,128)S(1)} custom-call(f32[128,128]{1,0:T(8,128)S(1)} %cholesky.580), custom_call_target="Cholesky" | custom-call | tf_op jit(solution)/shard_map/jit(cholesky)/cholesky | solution.py:70
  437.3 9.8 %custom-call.62 = f32[1,128,128]{1,2,0:T(8,128)S(1)} custom-call(f32[1,128,128]{2,1,0:T(8,128)S(1)} %get-tuple-element.77), custom_call_target="InvertDiagBlocksLowerTriangular" | custom-call | tf_op jit(solution)/shard_map/jit(cholesky)/cholesky | solution.py:70
  447.1 2.5 cholesky.255
  449.6 2.3 constant_dynamic-update-slice_fusion.32
  453.5 11.9 %cholesky.244 = f32[128,128]{1,0:T(8,128)S(1)} custom-call(f32[128,128]{1,0:T(8,128)S(1)} %cholesky.584), custom_call_target="Cholesky" | custom-call | tf_op jit(solution)/shard_map/jit(cholesky)/cholesky | solution.py:70
  466.0 9.8 %custom-call.63 = f32[1,128,128]{1,2,0:T(8,128)S(1)} custom-call(f32[1,128,128]{2,1,0:T(8,128)S(1)} %get-tuple-element.74), custom_call_target="InvertDiagBlocksLowerTriangular" | custom-call | tf_op jit(solution)/shard_map/jit(cholesky)/cholesky | solution.py:70
  479.2 11.7 %cholesky.468 = f32[128,128]{1,0:T(8,128)S(1)} custom-call(f32[128,128]{1,0:T(8,128)S(1)} %cholesky.589), custom_call_target="Cholesky" | custom-call | tf_op jit(solution)/shard_map/jit(cholesky)/cholesky | solution.py:70
  492.2 9.8 %custom-call.64 = f32[1,128,128]{1,2,0:T(8,128)S(1)} custom-call(f32[1,128,128]{2,1,0:T(8,128)S(1)} %get-tuple-element.71), custom_call_target="InvertDiagBlocksLowerTriangular" | custom-call | tf_op jit(solution)/shard_map/jit(cholesky)/cholesky | solution.py:70
  503.1 2.4 convolution_subtract_fusion.7
  505.5 12.1 %cholesky.487 = f32[128,128]{1,0:T(8,128)S(1)} custom-call(f32[128,128]{1,0:T(8,128)S(1)} %cholesky.594), custom_call_target="Cholesky" | custom-call | tf_op jit(solution)/shard_map/jit(cholesky)/cholesky | solution.py:70
  519.0 9.8 %custom-call.65 = f32[1,128,128]{1,2,0:T(8,128)S(1)} custom-call(f32[1,128,128]{2,1,0:T(8,128)S(1)} %get-tuple-element.68), custom_call_target="InvertDiagBlocksLowerTriangular" | custom-call | tf_op jit(solution)/shard_map/jit(cholesky)/cholesky | solution.py:70
  529.9 2.3 convolution_subtract_fusion.8
  532.2 11.7 %cholesky.506 = f32[128,128]{1,0:T(8,128)S(1)} custom-call(f32[128,128]{1,0:T(8,128)S(1)} %cholesky.599), custom_call_target="Cholesky" | custom-call | tf_op jit(solution)/shard_map/jit(cholesky)/cholesky | solution.py:70
  545.2 10.0 %custom-call.66 = f32[1,128,128]{1,2,0:T(8,128)S(1)} custom-call(f32[1,128,128]{2,1,0:T(8,128)S(1)} %get-tuple-element.65), custom_call_target="InvertDiagBlocksLowerTriangular" | custom-call | tf_op jit(solution)/shard_map/jit(cholesky)/cholesky | solution.py:70
  558.4 11.7 %cholesky.526 = f32[128,128]{1,0:T(8,128)S(1)} custom-call(f32[128,128]{1,0:T(8,128)S(1)} %cholesky.604), custom_call_target="Cholesky" | custom-call | tf_op jit(solution)/shard_map/jit(cholesky)/cholesky | solution.py:70
  571.4 9.8 %custom-call.67 = f32[1,128,128]{1,2,0:T(8,128)S(1)} custom-call(f32[1,128,128]{2,1,0:T(8,128)S(1)} %get-tuple-element.62), custom_call_target="InvertDiagBlocksLowerTriangular" | custom-call | tf_op jit(solution)/shard_map/jit(cholesky)/cholesky | solution.py:70
  584.2 11.9 %cholesky.546 = f32[128,128]{1,0:T(8,128)S(1)} custom-call(f32[128,128]{1,0:T(8,128)S(1)} %cholesky.609), custom_call_target="Cholesky" | custom-call | tf_op jit(solution)/shard_map/jit(cholesky)/cholesky | solution.py:70
  597.4 9.8 %custom-call.68 = f32[1,128,128]{1,2,0:T(8,128)S(1)} custom-call(f32[1,128,128]{2,1,0:T(8,128)S(1)} %get-tuple-element.59), custom_call_target="InvertDiagBlocksLowerTriangular" | custom-call | tf_op jit(solution)/shard_map/jit(cholesky)/cholesky | solution.py:70
  609.9 11.7 %cholesky.564 = f32[128,128]{1,0:T(8,128)S(1)} custom-call(f32[128,128]{1,0:T(8,128)S(1)} %convolution_subtract_fusion.11), custom_call_target="Cholesky" | custom-call | tf_op jit(solution)/shard_map/jit(cholesky)/cholesky | solution.py:70
  628.5 4.9 select_select_fusion
  633.4 23.9 %while.1 = (s32[]{:T(128)}, f32[1024,1024]{1,0:T(8,128)}, s32[8,2]{0,1:T(2,128)S(1)}, f32[8,128,128]{2,1,0:T(8,128)S(1)}, s32[]{:T(128)}) while((s32[]{:T(128)}, f32[1024,1024]{1,0:T(8,128)}, s32[8,2]{0,1:T(2,128)S(1)}, f32[8,128,128]{2,1,0:T(8,128)S(1)}, s32[]{:T(128)}) %tuple.61), condition=%wide.while_cond, body=%wide.while_body.sunk | while | flops 2 | bytes 131189 | solution.py:71
  634.1 2.3 bitcast_dynamic-update-slice_fusion.2
  637.1 2.3 bitcast_dynamic-update-slice_fusion.2
  640.1 2.3 bitcast_dynamic-update-slice_fusion.2
  643.1 2.3 bitcast_dynamic-update-slice_fusion.2
  646.1 2.3 bitcast_dynamic-update-slice_fusion.2
  649.1 2.3 bitcast_dynamic-update-slice_fusion.2
  652.1 2.3 bitcast_dynamic-update-slice_fusion.2
  657.3 79.0 %custom-call.69 = f32[8,128,128]{1,2,0:T(8,128)S(1)} custom-call(f32[8,128,128]{2,1,0:T(8,128)S(1)} %get-tuple-element.12), custom_call_target="InvertDiagBlocksLowerTriangular" | custom-call | tf_op jit(solution)/shard_map/triangular_solve | solution.py:71
  747.7 2.8 convolution_subtract_fusion.2
  751.2 3.0 convolution_subtract_fusion.1
  754.8 3.4 convolution_subtract_fusion.3
  758.9 2.4 fusion.52
  761.3 4.7 convolution_add_fusion
  (121 shorter events, 73.0 us)
Async XLA Ops:
  6.5 237.5 %all-gather.3.cloned.1.call-start = ((), (), s32[]{:S(2)}) async-start(), calls=%async_computation | async-start | bytes 10485760 | tf_op jit(solution)/shard_map/all_gather | solution.py:66
  7.8 10.7 %collective-permute-start = (bf16[1024,256]{1,0:T(8,128)(2,1)S(1)}, bf16[1024,256]{1,0:T(8,128)(2,1)S(1)}, u32[]{:S(2)}, u32[]{:S(2)}) collective-permute-start(bf16[1024,256]{1,0:T(8,128)(2,1)S(1)} %get-tuple-element.29), channel_id=1, source_target_pairs={{0,4},{4,8},{8,12},{12,16},{16,20},{20,24},{24,28},{28,32},{32,36}... | collective-permute-start | bytes 1572872 | tf_op jit(solution)/shard_map/ppermute | solution.py:20
  12.4 10.6 %collective-permute-start.1 = (bf16[1024,256]{1,0:T(8,128)(2,1)S(1)}, bf16[1024,256]{1,0:T(8,128)(2,1)}, u32[]{:S(2)}, u32[]{:S(2)}) collective-permute-start(bf16[1024,256]{1,0:T(8,128)(2,1)S(1)} %get-tuple-element.30), channel_id=1, source_target_pairs={{4,0},{8,4},{12,8},{16,12},{20,16},{24,20},{28,24},{32,28},{36,32}... | collective-permute-start | bytes 1572872 | tf_op jit(solution)/shard_map/ppermute | solution.py:21
  18.5 0.8 copy-start.12
  32.7 7.5 copy-start.7
  40.3 2.0 copy-start
  42.4 8.0 %collective-permute-start.2 = (bf16[1024,256]{1,0:T(8,128)(2,1)S(1)}, bf16[1024,256]{1,0:T(8,128)(2,1)S(1)}, u32[]{:S(2)}, u32[]{:S(2)}) collective-permute-start(bf16[1024,256]{1,0:T(8,128)(2,1)S(1)} %get-tuple-element.27), channel_id=1, source_target_pairs={{0,4},{4,8},{8,12},{12,16},{16,20},{20,24},{24,28},{28,32},{32,36}... | collective-permute-start | bytes 1572872 | tf_op jit(solution)/shard_map/ppermute | solution.py:20
  44.3 10.5 %collective-permute-start.3 = (bf16[1024,256]{1,0:T(8,128)(2,1)S(1)}, bf16[1024,256]{1,0:T(8,128)(2,1)S(1)}, u32[]{:S(2)}, u32[]{:S(2)}) collective-permute-start(bf16[1024,256]{1,0:T(8,128)(2,1)S(1)} %get-tuple-element.28), channel_id=1, source_target_pairs={{4,0},{8,4},{12,8},{16,12},{20,16},{24,20},{28,24},{32,28},{36,32}... | collective-permute-start | bytes 1572872 | tf_op jit(solution)/shard_map/ppermute | solution.py:21
  66.2 7.5 copy-start.1
  73.7 2.1 copy-start.4
  75.9 8.0 %collective-permute-start.4 = (bf16[1024,256]{1,0:T(8,128)(2,1)S(1)}, bf16[1024,256]{1,0:T(8,128)(2,1)S(1)}, u32[]{:S(2)}, u32[]{:S(2)}) collective-permute-start(bf16[1024,256]{1,0:T(8,128)(2,1)S(1)} %get-tuple-element.25), channel_id=1, source_target_pairs={{0,4},{4,8},{8,12},{12,16},{16,20},{20,24},{24,28},{28,32},{32,36}... | collective-permute-start | bytes 1572872 | tf_op jit(solution)/shard_map/ppermute | solution.py:20
  77.8 10.5 %collective-permute-start.5 = (bf16[1024,256]{1,0:T(8,128)(2,1)S(1)}, bf16[1024,256]{1,0:T(8,128)(2,1)S(1)}, u32[]{:S(2)}, u32[]{:S(2)}) collective-permute-start(bf16[1024,256]{1,0:T(8,128)(2,1)S(1)} %get-tuple-element.26), channel_id=1, source_target_pairs={{4,0},{8,4},{12,8},{16,12},{20,16},{24,20},{28,24},{32,28},{36,32}... | collective-permute-start | bytes 1572872 | tf_op jit(solution)/shard_map/ppermute | solution.py:21
  99.6 7.5 copy-start.2
  99.6 8.0 %copy-start.5 = (f32[32,256,128,1]{1,2,3,0:T(8,128)S(1)}, f32[32,256,128,1]{1,2,3,0:T(8,128)}, u32[]{:S(2)}) copy-start(f32[32,256,128,1]{1,2,3,0:T(8,128)} %copy-done.4) | copy-start | bytes 12582916
  107.6 2.6 copy-start.8
  110.3 8.0 %collective-permute-start.6 = (bf16[1024,256]{1,0:T(8,128)(2,1)S(1)}, bf16[1024,256]{1,0:T(8,128)(2,1)S(1)}, u32[]{:S(2)}, u32[]{:S(2)}) collective-permute-start(bf16[1024,256]{1,0:T(8,128)(2,1)S(1)} %get-tuple-element.23), channel_id=1, source_target_pairs={{0,4},{4,8},{8,12},{12,16},{16,20},{20,24},{24,28},{28,32},{32,36}... | collective-permute-start | bytes 1572872 | tf_op jit(solution)/shard_map/ppermute | solution.py:20
  112.2 12.1 %collective-permute-start.7 = (bf16[1024,256]{1,0:T(8,128)(2,1)S(1)}, bf16[1024,256]{1,0:T(8,128)(2,1)S(1)}, u32[]{:S(2)}, u32[]{:S(2)}) collective-permute-start(bf16[1024,256]{1,0:T(8,128)(2,1)S(1)} %get-tuple-element.24), channel_id=1, source_target_pairs={{4,0},{8,4},{12,8},{16,12},{20,16},{24,20},{28,24},{32,28},{36,32}... | collective-permute-start | bytes 1572872 | tf_op jit(solution)/shard_map/ppermute | solution.py:21
  135.7 7.5 copy-start.3
  135.7 8.0 %copy-start.6 = (f32[32,256,128,1]{1,2,3,0:T(8,128)S(1)}, f32[32,256,128,1]{1,2,3,0:T(8,128)}, u32[]{:S(2)}) copy-start(f32[32,256,128,1]{1,2,3,0:T(8,128)} %copy-done.4) | copy-start | bytes 12582916
  135.7 9.2 %copy-start.9 = (f32[32,256,128,1]{1,2,3,0:T(8,128)S(1)}, f32[32,256,128,1]{1,2,3,0:T(8,128)}, u32[]{:S(2)}) copy-start(f32[32,256,128,1]{1,2,3,0:T(8,128)} %copy-done.8) | copy-start | bytes 12582916
  149.3 209.5 %all-reduce.3.cloned.1.call-start = ((), (), s32[]{:S(2)}) async-start(), calls=%async_computation.1 | async-start | bytes 2097152 | tf_op jit(solution)/shard_map/psum | solution.py:68
  252.5 156.1 %all-gather.5.cloned.1.call-start = ((), (), s32[]{:S(2)}) async-start(), calls=%async_computation.2 | async-start | bytes 5242880 | tf_op jit(solution)/shard_map/all_gather | solution.py:69
  423.6 1.9 copy-start.11
  736.3 3.2 copy-start.10
  747.7 11.2 %slice-start = ((s8[8388608]{0:T(1024)(128)(4,1)}), s8[4194304]{0:T(1024)(128)(4,1)S(1)}, s32[]{:S(2)}) async-start(s8[8388608]{0:T(1024)(128)(4,1)} %bitcast.197), calls=%async_computation.3 | async-start | bytes 8388608
  751.2 7.7 slice-start.1
Sparse Core Ops, SparseCore 0:
  149.4 94.5 all-gather.2
  252.6 106.2 all-reduce.2
  360.6 47.9 all-gather.4
where the time goes:
time: 782 us; the launch traced here: 773 us
  other arithmetic  287 us (37%)
  waiting for transfers between devices  280 us (36%)
  matrix products  91 us (12%)
  local copies, waits for them, and re-layouts  75.8 us (10%)
  starting transfers between devices  20.1 us (3%)
  between operations  18.8 us (2%)
    another operation x30, other arithmetic, shards(): lower = jnp.linalg.cholesky(gram_matrix)  172 us
    psum x1, waiting for transfers between devices, shards(): summed = lax.psum(panel, 'rows')  106 us
    all_gather x1, waiting for transfers between devices, shards(): whole_block = lax.all_gather(final, 'vecs', axis=1, tiled=True)  94.6 us
    another operation x3, other arithmetic, shards(): lax.linalg.triangular_solve(lower, identity, left_side=True, lower=True)  83.9 us
    all_gather x1, waiting for transfers between devices, shards(): lax.all_gather(summed, 'vecs', axis=0, tiled=True) / total_rows  46.9 us
    gather x4, local copies, waits for them, and re-layouts, product(): picked = stacked[local_index]  36.1 us
    dot_general x4, matrix products, product(): jnp.einsum('rjab,rjbk->rak', blocks, picked, preferred_element_type=jnp.f...  30.1 us
    another operation x24, local copies, waits for them, and re-layouts  23.8 us
  transfers between devices with their start and end apart: 11, of which 11 were waited for; matrix products, arithmetic and copies ran while one was open for 0% of the time, Pallas kernels for 0%

commit v1 on v0

v1 whole, which is shorter than its diff:
```python
import functools

import jax
import jax.numpy as jnp
from jax import lax
from jax.experimental import pallas as pl
from jax.experimental.pallas import tpu as pltpu
from jax.sharding import PartitionSpec as P

DEGREE = 4
filter_center = 0.25
filter_radius = 1.25

F32 = jnp.float32
BF = jnp.bfloat16
EXACT = lax.Precision.HIGHEST
SIZE = 128
REACH = 8
MIB = 1 << 20

ANY = pl.BlockSpec(memory_space=pl.ANY)


def params(mib):
    return pltpu.CompilerParams(vmem_limit_bytes=mib * MIB)


def load_all(pairs, sems):
    copies = [pltpu.make_async_copy(src, dst, sems.at[n]) for n, (src, dst) in enumerate(pairs)]
    for copy in copies:
        copy.start()
    for copy in copies:
        copy.wait()


def row_product(idx, row, shift, blocks_ref, r, pad):
    count = blocks_ref.shape[1]
    left = jnp.concatenate([blocks_ref[r, j] for j in range(count)], axis=1)
    right = jnp.concatenate([pad[idx[row, j] - shift] for j in range(count)], axis=0)
    return jnp.dot(left, right, preferred_element_type=F32)


def recurrence(step, product, current, older):
    scale = (2.0 if step else 1.0) / filter_radius
    newer = scale * product - (scale * filter_center) * current.astype(F32)
    return newer - older.astype(F32) if step else newer


def edge_kernel(step, last, offsets, idx, place, *refs):
    refs = list(refs)
    take = lambda n: [refs.pop(0) for _ in range(n)]
    blocks = take(2)
    before, low, mid, high, after = take(5)
    current = take(2)
    older = take(2) if step else [None, None]
    if last:
        (mid_new,) = take(1)
        sends = take(4)
        pad, sems, final_low, final_high, out_sems = take(5)
        rounded = [final_low, final_high]
    else:
        fresh = take(2)
        rounded = take(2)
        pad, sems = take(2)
    g = pl.program_id(0)
    per = blocks[0].shape[0]

    @pl.when(g == 0)
    def _():
        load_all(
            [
                (before, pad.at[pl.ds(0, 8)]),
                (low.at[pl.ds(offsets[0], 8)], pad.at[pl.ds(8, 8)]),
                (mid.at[pl.ds(offsets[1], 16)], pad.at[pl.ds(16, 16)]),
                (high.at[pl.ds(offsets[2], 8)], pad.at[pl.ds(32, 8)]),
                (after, pad.at[pl.ds(40, 8)]),
            ],
            sems,
        )

    for side in range(2):
        for r in range(per):
            row = 24 * side + g * per + r
            product = row_product(idx, row, 0, blocks[side], r, pad)
            old = older[side][r] if step else None
            newer = recurrence(step, product, current[side][r], old)
            if last:
                rounded[side][g * per + r] = newer.astype(BF)
            else:
                fresh[side][r] = newer
                rounded[side][r] = newer.astype(BF)

    if last:

        @pl.when(g == pl.num_programs(0) - 1)
        def _():
            sources = [final_low, mid_new.at[pl.ds(0, 8)], mid_new.at[pl.ds(8, 8)], final_high]
            for s in range(4):
                for q in range(4):

                    @pl.when(lax.rem(place[0] + s, 4) == q)
                    def _():
                        pltpu.make_async_copy(sources[q], sends[s], out_sems.at[s]).start()

            for s in range(4):
                pltpu.make_async_copy(final_low, sends[s], out_sems.at[s]).wait()


def middle_kernel(step, last, offsets, idx, *refs):
    refs = list(refs)
    take = lambda n: [refs.pop(0) for _ in range(n)]
    (blocks,) = take(1)
    low, mid, high = take(3)
    (current,) = take(1)
    older = take(1)[0] if step else None
    fresh = None if last else take(1)[0]
    rounded, pad, sems = take(3)
    g = pl.program_id(0)
    per = blocks.shape[0]

    @pl.when(g == 0)
    def _():
        load_all(
            [
                (low.at[pl.ds(offsets[0], 8)], pad.at[pl.ds(0, 8)]),
                (mid.at[pl.ds(offsets[1], 16)], pad.at[pl.ds(8, 16)]),
                (high.at[pl.ds(offsets[2], 8)], pad.at[pl.ds(24, 8)]),
            ],
            sems,
        )

    for r in range(per):
        product = row_product(idx, 8 + g * per + r, 8, blocks, r, pad)
        newer = recurrence(step, product, current[r], older[r] if step else None)
        if not last:
            fresh[r] = newer
        rounded[r] = newer.astype(BF)


def spec_rows(per, width, first):
    return pl.BlockSpec((per, SIZE, width), lambda g, *_: (g + first // per, 0, 0))


def filter_edges(step, last, idx, place, blocks, halo, rounded, current, older, mid_new):
    width = rounded[0][0].shape[-1]
    per = 2
    nnz = blocks.shape[1]
    block_spec = lambda first: pl.BlockSpec((per, nnz, SIZE, SIZE), lambda g, *_: (g + first // per, 0, 0, 0))
    in_specs = [block_spec(0), block_spec(24)] + [ANY] * 5
    operands = [blocks, blocks, halo[0], rounded[0][0], rounded[1][0], rounded[2][0], halo[1]]
    for group in [current] + ([older] if step else []):
        for piece in (0, 2):
            in_specs.append(spec_rows(per, width, group[piece][1]))
            operands.append(group[piece][0])
    scratch = [pltpu.VMEM((48, SIZE, width), BF), pltpu.SemaphoreType.DMA((5,))]
    if last:
        in_specs.append(ANY)
        operands.append(mid_new)
        out_shape = [jax.ShapeDtypeStruct((8, SIZE, width), BF)] * 4
        out_specs = [ANY] * 4
        scratch += [pltpu.VMEM((8, SIZE, width), BF)] * 2 + [pltpu.SemaphoreType.DMA((4,))]
    else:
        out_shape = [jax.ShapeDtypeStruct((8, SIZE, width), F32)] * 2 + [jax.ShapeDtypeStruct((8, SIZE, width), BF)] * 2
        out_specs = [spec_rows(per, width, 0)] * 4
    offsets = tuple(piece[1] for piece in rounded)
    return pl.pallas_call(
        functools.partial(edge_kernel, step, last, offsets),
        out_shape=out_shape,
        grid_spec=pltpu.PrefetchScalarGridSpec(
            num_scalar_prefetch=2,
            grid=(8 // per,),
            in_specs=in_specs,
            out_specs=out_specs,
            scratch_shapes=scratch,
        ),
        compiler_params=params(24),
        cost_estimate=pl.CostEstimate(flops=16 * 5 * 2 * 128 * 128 * 256, bytes_accessed=12 * MIB, transcendentals=0),
        name="filter_edges",
    )(idx, place, *operands)


def filter_middle(step, last, idx, blocks, rounded, current, older):
    width = rounded[0][0].shape[-1]
    per = 4
    nnz = blocks.shape[1]
    in_specs = [pl.BlockSpec((per, nnz, SIZE, SIZE), lambda g, *_: (g + 8 // per, 0, 0, 0))] + [ANY] * 3
    operands = [blocks] + [piece[0] for piece in rounded]
    for group in [current] + ([older] if step else []):
        in_specs.append(spec_rows(per, width, group[1][1]))
        operands.append(group[1][0])
    out_shape = [jax.ShapeDtypeStruct((16, SIZE, width), F32), jax.ShapeDtypeStruct((16, SIZE, width), BF)]
    if last:
        out_shape = out_shape[1:]
    offsets = tuple(piece[1] for piece in rounded)
    return pl.pallas_call(
        functools.partial(middle_kernel, step, last, offsets),
        out_shape=out_shape,
        grid_spec=pltpu.PrefetchScalarGridSpec(
            num_scalar_prefetch=1,
            grid=(16 // per,),
            in_specs=in_specs,
            out_specs=[spec_rows(per, width, 0)] * len(out_shape),
            scratch_shapes=[pltpu.VMEM((32, SIZE, width), BF), pltpu.SemaphoreType.DMA((3,))],
        ),
        compiler_params=params(24),
        cost_estimate=pl.CostEstimate(flops=16 * 5 * 2 * 128 * 128 * 256, bytes_accessed=12 * MIB, transcendentals=0),
        name="filter_middle",
    )(idx, *operands)


def exchange_halo(low, high):
    count = lax.axis_size("rows")
    up = [(i, i + 1) for i in range(count - 1)]
    down = [(j, i) for i, j in up]
    return lax.ppermute(high, "rows", up), lax.ppermute(low, "rows", down)


PAIRS = [(a, b) for a in range(4) for b in range(a, 4)]
HALF = len(PAIRS) // 2


def gram_kernel(total_rows, place, own, got1, got2, got3, keep, send, stacked, f, g, sems, out_sems):
    pieces = [own, got1, got2, got3]
    x, core = place[0], place[1]
    load_all([(pieces[s], f.at[lax.rem(x + 4 - s, 4)]) for s in range(4)], sems)
    copy_f = pltpu.make_async_copy(f, stacked, out_sems.at[2])
    copy_f.start()
    depth = 8 * SIZE
    width = f.shape[-1]
    for a in range(4):
        left = f[a].reshape(depth, width).T
        for b in range(a, 4):
            n = PAIRS.index((a, b))
            tile = jnp.dot(left, f[b].reshape(depth, width), preferred_element_type=F32) * (1.0 / total_rows)
            for r in range(2):
                for c in range(2):
                    g[n // HALF, n % HALF, r, c] = tile[r * SIZE : (r + 1) * SIZE, c * SIZE : (c + 1) * SIZE]
    copy_keep = pltpu.make_async_copy(g.at[core], keep, out_sems.at[0])
    copy_send = pltpu.make_async_copy(g.at[1 - core], send, out_sems.at[1])
    copy_keep.start()
    copy_send.start()
    copy_keep.wait()
    copy_send.wait()
    copy_f.wait()


def gram(total_rows, place, own, got):
    width = own.shape[-1]
    half = jax.ShapeDtypeStruct((HALF, 2, 2, SIZE, SIZE), F32)
    return pl.pallas_call(
        functools.partial(gram_kernel, total_rows),
        out_shape=[half, half, jax.ShapeDtypeStruct((4, 8, SIZE, width), BF)],
        grid_spec=pltpu.PrefetchScalarGridSpec(
            num_scalar_prefetch=1,
            grid=(),
            in_specs=[ANY] * 4,
            out_specs=[ANY] * 3,
            scratch_shapes=[
                pltpu.VMEM((4, 8, SIZE, width), BF),
                pltpu.VMEM((2, HALF, 2, 2, SIZE, SIZE), F32),
                pltpu.SemaphoreType.DMA((4,)),
                pltpu.SemaphoreType.DMA((3,)),
            ],
        ),
        compiler_params=params(24),
        cost_estimate=pl.CostEstimate(flops=10 * 2 * 1024 * 256 * 256, bytes_accessed=8 * MIB, transcendentals=0),
        name="gram",
    )(place, own, *got)


def sum_everywhere(keep, send):
    rows = lax.axis_size("rows")
    vecs = lax.axis_size("vecs")
    swap = [(i, i ^ 1) for i in range(rows)]
    groups = [list(range(c, rows, 2)) for c in range(2)]
    count = rows // 2
    mine = keep + lax.ppermute(send, "rows", swap)
    parts = mine.reshape(count, -1, SIZE)
    parts = lax.all_to_all(parts, "rows", 0, 0, axis_index_groups=groups, tiled=True)
    part = jnp.sum(parts, axis=0)
    others = [lax.ppermute(part, "vecs", [(i, (i + s) % vecs) for i in range(vecs)]) for s in range(1, vecs)]
    part = part + sum(others)
    spread_out = jnp.broadcast_to(part[None], (count,) + part.shape)
    mine = lax.all_to_all(spread_out, "rows", 0, 0, axis_index_groups=groups, tiled=True).reshape(keep.shape)
    return mine, lax.ppermute(mine, "rows", swap)


def recip(x):
    y = pl.reciprocal(x, approx=True)
    return y * (2.0 - x * y)


def inv_sqrt(x):
    y = lax.rsqrt(x)
    return y * (1.5 - 0.5 * x * (y * y))


def spread(x):
    return jnp.broadcast_to(x, (8, SIZE))


def eliminate(rows):
    count = len(rows)
    lane = lax.broadcasted_iota(jnp.int32, (8, SIZE), 1)
    sub = lax.broadcasted_iota(jnp.int32, (8, SIZE), 0)
    done = []
    for k in range(count):
        base = 8 * k
        inside = (lane >= base) & (lane < base + 8)
        cols = {(q, i): spread(rows[i][:, base + q : base + q + 1]) for i in range(k, count) for q in range(8)}
        s = {(r, q): spread(cols[q, k][r : r + 1, :]) for r in range(8) for q in range(r + 1)}
        own = jnp.where(inside, jnp.where(lane == base + sub, 1.0, 0.0), rows[k])
        row = [spread(own[q : q + 1, :]) for q in range(8)]
        inv = {}
        m = {}
        for j in range(8):
            inv[j] = recip(s[j, j])
            for i in range(j + 1, 8):
                m[i, j] = s[i, j] * inv[j]
            for i in range(j + 1, 8):
                for t in range(j + 1, i + 1):
                    s[i, t] = s[i, t] - m[i, j] * s[t, j]
                row[i] = row[i] - m[i, j] * row[j]
        out = None
        for p in range(8):
            scaled = row[p] * inv_sqrt(s[p, p])
            out = scaled if out is None else jnp.where(sub == p, scaled, out)
        done.append(jnp.where(lane <= base + sub, out, 0.0))
        z = [row[p] * inv[p] for p in range(8)]
        for q in range(6, -1, -1):
            for p in range(7, q, -1):
                z[q] = z[q] - m[p, q] * z[p]
        for i in range(k + 1, count):
            total = jnp.where(inside, 0.0, rows[i])
            for q in range(8):
                total = total - cols[q, i] * z[q]
            rows[i] = total
    return done


def factor_kernel(place, mine, other, high_ref, low_ref, w, panel, diag, sems):
    n = w.shape[0]
    x, core = place[0], place[1]

    def copies(halves):
        return [
            pltpu.make_async_copy(
                halves[m // HALF].at[m % HALF], w.at[pl.ds(2 * a, 2), pl.ds(2 * b, 2)], sems.at[m]
            )
            for m, (a, b) in enumerate(PAIRS)
        ]

    @pl.when(core == 0)
    def _():
        for copy in copies([mine, other]):
            copy.start()

    @pl.when(core == 1)
    def _():
        for copy in copies([other, mine]):
            copy.start()

    for copy in copies([mine, other]):
        copy.wait()

    def step(k, _):
        done = eliminate([w[k, k, pl.ds(8 * r, 8), :] for r in range(16)])
        for r in range(16):
            diag[pl.ds(8 * r, 8), :] = done[r]
        inverse = diag[...]
        for c in range(n):
            panel[c] = jnp.dot(inverse, w[k, c], preferred_element_type=F32, precision=EXACT)
        panel[k] = inverse
        for c in range(n):
            w[k, c] = panel[c]

        def below(i, _):
            w[i, k] = jnp.zeros((SIZE, SIZE), F32)
            left = panel[i].T
            for c in range(n):
                w[i, c] = w[i, c] - jnp.dot(left, panel[c], preferred_element_type=F32, precision=EXACT)
            return 0

        lax.fori_loop(k + 1, n, below, 0)
        return 0

    for i in range(n):
        for c in range(i - i % 2):
            w[i, c] = jnp.zeros((SIZE, SIZE), F32)
    lax.fori_loop(0, n, step, 0)
    for r in range(2):
        for c in range(n):
            i = 2 * x + r
            value = jnp.where(c <= i, w[i, c], 0.0)
            high = value.astype(BF)
            high_ref[pl.ds(SIZE * r, SIZE), pl.ds(SIZE * c, SIZE)] = high
            low_ref[pl.ds(SIZE * r, SIZE), pl.ds(SIZE * c, SIZE)] = (value - high.astype(F32)).astype(BF)


def factor(place, mine, other):
    n = 8
    vmem = pl.BlockSpec(memory_space=pltpu.VMEM)
    return pl.pallas_call(
        factor_kernel,
        out_shape=[jax.ShapeDtypeStruct((2 * SIZE, n * SIZE), BF)] * 2,
        grid_spec=pltpu.PrefetchScalarGridSpec(
            num_scalar_prefetch=1,
            grid=(),
            in_specs=[ANY] * 2,
            out_specs=[vmem] * 2,
            scratch_shapes=[
                pltpu.VMEM((n, n, SIZE, SIZE), F32),
                pltpu.VMEM((n, SIZE, SIZE), F32),
                pltpu.VMEM((SIZE, SIZE), F32),
                pltpu.SemaphoreType.DMA((len(PAIRS),)),
            ],
        ),
        compiler_params=params(24),
        cost_estimate=pl.CostEstimate(flops=80_000_000_000, bytes_accessed=4 * MIB, transcendentals=0),
        name="factor",
    )(place, mine, other)


def apply_kernel(place, f0, f1, f2, f3, high, low, out):
    x = place[0]
    t = pl.program_id(0)
    per = f0.shape[1]
    width = f0.shape[-1]
    dims = (((1,), (1,)), ((), ()))
    for s, f in enumerate((f0, f1, f2, f3)):
        quarter = lax.rem(x + 4 - s, 4)
        left = jnp.concatenate([f[p].reshape(per * SIZE, width) for p in range(4)], axis=1)
        value = lax.dot_general(left, high[...], dims, preferred_element_type=F32)
        value = value + lax.dot_general(left, low[...], dims, preferred_element_type=F32)
        out[quarter, pl.ds(t * per, per)] = value.reshape(per, SIZE, width)


def apply(place, pieces, high, low):
    width = pieces[0].shape[-1]
    per = 2
    whole = pl.BlockSpec(high.shape, lambda t, *_: (0, 0))
    return pl.pallas_call(
        apply_kernel,
        out_shape=jax.ShapeDtypeStruct((4, 8, SIZE, width), F32),
        grid_spec=pltpu.PrefetchScalarGridSpec(
            num_scalar_prefetch=1,
            grid=(8 // per,),
            in_specs=[pl.BlockSpec((4, per, SIZE, width), lambda t, *_: (0, t, 0, 0))] * 4 + [whole, whole],
            out_specs=pl.BlockSpec((4, 8, SIZE, width), lambda t, *_: (0, 0, 0, 0)),
        ),
        compiler_params=params(32),
        cost_estimate=pl.CostEstimate(flops=4 * 1024 * 1024 * 256 * 4, bytes_accessed=14 * MIB, transcendentals=0),
        name="apply",
    )(place, *pieces, high, low)


def shards(vectors, blocks, columns):
    block_rows = blocks.shape[0]
    width = vectors.shape[1]
    row = lax.axis_index("rows")
    x = lax.axis_index("vecs")
    vecs = lax.axis_size("vecs")
    total_rows = vectors.shape[0] * lax.axis_size("rows")
    idx = columns - row * block_rows + REACH
    place = jnp.stack([x, lax.rem(row, 2)]).astype(jnp.int32)
    start = vectors.reshape(block_rows, SIZE, width)
    older = None
    current = rounded = [(start, 0), (start, 8), (start, 24)]
    low, high = start[:8], start[24:]
    for step in range(DEGREE):
        last = step == DEGREE - 1
        halo = exchange_halo(low, high)
        middle = filter_middle(step, last, idx, blocks, rounded, current, older)
        mid_new = middle[-1]
        edges = filter_edges(step, last, idx, place, blocks, halo, rounded, current, older, mid_new)
        if not last:
            fresh_low, fresh_high, low, high = edges
            older = current
            current = [(fresh_low, 0), (middle[0], 0), (fresh_high, 0)]
            rounded = [(low, 0), (mid_new, 0), (high, 0)]
    shift = lambda a, s: lax.ppermute(a, "vecs", [(i, (i + s) % vecs) for i in range(vecs)])
    got = [shift(edges[s], s) for s in range(1, vecs)]
    keep, send, quarter = gram(total_rows, place, edges[0], got)
    mine, other = sum_everywhere(keep, send)
    quarter, mine, other = lax.optimization_barrier((quarter, mine, other))
    pieces = [quarter] + [shift(quarter, s) for s in range(1, vecs)]
    inverse_high, inverse_low = factor(place, mine, other)
    return apply(place, pieces, inverse_high, inverse_low).reshape(vectors.shape)


def solution(mesh):
    in_specs = (P("rows", "vecs"), P("rows", None, None, None), P("rows", None))
    out_specs = P("rows", "vecs")
    return jax.shard_map(shards, mesh=mesh, in_specs=in_specs, out_specs=out_specs, check_vma=False)
```

time: 782 us -> 273 us (0.35); the launches traced: 773 us -> 272 us
  other arithmetic: 287 us -> 0.34 us
  waiting for transfers between devices: 280 us -> 73.8 us
  Pallas kernels: 0 us -> 103 us
  matrix products: 91 us -> 0 us
  local copies, waits for them, and re-layouts: 75.8 us -> 5.66 us
  blocking collectives: 0 us -> 55.4 us
  between operations: 18.8 us -> 0.26 us
  starting transfers between devices: 20.1 us -> 33.6 us
    another operation x33 -> x1, other arithmetic: 256 us -> 0.07 us  [shards(): place = jnp.stack([x, lax.rem(row, 2)]).astype(jnp.int32)]
    all_gather x2 -> x0, waiting for transfers between devices: 142 us -> none  [the longest x1 94.6 us: shards(): whole_block = lax.all_gather(final, 'vecs', axis=1, tiled=True)]
    psum x1 -> x0, waiting for transfers between devices: 106 us -> none  [shards(): summed = lax.psum(panel, 'rows')]
    pallas_call x0 -> x11, Pallas kernels: none -> 103 us  [the longest x1 70.7 us: factor(): pl.pallas_call(factor_kernel, out_shape=[jax.ShapeDtypeStruct((2 * SIZE,...]
    all_to_all x0 -> x2, blocking collectives: none -> 55.4 us  [the longest x1 34.9 us: sum_everywhere(): lax.all_to_all(parts, 'rows', 0, 0, axis_index_groups=groups, tiled=True)]
    dot_general x7 -> x0, matrix products: 45.7 us -> none  [the longest x4 30.1 us: product(): jnp.einsum('rjab,rjbk->rak', blocks, picked, preferred_element_type=jnp.f...]
    another operation x29 -> x0, matrix products: 45.3 us -> none  [the longest x14 22.9 us: shards(): lower = jnp.linalg.cholesky(gram_matrix)]
    ppermute x8 -> x19, waiting for transfers between devices: 32.3 us -> 73.8 us  [the longest x6 39.9 us: shards(): lax.ppermute(a, 'vecs', [(i, (i + s) % vecs) for i in range(vecs)])]
  transfers between devices with their start and end apart: 11 -> 19, of which waited for: 11 -> 15; matrix products, arithmetic and copies ran while one was open for 0% -> 0% of each run, Pallas kernels for 0% -> 30%
where the time goes in v1:
time: 273 us; the launch traced here: 272 us
  Pallas kernels  103 us (38%)
  waiting for transfers between devices  73.8 us (27%)
  blocking collectives  55.4 us (20%)
  starting transfers between devices  33.6 us (12%)
  local copies, waits for them, and re-layouts  5.66 us (2%)
    pallas_call x1, Pallas kernels, factor(): pl.pallas_call(factor_kernel, out_shape=[jax.ShapeDtypeStruct((2 * SIZE,...  70.7 us
    ppermute x6, waiting for transfers between devices, shards(): lax.ppermute(a, 'vecs', [(i, (i + s) % vecs) for i in range(vecs)])  39.9 us
    all_to_all x1, blocking collectives, sum_everywhere(): lax.all_to_all(parts, 'rows', 0, 0, axis_index_groups=groups, tiled=True)  34.9 us
    ppermute x8, waiting for transfers between devices, exchange_halo(): return (lax.ppermute(high, 'rows', up), lax.ppermute(low, 'rows', down))  23.8 us
    all_to_all x1, blocking collectives, sum_everywhere(): lax.all_to_all(spread_out, 'rows', 0, 0, axis_index_groups=groups, tiled=...  20.5 us
    ppermute x8, starting transfers between devices, exchange_halo(): return (lax.ppermute(high, 'rows', up), lax.ppermute(low, 'rows', down))  19.6 us
    pallas_call x4, Pallas kernels, filter_edges(): pl.pallas_call(functools.partial(edge_kernel, step, last, offsets), out_s...  11.3 us
    pallas_call x4, Pallas kernels, filter_middle(): pl.pallas_call(functools.partial(middle_kernel, step, last, offsets), out...  10.4 us
  transfers between devices with their start and end apart: 19, of which 15 were waited for; matrix products, arithmetic and copies ran while one was open for 0% of the time, Pallas kernels for 30%

profile of v1, /device:TPU:1, one launch (start us, length us, event | category | flops | bytes accessed | tf_op | source)
XLA Modules:
  0.0 272.4 jit_solution(17011102354155841632)
XLA Ops:
  0.0 0.0 copy-start.3
  0.0 1.4 fusion
  1.4 4.6 %collective-permute-start = (bf16[8,128,256]{2,1,0:T(8,128)(2,1)S(1)}, bf16[8,128,256]{2,1,0:T(8,128)(2,1)S(1)}, u32[]{:S(2)}, u32[]{:S(2)}) collective-permute-start(bf16[8,128,256]{2,1,0:T(8,128)(2,1)S(1)} %bitcast.26), channel_id=1, source_target_pairs={{0,4},{4,8},{8,12},{12,16},{16,20},{20,24},{24,28},{28,32},{32,36}... | collective-permute-start | bytes 1572872 | tf_op jit(solution)/shard_map/ppermute | solution.py:215
  6.0 1.9 collective-permute-start.1
  7.9 0.0 copy-done.3
  7.9 0.1 copy.4
  8.0 0.1 pad_add_fusion.place
  8.1 4.0 %collective-permute-done.refs_2_ = bf16[8,128,256]{2,1,0:T(8,128)(2,1)S(1)} collective-permute-done((bf16[8,128,256]{2,1,0:T(8,128)(2,1)S(1)}, bf16[8,128,256]{2,1,0:T(8,128)(2,1)S(1)}, u32[]{:S(2)}, u32[]{:S(2)}) %collective-permute-start) | collective-permute-done | bytes 524320 | tf_op jit(solution)/shard_map/ppermute | solution.py:215
  12.1 4.4 %collective-permute-done.1.refs_6_ = bf16[8,128,256]{2,1,0:T(8,128)(2,1)S(1)} collective-permute-done((bf16[8,128,256]{2,1,0:T(8,128)(2,1)S(1)}, bf16[8,128,256]{2,1,0:T(8,128)(2,1)S(1)}, u32[]{:S(2)}, u32[]{:S(2)}) %collective-permute-start.1) | collective-permute-done | bytes 524320 | tf_op jit(solution)/shard_map/ppermute | solution.py:215
  16.5 2.5 copy-done
  19.0 1.6 copy-done.1
  20.6 2.7 %filter_edges.4 = (f32[8,128,256]{2,1,0:T(8,128)S(1)}, f32[8,128,256]{2,1,0:T(8,128)S(1)}, bf16[8,128,256]{2,1,0:T(8,128)(2,1)S(1)}, bf16[8,128,256]{2,1,0:T(8,128)(2,1)S(1)}) custom-call(s32[32,5]{1,0:T(8,128)S(1)} %subtract_add_fusion.idx, s32[2]{0:T(128)S(1)} %pad_add_fusion.place, bf16[32,5,128,128]{3,2,1,0:T(8,128)(2,1)S(1)} %copy-done, ...), custom_call_target="tpu_custom_call" | custom-call | flops 671088640 | bytes 12582912 | tf_op jit(solution)/shard_map/filter_edges/pallas_call | solution.py:166
  23.3 1.9 collective-permute-start.2
  25.2 2.4 collective-permute-start.3
  27.7 0.0 slice-done
  27.7 0.0 slice-done.1
  27.7 0.0 copy-done.2
  27.7 2.6 filter_middle.4
  30.3 1.0 collective-permute-done.2.refs_2_
  31.3 4.4 %collective-permute-done.3.refs_6_ = bf16[8,128,256]{2,1,0:T(8,128)(2,1)S(1)} collective-permute-done((bf16[8,128,256]{2,1,0:T(8,128)(2,1)S(1)}, bf16[8,128,256]{2,1,0:T(8,128)(2,1)S(1)}, u32[]{:S(2)}, u32[]{:S(2)}) %collective-permute-start.3) | collective-permute-done | bytes 524320 | tf_op jit(solution)/shard_map/ppermute | solution.py:215
  35.7 2.8 %filter_edges.5 = (f32[8,128,256]{2,1,0:T(8,128)S(1)}, f32[8,128,256]{2,1,0:T(8,128)S(1)}, bf16[8,128,256]{2,1,0:T(8,128)(2,1)S(1)}, bf16[8,128,256]{2,1,0:T(8,128)(2,1)S(1)}) custom-call(s32[32,5]{1,0:T(8,128)S(1)} %subtract_add_fusion.idx, s32[2]{0:T(128)S(1)} %pad_add_fusion.place, bf16[32,5,128,128]{3,2,1,0:T(8,128)(2,1)S(1)} %bitcast.9, ...), custom_call_target="tpu_custom_call" | custom-call | flops 671088640 | bytes 12582912 | tf_op jit(solution)/shard_map/filter_edges/pallas_call | solution.py:166
  38.5 1.9 collective-permute-start.4
  40.4 2.4 collective-permute-start.5
  42.9 2.6 filter_middle.5
  45.5 1.0 collective-permute-done.4.refs_2_
  46.5 4.4 %collective-permute-done.5.refs_6_ = bf16[8,128,256]{2,1,0:T(8,128)(2,1)S(1)} collective-permute-done((bf16[8,128,256]{2,1,0:T(8,128)(2,1)S(1)}, bf16[8,128,256]{2,1,0:T(8,128)(2,1)S(1)}, u32[]{:S(2)}, u32[]{:S(2)}) %collective-permute-start.5) | collective-permute-done | bytes 524320 | tf_op jit(solution)/shard_map/ppermute | solution.py:215
  50.9 2.7 %filter_edges.6 = (f32[8,128,256]{2,1,0:T(8,128)S(1)}, f32[8,128,256]{2,1,0:T(8,128)S(1)}, bf16[8,128,256]{2,1,0:T(8,128)(2,1)S(1)}, bf16[8,128,256]{2,1,0:T(8,128)(2,1)S(1)}) custom-call(s32[32,5]{1,0:T(8,128)S(1)} %subtract_add_fusion.idx, s32[2]{0:T(128)S(1)} %pad_add_fusion.place, bf16[32,5,128,128]{3,2,1,0:T(8,128)(2,1)S(1)} %bitcast.9, ...), custom_call_target="tpu_custom_call" | custom-call | flops 671088640 | bytes 12582912 | tf_op jit(solution)/shard_map/filter_edges/pallas_call | solution.py:166
  53.7 1.9 collective-permute-start.6
  55.6 2.4 collective-permute-start.7
  58.0 2.6 filter_middle.6
  60.6 2.6 filter_middle.7.refs_11_
  63.2 0.0 collective-permute-done.6.refs_2_
  63.3 4.5 %collective-permute-done.7.refs_6_ = bf16[8,128,256]{2,1,0:T(8,128)(2,1)S(1)} collective-permute-done((bf16[8,128,256]{2,1,0:T(8,128)(2,1)S(1)}, bf16[8,128,256]{2,1,0:T(8,128)(2,1)S(1)}, u32[]{:S(2)}, u32[]{:S(2)}) %collective-permute-start.7) | collective-permute-done | bytes 524320 | tf_op jit(solution)/shard_map/ppermute | solution.py:215
  67.8 3.1 %filter_edges.7 = (bf16[8,128,256]{2,1,0:T(8,128)(2,1)S(1)}, bf16[8,128,256]{2,1,0:T(8,128)(2,1)S(1)}, bf16[8,128,256]{2,1,0:T(8,128)(2,1)S(1)}, bf16[8,128,256]{2,1,0:T(8,128)(2,1)S(1)}) custom-call(s32[32,5]{1,0:T(8,128)S(1)} %subtract_add_fusion.idx, s32[2]{0:T(128)S(1)} %pad_add_fusion.place, bf16[32,5,128,128]{3,2,1,0:T(8,128)(2,1)S(1)} %bitcast.9, ...), custom_call_target="tpu_custom_call" | custom-call | flops 671088640 | bytes 12582912 | tf_op jit(solution)/shard_map/filter_edges/pallas_call | solution.py:166
  70.8 1.3 collective-permute-start.8
  72.1 2.5 collective-permute-start.9
  74.6 1.1 collective-permute-start.10
  75.7 9.4 %collective-permute-done.8.got1 = bf16[8,128,256]{2,1,0:T(8,128)(2,1)S(1)} collective-permute-done((bf16[8,128,256]{2,1,0:T(8,128)(2,1)S(1)}, bf16[8,128,256]{2,1,0:T(8,128)(2,1)S(1)}, u32[]{:S(2)}, u32[]{:S(2)}) %collective-permute-start.8) | collective-permute-done | bytes 524320 | tf_op jit(solution)/shard_map/ppermute | solution.py:481
  85.1 8.2 %collective-permute-done.9.got2 = bf16[8,128,256]{2,1,0:T(8,128)(2,1)S(1)} collective-permute-done((bf16[8,128,256]{2,1,0:T(8,128)(2,1)S(1)}, bf16[8,128,256]{2,1,0:T(8,128)(2,1)S(1)}, u32[]{:S(2)}, u32[]{:S(2)}) %collective-permute-start.9) | collective-permute-done | bytes 524320 | tf_op jit(solution)/shard_map/ppermute | solution.py:481
  93.3 0.0 collective-permute-done.10.got3
  93.3 2.6 gram.1
  96.0 0.1 collective-permute-start.11
  96.1 3.0 %collective-permute-done.11 = f32[5,2,2,128,128]{4,3,2,1,0:T(8,128)S(1)} collective-permute-done((f32[5,2,2,128,128]{4,3,2,1,0:T(8,128)S(1)}, f32[5,2,2,128,128]{4,3,2,1,0:T(8,128)S(1)}, u32[]{:S(2)}, u32[]{:S(2)}) %collective-permute-start.11) | collective-permute-done | bytes 1310752 | tf_op jit(solution)/shard_map/ppermute | solution.py:277
  99.1 0.2 add.20
  99.3 34.9 %all_to_all.10 = f32[16,160,128]{2,1,0:T(8,128)S(1)} all-to-all(f32[16,160,128]{2,1,0:T(8,128)S(1)} %bitcast.24), channel_id=1, replica_groups={{0,8,16,24,32,40,48,56,64,72,80,88,96,104,112,120},{4,12,20,28,36,44,52..., dimensions={0} | all-to-all | bytes 2621440 | tf_op jit(solution)/shard_map/all_to_all | solution.py:279
  134.2 0.1 reduce_sum.9
  134.3 2.4 collective-permute-start.14
  136.7 1.1 collective-permute-start.13
  137.8 0.0 collective-permute-start.12
  137.8 0.3 collective-permute-done.14
  138.2 3.3 %collective-permute-done.13 = f32[160,128]{1,0:T(8,128)S(1)} collective-permute-done((f32[160,128]{1,0:T(8,128)S(1)}, f32[160,128]{1,0:T(8,128)S(1)}, u32[]{:S(2)}, u32[]{:S(2)}) %collective-permute-start.13) | collective-permute-done | bytes 81952 | tf_op jit(solution)/shard_map/ppermute | solution.py:281
  141.5 0.9 collective-permute-done.12
  142.4 0.1 broadcast_in_dim.2
  142.5 20.5 %all_to_all.11 = f32[16,160,128]{2,1,0:T(8,128)S(1)} all-to-all(f32[16,160,128]{2,1,0:T(8,128)S(1)} %broadcast_in_dim.2), channel_id=1, replica_groups={{0,8,16,24,32,40,48,56,64,72,80,88,96,104,112,120},{4,12,20,28,36,44,52..., dimensions={0} | all-to-all | bytes 2621440 | tf_op jit(solution)/shard_map/all_to_all | solution.py:284
  162.9 3.6 %collective-permute-start.15 = (f32[5,2,2,128,128]{4,3,2,1,0:T(8,128)S(1)}, f32[5,2,2,128,128]{4,3,2,1,0:T(8,128)S(1)}, u32[]{:S(2)}, u32[]{:S(2)}) collective-permute-start(f32[5,2,2,128,128]{4,3,2,1,0:T(8,128)S(1)} %bitcast.22), channel_id=1, source_target_pairs={{0,4},{4,0},{8,12},{12,8},{16,20},{20,16},{24,28},{28,24},{32,36},... | collective-permute-start | bytes 3932168 | tf_op jit(solution)/shard_map/ppermute | solution.py:285
  166.6 2.7 collective-permute-done.15.other
  169.2 0.8 collective-permute-start.18
  170.1 0.9 collective-permute-start.17
  171.0 0.1 collective-permute-start.16
  171.1 70.7 %factor.1 = (bf16[256,1024]{1,0:T(8,128)(2,1)S(1)}, bf16[256,1024]{1,0:T(8,128)(2,1)S(1)}) custom-call(s32[2]{0:T(128)S(1)} %pad_add_fusion.place, f32[5,2,2,128,128]{4,3,2,1,0:T(8,128)S(1)} %bitcast.23, f32[5,2,2,128,128]{4,3,2,1,0:T(8,128)S(1)} %collective-permute-done.15.other), custom_call_target="tpu_custom_call" | custom-call | flops 80000000000 | bytes 4194304 | tf_op jit(solution)/shard_map/factor/pallas_call | solution.py:403
  241.8 0.0 collective-permute-done.18.f3
  241.8 0.0 collective-permute-done.17.f2
  241.8 22.2 %collective-permute-done.16.f1 = bf16[4,8,128,256]{3,2,1,0:T(8,128)(2,1)S(1)} collective-permute-done((bf16[4,8,128,256]{3,2,1,0:T(8,128)(2,1)S(1)}, bf16[4,8,128,256]{3,2,1,0:T(8,128)(2,1)S(1)}, u32[]{:S(2)}, u32[]{:S(2)}) %collective-permute-start.16) | collective-permute-done | bytes 2097184 | tf_op jit(solution)/shard_map/ppermute | solution.py:481
  264.1 8.4 %apply.1 = f32[4,8,128,256]{3,2,1,0:T(8,128)} custom-call(s32[2]{0:T(128)S(1)} %pad_add_fusion.place, bf16[4,8,128,256]{3,2,1,0:T(8,128)(2,1)S(1)} %get-tuple-element.60.f0, bf16[4,8,128,256]{3,2,1,0:T(8,128)(2,1)S(1)} %collective-permute-done.16.f1, bf16[4,8,128,256]{3,2,1,0:T(8,128)(2,1)S(1)} %collective-permute-done.17.f2, ...), custom_call_target="tpu_custom_call" | custom-call | flops 4294967296 | bytes 14680064 | tf_op jit(solution)/shard_map/apply/pallas_call | solution.py:442
  (8 shorter events, 0.0 us)
Async XLA Ops:
  0.0 7.9 %copy-start.3 = (s32[32,5]{0,1:T(8,128)S(1)}, s32[32,5]{0,1:T(8,128)}, u32[]{:S(2)}) copy-start(s32[32,5]{0,1:T(8,128)} %param.5) | copy-start | bytes 1924
  0.0 27.7 %slice-start = ((s8[5242880]{0:T(1024)(128)(4,1)}), s8[1048576]{0:T(1024)(128)(4,1)S(1)}, s32[]{:S(2)}) async-start(s8[5242880]{0:T(1024)(128)(4,1)} %bitcast.8), calls=%async_computation.2 | async-start | bytes 2097152
  1.4 10.7 %collective-permute-start = (bf16[8,128,256]{2,1,0:T(8,128)(2,1)S(1)}, bf16[8,128,256]{2,1,0:T(8,128)(2,1)S(1)}, u32[]{:S(2)}, u32[]{:S(2)}) collective-permute-start(bf16[8,128,256]{2,1,0:T(8,128)(2,1)S(1)} %bitcast.26), channel_id=1, source_target_pairs={{0,4},{4,8},{8,12},{12,16},{16,20},{20,24},{24,28},{28,32},{32,36}... | collective-permute-start | bytes 1572872 | tf_op jit(solution)/shard_map/ppermute | solution.py:215
  6.0 10.5 %collective-permute-start.1 = (bf16[8,128,256]{2,1,0:T(8,128)(2,1)S(1)}, bf16[8,128,256]{2,1,0:T(8,128)(2,1)S(1)}, u32[]{:S(2)}, u32[]{:S(2)}) collective-permute-start(bf16[8,128,256]{2,1,0:T(8,128)(2,1)S(1)} %bitcast.25), channel_id=1, source_target_pairs={{4,0},{8,4},{12,8},{16,12},{20,16},{24,20},{28,24},{32,28},{36,32}... | collective-permute-start | bytes 1572872 | tf_op jit(solution)/shard_map/ppermute | solution.py:215
  16.5 2.5 copy-start
  19.0 1.6 copy-start.1
  20.5 7.1 %slice-start.1 = ((s8[5242880]{0:T(1024)(128)(4,1)}), s8[4194304]{0:T(1024)(128)(4,1)S(1)}, s32[]{:S(2)}) async-start(s8[5242880]{0:T(1024)(128)(4,1)} %bitcast.8), calls=%async_computation.3 | async-start | bytes 8388608
  20.5 7.1 %copy-start.2 = (bf16[4096,256]{1,0:T(8,128)(2,1)S(1)}, bf16[4096,256]{1,0:T(8,128)(2,1)}, u32[]{:S(2)}) copy-start(bf16[4096,256]{1,0:T(8,128)(2,1)} %param.3) | copy-start | bytes 6291460
  23.3 8.0 %collective-permute-start.2 = (bf16[8,128,256]{2,1,0:T(8,128)(2,1)S(1)}, bf16[8,128,256]{2,1,0:T(8,128)(2,1)S(1)}, u32[]{:S(2)}, u32[]{:S(2)}) collective-permute-start(bf16[8,128,256]{2,1,0:T(8,128)(2,1)S(1)} %get-tuple-element.35.refs_5_.refs_3_), channel_id=1, source_target_pairs={{0,4},{4,8},{8,12},{12,16},{16,20},{20,24},{24,28},{28,32},{32,36}... | collective-permute-start | bytes 1572872 | tf_op jit(solution)/shard_map/ppermute | solution.py:215
  25.2 10.5 %collective-permute-start.3 = (bf16[8,128,256]{2,1,0:T(8,128)(2,1)S(1)}, bf16[8,128,256]{2,1,0:T(8,128)(2,1)S(1)}, u32[]{:S(2)}, u32[]{:S(2)}) collective-permute-start(bf16[8,128,256]{2,1,0:T(8,128)(2,1)S(1)} %get-tuple-element.36.refs_3_.refs_1_), channel_id=1, source_target_pairs={{4,0},{8,4},{12,8},{16,12},{20,16},{24,20},{28,24},{32,28},{36,32}... | collective-permute-start | bytes 1572872 | tf_op jit(solution)/shard_map/ppermute | solution.py:215
  38.5 8.0 %collective-permute-start.4 = (bf16[8,128,256]{2,1,0:T(8,128)(2,1)S(1)}, bf16[8,128,256]{2,1,0:T(8,128)(2,1)S(1)}, u32[]{:S(2)}, u32[]{:S(2)}) collective-permute-start(bf16[8,128,256]{2,1,0:T(8,128)(2,1)S(1)} %get-tuple-element.40.refs_5_.refs_3_), channel_id=1, source_target_pairs={{0,4},{4,8},{8,12},{12,16},{16,20},{20,24},{24,28},{28,32},{32,36}... | collective-permute-start | bytes 1572872 | tf_op jit(solution)/shard_map/ppermute | solution.py:215
  40.4 10.5 %collective-permute-start.5 = (bf16[8,128,256]{2,1,0:T(8,128)(2,1)S(1)}, bf16[8,128,256]{2,1,0:T(8,128)(2,1)S(1)}, u32[]{:S(2)}, u32[]{:S(2)}) collective-permute-start(bf16[8,128,256]{2,1,0:T(8,128)(2,1)S(1)} %get-tuple-element.41.refs_3_.refs_1_), channel_id=1, source_target_pairs={{4,0},{8,4},{12,8},{16,12},{20,16},{24,20},{28,24},{32,28},{36,32}... | collective-permute-start | bytes 1572872 | tf_op jit(solution)/shard_map/ppermute | solution.py:215
  53.7 9.6 %collective-permute-start.6 = (bf16[8,128,256]{2,1,0:T(8,128)(2,1)S(1)}, bf16[8,128,256]{2,1,0:T(8,128)(2,1)S(1)}, u32[]{:S(2)}, u32[]{:S(2)}) collective-permute-start(bf16[8,128,256]{2,1,0:T(8,128)(2,1)S(1)} %get-tuple-element.46.refs_3_.refs_5_), channel_id=1, source_target_pairs={{0,4},{4,8},{8,12},{12,16},{16,20},{20,24},{24,28},{28,32},{32,36}... | collective-permute-start | bytes 1572872 | tf_op jit(solution)/shard_map/ppermute | solution.py:215
  55.6 12.2 %collective-permute-start.7 = (bf16[8,128,256]{2,1,0:T(8,128)(2,1)S(1)}, bf16[8,128,256]{2,1,0:T(8,128)(2,1)S(1)}, u32[]{:S(2)}, u32[]{:S(2)}) collective-permute-start(bf16[8,128,256]{2,1,0:T(8,128)(2,1)S(1)} %get-tuple-element.47.refs_1_.refs_3_), channel_id=1, source_target_pairs={{4,0},{8,4},{12,8},{16,12},{20,16},{24,20},{28,24},{32,28},{36,32}... | collective-permute-start | bytes 1572872 | tf_op jit(solution)/shard_map/ppermute | solution.py:215
  70.8 14.3 %collective-permute-start.8 = (bf16[8,128,256]{2,1,0:T(8,128)(2,1)S(1)}, bf16[8,128,256]{2,1,0:T(8,128)(2,1)S(1)}, u32[]{:S(2)}, u32[]{:S(2)}) collective-permute-start(bf16[8,128,256]{2,1,0:T(8,128)(2,1)S(1)} %get-tuple-element.54), channel_id=1, source_target_pairs={{0,1},{1,2},{2,3},{3,0},{4,5},{5,6},{6,7},{7,4},{8,9},{9,10},{10,1... | collective-permute-start | bytes 1572872 | tf_op jit(solution)/shard_map/ppermute | solution.py:481
  72.1 21.2 %collective-permute-start.9 = (bf16[8,128,256]{2,1,0:T(8,128)(2,1)S(1)}, bf16[8,128,256]{2,1,0:T(8,128)(2,1)S(1)}, u32[]{:S(2)}, u32[]{:S(2)}) collective-permute-start(bf16[8,128,256]{2,1,0:T(8,128)(2,1)S(1)} %get-tuple-element.55), channel_id=1, source_target_pairs={{0,2},{1,3},{2,0},{3,1},{4,6},{5,7},{6,4},{7,5},{8,10},{9,11},{10,... | collective-permute-start | bytes 1572872 | tf_op jit(solution)/shard_map/ppermute | solution.py:481
  74.6 18.8 %collective-permute-start.10 = (bf16[8,128,256]{2,1,0:T(8,128)(2,1)S(1)}, bf16[8,128,256]{2,1,0:T(8,128)(2,1)S(1)}, u32[]{:S(2)}, u32[]{:S(2)}) collective-permute-start(bf16[8,128,256]{2,1,0:T(8,128)(2,1)S(1)} %get-tuple-element.56), channel_id=1, source_target_pairs={{0,3},{1,0},{2,1},{3,2},{4,7},{5,4},{6,5},{7,6},{8,11},{9,8},{10,9... | collective-permute-start | bytes 1572872 | tf_op jit(solution)/shard_map/ppermute | solution.py:481
  96.0 3.1 %collective-permute-start.11 = (f32[5,2,2,128,128]{4,3,2,1,0:T(8,128)S(1)}, f32[5,2,2,128,128]{4,3,2,1,0:T(8,128)S(1)}, u32[]{:S(2)}, u32[]{:S(2)}) collective-permute-start(f32[5,2,2,128,128]{4,3,2,1,0:T(8,128)S(1)} %get-tuple-element.59), channel_id=1, source_target_pairs={{0,4},{4,0},{8,12},{12,8},{16,20},{20,16},{24,28},{28,24},{32,36},... | collective-permute-start | bytes 3932168 | tf_op jit(solution)/shard_map/ppermute | solution.py:277
  134.3 3.9 %collective-permute-start.14 = (f32[160,128]{1,0:T(8,128)S(1)}, f32[160,128]{1,0:T(8,128)S(1)}, u32[]{:S(2)}, u32[]{:S(2)}) collective-permute-start(f32[160,128]{1,0:T(8,128)S(1)} %reduce_sum.9), channel_id=1, source_target_pairs={{0,3},{1,0},{2,1},{3,2},{4,7},{5,4},{6,5},{7,6},{8,11},{9,8},{10,9... | collective-permute-start | bytes 245768 | tf_op jit(solution)/shard_map/ppermute | solution.py:281
  136.7 4.8 %collective-permute-start.13 = (f32[160,128]{1,0:T(8,128)S(1)}, f32[160,128]{1,0:T(8,128)S(1)}, u32[]{:S(2)}, u32[]{:S(2)}) collective-permute-start(f32[160,128]{1,0:T(8,128)S(1)} %reduce_sum.9), channel_id=1, source_target_pairs={{0,2},{1,3},{2,0},{3,1},{4,6},{5,7},{6,4},{7,5},{8,10},{9,11},{10,... | collective-permute-start | bytes 245768 | tf_op jit(solution)/shard_map/ppermute | solution.py:281
  137.8 4.6 %collective-permute-start.12 = (f32[160,128]{1,0:T(8,128)S(1)}, f32[160,128]{1,0:T(8,128)S(1)}, u32[]{:S(2)}, u32[]{:S(2)}) collective-permute-start(f32[160,128]{1,0:T(8,128)S(1)} %reduce_sum.9), channel_id=1, source_target_pairs={{0,1},{1,2},{2,3},{3,0},{4,5},{5,6},{6,7},{7,4},{8,9},{9,10},{10,1... | collective-permute-start | bytes 245768 | tf_op jit(solution)/shard_map/ppermute | solution.py:281
  162.9 6.3 %collective-permute-start.15 = (f32[5,2,2,128,128]{4,3,2,1,0:T(8,128)S(1)}, f32[5,2,2,128,128]{4,3,2,1,0:T(8,128)S(1)}, u32[]{:S(2)}, u32[]{:S(2)}) collective-permute-start(f32[5,2,2,128,128]{4,3,2,1,0:T(8,128)S(1)} %bitcast.22), channel_id=1, source_target_pairs={{0,4},{4,0},{8,12},{12,8},{16,20},{20,16},{24,28},{28,24},{32,36},... | collective-permute-start | bytes 3932168 | tf_op jit(solution)/shard_map/ppermute | solution.py:285
  169.2 72.5 %collective-permute-start.18 = (bf16[4,8,128,256]{3,2,1,0:T(8,128)(2,1)S(1)}, bf16[4,8,128,256]{3,2,1,0:T(8,128)(2,1)S(1)}, u32[]{:S(2)}, u32[]{:S(2)}) collective-permute-start(bf16[4,8,128,256]{3,2,1,0:T(8,128)(2,1)S(1)} %get-tuple-element.60.f0), channel_id=1, source_target_pairs={{0,3},{1,0},{2,1},{3,2},{4,7},{5,4},{6,5},{7,6},{8,11},{9,8},{10,9... | collective-permute-start | bytes 6291464 | tf_op jit(solution)/shard_map/ppermute | solution.py:481
  170.1 71.7 %collective-permute-start.17 = (bf16[4,8,128,256]{3,2,1,0:T(8,128)(2,1)S(1)}, bf16[4,8,128,256]{3,2,1,0:T(8,128)(2,1)S(1)}, u32[]{:S(2)}, u32[]{:S(2)}) collective-permute-start(bf16[4,8,128,256]{3,2,1,0:T(8,128)(2,1)S(1)} %get-tuple-element.60.f0), channel_id=1, source_target_pairs={{0,2},{1,3},{2,0},{3,1},{4,6},{5,7},{6,4},{7,5},{8,10},{9,11},{10,... | collective-permute-start | bytes 6291464 | tf_op jit(solution)/shard_map/ppermute | solution.py:481
  171.0 93.1 %collective-permute-start.16 = (bf16[4,8,128,256]{3,2,1,0:T(8,128)(2,1)S(1)}, bf16[4,8,128,256]{3,2,1,0:T(8,128)(2,1)S(1)}, u32[]{:S(2)}, u32[]{:S(2)}) collective-permute-start(bf16[4,8,128,256]{3,2,1,0:T(8,128)(2,1)S(1)} %get-tuple-element.60.f0), channel_id=1, source_target_pairs={{0,1},{1,2},{2,3},{3,0},{4,5},{5,6},{6,7},{7,4},{8,9},{9,10},{10,1... | collective-permute-start | bytes 6291464 | tf_op jit(solution)/shard_map/ppermute | solution.py:481

commit v2 on v1

v2 whole, which is shorter than its diff:
```python
import functools

import jax
import jax.numpy as jnp
from jax import lax
from jax.experimental import pallas as pl
from jax.experimental.pallas import tpu as pltpu
from jax.sharding import PartitionSpec as P

DEGREE = 4
filter_center = 0.25
filter_radius = 1.25

F32 = jnp.float32
BF = jnp.bfloat16
EXACT = lax.Precision.HIGHEST
SIZE = 128
REACH = 8
MIB = 1 << 20

ANY = pl.BlockSpec(memory_space=pl.ANY)


def params(mib):
    return pltpu.CompilerParams(vmem_limit_bytes=mib * MIB)


def load_all(pairs, sems):
    copies = [pltpu.make_async_copy(src, dst, sems.at[n]) for n, (src, dst) in enumerate(pairs)]
    for copy in copies:
        copy.start()
    for copy in copies:
        copy.wait()


def row_product(idx, row, shift, blocks_ref, r, pad):
    count = blocks_ref.shape[1]
    left = jnp.concatenate([blocks_ref[r, j] for j in range(count)], axis=1)
    right = jnp.concatenate([pad[idx[row, j] - shift] for j in range(count)], axis=0)
    return jnp.dot(left, right, preferred_element_type=F32)


def recurrence(step, product, current, older):
    scale = (2.0 if step else 1.0) / filter_radius
    newer = scale * product - (scale * filter_center) * current.astype(F32)
    return newer - older.astype(F32) if step else newer


def far_kernel(step, last, source_at, idx, place, *refs):
    refs = list(refs)
    take = lambda n: [refs.pop(0) for _ in range(n)]
    (blocks,) = take(1)
    halo, far, mid = take(3)
    (current,) = take(1)
    older = take(1)[0] if step else None
    if last:
        near_new, mid_new = take(2)
        sends = take(4)
        pad, sems, rounded, out_sems = take(4)
    else:
        fresh, rounded = take(2)
        pad, sems = take(2)
    g = pl.program_id(0)
    per = blocks.shape[0]
    core = place[1]
    far_at = 24 * core if source_at else 0
    mid_at = 8 if source_at else 0

    @pl.when(g == 0)
    def _():
        load_all(
            [
                (halo, pad.at[pl.ds(16 * core, 8)]),
                (far.at[pl.ds(far_at, 8)], pad.at[pl.ds(8, 8)]),
                (mid.at[pl.ds(mid_at + 8 * core, 8)], pad.at[pl.ds(16 * (1 - core), 8)]),
            ],
            sems,
        )

    for r in range(per):
        product = row_product(idx, 24 * core + g * per + r, 24 * core, blocks, r, pad)
        newer = recurrence(step, product, current[r], older[r] if step else None)
        if last:
            rounded[g * per + r] = newer.astype(BF)
        else:
            fresh[r] = newer
            rounded[r] = newer.astype(BF)

    if last:

        @pl.when(g == pl.num_programs(0) - 1)
        def _():
            sources = {
                0: [rounded, mid_new.at[pl.ds(0, 8)], mid_new.at[pl.ds(8, 8)], near_new],
                1: [near_new, mid_new.at[pl.ds(0, 8)], mid_new.at[pl.ds(8, 8)], rounded],
            }
            for s in range(4):
                for q in range(4):
                    for c in range(2):

                        @pl.when((lax.rem(place[0] + s, 4) == q) & (core == c))
                        def _():
                            pltpu.make_async_copy(sources[c][q], sends[s], out_sems.at[s]).start()

            for s in range(4):
                pltpu.make_async_copy(rounded, sends[s], out_sems.at[s]).wait()


def rest_kernel(step, last, source_at, idx, place, *refs):
    refs = list(refs)
    take = lambda n: [refs.pop(0) for _ in range(n)]
    blocks = take(2)
    halo, near, mid, far = take(4)
    current = take(2)
    older = take(2) if step else None
    fresh = None if last else take(2)
    rounded = take(2)
    pad, sems = take(2)
    g = pl.program_id(0)
    core = place[1]
    near_at = 24 * (1 - core)
    far_at = 24 * core

    @pl.when(g == 0)
    def _():
        load_all(
            [
                (halo, pad.at[pl.ds(40 * (1 - core), 8)]),
                (near.at[pl.ds(near_at if source_at else 0, 8)], pad.at[pl.ds(8 + near_at, 8)]),
                (mid.at[pl.ds(8 if source_at else 0, 16)], pad.at[pl.ds(16, 16)]),
                (far.at[pl.ds(far_at if source_at else 0, 8)], pad.at[pl.ds(8 + far_at, 8)]),
            ],
            sems,
        )

    for n, first in enumerate((near_at, 8)):
        per = blocks[n].shape[0]
        for r in range(per):
            product = row_product(idx, first + g * per + r, 0, blocks[n], r, pad)
            newer = recurrence(step, product, current[n][r], older[n][r] if step else None)
            if not last:
                fresh[n][r] = newer
            rounded[n][r] = newer.astype(BF)


def filter_call(kernel, name, step, last, source_at, idx, place, parts, moved, halo, rounded, current, older, extra):
    width = halo.shape[-1]
    nnz = parts["blocks"].shape[1]
    blocks = parts["blocks"]
    in_specs, operands, shapes, out_specs = [], [], [], []
    groups = parts["groups"]
    for key, count, per, first in groups:
        in_specs.append(
            pl.BlockSpec((per, nnz, SIZE, SIZE), lambda g, idx, place, per=per, first=first: (g + first(place[1]) // per, 0, 0, 0))
        )
        operands.append(blocks)
    in_specs += [ANY] * (1 + len(moved))
    operands += [halo] + [rounded[key] for key in moved]
    for arrays in [current] + ([older] if step else []):
        at = arrays.get("whole", False)
        for key, count, per, first in groups:
            index = (
                (lambda g, idx, place, per=per, first=first: (g + first(place[1]) // per, 0, 0))
                if at
                else (lambda g, idx, place: (g, 0, 0))
            )
            in_specs.append(pl.BlockSpec((per, SIZE, width), index))
            operands.append(arrays[key])
    scratch = [pltpu.VMEM((parts["window"], SIZE, width), BF), pltpu.SemaphoreType.DMA((1 + len(moved),))]
    for kind in (F32, BF):
        if kind is F32 and last:
            continue
        for key, count, per, first in groups:
            shapes.append(jax.ShapeDtypeStruct((count, SIZE, width), kind))
            out_specs.append(pl.BlockSpec((per, SIZE, width), lambda g, idx, place: (g, 0, 0)))
    if extra:
        in_specs += [ANY] * len(extra)
        operands += extra
        shapes = [jax.ShapeDtypeStruct((8, SIZE, width), BF)] * 4
        out_specs = [ANY] * 4
        scratch += [pltpu.VMEM((8, SIZE, width), BF), pltpu.SemaphoreType.DMA((4,))]
    total = sum(count for _, count, _, _ in groups)
    return pl.pallas_call(
        functools.partial(kernel, step, last, source_at),
        out_shape=shapes,
        grid_spec=pltpu.PrefetchScalarGridSpec(
            num_scalar_prefetch=2,
            grid=(4,),
            in_specs=in_specs,
            out_specs=out_specs,
            scratch_shapes=scratch,
        ),
        compiler_params=params(24),
        cost_estimate=pl.CostEstimate(
            flops=total * nnz * 2 * SIZE * SIZE * width, bytes_accessed=total * MIB // 2, transcendentals=0
        ),
        name=name,
    )(idx, place, *operands)


def chebyshev(vectors, blocks, idx, place):
    rows = lax.axis_size("rows")
    core = place[1]
    within = [(i, i ^ 1) for i in range(rows)]
    between = [(i, i + 1 if i % 2 else i - 1) for i in range(1, rows - 1)]
    far_group = ("far", 8, 2, lambda c: 24 * c)
    near_group = ("near", 8, 2, lambda c: 24 * (1 - c))
    mid_group = ("mid", 16, 4, lambda c: 8)
    far_parts = dict(blocks=blocks, groups=[far_group], window=24)
    rest_parts = dict(blocks=blocks, groups=[near_group, mid_group], window=48)
    start = dict(near=vectors, mid=vectors, far=vectors, whole=True)
    rounded = current = start
    older = None
    far_out = lax.dynamic_slice_in_dim(vectors, 24 * core, 8, 0)
    near_out = lax.dynamic_slice_in_dim(vectors, 24 * (1 - core), 8, 0)
    for step in range(DEGREE):
        last = step == DEGREE - 1
        far_halo = lax.ppermute(far_out, "rows", between)
        near_halo = lax.ppermute(near_out, "rows", within)
        common = (step, last, step == 0, idx, place)
        rest = filter_call(
            rest_kernel, "filter_rest", *common, rest_parts, ["near", "mid", "far"], near_halo, rounded, current, older, None
        )
        extra = rest if last else None
        far = filter_call(
            far_kernel, "filter_far", *common, far_parts, ["far", "mid"], far_halo, rounded, current, older, extra
        )
        if last:
            return far
        older = current
        current = dict(near=rest[0], mid=rest[1], far=far[0])
        rounded = dict(near=rest[2], mid=rest[3], far=far[1])
        near_out, far_out = rounded["near"], rounded["far"]


PAIRS = [(a, b) for a in range(4) for b in range(a, 4)]
HALF = len(PAIRS) // 2


def gram_kernel(total_rows, place, own, got1, got2, got3, keep, send, next1, next2, next3, f, g, sems, out_sems):
    pieces = [own, got1, got2, got3]
    x, core = place[0], place[1]
    load_all([(pieces[s], f.at[lax.rem(x + 4 - s, 4)]) for s in range(4)], sems)
    copies = [
        pltpu.make_async_copy(f.at[lax.rem(x + s + r, 4)], out.at[r - 1], out_sems.at[3 * s + r - 2])
        for s, out in ((1, next1), (2, next2), (3, next3))
        for r in (1, 2, 3)
    ]
    for copy in copies:
        copy.start()
    depth = 8 * SIZE
    width = f.shape[-1]
    for a in range(4):
        left = f[a].reshape(depth, width).T
        for b in range(a, 4):
            n = PAIRS.index((a, b))
            tile = jnp.dot(left, f[b].reshape(depth, width), preferred_element_type=F32)
            g[n // HALF, n % HALF] = tile * (1.0 / total_rows)
    copies.append(pltpu.make_async_copy(g.at[core], keep, out_sems.at[0]))
    copies.append(pltpu.make_async_copy(g.at[1 - core], send, out_sems.at[1]))
    for copy in copies[-2:]:
        copy.start()
    for copy in copies:
        copy.wait()


def gram(total_rows, place, own, got):
    width = own.shape[-1]
    half = jax.ShapeDtypeStruct((HALF, width, width), F32)
    return pl.pallas_call(
        functools.partial(gram_kernel, total_rows),
        out_shape=[half, half] + [jax.ShapeDtypeStruct((3, 8, SIZE, width), BF)] * 3,
        grid_spec=pltpu.PrefetchScalarGridSpec(
            num_scalar_prefetch=1,
            grid=(),
            in_specs=[ANY] * 4,
            out_specs=[ANY] * 5,
            scratch_shapes=[
                pltpu.VMEM((4, 8, SIZE, width), BF),
                pltpu.VMEM((2, HALF, width, width), F32),
                pltpu.SemaphoreType.DMA((4,)),
                pltpu.SemaphoreType.DMA((11,)),
            ],
        ),
        compiler_params=params(24),
        cost_estimate=pl.CostEstimate(flops=10 * 2 * 1024 * 256 * 256, bytes_accessed=8 * MIB, transcendentals=0),
        name="gram",
    )(place, own, *got)


def sum_everywhere(keep, send):
    rows = lax.axis_size("rows")
    vecs = lax.axis_size("vecs")
    swap = [(i, i ^ 1) for i in range(rows)]
    groups = [list(range(c, rows, 2)) for c in range(2)]
    count = rows // 2
    mine = keep + lax.ppermute(send, "rows", swap)
    parts = mine.reshape(count, -1, SIZE)
    parts = lax.all_to_all(parts, "rows", 0, 0, axis_index_groups=groups, tiled=True)
    part = jnp.sum(parts, axis=0)
    others = [lax.ppermute(part, "vecs", [(i, (i + s) % vecs) for i in range(vecs)]) for s in range(1, vecs)]
    part = part + sum(others)
    spread_out = jnp.broadcast_to(part[None], (count,) + part.shape)
    mine = lax.all_to_all(spread_out, "rows", 0, 0, axis_index_groups=groups, tiled=True).reshape(keep.shape)
    return mine, lax.ppermute(mine, "rows", swap), part


def recip(x):
    return pl.reciprocal(x, approx=True)


def inv_sqrt(x):
    y = lax.rsqrt(x)
    return y * (1.5 - 0.5 * x * (y * y))


def spread(x):
    return jnp.broadcast_to(x, (8, SIZE))


def tree_sum(terms):
    while len(terms) > 1:
        terms = [terms[i] + terms[i + 1] if i + 1 < len(terms) else terms[i] for i in range(0, len(terms), 2)]
    return terms[0]


def eliminate(rows):
    count = len(rows)
    lane = lax.broadcasted_iota(jnp.int32, (8, SIZE), 1)
    sub = lax.broadcasted_iota(jnp.int32, (8, SIZE), 0)
    done = []
    for k in range(count):
        base = 8 * k
        inside = (lane >= base) & (lane < base + 8)
        cols = {(q, i): spread(rows[i][:, base + q : base + q + 1]) for i in range(k, count) for q in range(8)}
        s = {(r, q): spread(cols[q, k][r : r + 1, :]) for r in range(8) for q in range(r + 1)}
        own = jnp.where(inside, jnp.where(lane == base + sub, 1.0, 0.0), rows[k])
        row = [spread(own[q : q + 1, :]) for q in range(8)]
        inv = {}
        m = {}
        for j in range(8):
            inv[j] = recip(s[j, j])
            for i in range(j + 1, 8):
                m[i, j] = s[i, j] * inv[j]
            for i in range(j + 1, 8):
                for t in range(j + 1, i + 1):
                    term = (s[i, j] * s[t, j]) * inv[j] if i == t else m[i, j] * s[t, j]
                    s[i, t] = s[i, t] - term
                row[i] = row[i] - m[i, j] * row[j]
        out = None
        for p in range(8):
            scaled = row[p] * inv_sqrt(s[p, p])
            out = scaled if out is None else jnp.where(sub == p, scaled, out)
        done.append(jnp.where(lane <= base + sub, out, 0.0))
        z = [row[p] * inv[p] for p in range(8)]
        for q in range(6, -1, -1):
            for p in range(7, q, -1):
                z[q] = z[q] - m[p, q] * z[p]
        for i in range(k + 1, count):
            rows[i] = jnp.where(inside, 0.0, rows[i]) - tree_sum([cols[q, i] * z[q] for q in range(8)])
    return done


def split3(value):
    high = value.astype(BF)
    rest = value - high.astype(F32)
    mid = rest.astype(BF)
    return high, mid, (rest - mid.astype(F32)).astype(BF)


def factor_kernel(place, mine, other, high_ref, low_ref, w, diag, following, left, right, sems):
    n = 8
    x, core = place[0], place[1]
    at = lambda i: pl.ds(pl.multiple_of(i * SIZE, SIZE), SIZE)
    exact = functools.partial(jnp.dot, preferred_element_type=F32, precision=EXACT)

    def copies(halves):
        return [
            pltpu.make_async_copy(
                halves[m // HALF].at[m % HALF], w.at[pl.ds(256 * a, 256), pl.ds(256 * b, 256)], sems.at[m]
            )
            for m, (a, b) in enumerate(PAIRS)
        ]

    @pl.when(core == 0)
    def _():
        for copy in copies([mine, other]):
            copy.start()

    @pl.when(core == 1)
    def _():
        for copy in copies([other, mine]):
            copy.start()

    diag[...] = jnp.zeros(diag.shape, F32)
    left[...] = jnp.zeros(left.shape, BF)
    for copy in copies([mine, other]):
        copy.wait()
    for a in range(1, 4):
        w[pl.ds(256 * a, 256), pl.ds(0, 256 * a)] = jnp.zeros((256, 256 * a), F32)
    w[pl.ds(n * SIZE, (n - 1) * SIZE), :] = jnp.zeros(((n - 1) * SIZE, n * SIZE), F32)
    following[...] = w[pl.ds(0, SIZE), pl.ds(0, SIZE)]

    def step(k, _):
        done = eliminate([following[pl.ds(8 * r, 8), :] for r in range(16)])
        p = jnp.maximum(k - 1, 0)
        x_prev = diag[...]
        w[at(p), :] = jnp.where(k > 0, exact(x_prev, w[at(p), :]), w[at(p), :])
        w[at(p), at(p)] = jnp.where(k > 0, x_prev, w[at(p), at(p)])
        high, mid, low = split3(jnp.where(k > 0, w[at(p), :], 0.0))
        for t, v in enumerate((high, mid, low, high, mid, high)):
            right[pl.ds(SIZE * t, SIZE), :] = v
        for c in range(n):
            cut = slice(SIZE * c, SIZE * c + SIZE)
            high_t, mid_t, low_t = high[:, cut].T, mid[:, cut].T, low[:, cut].T
            for t, v in enumerate((high_t, high_t, high_t, mid_t, mid_t, low_t)):
                left[pl.ds(SIZE * c, SIZE), pl.ds(SIZE * t, SIZE)] = v
        for t in range(n - 1):
            w[at(k + t), at(p)] = jnp.zeros((SIZE, SIZE), F32)
        for t in range(n - 1):
            w[at(k + t), :] = w[at(k + t), :] - jnp.dot(left[at(k + t), :], right[...], preferred_element_type=F32)
        for r in range(16):
            diag[pl.ds(8 * r, 8), :] = done[r]
        q = jnp.minimum(k + 1, n - 1)
        ahead = exact(diag[...], w[at(k), at(q)])
        following[...] = w[at(q), at(q)] - exact(ahead.T, ahead)
        return 0

    lax.fori_loop(0, n, step, 0)
    end = pl.ds((n - 1) * SIZE, SIZE)
    w[end, :] = exact(diag[...], w[end, :])
    w[end, end] = diag[...]
    for r in range(2):
        row = 2 * x + r
        for c in range(n):
            column = 2 * lax.rem(x + c // 2, 4) + c % 2
            value = jnp.where(column <= row, w[at(row), at(column)], 0.0)
            high = value.astype(BF)
            high_ref[pl.ds(SIZE * r, SIZE), pl.ds(SIZE * c, SIZE)] = high
            low_ref[pl.ds(SIZE * r, SIZE), pl.ds(SIZE * c, SIZE)] = (value - high.astype(F32)).astype(BF)


def factor(place, mine, other):
    n = 8
    vmem = pl.BlockSpec(memory_space=pltpu.VMEM)
    return pl.pallas_call(
        factor_kernel,
        out_shape=[jax.ShapeDtypeStruct((2 * SIZE, n * SIZE), BF)] * 2,
        grid_spec=pltpu.PrefetchScalarGridSpec(
            num_scalar_prefetch=1,
            grid=(),
            in_specs=[ANY] * 2,
            out_specs=[vmem] * 2,
            scratch_shapes=[
                pltpu.VMEM(((2 * n - 1) * SIZE, n * SIZE), F32),
                pltpu.VMEM((SIZE, SIZE), F32),
                pltpu.VMEM((SIZE, SIZE), F32),
                pltpu.VMEM(((2 * n - 1) * SIZE, 6 * SIZE), BF),
                pltpu.VMEM((6 * SIZE, n * SIZE), BF),
                pltpu.SemaphoreType.DMA((len(PAIRS),)),
            ],
        ),
        compiler_params=params(32),
        cost_estimate=pl.CostEstimate(flops=20_000_000_000, bytes_accessed=4 * MIB, transcendentals=0),
        name="factor",
    )(place, mine, other)


def apply_kernel(place, *refs):
    own, got, far = refs[0:4], refs[4:7], refs[7:10]
    high, low, out, tiles, sems = refs[10:]
    x = place[0]
    t = pl.program_id(0)
    steps = pl.num_programs(0)
    per = own[0].shape[0]
    width = own[0].shape[-1]
    dims = (((1,), (1,)), ((), ()))
    slot = lax.rem(t, 2)

    def copies(slot, t):
        return [
            pltpu.make_async_copy(
                tiles.at[slot, s], out.at[lax.rem(x + 4 - s, 4), pl.ds(t * per, per)], sems.at[slot, s]
            )
            for s in range(4)
        ]

    @pl.when(t >= 2)
    def _():
        for copy in copies(slot, t - 2):
            copy.wait()

    for s in range(4):
        if s == 0:
            panels = [own[0][...], got[2][...], got[1][...], got[0][...]]
        else:
            panels = [own[4 - s][...]] + [far[s - 1][r] for r in range(3)]
        left = jnp.concatenate([p.reshape(per * SIZE, width) for p in panels], axis=1)
        value = lax.dot_general(left, high[...], dims, preferred_element_type=F32)
        value = value + lax.dot_general(left, low[...], dims, preferred_element_type=F32)
        tiles[slot, s] = value.reshape(per, SIZE, width)
    for copy in copies(slot, t):
        copy.start()

    @pl.when(t == steps - 1)
    def _():
        for copy in copies(1 - slot, t - 1) + copies(slot, t):
            copy.wait()


def apply(place, own, got, far, high, low):
    width = own[0].shape[-1]
    per = 2
    whole = pl.BlockSpec(high.shape, lambda t, *_: (0, 0))
    rows = pl.BlockSpec((per, SIZE, width), lambda t, *_: (t, 0, 0))
    return pl.pallas_call(
        apply_kernel,
        out_shape=jax.ShapeDtypeStruct((4, 8, SIZE, width), F32),
        grid_spec=pltpu.PrefetchScalarGridSpec(
            num_scalar_prefetch=1,
            grid=(8 // per,),
            in_specs=[rows] * 7 + [pl.BlockSpec((3, per, SIZE, width), lambda t, *_: (0, t, 0, 0))] * 3 + [whole, whole],
            out_specs=ANY,
            scratch_shapes=[pltpu.VMEM((2, 4, per, SIZE, width), F32), pltpu.SemaphoreType.DMA((2, 4))],
        ),
        compiler_params=params(32),
        cost_estimate=pl.CostEstimate(flops=4 * 1024 * 1024 * 256 * 4, bytes_accessed=14 * MIB, transcendentals=0),
        name="apply",
    )(place, *own, *got, *far, high, low)


def shards(vectors, blocks, columns):
    block_rows = blocks.shape[0]
    width = vectors.shape[1]
    row = lax.axis_index("rows")
    x = lax.axis_index("vecs")
    vecs = lax.axis_size("vecs")
    total_rows = vectors.shape[0] * lax.axis_size("rows")
    idx = columns - row * block_rows + REACH
    place = jnp.stack([x, lax.rem(row, 2)]).astype(jnp.int32)
    own = chebyshev(vectors.reshape(block_rows, SIZE, width), blocks, idx, place)
    shift = lambda a, s: lax.ppermute(a, "vecs", [(i, (i + s) % vecs) for i in range(vecs)])
    got = [shift(own[s], s) for s in range(1, vecs)]
    keep, send, *following = gram(total_rows, place, own[0], got)
    mine, other, part = sum_everywhere(keep, send)
    far = [shift(following[s - 1], s) for s in range(1, vecs)]
    inverse_high, inverse_low = factor(place, mine, other)
    return apply(place, own, got, far, inverse_high, inverse_low).reshape(vectors.shape)


def solution(mesh):
    in_specs = (P("rows", "vecs"), P("rows", None, None, None), P("rows", None))
    out_specs = P("rows", "vecs")
    return jax.shard_map(shards, mesh=mesh, in_specs=in_specs, out_specs=out_specs, check_vma=False)
```

time: 273 us -> 235 us (0.86)
  Pallas kernels: 103 us -> 80.7 us
  waiting for transfers between devices: 73.8 us -> 53.4 us
  local copies, waits for them, and re-layouts: 5.66 us -> 12.7 us
  starting transfers between devices: 33.6 us -> 28.2 us
  blocking collectives: 55.4 us -> 59 us
    pallas_call x1, Pallas kernels: 70.7 us -> 48 us  [factor(): pl.pallas_call(factor_kernel, out_shape=[jax.ShapeDtypeStruct((2 * SIZE,...]
    ppermute x9, waiting for transfers between devices: 26.4 us -> 13.6 us  [the longest x4 13.6 us: chebyshev(): far_halo = lax.ppermute(far_out, 'rows', between)]
    ppermute x6, waiting for transfers between devices: 39.9 us -> 33.3 us  [shards(): lax.ppermute(a, 'vecs', [(i, (i + s) % vecs) for i in range(vecs)])]
    ppermute x9, starting transfers between devices: 23.2 us -> 17.8 us  [the longest x4 12.7 us: chebyshev(): far_halo = lax.ppermute(far_out, 'rows', between)]
    unnamed x13 -> x39, local copies, waits for them, and re-layouts: 4.18 us -> 7.37 us
    reshape x0 -> x2, local copies, waits for them, and re-layouts: none -> 2.78 us  [the longest x1 1.64 us: sum_everywhere(): lax.all_to_all(spread_out, 'rows', 0, 0, axis_index_groups=groups, tiled=...]
  transfers between devices with their start and end apart: 19 -> 19, of which waited for: 15 -> 11; matrix products, arithmetic and copies ran while one was open for 0% -> 0% of each run, Pallas kernels for 30% -> 29%
where the time goes in v2:
time: 235 us
  Pallas kernels  80.7 us (34%)
  blocking collectives  59 us (25%)
  waiting for transfers between devices  53.4 us (23%)
  starting transfers between devices  28.2 us (12%)
  local copies, waits for them, and re-layouts  12.7 us (5%)
    pallas_call x1, Pallas kernels, factor(): pl.pallas_call(factor_kernel, out_shape=[jax.ShapeDtypeStruct((2 * SIZE,...  48 us
    all_to_all x1, blocking collectives, sum_everywhere(): lax.all_to_all(parts, 'rows', 0, 0, axis_index_groups=groups, tiled=True)  37.4 us
    ppermute x6, waiting for transfers between devices, shards(): lax.ppermute(a, 'vecs', [(i, (i + s) % vecs) for i in range(vecs)])  33.3 us
    pallas_call x8, Pallas kernels, filter_call(): pl.pallas_call(functools.partial(kernel, step, last, source_at), out_shap...  22.6 us
    all_to_all x1, blocking collectives, sum_everywhere(): lax.all_to_all(spread_out, 'rows', 0, 0, axis_index_groups=groups, tiled=...  21.6 us
    ppermute x4, waiting for transfers between devices, chebyshev(): far_halo = lax.ppermute(far_out, 'rows', between)  13.6 us
    ppermute x4, starting transfers between devices, chebyshev(): far_halo = lax.ppermute(far_out, 'rows', between)  12.7 us
    ppermute x6, starting transfers between devices, shards(): lax.ppermute(a, 'vecs', [(i, (i + s) % vecs) for i in range(vecs)])  7.68 us
  transfers between devices with their start and end apart: 19, of which 11 were waited for; matrix products, arithmetic and copies ran while one was open for 0% of the time, Pallas kernels for 29%

profile of v2, /device:TPU:1, one launch (start us, length us, event | category | flops | bytes accessed | tf_op | source)
XLA Modules:
  0.0 235.0 jit_solution(8214539214065966009)
XLA Ops:
  0.0 2.4 %constant_dynamic-slice_fusion = (bf16[8,128,256]{2,1,0:T(8,128)(2,1)}, bf16[8,128,256]{2,1,0:T(8,128)(2,1)}) fusion(bf16[32,128,256]{2,1,0:T(8,128)(2,1)} %bitcast.4, s32[]{:T(128)S(6)} %select_n.7, s32[]{:T(128)S(6)} %select_n.6), kind=kLoop, calls=%fused_computation.3 | loop fusion | bytes 2097160 | tf_op jit(solution)/shard_map/dynamic_slice | solution.py:215
  2.4 1.4 collective-permute-start.2
  3.9 3.2 %collective-permute-start = (bf16[8,128,256]{2,1,0:T(8,128)(2,1)}, bf16[8,128,256]{2,1,0:T(8,128)(2,1)S(1)}, u32[]{:S(2)}, u32[]{:S(2)}) collective-permute-start(bf16[8,128,256]{2,1,0:T(8,128)(2,1)} %get-tuple-element.68), channel_id=1, source_target_pairs={{4,8},{8,4},{12,16},{16,12},{20,24},{24,20},{28,32},{32,28},{36,40... | collective-permute-start | bytes 1572872 | tf_op jit(solution)/shard_map/ppermute | solution.py:218
  7.0 0.1 pad_add_fusion.place
  7.1 0.1 copy.4
  7.2 0.0 collective-permute-done.2.refs_2_
  7.2 0.0 copy-start
  7.2 2.5 %copy-done = bf16[32,5,128,128]{3,2,1,0:T(8,128)(2,1)S(1)} copy-done((bf16[32,5,128,128]{3,2,1,0:T(8,128)(2,1)S(1)}, bf16[32,5,128,128]{3,2,1,0:T(8,128)(2,1)}, u32[]{:S(2)}) %copy-start) | copy-done | bytes 5242904
  9.7 3.2 %filter_rest.4 = (f32[8,128,256]{2,1,0:T(8,128)S(1)}, f32[16,128,256]{2,1,0:T(8,128)S(1)}, bf16[8,128,256]{2,1,0:T(8,128)(2,1)S(1)}, bf16[16,128,256]{2,1,0:T(8,128)(2,1)S(1)}) custom-call(s32[32,5]{1,0:T(8,128)S(1)} %subtract_add_fusion.idx, s32[2]{0:T(128)S(1)} %pad_add_fusion.place, bf16[32,5,128,128]{3,2,1,0:T(8,128)(2,1)S(1)} %copy-done, ...), custom_call_target="tpu_custom_call" | custom-call | flops 1006632960 | bytes 12582912 | tf_op jit(solution)/shard_map/filter_rest/pallas_call | solution.py:183
  12.9 0.1 collective-permute-start.4
  13.0 1.5 collective-permute-done.refs_1_
  14.6 2.2 filter_far.4
  16.8 3.2 %collective-permute-start.1 = (bf16[8,128,256]{2,1,0:T(8,128)(2,1)S(1)}, bf16[8,128,256]{2,1,0:T(8,128)(2,1)S(1)}, u32[]{:S(2)}, u32[]{:S(2)}) collective-permute-start(bf16[8,128,256]{2,1,0:T(8,128)(2,1)S(1)} %get-tuple-element.36.refs_2_.refs_5_), channel_id=1, source_target_pairs={{4,8},{8,4},{12,16},{16,12},{20,24},{24,20},{28,32},{32,28},{36,40... | collective-permute-start | bytes 1572872 | tf_op jit(solution)/shard_map/ppermute | solution.py:218
  19.9 0.0 collective-permute-done.4.refs_2_
  20.0 3.4 %filter_rest.5 = (f32[8,128,256]{2,1,0:T(8,128)S(1)}, f32[16,128,256]{2,1,0:T(8,128)S(1)}, bf16[8,128,256]{2,1,0:T(8,128)(2,1)S(1)}, bf16[16,128,256]{2,1,0:T(8,128)(2,1)S(1)}) custom-call(s32[32,5]{1,0:T(8,128)S(1)} %subtract_add_fusion.idx, s32[2]{0:T(128)S(1)} %pad_add_fusion.place, bf16[32,5,128,128]{3,2,1,0:T(8,128)(2,1)S(1)} %copy-done, ...), custom_call_target="tpu_custom_call" | custom-call | flops 1006632960 | bytes 12582912 | tf_op jit(solution)/shard_map/filter_rest/pallas_call | solution.py:183
  23.3 0.1 collective-permute-start.6
  23.4 3.9 %collective-permute-done.1.refs_1_ = bf16[8,128,256]{2,1,0:T(8,128)(2,1)S(1)} collective-permute-done((bf16[8,128,256]{2,1,0:T(8,128)(2,1)S(1)}, bf16[8,128,256]{2,1,0:T(8,128)(2,1)S(1)}, u32[]{:S(2)}, u32[]{:S(2)}) %collective-permute-start.1) | collective-permute-done | bytes 524320 | tf_op jit(solution)/shard_map/ppermute | solution.py:218
  27.3 2.2 filter_far.5
  29.5 3.2 %collective-permute-start.3 = (bf16[8,128,256]{2,1,0:T(8,128)(2,1)S(1)}, bf16[8,128,256]{2,1,0:T(8,128)(2,1)S(1)}, u32[]{:S(2)}, u32[]{:S(2)}) collective-permute-start(bf16[8,128,256]{2,1,0:T(8,128)(2,1)S(1)} %get-tuple-element.39.refs_2_.refs_5_), channel_id=1, source_target_pairs={{4,8},{8,4},{12,16},{16,12},{20,24},{24,20},{28,32},{32,28},{36,40... | collective-permute-start | bytes 1572872 | tf_op jit(solution)/shard_map/ppermute | solution.py:218
  32.7 0.0 collective-permute-done.6.refs_2_
  32.7 3.3 %filter_rest.6 = (f32[8,128,256]{2,1,0:T(8,128)S(1)}, f32[16,128,256]{2,1,0:T(8,128)S(1)}, bf16[8,128,256]{2,1,0:T(8,128)(2,1)S(1)}, bf16[16,128,256]{2,1,0:T(8,128)(2,1)S(1)}) custom-call(s32[32,5]{1,0:T(8,128)S(1)} %subtract_add_fusion.idx, s32[2]{0:T(128)S(1)} %pad_add_fusion.place, bf16[32,5,128,128]{3,2,1,0:T(8,128)(2,1)S(1)} %copy-done, ...), custom_call_target="tpu_custom_call" | custom-call | flops 1006632960 | bytes 12582912 | tf_op jit(solution)/shard_map/filter_rest/pallas_call | solution.py:183
  36.0 0.1 collective-permute-start.7
  36.1 3.9 %collective-permute-done.3.refs_1_ = bf16[8,128,256]{2,1,0:T(8,128)(2,1)S(1)} collective-permute-done((bf16[8,128,256]{2,1,0:T(8,128)(2,1)S(1)}, bf16[8,128,256]{2,1,0:T(8,128)(2,1)S(1)}, u32[]{:S(2)}, u32[]{:S(2)}) %collective-permute-start.3) | collective-permute-done | bytes 524320 | tf_op jit(solution)/shard_map/ppermute | solution.py:218
  40.0 2.2 filter_far.6
  42.2 3.2 %collective-permute-start.5 = (bf16[8,128,256]{2,1,0:T(8,128)(2,1)S(1)}, bf16[8,128,256]{2,1,0:T(8,128)(2,1)S(1)}, u32[]{:S(2)}, u32[]{:S(2)}) collective-permute-start(bf16[8,128,256]{2,1,0:T(8,128)(2,1)S(1)} %get-tuple-element.45.refs_5_.refs_2_), channel_id=1, source_target_pairs={{4,8},{8,4},{12,16},{16,12},{20,24},{24,20},{28,32},{32,28},{36,40... | collective-permute-start | bytes 1572872 | tf_op jit(solution)/shard_map/ppermute | solution.py:218
  45.4 0.0 collective-permute-done.7.refs_2_
  45.4 3.3 %filter_rest.7 = (bf16[8,128,256]{2,1,0:T(8,128)(2,1)S(1)}, bf16[16,128,256]{2,1,0:T(8,128)(2,1)S(1)}) custom-call(s32[32,5]{1,0:T(8,128)S(1)} %subtract_add_fusion.idx, s32[2]{0:T(128)S(1)} %pad_add_fusion.place, bf16[32,5,128,128]{3,2,1,0:T(8,128)(2,1)S(1)} %copy-done, bf16[32,5,128,128]{3,2,1,0:T(8,128)(2,1)S(1)} %copy-done, ...), custom_call_target="tpu_custom_call" | custom-call | flops 1006632960 | bytes 12582912 | tf_op jit(solution)/shard_map/filter_rest/pallas_call | solution.py:183
  48.7 4.3 %collective-permute-done.5.refs_1_ = bf16[8,128,256]{2,1,0:T(8,128)(2,1)S(1)} collective-permute-done((bf16[8,128,256]{2,1,0:T(8,128)(2,1)S(1)}, bf16[8,128,256]{2,1,0:T(8,128)(2,1)S(1)}, u32[]{:S(2)}, u32[]{:S(2)}) %collective-permute-start.5) | collective-permute-done | bytes 524320 | tf_op jit(solution)/shard_map/ppermute | solution.py:218
  53.0 2.8 %filter_far.7 = (bf16[8,128,256]{2,1,0:T(8,128)(2,1)S(1)}, bf16[8,128,256]{2,1,0:T(8,128)(2,1)S(1)}, bf16[8,128,256]{2,1,0:T(8,128)(2,1)S(1)}, bf16[8,128,256]{2,1,0:T(8,128)(2,1)S(1)}) custom-call(s32[32,5]{1,0:T(8,128)S(1)} %subtract_add_fusion.idx, s32[2]{0:T(128)S(1)} %pad_add_fusion.place, bf16[32,5,128,128]{3,2,1,0:T(8,128)(2,1)S(1)} %copy-done, ...), custom_call_target="tpu_custom_call" | custom-call | flops 335544320 | bytes 4194304 | tf_op jit(solution)/shard_map/filter_far/pallas_call | solution.py:183
  55.8 2.6 %collective-permute-start.10 = (bf16[8,128,256]{2,1,0:T(8,128)(2,1)S(1)}, bf16[8,128,256]{2,1,0:T(8,128)(2,1)S(1)}, u32[]{:S(2)}, u32[]{:S(2)}) collective-permute-start(bf16[8,128,256]{2,1,0:T(8,128)(2,1)S(1)} %get-tuple-element.59.refs_3_), channel_id=1, source_target_pairs={{0,3},{1,0},{2,1},{3,2},{4,7},{5,4},{6,5},{7,6},{8,11},{9,8},{10,9... | collective-permute-start | bytes 1572872 | tf_op jit(solution)/shard_map/ppermute | solution.py:542
  58.5 0.8 copy-done.10
  59.3 0.8 copy-done.6
  60.1 1.7 collective-permute-start.9
  61.8 0.8 copy-done.8
  62.6 9.3 %collective-permute-done.10.got3.refs_6_ = bf16[8,128,256]{2,1,0:T(8,128)(2,1)S(1)} collective-permute-done((bf16[8,128,256]{2,1,0:T(8,128)(2,1)S(1)}, bf16[8,128,256]{2,1,0:T(8,128)(2,1)S(1)}, u32[]{:S(2)}, u32[]{:S(2)}) %collective-permute-start.10) | collective-permute-done | bytes 524320 | tf_op jit(solution)/shard_map/ppermute | solution.py:542
  71.9 4.0 %collective-permute-done.8.got1.refs_4_ = bf16[8,128,256]{2,1,0:T(8,128)(2,1)S(1)} collective-permute-done((bf16[8,128,256]{2,1,0:T(8,128)(2,1)S(1)}, bf16[8,128,256]{2,1,0:T(8,128)(2,1)S(1)}, u32[]{:S(2)}, u32[]{:S(2)}) %collective-permute-start.8) | collective-permute-done | bytes 524320 | tf_op jit(solution)/shard_map/ppermute | solution.py:542
  75.9 0.0 collective-permute-done.9.got2.refs_5_
  75.9 2.9 %gram.1 = (f32[5,256,256]{2,1,0:T(8,128)S(1)}, f32[5,256,256]{2,1,0:T(8,128)S(1)}, bf16[3,8,128,256]{3,2,1,0:T(8,128)(2,1)S(1)}, bf16[3,8,128,256]{3,2,1,0:T(8,128)(2,1)S(1)}, bf16[3,8,128,256]{3,2,1,0:T(8,128)(2,1)S(1)}) custom-call(s32[2]{0:T(128)S(1)} %pad_add_fusion.place, bf16[8,128,256]{2,1,0:T(8,128)(2,1)S(1)} %get-tuple-element.56.own.refs_0_, ...), custom_call_target="tpu_custom_call" | custom-call | flops 1342177280 | bytes 8388608 | tf_op jit(solution)/shard_map/gram/pallas_call | solution.py:270
  78.8 1.2 copy-done.2
  80.0 1.1 copy-done.3
  81.2 3.0 %collective-permute-done.14 = f32[5,256,256]{2,1,0:T(8,128)S(1)} collective-permute-done((f32[5,256,256]{2,1,0:T(8,128)S(1)}, f32[5,256,256]{2,1,0:T(8,128)S(1)}, u32[]{:S(2)}, u32[]{:S(2)}) %collective-permute-start.14) | collective-permute-done | bytes 1310752 | tf_op jit(solution)/shard_map/ppermute | solution.py:297
  84.2 0.2 add.28
  84.4 1.1 reshape.14
  85.6 37.4 %all_to_all.10 = f32[16,160,128]{2,1,0:T(8,128)S(1)} all-to-all(f32[16,160,128]{2,1,0:T(8,128)} %reshape.14), channel_id=1, replica_groups={{0,8,16,24,32,40,48,56,64,72,80,88,96,104,112,120},{4,12,20,28,36,44,52..., dimensions={0} | all-to-all | bytes 2621440 | tf_op jit(solution)/shard_map/all_to_all | solution.py:299
  123.0 0.1 reduce_sum.9
  123.1 0.1 collective-permute-start.15
  123.1 0.7 collective-permute-start.16
  123.9 1.9 collective-permute-start.17
  125.8 2.7 %collective-permute-done.15 = f32[160,128]{1,0:T(8,128)S(1)} collective-permute-done((f32[160,128]{1,0:T(8,128)S(1)}, f32[160,128]{1,0:T(8,128)S(1)}, u32[]{:S(2)}, u32[]{:S(2)}) %collective-permute-start.15) | collective-permute-done | bytes 81952 | tf_op jit(solution)/shard_map/ppermute | solution.py:301
  128.5 0.0 collective-permute-done.16
  128.5 0.9 collective-permute-done.17
  129.4 0.1 broadcast_in_dim.2
  129.5 21.6 %all_to_all.11 = f32[16,160,128]{2,1,0:T(8,128)} all-to-all(f32[16,160,128]{2,1,0:T(8,128)S(1)} %broadcast_in_dim.2), channel_id=1, replica_groups={{0,8,16,24,32,40,48,56,64,72,80,88,96,104,112,120},{4,12,20,28,36,44,52..., dimensions={0} | all-to-all | bytes 2621440 | tf_op jit(solution)/shard_map/all_to_all | solution.py:304
  151.1 1.6 reshape.15.mine
  152.7 3.4 %collective-permute-start.18 = (f32[5,256,256]{2,1,0:T(8,128)S(1)}, f32[5,256,256]{2,1,0:T(8,128)S(1)}, u32[]{:S(2)}, u32[]{:S(2)}) collective-permute-start(f32[5,256,256]{2,1,0:T(8,128)S(1)} %reshape.15.mine), channel_id=1, source_target_pairs={{0,4},{4,0},{8,12},{12,8},{16,20},{20,16},{24,28},{28,24},{32,36},... | collective-permute-start | bytes 3932168 | tf_op jit(solution)/shard_map/ppermute | solution.py:305
  156.2 0.9 collective-permute-start.11
  157.1 1.5 collective-permute-start.12
  158.6 1.0 collective-permute-start.13
  159.5 0.0 collective-permute-done.18.other
  159.5 48.0 %factor.1 = (bf16[256,1024]{1,0:T(8,128)(2,1)S(1)}, bf16[256,1024]{1,0:T(8,128)(2,1)S(1)}) custom-call(s32[2]{0:T(128)S(1)} %pad_add_fusion.place, f32[5,256,256]{2,1,0:T(8,128)S(1)} %reshape.15.mine, f32[5,256,256]{2,1,0:T(8,128)S(1)} %collective-permute-done.18.other), custom_call_target="tpu_custom_call" | custom-call | flops 20000000000 | bytes 4194304 | tf_op jit(solution)/shard_map/factor/pallas_call | solution.py:446
  207.5 0.0 collective-permute-done.11.refs_7_
  207.5 19.4 %collective-permute-done.12.refs_8_ = bf16[3,8,128,256]{3,2,1,0:T(8,128)(2,1)S(1)} collective-permute-done((bf16[3,8,128,256]{3,2,1,0:T(8,128)(2,1)}, bf16[3,8,128,256]{3,2,1,0:T(8,128)(2,1)S(1)}, u32[]{:S(2)}, u32[]{:S(2)}) %collective-permute-start.12) | collective-permute-done | bytes 1572896 | tf_op jit(solution)/shard_map/ppermute | solution.py:542
  227.0 0.6 collective-permute-done.13.refs_9_
  227.6 7.2 %apply.1 = f32[4,8,128,256]{3,2,1,0:T(8,128)} custom-call(s32[2]{0:T(128)S(1)} %pad_add_fusion.place, bf16[8,128,256]{2,1,0:T(8,128)(2,1)S(1)} %copy-done.5, bf16[8,128,256]{2,1,0:T(8,128)(2,1)S(1)} %copy-done.7, bf16[8,128,256]{2,1,0:T(8,128)(2,1)S(1)} %copy-done.9, bf16[8,128,256]{2,1,0:T(8,128)(2,1)S(1)} %copy-done.11, ...), custom_call_target="tpu_custom_call" | custom-call | flops 4294967296 | bytes 14680064 | tf_op jit(solution)/shard_map/apply/pallas_call | solution.py:516
  (35 shorter events, 0.1 us)
Async XLA Ops:
  0.0 7.2 %copy-start.1 = (bf16[4096,256]{1,0:T(8,128)(2,1)S(1)}, bf16[4096,256]{1,0:T(8,128)(2,1)}, u32[]{:S(2)}) copy-start(bf16[4096,256]{1,0:T(8,128)(2,1)} %param.3) | copy-start | bytes 6291460
  0.0 7.1 %copy-start.18 = (s32[32,5]{0,1:T(8,128)S(1)}, s32[32,5]{0,1:T(8,128)}, u32[]{:S(2)}) copy-start(s32[32,5]{0,1:T(8,128)} %param.5) | copy-start | bytes 1924
  2.4 4.8 %collective-permute-start.2 = (bf16[8,128,256]{2,1,0:T(8,128)(2,1)}, bf16[8,128,256]{2,1,0:T(8,128)(2,1)S(1)}, u32[]{:S(2)}, u32[]{:S(2)}) collective-permute-start(bf16[8,128,256]{2,1,0:T(8,128)(2,1)} %get-tuple-element.67), channel_id=1, source_target_pairs={{0,4},{4,0},{8,12},{12,8},{16,20},{20,16},{24,28},{28,24},{32,36},... | collective-permute-start | bytes 1572872 | tf_op jit(solution)/shard_map/ppermute | solution.py:219
  3.9 10.7 %collective-permute-start = (bf16[8,128,256]{2,1,0:T(8,128)(2,1)}, bf16[8,128,256]{2,1,0:T(8,128)(2,1)S(1)}, u32[]{:S(2)}, u32[]{:S(2)}) collective-permute-start(bf16[8,128,256]{2,1,0:T(8,128)(2,1)} %get-tuple-element.68), channel_id=1, source_target_pairs={{4,8},{8,4},{12,16},{16,12},{20,24},{24,20},{28,32},{32,28},{36,40... | collective-permute-start | bytes 1572872 | tf_op jit(solution)/shard_map/ppermute | solution.py:218
  7.2 2.5 %copy-start = (bf16[32,5,128,128]{3,2,1,0:T(8,128)(2,1)S(1)}, bf16[32,5,128,128]{3,2,1,0:T(8,128)(2,1)}, u32[]{:S(2)}) copy-start(bf16[32,5,128,128]{3,2,1,0:T(8,128)(2,1)} %refs_0_.15) | copy-start | bytes 15728644
  12.9 7.0 %collective-permute-start.4 = (bf16[8,128,256]{2,1,0:T(8,128)(2,1)S(1)}, bf16[8,128,256]{2,1,0:T(8,128)(2,1)S(1)}, u32[]{:S(2)}, u32[]{:S(2)}) collective-permute-start(bf16[8,128,256]{2,1,0:T(8,128)(2,1)S(1)} %get-tuple-element.40.refs_3_), channel_id=1, source_target_pairs={{0,4},{4,0},{8,12},{12,8},{16,20},{20,16},{24,28},{28,24},{32,36},... | collective-permute-start | bytes 1572872 | tf_op jit(solution)/shard_map/ppermute | solution.py:219
  16.8 10.5 %collective-permute-start.1 = (bf16[8,128,256]{2,1,0:T(8,128)(2,1)S(1)}, bf16[8,128,256]{2,1,0:T(8,128)(2,1)S(1)}, u32[]{:S(2)}, u32[]{:S(2)}) collective-permute-start(bf16[8,128,256]{2,1,0:T(8,128)(2,1)S(1)} %get-tuple-element.36.refs_2_.refs_5_), channel_id=1, source_target_pairs={{4,8},{8,4},{12,16},{16,12},{20,24},{24,20},{28,32},{32,28},{36,40... | collective-permute-start | bytes 1572872 | tf_op jit(solution)/shard_map/ppermute | solution.py:218
  23.3 9.4 %collective-permute-start.6 = (bf16[8,128,256]{2,1,0:T(8,128)(2,1)S(1)}, bf16[8,128,256]{2,1,0:T(8,128)(2,1)S(1)}, u32[]{:S(2)}, u32[]{:S(2)}) collective-permute-start(bf16[8,128,256]{2,1,0:T(8,128)(2,1)S(1)} %get-tuple-element.46.refs_3_), channel_id=1, source_target_pairs={{0,4},{4,0},{8,12},{12,8},{16,20},{20,16},{24,28},{28,24},{32,36},... | collective-permute-start | bytes 1572872 | tf_op jit(solution)/shard_map/ppermute | solution.py:219
  29.5 10.5 %collective-permute-start.3 = (bf16[8,128,256]{2,1,0:T(8,128)(2,1)S(1)}, bf16[8,128,256]{2,1,0:T(8,128)(2,1)S(1)}, u32[]{:S(2)}, u32[]{:S(2)}) collective-permute-start(bf16[8,128,256]{2,1,0:T(8,128)(2,1)S(1)} %get-tuple-element.39.refs_2_.refs_5_), channel_id=1, source_target_pairs={{4,8},{8,4},{12,16},{16,12},{20,24},{24,20},{28,32},{32,28},{36,40... | collective-permute-start | bytes 1572872 | tf_op jit(solution)/shard_map/ppermute | solution.py:218
  36.0 9.4 %collective-permute-start.7 = (bf16[8,128,256]{2,1,0:T(8,128)(2,1)S(1)}, bf16[8,128,256]{2,1,0:T(8,128)(2,1)S(1)}, u32[]{:S(2)}, u32[]{:S(2)}) collective-permute-start(bf16[8,128,256]{2,1,0:T(8,128)(2,1)S(1)} %get-tuple-element.51.refs_3_), channel_id=1, source_target_pairs={{0,4},{4,0},{8,12},{12,8},{16,20},{20,16},{24,28},{28,24},{32,36},... | collective-permute-start | bytes 1572872 | tf_op jit(solution)/shard_map/ppermute | solution.py:219
  42.2 10.8 %collective-permute-start.5 = (bf16[8,128,256]{2,1,0:T(8,128)(2,1)S(1)}, bf16[8,128,256]{2,1,0:T(8,128)(2,1)S(1)}, u32[]{:S(2)}, u32[]{:S(2)}) collective-permute-start(bf16[8,128,256]{2,1,0:T(8,128)(2,1)S(1)} %get-tuple-element.45.refs_5_.refs_2_), channel_id=1, source_target_pairs={{4,8},{8,4},{12,16},{16,12},{20,24},{24,20},{28,32},{32,28},{36,40... | collective-permute-start | bytes 1572872 | tf_op jit(solution)/shard_map/ppermute | solution.py:218
  55.8 23.0 %copy-start.4 = (bf16[8,128,256]{2,1,0:T(8,128)(2,1)}, bf16[8,128,256]{2,1,0:T(8,128)(2,1)S(1)}, u32[]{:S(2)}) copy-start(bf16[8,128,256]{2,1,0:T(8,128)(2,1)S(1)} %get-tuple-element.56.own.refs_0_) | copy-start | bytes 1572868
  55.8 16.1 %collective-permute-start.10 = (bf16[8,128,256]{2,1,0:T(8,128)(2,1)S(1)}, bf16[8,128,256]{2,1,0:T(8,128)(2,1)S(1)}, u32[]{:S(2)}, u32[]{:S(2)}) collective-permute-start(bf16[8,128,256]{2,1,0:T(8,128)(2,1)S(1)} %get-tuple-element.59.refs_3_), channel_id=1, source_target_pairs={{0,3},{1,0},{2,1},{3,2},{4,7},{5,4},{6,5},{7,6},{8,11},{9,8},{10,9... | collective-permute-start | bytes 1572872 | tf_op jit(solution)/shard_map/ppermute | solution.py:542
  58.5 0.8 copy-start.10
  59.3 16.6 %collective-permute-start.8 = (bf16[8,128,256]{2,1,0:T(8,128)(2,1)S(1)}, bf16[8,128,256]{2,1,0:T(8,128)(2,1)S(1)}, u32[]{:S(2)}, u32[]{:S(2)}) collective-permute-start(bf16[8,128,256]{2,1,0:T(8,128)(2,1)S(1)} %get-tuple-element.57.refs_1_), channel_id=1, source_target_pairs={{0,1},{1,2},{2,3},{3,0},{4,5},{5,6},{6,7},{7,4},{8,9},{9,10},{10,1... | collective-permute-start | bytes 1572872 | tf_op jit(solution)/shard_map/ppermute | solution.py:542
  59.3 0.8 copy-start.6
  60.1 15.8 %collective-permute-start.9 = (bf16[8,128,256]{2,1,0:T(8,128)(2,1)S(1)}, bf16[8,128,256]{2,1,0:T(8,128)(2,1)S(1)}, u32[]{:S(2)}, u32[]{:S(2)}) collective-permute-start(bf16[8,128,256]{2,1,0:T(8,128)(2,1)S(1)} %get-tuple-element.58.refs_2_), channel_id=1, source_target_pairs={{0,2},{1,3},{2,0},{3,1},{4,6},{5,7},{6,4},{7,5},{8,10},{9,11},{10,... | collective-permute-start | bytes 1572872 | tf_op jit(solution)/shard_map/ppermute | solution.py:542
  61.8 0.8 copy-start.8
  71.9 6.9 %copy-start.12 = (bf16[8,128,256]{2,1,0:T(8,128)(2,1)}, bf16[8,128,256]{2,1,0:T(8,128)(2,1)S(1)}, u32[]{:S(2)}) copy-start(bf16[8,128,256]{2,1,0:T(8,128)(2,1)S(1)} %collective-permute-done.10.got3.refs_6_) | copy-start | bytes 1572868
  75.9 3.0 %copy-start.14 = (bf16[8,128,256]{2,1,0:T(8,128)(2,1)}, bf16[8,128,256]{2,1,0:T(8,128)(2,1)S(1)}, u32[]{:S(2)}) copy-start(bf16[8,128,256]{2,1,0:T(8,128)(2,1)S(1)} %collective-permute-done.8.got1.refs_4_) | copy-start | bytes 1572868
  75.9 3.0 %copy-start.16 = (bf16[8,128,256]{2,1,0:T(8,128)(2,1)}, bf16[8,128,256]{2,1,0:T(8,128)(2,1)S(1)}, u32[]{:S(2)}) copy-start(bf16[8,128,256]{2,1,0:T(8,128)(2,1)S(1)} %collective-permute-done.9.got2.refs_5_) | copy-start | bytes 1572868
  78.8 1.2 copy-start.2
  80.0 1.1 copy-start.3
  81.2 3.0 %collective-permute-start.14 = (f32[5,256,256]{2,1,0:T(8,128)S(1)}, f32[5,256,256]{2,1,0:T(8,128)S(1)}, u32[]{:S(2)}, u32[]{:S(2)}) collective-permute-start(f32[5,256,256]{2,1,0:T(8,128)S(1)} %get-tuple-element.64), channel_id=1, source_target_pairs={{0,4},{4,0},{8,12},{12,8},{16,20},{20,16},{24,28},{28,24},{32,36},... | collective-permute-start | bytes 3932168 | tf_op jit(solution)/shard_map/ppermute | solution.py:297
  123.1 5.4 %collective-permute-start.15 = (f32[160,128]{1,0:T(8,128)S(1)}, f32[160,128]{1,0:T(8,128)S(1)}, u32[]{:S(2)}, u32[]{:S(2)}) collective-permute-start(f32[160,128]{1,0:T(8,128)S(1)} %reduce_sum.9), channel_id=1, source_target_pairs={{0,1},{1,2},{2,3},{3,0},{4,5},{5,6},{6,7},{7,4},{8,9},{9,10},{10,1... | collective-permute-start | bytes 245768 | tf_op jit(solution)/shard_map/ppermute | solution.py:301
  123.1 5.4 %collective-permute-start.16 = (f32[160,128]{1,0:T(8,128)S(1)}, f32[160,128]{1,0:T(8,128)S(1)}, u32[]{:S(2)}, u32[]{:S(2)}) collective-permute-start(f32[160,128]{1,0:T(8,128)S(1)} %reduce_sum.9), channel_id=1, source_target_pairs={{0,2},{1,3},{2,0},{3,1},{4,6},{5,7},{6,4},{7,5},{8,10},{9,11},{10,... | collective-permute-start | bytes 245768 | tf_op jit(solution)/shard_map/ppermute | solution.py:301
  123.9 5.5 %collective-permute-start.17 = (f32[160,128]{1,0:T(8,128)S(1)}, f32[160,128]{1,0:T(8,128)S(1)}, u32[]{:S(2)}, u32[]{:S(2)}) collective-permute-start(f32[160,128]{1,0:T(8,128)S(1)} %reduce_sum.9), channel_id=1, source_target_pairs={{0,3},{1,0},{2,1},{3,2},{4,7},{5,4},{6,5},{7,6},{8,11},{9,8},{10,9... | collective-permute-start | bytes 245768 | tf_op jit(solution)/shard_map/ppermute | solution.py:301
  152.7 6.8 %collective-permute-start.18 = (f32[5,256,256]{2,1,0:T(8,128)S(1)}, f32[5,256,256]{2,1,0:T(8,128)S(1)}, u32[]{:S(2)}, u32[]{:S(2)}) collective-permute-start(f32[5,256,256]{2,1,0:T(8,128)S(1)} %reshape.15.mine), channel_id=1, source_target_pairs={{0,4},{4,0},{8,12},{12,8},{16,20},{20,16},{24,28},{28,24},{32,36},... | collective-permute-start | bytes 3932168 | tf_op jit(solution)/shard_map/ppermute | solution.py:305
  156.2 51.3 %collective-permute-start.11 = (bf16[3,8,128,256]{3,2,1,0:T(8,128)(2,1)}, bf16[3,8,128,256]{3,2,1,0:T(8,128)(2,1)S(1)}, u32[]{:S(2)}, u32[]{:S(2)}) collective-permute-start(bf16[3,8,128,256]{3,2,1,0:T(8,128)(2,1)} %copy-done.3), channel_id=1, source_target_pairs={{0,1},{1,2},{2,3},{3,0},{4,5},{5,6},{6,7},{7,4},{8,9},{9,10},{10,1... | collective-permute-start | bytes 4718600 | tf_op jit(solution)/shard_map/ppermute | solution.py:542
  157.1 69.9 %collective-permute-start.12 = (bf16[3,8,128,256]{3,2,1,0:T(8,128)(2,1)}, bf16[3,8,128,256]{3,2,1,0:T(8,128)(2,1)S(1)}, u32[]{:S(2)}, u32[]{:S(2)}) collective-permute-start(bf16[3,8,128,256]{3,2,1,0:T(8,128)(2,1)} %copy-done.2), channel_id=1, source_target_pairs={{0,2},{1,3},{2,0},{3,1},{4,6},{5,7},{6,4},{7,5},{8,10},{9,11},{10,... | collective-permute-start | bytes 4718600 | tf_op jit(solution)/shard_map/ppermute | solution.py:542
  158.5 69.0 %copy-start.5 = (bf16[8,128,256]{2,1,0:T(8,128)(2,1)S(1)}, bf16[8,128,256]{2,1,0:T(8,128)(2,1)}, u32[]{:S(2)}) copy-start(bf16[8,128,256]{2,1,0:T(8,128)(2,1)} %copy-done.4) | copy-start | bytes 1572868
  158.5 69.0 %copy-start.7 = (bf16[8,128,256]{2,1,0:T(8,128)(2,1)S(1)}, bf16[8,128,256]{2,1,0:T(8,128)(2,1)}, u32[]{:S(2)}) copy-start(bf16[8,128,256]{2,1,0:T(8,128)(2,1)} %copy-done.6) | copy-start | bytes 1572868
  158.5 69.0 %copy-start.9 = (bf16[8,128,256]{2,1,0:T(8,128)(2,1)S(1)}, bf16[8,128,256]{2,1,0:T(8,128)(2,1)}, u32[]{:S(2)}) copy-start(bf16[8,128,256]{2,1,0:T(8,128)(2,1)} %copy-done.8) | copy-start | bytes 1572868
  158.5 69.0 %copy-start.11 = (bf16[8,128,256]{2,1,0:T(8,128)(2,1)S(1)}, bf16[8,128,256]{2,1,0:T(8,128)(2,1)}, u32[]{:S(2)}) copy-start(bf16[8,128,256]{2,1,0:T(8,128)(2,1)} %copy-done.10) | copy-start | bytes 1572868
  158.6 69.0 %copy-start.13 = (bf16[8,128,256]{2,1,0:T(8,128)(2,1)S(1)}, bf16[8,128,256]{2,1,0:T(8,128)(2,1)}, u32[]{:S(2)}) copy-start(bf16[8,128,256]{2,1,0:T(8,128)(2,1)} %copy-done.12) | copy-start | bytes 1572868
  158.6 69.0 %copy-start.15 = (bf16[8,128,256]{2,1,0:T(8,128)(2,1)S(1)}, bf16[8,128,256]{2,1,0:T(8,128)(2,1)}, u32[]{:S(2)}) copy-start(bf16[8,128,256]{2,1,0:T(8,128)(2,1)} %copy-done.14) | copy-start | bytes 1572868
  158.6 69.0 %copy-start.17 = (bf16[8,128,256]{2,1,0:T(8,128)(2,1)S(1)}, bf16[8,128,256]{2,1,0:T(8,128)(2,1)}, u32[]{:S(2)}) copy-start(bf16[8,128,256]{2,1,0:T(8,128)(2,1)} %copy-done.16) | copy-start | bytes 1572868
  158.6 69.0 %collective-permute-start.13 = (bf16[3,8,128,256]{3,2,1,0:T(8,128)(2,1)S(1)}, bf16[3,8,128,256]{3,2,1,0:T(8,128)(2,1)S(1)}, u32[]{:S(2)}, u32[]{:S(2)}) collective-permute-start(bf16[3,8,128,256]{3,2,1,0:T(8,128)(2,1)S(1)} %get-tuple-element.62), channel_id=1, source_target_pairs={{0,3},{1,0},{2,1},{3,2},{4,7},{5,4},{6,5},{7,6},{8,11},{9,8},{10,9... | collective-permute-start | bytes 4718600 | tf_op jit(solution)/shard_map/ppermute | solution.py:542

commit v3 on v2

--- a/solution.py
+++ b/solution.py
@@ -295,7 +295,7 @@
     groups = [list(range(c, rows, 2)) for c in range(2)]
     count = rows // 2
     mine = keep + lax.ppermute(send, "rows", swap)
-    parts = mine.reshape(count, -1, SIZE)
+    parts = mine.reshape(count, -1, mine.shape[-1])
     parts = lax.all_to_all(parts, "rows", 0, 0, axis_index_groups=groups, tiled=True)
     part = jnp.sum(parts, axis=0)
     others = [lax.ppermute(part, "vecs", [(i, (i + s) % vecs) for i in range(vecs)]) for s in range(1, vecs)]
@@ -435,9 +435,10 @@
         for c in range(n):
             column = 2 * lax.rem(x + c // 2, 4) + c % 2
             value = jnp.where(column <= row, w[at(row), at(column)], 0.0)
+            value = value.T
             high = value.astype(BF)
-            high_ref[pl.ds(SIZE * r, SIZE), pl.ds(SIZE * c, SIZE)] = high
-            low_ref[pl.ds(SIZE * r, SIZE), pl.ds(SIZE * c, SIZE)] = (value - high.astype(F32)).astype(BF)
+            high_ref[pl.ds(SIZE * c, SIZE), pl.ds(SIZE * r, SIZE)] = high
+            low_ref[pl.ds(SIZE * c, SIZE), pl.ds(SIZE * r, SIZE)] = (value - high.astype(F32)).astype(BF)
 
 
 def factor(place, mine, other):
@@ -445,7 +446,7 @@
     vmem = pl.BlockSpec(memory_space=pltpu.VMEM)
     return pl.pallas_call(
         factor_kernel,
-        out_shape=[jax.ShapeDtypeStruct((2 * SIZE, n * SIZE), BF)] * 2,
+        out_shape=[jax.ShapeDtypeStruct((n * SIZE, 2 * SIZE), BF)] * 2,
         grid_spec=pltpu.PrefetchScalarGridSpec(
             num_scalar_prefetch=1,
             grid=(),
@@ -461,7 +462,7 @@
             ],
         ),
         compiler_params=params(32),
-        cost_estimate=pl.CostEstimate(flops=20_000_000_000, bytes_accessed=4 * MIB, transcendentals=0),
+        cost_estimate=pl.CostEstimate(flops=1_000_000, bytes_accessed=4 * MIB, transcendentals=0),
         name="factor",
     )(place, mine, other)
 
@@ -474,7 +475,6 @@
     steps = pl.num_programs(0)
     per = own[0].shape[0]
     width = own[0].shape[-1]
-    dims = (((1,), (1,)), ((), ()))
     slot = lax.rem(t, 2)
 
     def copies(slot, t):
@@ -496,8 +496,8 @@
         else:
             panels = [own[4 - s][...]] + [far[s - 1][r] for r in range(3)]
         left = jnp.concatenate([p.reshape(per * SIZE, width) for p in panels], axis=1)
-        value = lax.dot_general(left, high[...], dims, preferred_element_type=F32)
-        value = value + lax.dot_general(left, low[...], dims, preferred_element_type=F32)
+        value = jnp.dot(left, high[...], preferred_element_type=F32)
+        value = value + jnp.dot(left, low[...], preferred_element_type=F32)
         tiles[slot, s] = value.reshape(per, SIZE, width)
     for copy in copies(slot, t):
         copy.start()

time: 235 us -> 212 us (0.902)
  blocking collectives: 59 us -> 37.3 us
  local copies, waits for them, and re-layouts: 12.7 us -> 7.29 us
  starting transfers between devices: 28.2 us -> 33.3 us
    all_to_all x1 -> x0, blocking collectives: 21.6 us -> none  [sum_everywhere(): lax.all_to_all(spread_out, 'rows', 0, 0, axis_index_groups=groups, tiled=...]
    ppermute x6, waiting for transfers between devices: 33.3 us -> 14.7 us  [shards(): lax.ppermute(a, 'vecs', [(i, (i + s) % vecs) for i in range(vecs)])]
    all_to_all x0 -> x1, waiting for transfers between devices: none -> 13.7 us  [sum_everywhere(): lax.all_to_all(spread_out, 'rows', 0, 0, axis_index_groups=groups, tiled=...]
    unnamed x39 -> x35, local copies, waits for them, and re-layouts: 7.37 us -> 3.66 us
    all_to_all x0 -> x1, starting transfers between devices: none -> 3.71 us  [sum_everywhere(): lax.all_to_all(spread_out, 'rows', 0, 0, axis_index_groups=groups, tiled=...]
    reshape x2 -> x0, local copies, waits for them, and re-layouts: 2.78 us -> none  [the longest x1 1.64 us: sum_everywhere(): lax.all_to_all(spread_out, 'rows', 0, 0, axis_index_groups=groups, tiled=...]
    ppermute x1, waiting for transfers between devices: 0.01 us -> 2.66 us  [sum_everywhere(): return (mine, lax.ppermute(mine, 'rows', swap), part)]
  transfers between devices with their start and end apart: 19 -> 20, of which waited for: 11 -> 12; matrix products, arithmetic and copies ran while one was open for 0% -> 0% of each run, Pallas kernels for 29% -> 32%
where the time goes in v3:
time: 212 us
  Pallas kernels  81.5 us (38%)
  waiting for transfers between devices  51.5 us (24%)
  blocking collectives  37.3 us (18%)
  starting transfers between devices  33.3 us (16%)
  local copies, waits for them, and re-layouts  7.29 us (3%)
    pallas_call x1, Pallas kernels, factor(): pl.pallas_call(factor_kernel, out_shape=[jax.ShapeDtypeStruct((n * SIZE,...  48.1 us
    all_to_all x1, blocking collectives, sum_everywhere(): lax.all_to_all(parts, 'rows', 0, 0, axis_index_groups=groups, tiled=True)  37.3 us
    pallas_call x8, Pallas kernels, filter_call(): pl.pallas_call(functools.partial(kernel, step, last, source_at), out_shap...  22.2 us
    ppermute x6, waiting for transfers between devices, shards(): lax.ppermute(a, 'vecs', [(i, (i + s) % vecs) for i in range(vecs)])  14.7 us
    ppermute x4, waiting for transfers between devices, chebyshev(): far_halo = lax.ppermute(far_out, 'rows', between)  13.9 us
    all_to_all x1, waiting for transfers between devices, sum_everywhere(): lax.all_to_all(spread_out, 'rows', 0, 0, axis_index_groups=groups, tiled=...  13.7 us
    ppermute x4, starting transfers between devices, chebyshev(): far_halo = lax.ppermute(far_out, 'rows', between)  12.7 us
    pallas_call x1, Pallas kernels, apply(): pl.pallas_call(apply_kernel, out_shape=jax.ShapeDtypeStruct((4, 8, SIZE,...  8.32 us
  transfers between devices with their start and end apart: 20, of which 12 were waited for; matrix products, arithmetic and copies ran while one was open for 0% of the time, Pallas kernels for 32%

profile of v3, /device:TPU:1, one launch (start us, length us, event | category | flops | bytes accessed | tf_op | source)
XLA Modules:
  0.0 211.9 jit_solution(8444476068258519748)
XLA Ops:
  0.0 2.4 %constant_dynamic-slice_fusion = (bf16[8,128,256]{2,1,0:T(8,128)(2,1)}, bf16[8,128,256]{2,1,0:T(8,128)(2,1)}) fusion(bf16[32,128,256]{2,1,0:T(8,128)(2,1)} %bitcast.6, s32[]{:T(128)S(6)} %select_n.7, s32[]{:T(128)S(6)} %select_n.6), kind=kLoop, calls=%fused_computation.3 | loop fusion | bytes 2097160 | tf_op jit(solution)/shard_map/dynamic_slice | solution.py:215
  2.4 1.4 collective-permute-start.2
  3.9 3.2 %collective-permute-start = (bf16[8,128,256]{2,1,0:T(8,128)(2,1)}, bf16[8,128,256]{2,1,0:T(8,128)(2,1)S(1)}, u32[]{:S(2)}, u32[]{:S(2)}) collective-permute-start(bf16[8,128,256]{2,1,0:T(8,128)(2,1)} %get-tuple-element.68), channel_id=1, source_target_pairs={{4,8},{8,4},{12,16},{16,12},{20,24},{24,20},{28,32},{32,28},{36,40... | collective-permute-start | bytes 1572872 | tf_op jit(solution)/shard_map/ppermute | solution.py:218
  7.0 0.1 pad_add_fusion.place
  7.1 0.1 copy.4
  7.2 0.0 collective-permute-done.2.refs_2_
  7.2 0.0 copy-start
  7.2 2.5 %copy-done = bf16[32,5,128,128]{3,2,1,0:T(8,128)(2,1)S(1)} copy-done((bf16[32,5,128,128]{3,2,1,0:T(8,128)(2,1)S(1)}, bf16[32,5,128,128]{3,2,1,0:T(8,128)(2,1)}, u32[]{:S(2)}) %copy-start) | copy-done | bytes 5242904
  9.7 3.2 %filter_rest.4 = (f32[8,128,256]{2,1,0:T(8,128)S(1)}, f32[16,128,256]{2,1,0:T(8,128)S(1)}, bf16[8,128,256]{2,1,0:T(8,128)(2,1)S(1)}, bf16[16,128,256]{2,1,0:T(8,128)(2,1)S(1)}) custom-call(s32[32,5]{1,0:T(8,128)S(1)} %subtract_add_fusion.idx, s32[2]{0:T(128)S(1)} %pad_add_fusion.place, bf16[32,5,128,128]{3,2,1,0:T(8,128)(2,1)S(1)} %copy-done, ...), custom_call_target="tpu_custom_call" | custom-call | flops 1006632960 | bytes 12582912 | tf_op jit(solution)/shard_map/filter_rest/pallas_call | solution.py:183
  12.9 0.1 collective-permute-start.4
  13.0 1.6 collective-permute-done.refs_1_
  14.6 2.2 %filter_far.4 = (f32[8,128,256]{2,1,0:T(8,128)S(1)}, bf16[8,128,256]{2,1,0:T(8,128)(2,1)S(1)}) custom-call(s32[32,5]{1,0:T(8,128)S(1)} %subtract_add_fusion.idx, s32[2]{0:T(128)S(1)} %pad_add_fusion.place, bf16[32,5,128,128]{3,2,1,0:T(8,128)(2,1)S(1)} %copy-done, bf16[8,128,256]{2,1,0:T(8,128)(2,1)S(1)} %collective-permute-done.refs_1_, ...), custom_call_target="tpu_custom_call" | custom-call | flops 335544320 | bytes 4194304 | tf_op jit(solution)/shard_map/filter_far/pallas_call | solution.py:183
  16.7 3.2 %collective-permute-start.1 = (bf16[8,128,256]{2,1,0:T(8,128)(2,1)S(1)}, bf16[8,128,256]{2,1,0:T(8,128)(2,1)S(1)}, u32[]{:S(2)}, u32[]{:S(2)}) collective-permute-start(bf16[8,128,256]{2,1,0:T(8,128)(2,1)S(1)} %get-tuple-element.36.refs_2_.refs_5_), channel_id=1, source_target_pairs={{4,8},{8,4},{12,16},{16,12},{20,24},{24,20},{28,32},{32,28},{36,40... | collective-permute-start | bytes 1572872 | tf_op jit(solution)/shard_map/ppermute | solution.py:218
  19.9 0.0 collective-permute-done.4.refs_2_
  19.9 3.3 %filter_rest.5 = (f32[8,128,256]{2,1,0:T(8,128)S(1)}, f32[16,128,256]{2,1,0:T(8,128)S(1)}, bf16[8,128,256]{2,1,0:T(8,128)(2,1)S(1)}, bf16[16,128,256]{2,1,0:T(8,128)(2,1)S(1)}) custom-call(s32[32,5]{1,0:T(8,128)S(1)} %subtract_add_fusion.idx, s32[2]{0:T(128)S(1)} %pad_add_fusion.place, bf16[32,5,128,128]{3,2,1,0:T(8,128)(2,1)S(1)} %copy-done, ...), custom_call_target="tpu_custom_call" | custom-call | flops 1006632960 | bytes 12582912 | tf_op jit(solution)/shard_map/filter_rest/pallas_call | solution.py:183
  23.2 0.1 collective-permute-start.6
  23.3 3.9 %collective-permute-done.1.refs_1_ = bf16[8,128,256]{2,1,0:T(8,128)(2,1)S(1)} collective-permute-done((bf16[8,128,256]{2,1,0:T(8,128)(2,1)S(1)}, bf16[8,128,256]{2,1,0:T(8,128)(2,1)S(1)}, u32[]{:S(2)}, u32[]{:S(2)}) %collective-permute-start.1) | collective-permute-done | bytes 524320 | tf_op jit(solution)/shard_map/ppermute | solution.py:218
  27.2 2.2 %filter_far.5 = (f32[8,128,256]{2,1,0:T(8,128)S(1)}, bf16[8,128,256]{2,1,0:T(8,128)(2,1)S(1)}) custom-call(s32[32,5]{1,0:T(8,128)S(1)} %subtract_add_fusion.idx, s32[2]{0:T(128)S(1)} %pad_add_fusion.place, bf16[32,5,128,128]{3,2,1,0:T(8,128)(2,1)S(1)} %copy-done, bf16[8,128,256]{2,1,0:T(8,128)(2,1)S(1)} %collective-permute-done.1.refs_1_, ...), custom_call_target="tpu_custom_call" | custom-call | flops 335544320 | bytes 4194304 | tf_op jit(solution)/shard_map/filter_far/pallas_call | solution.py:183
  29.5 3.2 %collective-permute-start.3 = (bf16[8,128,256]{2,1,0:T(8,128)(2,1)S(1)}, bf16[8,128,256]{2,1,0:T(8,128)(2,1)S(1)}, u32[]{:S(2)}, u32[]{:S(2)}) collective-permute-start(bf16[8,128,256]{2,1,0:T(8,128)(2,1)S(1)} %get-tuple-element.39.refs_2_.refs_5_), channel_id=1, source_target_pairs={{4,8},{8,4},{12,16},{16,12},{20,24},{24,20},{28,32},{32,28},{36,40... | collective-permute-start | bytes 1572872 | tf_op jit(solution)/shard_map/ppermute | solution.py:218
  32.6 0.0 collective-permute-done.6.refs_2_
  32.6 3.2 %filter_rest.6 = (f32[8,128,256]{2,1,0:T(8,128)S(1)}, f32[16,128,256]{2,1,0:T(8,128)S(1)}, bf16[8,128,256]{2,1,0:T(8,128)(2,1)S(1)}, bf16[16,128,256]{2,1,0:T(8,128)(2,1)S(1)}) custom-call(s32[32,5]{1,0:T(8,128)S(1)} %subtract_add_fusion.idx, s32[2]{0:T(128)S(1)} %pad_add_fusion.place, bf16[32,5,128,128]{3,2,1,0:T(8,128)(2,1)S(1)} %copy-done, ...), custom_call_target="tpu_custom_call" | custom-call | flops 1006632960 | bytes 12582912 | tf_op jit(solution)/shard_map/filter_rest/pallas_call | solution.py:183
  35.9 0.1 collective-permute-start.7
  36.0 4.0 %collective-permute-done.3.refs_1_ = bf16[8,128,256]{2,1,0:T(8,128)(2,1)S(1)} collective-permute-done((bf16[8,128,256]{2,1,0:T(8,128)(2,1)S(1)}, bf16[8,128,256]{2,1,0:T(8,128)(2,1)S(1)}, u32[]{:S(2)}, u32[]{:S(2)}) %collective-permute-start.3) | collective-permute-done | bytes 524320 | tf_op jit(solution)/shard_map/ppermute | solution.py:218
  40.0 2.2 %filter_far.6 = (f32[8,128,256]{2,1,0:T(8,128)S(1)}, bf16[8,128,256]{2,1,0:T(8,128)(2,1)S(1)}) custom-call(s32[32,5]{1,0:T(8,128)S(1)} %subtract_add_fusion.idx, s32[2]{0:T(128)S(1)} %pad_add_fusion.place, bf16[32,5,128,128]{3,2,1,0:T(8,128)(2,1)S(1)} %copy-done, bf16[8,128,256]{2,1,0:T(8,128)(2,1)S(1)} %collective-permute-done.3.refs_1_, ...), custom_call_target="tpu_custom_call" | custom-call | flops 335544320 | bytes 4194304 | tf_op jit(solution)/shard_map/filter_far/pallas_call | solution.py:183
  42.2 3.2 %collective-permute-start.5 = (bf16[8,128,256]{2,1,0:T(8,128)(2,1)S(1)}, bf16[8,128,256]{2,1,0:T(8,128)(2,1)S(1)}, u32[]{:S(2)}, u32[]{:S(2)}) collective-permute-start(bf16[8,128,256]{2,1,0:T(8,128)(2,1)S(1)} %get-tuple-element.45.refs_5_.refs_2_), channel_id=1, source_target_pairs={{4,8},{8,4},{12,16},{16,12},{20,24},{24,20},{28,32},{32,28},{36,40... | collective-permute-start | bytes 1572872 | tf_op jit(solution)/shard_map/ppermute | solution.py:218
  45.3 0.0 collective-permute-done.7.refs_2_
  45.3 3.2 %filter_rest.7 = (bf16[8,128,256]{2,1,0:T(8,128)(2,1)S(1)}, bf16[16,128,256]{2,1,0:T(8,128)(2,1)S(1)}) custom-call(s32[32,5]{1,0:T(8,128)S(1)} %subtract_add_fusion.idx, s32[2]{0:T(128)S(1)} %pad_add_fusion.place, bf16[32,5,128,128]{3,2,1,0:T(8,128)(2,1)S(1)} %copy-done, bf16[32,5,128,128]{3,2,1,0:T(8,128)(2,1)S(1)} %copy-done, ...), custom_call_target="tpu_custom_call" | custom-call | flops 1006632960 | bytes 12582912 | tf_op jit(solution)/shard_map/filter_rest/pallas_call | solution.py:183
  48.6 4.4 %collective-permute-done.5.refs_1_ = bf16[8,128,256]{2,1,0:T(8,128)(2,1)S(1)} collective-permute-done((bf16[8,128,256]{2,1,0:T(8,128)(2,1)S(1)}, bf16[8,128,256]{2,1,0:T(8,128)(2,1)S(1)}, u32[]{:S(2)}, u32[]{:S(2)}) %collective-permute-start.5) | collective-permute-done | bytes 524320 | tf_op jit(solution)/shard_map/ppermute | solution.py:218
  53.0 2.7 %filter_far.7 = (bf16[8,128,256]{2,1,0:T(8,128)(2,1)S(1)}, bf16[8,128,256]{2,1,0:T(8,128)(2,1)S(1)}, bf16[8,128,256]{2,1,0:T(8,128)(2,1)S(1)}, bf16[8,128,256]{2,1,0:T(8,128)(2,1)S(1)}) custom-call(s32[32,5]{1,0:T(8,128)S(1)} %subtract_add_fusion.idx, s32[2]{0:T(128)S(1)} %pad_add_fusion.place, bf16[32,5,128,128]{3,2,1,0:T(8,128)(2,1)S(1)} %copy-done, ...), custom_call_target="tpu_custom_call" | custom-call | flops 335544320 | bytes 4194304 | tf_op jit(solution)/shard_map/filter_far/pallas_call | solution.py:183
  55.7 0.0 copy-start.4
  55.7 0.0 copy-start.6
  55.7 2.6 %collective-permute-start.10 = (bf16[8,128,256]{2,1,0:T(8,128)(2,1)S(1)}, bf16[8,128,256]{2,1,0:T(8,128)(2,1)S(1)}, u32[]{:S(2)}, u32[]{:S(2)}) collective-permute-start(bf16[8,128,256]{2,1,0:T(8,128)(2,1)S(1)} %get-tuple-element.59.refs_3_), channel_id=1, source_target_pairs={{0,3},{1,0},{2,1},{3,2},{4,7},{5,4},{6,5},{7,6},{8,11},{9,8},{10,9... | collective-permute-start | bytes 1572872 | tf_op jit(solution)/shard_map/ppermute | solution.py:542
  58.4 0.0 collective-permute-start.8
  58.4 1.7 collective-permute-start.9
  60.1 11.3 %collective-permute-done.10.got3.refs_6_ = bf16[8,128,256]{2,1,0:T(8,128)(2,1)S(1)} collective-permute-done((bf16[8,128,256]{2,1,0:T(8,128)(2,1)S(1)}, bf16[8,128,256]{2,1,0:T(8,128)(2,1)S(1)}, u32[]{:S(2)}, u32[]{:S(2)}) %collective-permute-start.10) | collective-permute-done | bytes 524320 | tf_op jit(solution)/shard_map/ppermute | solution.py:542
  71.4 3.4 %collective-permute-done.8.got1.refs_4_ = bf16[8,128,256]{2,1,0:T(8,128)(2,1)S(1)} collective-permute-done((bf16[8,128,256]{2,1,0:T(8,128)(2,1)S(1)}, bf16[8,128,256]{2,1,0:T(8,128)(2,1)S(1)}, u32[]{:S(2)}, u32[]{:S(2)}) %collective-permute-start.8) | collective-permute-done | bytes 524320 | tf_op jit(solution)/shard_map/ppermute | solution.py:542
  74.8 0.0 collective-permute-done.9.got2.refs_5_
  74.8 2.9 %gram.1 = (f32[5,256,256]{2,1,0:T(8,128)S(1)}, f32[5,256,256]{2,1,0:T(8,128)S(1)}, bf16[3,8,128,256]{3,2,1,0:T(8,128)(2,1)S(1)}, bf16[3,8,128,256]{3,2,1,0:T(8,128)(2,1)S(1)}, bf16[3,8,128,256]{3,2,1,0:T(8,128)(2,1)S(1)}) custom-call(s32[2]{0:T(128)S(1)} %pad_add_fusion.place, bf16[8,128,256]{2,1,0:T(8,128)(2,1)S(1)} %get-tuple-element.56.own.refs_0_, ...), custom_call_target="tpu_custom_call" | custom-call | flops 1342177280 | bytes 8388608 | tf_op jit(solution)/shard_map/gram/pallas_call | solution.py:270
  77.8 0.0 copy-start.3
  77.8 0.1 collective-permute-start.14
  77.9 3.0 %collective-permute-done.14 = f32[5,256,256]{2,1,0:T(8,128)S(1)} collective-permute-done((f32[5,256,256]{2,1,0:T(8,128)S(1)}, f32[5,256,256]{2,1,0:T(8,128)S(1)}, u32[]{:S(2)}, u32[]{:S(2)}) %collective-permute-start.14) | collective-permute-done | bytes 1310752 | tf_op jit(solution)/shard_map/ppermute | solution.py:297
  80.9 0.2 add.28
  81.1 37.3 %all_to_all.10 = f32[16,80,256]{2,1,0:T(8,128)S(1)} all-to-all(f32[16,80,256]{2,1,0:T(8,128)S(1)} %bitcast.20), channel_id=1, replica_groups={{0,8,16,24,32,40,48,56,64,72,80,88,96,104,112,120},{4,12,20,28,36,44,52..., dimensions={0} | all-to-all | bytes 2621440 | tf_op jit(solution)/shard_map/all_to_all | solution.py:299
  118.4 0.1 reduce_sum.9
  118.5 0.1 collective-permute-start.15
  118.6 0.9 collective-permute-start.16
  119.5 1.7 collective-permute-start.17
  121.2 2.3 %collective-permute-done.15 = f32[80,256]{1,0:T(8,128)S(1)} collective-permute-done((f32[80,256]{1,0:T(8,128)S(1)}, f32[80,256]{1,0:T(8,128)S(1)}, u32[]{:S(2)}, u32[]{:S(2)}) %collective-permute-start.15) | collective-permute-done | bytes 81952 | tf_op jit(solution)/shard_map/ppermute | solution.py:301
  123.5 0.4 collective-permute-done.16
  124.0 0.8 collective-permute-done.17
  124.8 1.2 broadcast_in_dim.2
  126.0 3.7 %all-to-all-start.1 = ((f32[16,80,256]{2,1,0:T(8,128)}), f32[16,80,256]{2,1,0:T(8,128)S(1)}, u32[]{:S(2)}, u32[]{:S(2)}) async-start(f32[16,80,256]{2,1,0:T(8,128)} %broadcast_in_dim.2), calls=%async_computation.1 | async-start | bytes 2621440 | tf_op jit(solution)/shard_map/all_to_all | solution.py:304
  129.8 1.2 collective-permute-start.11
  131.0 1.8 collective-permute-start.12
  132.8 0.7 collective-permute-start.13
  133.5 13.7 %all-to-all-done.1 = f32[16,80,256]{2,1,0:T(8,128)S(1)} async-done(((f32[16,80,256]{2,1,0:T(8,128)}), f32[16,80,256]{2,1,0:T(8,128)S(1)}, u32[]{:S(2)}, u32[]{:S(2)}) %all-to-all-start.1) | async-done | bytes 1310752 | tf_op jit(solution)/shard_map/all_to_all | solution.py:304
  147.2 4.4 %collective-permute-start.18 = (f32[5,256,256]{2,1,0:T(8,128)S(1)}, f32[5,256,256]{2,1,0:T(8,128)S(1)}, u32[]{:S(2)}, u32[]{:S(2)}) collective-permute-start(f32[5,256,256]{2,1,0:T(8,128)S(1)} %bitcast.18), channel_id=1, source_target_pairs={{0,4},{4,0},{8,12},{12,8},{16,20},{20,16},{24,28},{28,24},{32,36},... | collective-permute-start | bytes 3932168 | tf_op jit(solution)/shard_map/ppermute | solution.py:305
  151.5 2.7 %collective-permute-done.18.other = f32[5,256,256]{2,1,0:T(8,128)S(1)} collective-permute-done((f32[5,256,256]{2,1,0:T(8,128)S(1)}, f32[5,256,256]{2,1,0:T(8,128)S(1)}, u32[]{:S(2)}, u32[]{:S(2)}) %collective-permute-start.18) | collective-permute-done | bytes 1310752 | tf_op jit(solution)/shard_map/ppermute | solution.py:305
  154.2 48.1 %factor.1 = (bf16[1024,256]{1,0:T(8,128)(2,1)S(1)}, bf16[1024,256]{1,0:T(8,128)(2,1)S(1)}) custom-call(s32[2]{0:T(128)S(1)} %pad_add_fusion.place, f32[5,256,256]{2,1,0:T(8,128)S(1)} %bitcast.19, f32[5,256,256]{2,1,0:T(8,128)S(1)} %collective-permute-done.18.other), custom_call_target="tpu_custom_call" | custom-call | flops 1000000 | bytes 4194304 | tf_op jit(solution)/shard_map/factor/pallas_call | solution.py:447
  202.3 0.0 collective-permute-done.11.refs_7_
  202.3 0.0 collective-permute-done.12.refs_8_
  202.3 0.0 collective-permute-done.13.refs_9_
  202.4 1.0 copy-done.15
  203.4 8.3 %apply.1 = f32[4,8,128,256]{3,2,1,0:T(8,128)} custom-call(s32[2]{0:T(128)S(1)} %pad_add_fusion.place, bf16[8,128,256]{2,1,0:T(8,128)(2,1)S(1)} %get-tuple-element.56.own.refs_0_, bf16[8,128,256]{2,1,0:T(8,128)(2,1)S(1)} %copy-done.5, bf16[8,128,256]{2,1,0:T(8,128)(2,1)S(1)} %copy-done.7, bf16[8,128,256]{2,1,0:T(8,128)(2,1)S(1)} %copy-done.9, ...), custom_call_target="tpu_custom_call" | custom-call | flops 4294967296 | bytes 14680064 | tf_op jit(solution)/shard_map/apply/pallas_call | solution.py:516
  (30 shorter events, 0.1 us)
Async XLA Ops:
  0.0 7.2 %copy-start.1 = (bf16[4096,256]{1,0:T(8,128)(2,1)S(1)}, bf16[4096,256]{1,0:T(8,128)(2,1)}, u32[]{:S(2)}) copy-start(bf16[4096,256]{1,0:T(8,128)(2,1)} %param.3) | copy-start | bytes 6291460
  0.0 7.1 %copy-start.16 = (s32[32,5]{0,1:T(8,128)S(1)}, s32[32,5]{0,1:T(8,128)}, u32[]{:S(2)}) copy-start(s32[32,5]{0,1:T(8,128)} %param.5) | copy-start | bytes 1924
  2.4 4.8 %collective-permute-start.2 = (bf16[8,128,256]{2,1,0:T(8,128)(2,1)}, bf16[8,128,256]{2,1,0:T(8,128)(2,1)S(1)}, u32[]{:S(2)}, u32[]{:S(2)}) collective-permute-start(bf16[8,128,256]{2,1,0:T(8,128)(2,1)} %get-tuple-element.67), channel_id=1, source_target_pairs={{0,4},{4,0},{8,12},{12,8},{16,20},{20,16},{24,28},{28,24},{32,36},... | collective-permute-start | bytes 1572872 | tf_op jit(solution)/shard_map/ppermute | solution.py:219
  3.9 10.7 %collective-permute-start = (bf16[8,128,256]{2,1,0:T(8,128)(2,1)}, bf16[8,128,256]{2,1,0:T(8,128)(2,1)S(1)}, u32[]{:S(2)}, u32[]{:S(2)}) collective-permute-start(bf16[8,128,256]{2,1,0:T(8,128)(2,1)} %get-tuple-element.68), channel_id=1, source_target_pairs={{4,8},{8,4},{12,16},{16,12},{20,24},{24,20},{28,32},{32,28},{36,40... | collective-permute-start | bytes 1572872 | tf_op jit(solution)/shard_map/ppermute | solution.py:218
  7.2 2.5 %copy-start = (bf16[32,5,128,128]{3,2,1,0:T(8,128)(2,1)S(1)}, bf16[32,5,128,128]{3,2,1,0:T(8,128)(2,1)}, u32[]{:S(2)}) copy-start(bf16[32,5,128,128]{3,2,1,0:T(8,128)(2,1)} %refs_0_.15) | copy-start | bytes 15728644
  12.9 7.0 %collective-permute-start.4 = (bf16[8,128,256]{2,1,0:T(8,128)(2,1)S(1)}, bf16[8,128,256]{2,1,0:T(8,128)(2,1)S(1)}, u32[]{:S(2)}, u32[]{:S(2)}) collective-permute-start(bf16[8,128,256]{2,1,0:T(8,128)(2,1)S(1)} %get-tuple-element.40.refs_3_), channel_id=1, source_target_pairs={{0,4},{4,0},{8,12},{12,8},{16,20},{20,16},{24,28},{28,24},{32,36},... | collective-permute-start | bytes 1572872 | tf_op jit(solution)/shard_map/ppermute | solution.py:219
  16.7 10.5 %collective-permute-start.1 = (bf16[8,128,256]{2,1,0:T(8,128)(2,1)S(1)}, bf16[8,128,256]{2,1,0:T(8,128)(2,1)S(1)}, u32[]{:S(2)}, u32[]{:S(2)}) collective-permute-start(bf16[8,128,256]{2,1,0:T(8,128)(2,1)S(1)} %get-tuple-element.36.refs_2_.refs_5_), channel_id=1, source_target_pairs={{4,8},{8,4},{12,16},{16,12},{20,24},{24,20},{28,32},{32,28},{36,40... | collective-permute-start | bytes 1572872 | tf_op jit(solution)/shard_map/ppermute | solution.py:218
  23.2 9.4 %collective-permute-start.6 = (bf16[8,128,256]{2,1,0:T(8,128)(2,1)S(1)}, bf16[8,128,256]{2,1,0:T(8,128)(2,1)S(1)}, u32[]{:S(2)}, u32[]{:S(2)}) collective-permute-start(bf16[8,128,256]{2,1,0:T(8,128)(2,1)S(1)} %get-tuple-element.46.refs_3_), channel_id=1, source_target_pairs={{0,4},{4,0},{8,12},{12,8},{16,20},{20,16},{24,28},{28,24},{32,36},... | collective-permute-start | bytes 1572872 | tf_op jit(solution)/shard_map/ppermute | solution.py:219
  29.5 10.5 %collective-permute-start.3 = (bf16[8,128,256]{2,1,0:T(8,128)(2,1)S(1)}, bf16[8,128,256]{2,1,0:T(8,128)(2,1)S(1)}, u32[]{:S(2)}, u32[]{:S(2)}) collective-permute-start(bf16[8,128,256]{2,1,0:T(8,128)(2,1)S(1)} %get-tuple-element.39.refs_2_.refs_5_), channel_id=1, source_target_pairs={{4,8},{8,4},{12,16},{16,12},{20,24},{24,20},{28,32},{32,28},{36,40... | collective-permute-start | bytes 1572872 | tf_op jit(solution)/shard_map/ppermute | solution.py:218
  35.9 9.4 %collective-permute-start.7 = (bf16[8,128,256]{2,1,0:T(8,128)(2,1)S(1)}, bf16[8,128,256]{2,1,0:T(8,128)(2,1)S(1)}, u32[]{:S(2)}, u32[]{:S(2)}) collective-permute-start(bf16[8,128,256]{2,1,0:T(8,128)(2,1)S(1)} %get-tuple-element.51.refs_3_), channel_id=1, source_target_pairs={{0,4},{4,0},{8,12},{12,8},{16,20},{20,16},{24,28},{28,24},{32,36},... | collective-permute-start | bytes 1572872 | tf_op jit(solution)/shard_map/ppermute | solution.py:219
  42.2 10.8 %collective-permute-start.5 = (bf16[8,128,256]{2,1,0:T(8,128)(2,1)S(1)}, bf16[8,128,256]{2,1,0:T(8,128)(2,1)S(1)}, u32[]{:S(2)}, u32[]{:S(2)}) collective-permute-start(bf16[8,128,256]{2,1,0:T(8,128)(2,1)S(1)} %get-tuple-element.45.refs_5_.refs_2_), channel_id=1, source_target_pairs={{4,8},{8,4},{12,16},{16,12},{20,24},{24,20},{28,32},{32,28},{36,40... | collective-permute-start | bytes 1572872 | tf_op jit(solution)/shard_map/ppermute | solution.py:218
  55.7 22.0 %copy-start.4 = (bf16[8,128,256]{2,1,0:T(8,128)(2,1)}, bf16[8,128,256]{2,1,0:T(8,128)(2,1)S(1)}, u32[]{:S(2)}) copy-start(bf16[8,128,256]{2,1,0:T(8,128)(2,1)S(1)} %get-tuple-element.57.refs_1_) | copy-start | bytes 1572868
  55.7 22.0 %copy-start.6 = (bf16[8,128,256]{2,1,0:T(8,128)(2,1)}, bf16[8,128,256]{2,1,0:T(8,128)(2,1)S(1)}, u32[]{:S(2)}) copy-start(bf16[8,128,256]{2,1,0:T(8,128)(2,1)S(1)} %get-tuple-element.58.refs_2_) | copy-start | bytes 1572868
  55.7 22.0 %copy-start.8 = (bf16[8,128,256]{2,1,0:T(8,128)(2,1)}, bf16[8,128,256]{2,1,0:T(8,128)(2,1)S(1)}, u32[]{:S(2)}) copy-start(bf16[8,128,256]{2,1,0:T(8,128)(2,1)S(1)} %get-tuple-element.59.refs_3_) | copy-start | bytes 1572868
  55.7 15.7 %collective-permute-start.10 = (bf16[8,128,256]{2,1,0:T(8,128)(2,1)S(1)}, bf16[8,128,256]{2,1,0:T(8,128)(2,1)S(1)}, u32[]{:S(2)}, u32[]{:S(2)}) collective-permute-start(bf16[8,128,256]{2,1,0:T(8,128)(2,1)S(1)} %get-tuple-element.59.refs_3_), channel_id=1, source_target_pairs={{0,3},{1,0},{2,1},{3,2},{4,7},{5,4},{6,5},{7,6},{8,11},{9,8},{10,9... | collective-permute-start | bytes 1572872 | tf_op jit(solution)/shard_map/ppermute | solution.py:542
  58.4 16.4 %collective-permute-start.8 = (bf16[8,128,256]{2,1,0:T(8,128)(2,1)S(1)}, bf16[8,128,256]{2,1,0:T(8,128)(2,1)S(1)}, u32[]{:S(2)}, u32[]{:S(2)}) collective-permute-start(bf16[8,128,256]{2,1,0:T(8,128)(2,1)S(1)} %get-tuple-element.57.refs_1_), channel_id=1, source_target_pairs={{0,1},{1,2},{2,3},{3,0},{4,5},{5,6},{6,7},{7,4},{8,9},{9,10},{10,1... | collective-permute-start | bytes 1572872 | tf_op jit(solution)/shard_map/ppermute | solution.py:542
  58.4 16.4 %collective-permute-start.9 = (bf16[8,128,256]{2,1,0:T(8,128)(2,1)S(1)}, bf16[8,128,256]{2,1,0:T(8,128)(2,1)S(1)}, u32[]{:S(2)}, u32[]{:S(2)}) collective-permute-start(bf16[8,128,256]{2,1,0:T(8,128)(2,1)S(1)} %get-tuple-element.58.refs_2_), channel_id=1, source_target_pairs={{0,2},{1,3},{2,0},{3,1},{4,6},{5,7},{6,4},{7,5},{8,10},{9,11},{10,... | collective-permute-start | bytes 1572872 | tf_op jit(solution)/shard_map/ppermute | solution.py:542
  71.4 6.4 %copy-start.10 = (bf16[8,128,256]{2,1,0:T(8,128)(2,1)}, bf16[8,128,256]{2,1,0:T(8,128)(2,1)S(1)}, u32[]{:S(2)}) copy-start(bf16[8,128,256]{2,1,0:T(8,128)(2,1)S(1)} %collective-permute-done.10.got3.refs_6_) | copy-start | bytes 1572868
  74.8 3.0 %copy-start.12 = (bf16[8,128,256]{2,1,0:T(8,128)(2,1)}, bf16[8,128,256]{2,1,0:T(8,128)(2,1)S(1)}, u32[]{:S(2)}) copy-start(bf16[8,128,256]{2,1,0:T(8,128)(2,1)S(1)} %collective-permute-done.8.got1.refs_4_) | copy-start | bytes 1572868
  74.8 3.0 %copy-start.14 = (bf16[8,128,256]{2,1,0:T(8,128)(2,1)}, bf16[8,128,256]{2,1,0:T(8,128)(2,1)S(1)}, u32[]{:S(2)}) copy-start(bf16[8,128,256]{2,1,0:T(8,128)(2,1)S(1)} %collective-permute-done.9.got2.refs_5_) | copy-start | bytes 1572868
  77.8 3.3 %copy-start.2 = (bf16[3,8,128,256]{3,2,1,0:T(8,128)(2,1)}, bf16[3,8,128,256]{3,2,1,0:T(8,128)(2,1)S(1)}, u32[]{:S(2)}) copy-start(bf16[3,8,128,256]{3,2,1,0:T(8,128)(2,1)S(1)} %get-tuple-element.61) | copy-start | bytes 4718596
  77.8 3.3 %copy-start.3 = (bf16[3,8,128,256]{3,2,1,0:T(8,128)(2,1)}, bf16[3,8,128,256]{3,2,1,0:T(8,128)(2,1)S(1)}, u32[]{:S(2)}) copy-start(bf16[3,8,128,256]{3,2,1,0:T(8,128)(2,1)S(1)} %get-tuple-element.60) | copy-start | bytes 4718596
  77.8 3.1 %collective-permute-start.14 = (f32[5,256,256]{2,1,0:T(8,128)S(1)}, f32[5,256,256]{2,1,0:T(8,128)S(1)}, u32[]{:S(2)}, u32[]{:S(2)}) collective-permute-start(f32[5,256,256]{2,1,0:T(8,128)S(1)} %get-tuple-element.64), channel_id=1, source_target_pairs={{0,4},{4,0},{8,12},{12,8},{16,20},{20,16},{24,28},{28,24},{32,36},... | collective-permute-start | bytes 3932168 | tf_op jit(solution)/shard_map/ppermute | solution.py:297
  118.5 5.1 %collective-permute-start.15 = (f32[80,256]{1,0:T(8,128)S(1)}, f32[80,256]{1,0:T(8,128)S(1)}, u32[]{:S(2)}, u32[]{:S(2)}) collective-permute-start(f32[80,256]{1,0:T(8,128)S(1)} %reduce_sum.9), channel_id=1, source_target_pairs={{0,1},{1,2},{2,3},{3,0},{4,5},{5,6},{6,7},{7,4},{8,9},{9,10},{10,1... | collective-permute-start | bytes 245768 | tf_op jit(solution)/shard_map/ppermute | solution.py:301
  118.6 5.4 %collective-permute-start.16 = (f32[80,256]{1,0:T(8,128)S(1)}, f32[80,256]{1,0:T(8,128)S(1)}, u32[]{:S(2)}, u32[]{:S(2)}) collective-permute-start(f32[80,256]{1,0:T(8,128)S(1)} %reduce_sum.9), channel_id=1, source_target_pairs={{0,2},{1,3},{2,0},{3,1},{4,6},{5,7},{6,4},{7,5},{8,10},{9,11},{10,... | collective-permute-start | bytes 245768 | tf_op jit(solution)/shard_map/ppermute | solution.py:301
  119.5 5.3 %collective-permute-start.17 = (f32[80,256]{1,0:T(8,128)S(1)}, f32[80,256]{1,0:T(8,128)S(1)}, u32[]{:S(2)}, u32[]{:S(2)}) collective-permute-start(f32[80,256]{1,0:T(8,128)S(1)} %reduce_sum.9), channel_id=1, source_target_pairs={{0,3},{1,0},{2,1},{3,2},{4,7},{5,4},{6,5},{7,6},{8,11},{9,8},{10,9... | collective-permute-start | bytes 245768 | tf_op jit(solution)/shard_map/ppermute | solution.py:301
  126.0 21.1 %all-to-all-start.1 = ((f32[16,80,256]{2,1,0:T(8,128)}), f32[16,80,256]{2,1,0:T(8,128)S(1)}, u32[]{:S(2)}, u32[]{:S(2)}) async-start(f32[16,80,256]{2,1,0:T(8,128)} %broadcast_in_dim.2), calls=%async_computation.1 | async-start | bytes 2621440 | tf_op jit(solution)/shard_map/all_to_all | solution.py:304
  129.8 72.5 %collective-permute-start.11 = (bf16[3,8,128,256]{3,2,1,0:T(8,128)(2,1)}, bf16[3,8,128,256]{3,2,1,0:T(8,128)(2,1)}, u32[]{:S(2)}, u32[]{:S(2)}) collective-permute-start(bf16[3,8,128,256]{3,2,1,0:T(8,128)(2,1)} %copy-done.3), channel_id=1, source_target_pairs={{0,1},{1,2},{2,3},{3,0},{4,5},{5,6},{6,7},{7,4},{8,9},{9,10},{10,1... | collective-permute-start | bytes 4718600 | tf_op jit(solution)/shard_map/ppermute | solution.py:542
  131.0 71.3 %collective-permute-start.12 = (bf16[3,8,128,256]{3,2,1,0:T(8,128)(2,1)}, bf16[3,8,128,256]{3,2,1,0:T(8,128)(2,1)}, u32[]{:S(2)}, u32[]{:S(2)}) collective-permute-start(bf16[3,8,128,256]{3,2,1,0:T(8,128)(2,1)} %copy-done.2), channel_id=1, source_target_pairs={{0,2},{1,3},{2,0},{3,1},{4,6},{5,7},{6,4},{7,5},{8,10},{9,11},{10,... | collective-permute-start | bytes 4718600 | tf_op jit(solution)/shard_map/ppermute | solution.py:542
  132.8 69.5 %collective-permute-start.13 = (bf16[3,8,128,256]{3,2,1,0:T(8,128)(2,1)S(1)}, bf16[3,8,128,256]{3,2,1,0:T(8,128)(2,1)}, u32[]{:S(2)}, u32[]{:S(2)}) collective-permute-start(bf16[3,8,128,256]{3,2,1,0:T(8,128)(2,1)S(1)} %get-tuple-element.62), channel_id=1, source_target_pairs={{0,3},{1,0},{2,1},{3,2},{4,7},{5,4},{6,5},{7,6},{8,11},{9,8},{10,9... | collective-permute-start | bytes 4718600 | tf_op jit(solution)/shard_map/ppermute | solution.py:542
  147.1 55.2 %copy-start.5 = (bf16[8,128,256]{2,1,0:T(8,128)(2,1)S(1)}, bf16[8,128,256]{2,1,0:T(8,128)(2,1)}, u32[]{:S(2)}) copy-start(bf16[8,128,256]{2,1,0:T(8,128)(2,1)} %copy-done.4) | copy-start | bytes 1572868
  147.2 55.2 %copy-start.7 = (bf16[8,128,256]{2,1,0:T(8,128)(2,1)S(1)}, bf16[8,128,256]{2,1,0:T(8,128)(2,1)}, u32[]{:S(2)}) copy-start(bf16[8,128,256]{2,1,0:T(8,128)(2,1)} %copy-done.6) | copy-start | bytes 1572868
  147.2 55.2 %copy-start.9 = (bf16[8,128,256]{2,1,0:T(8,128)(2,1)S(1)}, bf16[8,128,256]{2,1,0:T(8,128)(2,1)}, u32[]{:S(2)}) copy-start(bf16[8,128,256]{2,1,0:T(8,128)(2,1)} %copy-done.8) | copy-start | bytes 1572868
  147.2 55.2 %copy-start.11 = (bf16[8,128,256]{2,1,0:T(8,128)(2,1)S(1)}, bf16[8,128,256]{2,1,0:T(8,128)(2,1)}, u32[]{:S(2)}) copy-start(bf16[8,128,256]{2,1,0:T(8,128)(2,1)} %copy-done.10) | copy-start | bytes 1572868
  147.2 55.2 %copy-start.13 = (bf16[8,128,256]{2,1,0:T(8,128)(2,1)S(1)}, bf16[8,128,256]{2,1,0:T(8,128)(2,1)}, u32[]{:S(2)}) copy-start(bf16[8,128,256]{2,1,0:T(8,128)(2,1)} %copy-done.12) | copy-start | bytes 1572868
  147.2 7.0 %collective-permute-start.18 = (f32[5,256,256]{2,1,0:T(8,128)S(1)}, f32[5,256,256]{2,1,0:T(8,128)S(1)}, u32[]{:S(2)}, u32[]{:S(2)}) collective-permute-start(f32[5,256,256]{2,1,0:T(8,128)S(1)} %bitcast.18), channel_id=1, source_target_pairs={{0,4},{4,0},{8,12},{12,8},{16,20},{20,16},{24,28},{28,24},{32,36},... | collective-permute-start | bytes 3932168 | tf_op jit(solution)/shard_map/ppermute | solution.py:305
  202.3 1.0 copy-start.15

commit v4 on v2

--- a/solution.py
+++ b/solution.py
@@ -53,13 +53,8 @@
     halo, far, mid = take(3)
     (current,) = take(1)
     older = take(1)[0] if step else None
-    if last:
-        near_new, mid_new = take(2)
-        sends = take(4)
-        pad, sems, rounded, out_sems = take(4)
-    else:
-        fresh, rounded = take(2)
-        pad, sems = take(2)
+    fresh = None if last else take(1)[0]
+    rounded, pad, sems = take(3)
     g = pl.program_id(0)
     per = blocks.shape[0]
     core = place[1]
@@ -80,30 +75,9 @@
     for r in range(per):
         product = row_product(idx, 24 * core + g * per + r, 24 * core, blocks, r, pad)
         newer = recurrence(step, product, current[r], older[r] if step else None)
-        if last:
-            rounded[g * per + r] = newer.astype(BF)
-        else:
+        if not last:
             fresh[r] = newer
-            rounded[r] = newer.astype(BF)
-
-    if last:
-
-        @pl.when(g == pl.num_programs(0) - 1)
-        def _():
-            sources = {
-                0: [rounded, mid_new.at[pl.ds(0, 8)], mid_new.at[pl.ds(8, 8)], near_new],
-                1: [near_new, mid_new.at[pl.ds(0, 8)], mid_new.at[pl.ds(8, 8)], rounded],
-            }
-            for s in range(4):
-                for q in range(4):
-                    for c in range(2):
-
-                        @pl.when((lax.rem(place[0] + s, 4) == q) & (core == c))
-                        def _():
-                            pltpu.make_async_copy(sources[c][q], sends[s], out_sems.at[s]).start()
-
-            for s in range(4):
-                pltpu.make_async_copy(rounded, sends[s], out_sems.at[s]).wait()
+        rounded[r] = newer.astype(BF)
 
 
 def rest_kernel(step, last, source_at, idx, place, *refs):
@@ -113,9 +87,14 @@
     halo, near, mid, far = take(4)
     current = take(2)
     older = take(2) if step else None
-    fresh = None if last else take(2)
-    rounded = take(2)
-    pad, sems = take(2)
+    if last:
+        sends = take(4)
+        pad, sems, near_new, mid_new, out_sems = take(5)
+        rounded = [near_new, mid_new]
+    else:
+        fresh = take(2)
+        rounded = take(2)
+        pad, sems = take(2)
     g = pl.program_id(0)
     core = place[1]
     near_at = 24 * (1 - core)
@@ -138,12 +117,31 @@
         for r in range(per):
             product = row_product(idx, first + g * per + r, 0, blocks[n], r, pad)
             newer = recurrence(step, product, current[n][r], older[n][r] if step else None)
-            if not last:
+            if last:
+                rounded[n][g * per + r] = newer.astype(BF)
+            else:
                 fresh[n][r] = newer
-            rounded[n][r] = newer.astype(BF)
-
-
-def filter_call(kernel, name, step, last, source_at, idx, place, parts, moved, halo, rounded, current, older, extra):
+                rounded[n][r] = newer.astype(BF)
+
+    if last:
+
+        @pl.when(g == pl.num_programs(0) - 1)
+        def _():
+            halves = [mid_new.at[pl.ds(0, 8)], mid_new.at[pl.ds(8, 8)]]
+            sources = {0: [near_new, halves[0], halves[1], near_new], 1: [near_new, halves[1], halves[0], near_new]}
+            for s in range(4):
+                for q in range(4):
+                    for c in range(2):
+
+                        @pl.when((lax.rem(place[2] + s, 4) == q) & (core == c))
+                        def _():
+                            pltpu.make_async_copy(sources[c][q], sends[s], out_sems.at[s]).start()
+
+            for s in range(4):
+                pltpu.make_async_copy(near_new, sends[s], out_sems.at[s]).wait()
+
+
+def filter_call(kernel, name, step, last, source_at, idx, place, parts, moved, halo, rounded, current, older, route):
     width = halo.shape[-1]
     nnz = parts["blocks"].shape[1]
     blocks = parts["blocks"]
@@ -173,12 +171,10 @@
         for key, count, per, first in groups:
             shapes.append(jax.ShapeDtypeStruct((count, SIZE, width), kind))
             out_specs.append(pl.BlockSpec((per, SIZE, width), lambda g, idx, place: (g, 0, 0)))
-    if extra:
-        in_specs += [ANY] * len(extra)
-        operands += extra
+    if route:
         shapes = [jax.ShapeDtypeStruct((8, SIZE, width), BF)] * 4
         out_specs = [ANY] * 4
-        scratch += [pltpu.VMEM((8, SIZE, width), BF), pltpu.SemaphoreType.DMA((4,))]
+        scratch += [pltpu.VMEM((count, SIZE, width), BF) for _, count, _, _ in groups] + [pltpu.SemaphoreType.DMA((4,))]
     total = sum(count for _, count, _, _ in groups)
     return pl.pallas_call(
         functools.partial(kernel, step, last, source_at),
@@ -219,30 +215,58 @@
         near_halo = lax.ppermute(near_out, "rows", within)
         common = (step, last, step == 0, idx, place)
         rest = filter_call(
-            rest_kernel, "filter_rest", *common, rest_parts, ["near", "mid", "far"], near_halo, rounded, current, older, None
+            rest_kernel, "filter_rest", *common, rest_parts, ["near", "mid", "far"], near_halo, rounded, current, older, last
         )
-        extra = rest if last else None
         far = filter_call(
-            far_kernel, "filter_far", *common, far_parts, ["far", "mid"], far_halo, rounded, current, older, extra
+            far_kernel, "filter_far", *common, far_parts, ["far", "mid"], far_halo, rounded, current, older, False
         )
         if last:
-            return far
+            return rest, far[0]
         older = current
         current = dict(near=rest[0], mid=rest[1], far=far[0])
         rounded = dict(near=rest[2], mid=rest[3], far=far[1])
         near_out, far_out = rounded["near"], rounded["far"]
 
 
-PAIRS = [(a, b) for a in range(4) for b in range(a, 4)]
+PAIRS = [(i, j) for i in range(8) for j in range(i, 8)]
 HALF = len(PAIRS) // 2
 
 
-def gram_kernel(total_rows, place, own, got1, got2, got3, keep, send, next1, next2, next3, f, g, sems, out_sems):
-    pieces = [own, got1, got2, got3]
-    x, core = place[0], place[1]
-    load_all([(pieces[s], f.at[lax.rem(x + 4 - s, 4)]) for s in range(4)], sems)
+def actual(label, core):
+    return label + core * (3 - 2 * label)
+
+
+def label_pairs(rows, vecs, shift, keep):
+    pairs = [(row, i, (i + shift) % vecs) for row in range(rows) for i in range(vecs)]
+    return [
+        (row * vecs + actual(i, row % 2), row * vecs + actual(j, row % 2)) for row, i, j in pairs if keep(j)
+    ]
+
+
+def gram_kernel(total_rows, place, *refs):
+    early, late = refs[0:4], refs[4:8]
+    keep, send, next1, next2, next3, f, g, sems, out_sems = refs[8:]
+    core, label = place[1], place[2]
+
+    def loads(pieces):
+        return [
+            pltpu.make_async_copy(pieces[s], f.at[actual(lax.rem(label + 4 - s, 4), core)], sems.at[s]) for s in range(4)
+        ]
+
+    @pl.when(label == 0)
+    def _():
+        for copy in loads(late):
+            copy.start()
+
+    @pl.when(label != 0)
+    def _():
+        for copy in loads(early):
+            copy.start()
+
+    for copy in loads(early):
+        copy.wait()
     copies = [
-        pltpu.make_async_copy(f.at[lax.rem(x + s + r, 4)], out.at[r - 1], out_sems.at[3 * s + r - 2])
+        pltpu.make_async_copy(f.at[actual(lax.rem(label + s + r, 4), core)], out.at[r - 1], out_sems.at[3 * s + r - 2])
         for s, out in ((1, next1), (2, next2), (3, next3))
         for r in (1, 2, 3)
     ]
@@ -253,9 +277,12 @@
     for a in range(4):
         left = f[a].reshape(depth, width).T
         for b in range(a, 4):
-            n = PAIRS.index((a, b))
-            tile = jnp.dot(left, f[b].reshape(depth, width), preferred_element_type=F32)
-            g[n // HALF, n % HALF] = tile * (1.0 / total_rows)
+            tile = jnp.dot(left, f[b].reshape(depth, width), preferred_element_type=F32) * (1.0 / total_rows)
+            for i in range(2):
+                for j in range(2):
+                    if 2 * a + i <= 2 * b + j:
+                        n = PAIRS.index((2 * a + i, 2 * b + j))
+                        g[n // HALF, n % HALF] = tile[i * SIZE : (i + 1) * SIZE, j * SIZE : (j + 1) * SIZE]
     copies.append(pltpu.make_async_copy(g.at[core], keep, out_sems.at[0]))
     copies.append(pltpu.make_async_copy(g.at[1 - core], send, out_sems.at[1]))
     for copy in copies[-2:]:
@@ -264,20 +291,20 @@
         copy.wait()
 
 
-def gram(total_rows, place, own, got):
-    width = own.shape[-1]
-    half = jax.ShapeDtypeStruct((HALF, width, width), F32)
+def gram(total_rows, place, early, late):
+    width = early[0].shape[-1]
+    half = jax.ShapeDtypeStruct((HALF, SIZE, SIZE), F32)
     return pl.pallas_call(
         functools.partial(gram_kernel, total_rows),
         out_shape=[half, half] + [jax.ShapeDtypeStruct((3, 8, SIZE, width), BF)] * 3,
         grid_spec=pltpu.PrefetchScalarGridSpec(
             num_scalar_prefetch=1,
             grid=(),
-            in_specs=[ANY] * 4,
+            in_specs=[ANY] * 8,
             out_specs=[ANY] * 5,
             scratch_shapes=[
                 pltpu.VMEM((4, 8, SIZE, width), BF),
-                pltpu.VMEM((2, HALF, width, width), F32),
+                pltpu.VMEM((2, HALF, SIZE, SIZE), F32),
                 pltpu.SemaphoreType.DMA((4,)),
                 pltpu.SemaphoreType.DMA((11,)),
             ],
@@ -285,7 +312,7 @@
         compiler_params=params(24),
         cost_estimate=pl.CostEstimate(flops=10 * 2 * 1024 * 256 * 256, bytes_accessed=8 * MIB, transcendentals=0),
         name="gram",
-    )(place, own, *got)
+    )(place, *early, *late)
 
 
 def sum_everywhere(keep, send):
@@ -295,14 +322,14 @@
     groups = [list(range(c, rows, 2)) for c in range(2)]
     count = rows // 2
     mine = keep + lax.ppermute(send, "rows", swap)
-    parts = mine.reshape(count, -1, SIZE)
+    parts = mine.reshape(count, -1, mine.shape[-1])
     parts = lax.all_to_all(parts, "rows", 0, 0, axis_index_groups=groups, tiled=True)
     part = jnp.sum(parts, axis=0)
     others = [lax.ppermute(part, "vecs", [(i, (i + s) % vecs) for i in range(vecs)]) for s in range(1, vecs)]
     part = part + sum(others)
     spread_out = jnp.broadcast_to(part[None], (count,) + part.shape)
     mine = lax.all_to_all(spread_out, "rows", 0, 0, axis_index_groups=groups, tiled=True).reshape(keep.shape)
-    return mine, lax.ppermute(mine, "rows", swap), part
+    return mine, lax.ppermute(mine, "rows", swap)
 
 
 def recip(x):
@@ -370,16 +397,16 @@
 
 def factor_kernel(place, mine, other, high_ref, low_ref, w, diag, following, left, right, sems):
     n = 8
-    x, core = place[0], place[1]
+    x, core, label = place[0], place[1], place[2]
     at = lambda i: pl.ds(pl.multiple_of(i * SIZE, SIZE), SIZE)
     exact = functools.partial(jnp.dot, preferred_element_type=F32, precision=EXACT)
 
     def copies(halves):
         return [
             pltpu.make_async_copy(
-                halves[m // HALF].at[m % HALF], w.at[pl.ds(256 * a, 256), pl.ds(256 * b, 256)], sems.at[m]
+                halves[m // HALF].at[m % HALF], w.at[pl.ds(SIZE * i, SIZE), pl.ds(SIZE * j, SIZE)], sems.at[m]
             )
-            for m, (a, b) in enumerate(PAIRS)
+            for m, (i, j) in enumerate(PAIRS)
         ]
 
     @pl.when(core == 0)
@@ -396,8 +423,8 @@
     left[...] = jnp.zeros(left.shape, BF)
     for copy in copies([mine, other]):
         copy.wait()
-    for a in range(1, 4):
-        w[pl.ds(256 * a, 256), pl.ds(0, 256 * a)] = jnp.zeros((256, 256 * a), F32)
+    for i in range(1, n):
+        w[pl.ds(SIZE * i, SIZE), pl.ds(0, SIZE * i)] = jnp.zeros((SIZE, SIZE * i), F32)
     w[pl.ds(n * SIZE, (n - 1) * SIZE), :] = jnp.zeros(((n - 1) * SIZE, n * SIZE), F32)
     following[...] = w[pl.ds(0, SIZE), pl.ds(0, SIZE)]
 
@@ -433,7 +460,7 @@
     for r in range(2):
         row = 2 * x + r
         for c in range(n):
-            column = 2 * lax.rem(x + c // 2, 4) + c % 2
+            column = 2 * actual(lax.rem(label + c // 2, 4), core) + c % 2
             value = jnp.where(column <= row, w[at(row), at(column)], 0.0)
             high = value.astype(BF)
             high_ref[pl.ds(SIZE * r, SIZE), pl.ds(SIZE * c, SIZE)] = high
@@ -461,26 +488,25 @@
             ],
         ),
         compiler_params=params(32),
-        cost_estimate=pl.CostEstimate(flops=20_000_000_000, bytes_accessed=4 * MIB, transcendentals=0),
+        cost_estimate=pl.CostEstimate(flops=1_000_000, bytes_accessed=4 * MIB, transcendentals=0),
         name="factor",
     )(place, mine, other)
 
 
 def apply_kernel(place, *refs):
-    own, got, far = refs[0:4], refs[4:7], refs[7:10]
-    high, low, out, tiles, sems = refs[10:]
-    x = place[0]
+    early, got_early, late, got_late, far = refs[0:4], refs[4:7], refs[7], refs[8:11], refs[11:14]
+    high, low, out, tiles, sems = refs[14:]
+    core, label = place[1], place[2]
     t = pl.program_id(0)
     steps = pl.num_programs(0)
-    per = own[0].shape[0]
-    width = own[0].shape[-1]
-    dims = (((1,), (1,)), ((), ()))
+    per = late.shape[0]
+    width = late.shape[-1]
     slot = lax.rem(t, 2)
 
     def copies(slot, t):
         return [
             pltpu.make_async_copy(
-                tiles.at[slot, s], out.at[lax.rem(x + 4 - s, 4), pl.ds(t * per, per)], sems.at[slot, s]
+                tiles.at[slot, s], out.at[actual(lax.rem(label + 4 - s, 4), core), pl.ds(t * per, per)], sems.at[slot, s]
             )
             for s in range(4)
         ]
@@ -490,11 +516,13 @@
         for copy in copies(slot, t - 2):
             copy.wait()
 
+    dims = (((1,), (1,)), ((), ()))
     for s in range(4):
+        own = jnp.where(lax.rem(label + 4 - s, 4) == 0, late[...], early[(4 - s) % 4][...])
         if s == 0:
-            panels = [own[0][...], got[2][...], got[1][...], got[0][...]]
+            panels = [own] + [jnp.where(label == 0, got_late[r][...], got_early[r][...]) for r in (2, 1, 0)]
         else:
-            panels = [own[4 - s][...]] + [far[s - 1][r] for r in range(3)]
+            panels = [own] + [far[s - 1][r] for r in range(3)]
         left = jnp.concatenate([p.reshape(per * SIZE, width) for p in panels], axis=1)
         value = lax.dot_general(left, high[...], dims, preferred_element_type=F32)
         value = value + lax.dot_general(left, low[...], dims, preferred_element_type=F32)
@@ -508,8 +536,8 @@
             copy.wait()
 
 
-def apply(place, own, got, far, high, low):
-    width = own[0].shape[-1]
+def apply(place, early, got_early, late, got_late, far, high, low):
+    width = late.shape[-1]
     per = 2
     whole = pl.BlockSpec(high.shape, lambda t, *_: (0, 0))
     rows = pl.BlockSpec((per, SIZE, width), lambda t, *_: (t, 0, 0))
@@ -519,14 +547,14 @@
         grid_spec=pltpu.PrefetchScalarGridSpec(
             num_scalar_prefetch=1,
             grid=(8 // per,),
-            in_specs=[rows] * 7 + [pl.BlockSpec((3, per, SIZE, width), lambda t, *_: (0, t, 0, 0))] * 3 + [whole, whole],
+            in_specs=[rows] * 11 + [pl.BlockSpec((3, per, SIZE, width), lambda t, *_: (0, t, 0, 0))] * 3 + [whole, whole],
             out_specs=ANY,
             scratch_shapes=[pltpu.VMEM((2, 4, per, SIZE, width), F32), pltpu.SemaphoreType.DMA((2, 4))],
         ),
         compiler_params=params(32),
         cost_estimate=pl.CostEstimate(flops=4 * 1024 * 1024 * 256 * 4, bytes_accessed=14 * MIB, transcendentals=0),
         name="apply",
-    )(place, *own, *got, *far, high, low)
+    )(place, *early, *got_early, late, *got_late, *far, high, low)
 
 
 def shards(vectors, blocks, columns):
@@ -537,15 +565,22 @@
     vecs = lax.axis_size("vecs")
     total_rows = vectors.shape[0] * lax.axis_size("rows")
     idx = columns - row * block_rows + REACH
-    place = jnp.stack([x, lax.rem(row, 2)]).astype(jnp.int32)
-    own = chebyshev(vectors.reshape(block_rows, SIZE, width), blocks, idx, place)
-    shift = lambda a, s: lax.ppermute(a, "vecs", [(i, (i + s) % vecs) for i in range(vecs)])
-    got = [shift(own[s], s) for s in range(1, vecs)]
-    keep, send, *following = gram(total_rows, place, own[0], got)
-    mine, other, part = sum_everywhere(keep, send)
-    far = [shift(following[s - 1], s) for s in range(1, vecs)]
+    core = lax.rem(row, 2)
+    label = actual(x, core)
+    place = jnp.stack([x, core, label]).astype(jnp.int32)
+    early, late = chebyshev(vectors.reshape(block_rows, SIZE, width), blocks, idx, place)
+    rows = lax.axis_size("rows")
+
+    def shift(a, s, keep):
+        return lax.ppermute(a, ("rows", "vecs"), label_pairs(rows, vecs, s, keep))
+
+    got_early = [shift(early[s], s, lambda j: j != 0) for s in range(1, vecs)]
+    got_late = [shift(late, s, lambda j: j == 0) for s in range(1, vecs)]
+    keep, send, *following = gram(total_rows, place, [early[0]] + got_early, [late] + got_late)
+    mine, other = sum_everywhere(keep, send)
+    far = [shift(following[s - 1], s, lambda j: True) for s in range(1, vecs)]
     inverse_high, inverse_low = factor(place, mine, other)
-    return apply(place, own, got, far, inverse_high, inverse_low).reshape(vectors.shape)
+    return apply(place, early, got_early, late, got_late, far, inverse_high, inverse_low).reshape(vectors.shape)
 
 
 def solution(mesh):

time: 235 us -> 221 us (0.940)
  blocking collectives: 59 us -> 31.7 us
  starting transfers between devices: 28.2 us -> 43.8 us
  waiting for transfers between devices: 53.4 us -> 44.7 us
    all_to_all x1 -> x0, blocking collectives: 21.6 us -> none  [sum_everywhere(): lax.all_to_all(spread_out, 'rows', 0, 0, axis_index_groups=groups, tiled=...]
    ppermute x7 -> x10, waiting for transfers between devices: 33.3 us -> 15.4 us  [the longest x9 13 us: shift(): return lax.ppermute(a, ('rows', 'vecs'), label_pairs(rows, vecs, s, keep))]
    all_to_all x0 -> x1, waiting for transfers between devices: none -> 13.3 us  [sum_everywhere(): lax.all_to_all(spread_out, 'rows', 0, 0, axis_index_groups=groups, tiled=...]
    ppermute x7 -> x10, starting transfers between devices: 11.1 us -> 21.5 us  [the longest x9 17.4 us: shift(): return lax.ppermute(a, ('rows', 'vecs'), label_pairs(rows, vecs, s, keep))]
    all_to_all x1, blocking collectives: 37.4 us -> 31.7 us  [sum_everywhere(): lax.all_to_all(parts, 'rows', 0, 0, axis_index_groups=groups, tiled=True)]
    ppermute x4, waiting for transfers between devices: 13.6 us -> 9.24 us  [chebyshev(): far_halo = lax.ppermute(far_out, 'rows', between)]
    all_to_all x0 -> x1, starting transfers between devices: none -> 3.7 us  [sum_everywhere(): lax.all_to_all(spread_out, 'rows', 0, 0, axis_index_groups=groups, tiled=...]
    unnamed x39 -> x45, local copies, waits for them, and re-layouts: 7.37 us -> 10.9 us
  transfers between devices with their start and end apart: 19 -> 23, of which waited for: 11 -> 10; matrix products, arithmetic and copies ran while one was open for 0% -> 0% of each run, Pallas kernels for 29% -> 33%
where the time goes in v4:
time: 221 us; the launch traced here: 219 us
  Pallas kernels  82.9 us (38%)
  waiting for transfers between devices  44.7 us (20%)
  starting transfers between devices  43.8 us (20%)
  blocking collectives  31.7 us (14%)
  local copies, waits for them, and re-layouts  14.5 us (7%)
    pallas_call x1, Pallas kernels, factor(): pl.pallas_call(factor_kernel, out_shape=[jax.ShapeDtypeStruct((2 * SIZE,...  48.6 us
    all_to_all x1, blocking collectives, sum_everywhere(): lax.all_to_all(parts, 'rows', 0, 0, axis_index_groups=groups, tiled=True)  31.7 us
    pallas_call x8, Pallas kernels, filter_call(): pl.pallas_call(functools.partial(kernel, step, last, source_at), out_shap...  22.6 us
    ppermute x9, starting transfers between devices, shift(): return lax.ppermute(a, ('rows', 'vecs'), label_pairs(rows, vecs, s, keep))  17.4 us
    all_to_all x1, waiting for transfers between devices, sum_everywhere(): lax.all_to_all(spread_out, 'rows', 0, 0, axis_index_groups=groups, tiled=...  13.3 us
    ppermute x9, waiting for transfers between devices, shift(): return lax.ppermute(a, ('rows', 'vecs'), label_pairs(rows, vecs, s, keep))  13 us
    ppermute x4, starting transfers between devices, chebyshev(): far_halo = lax.ppermute(far_out, 'rows', between)  12.7 us
    unnamed x45, local copies, waits for them, and re-layouts  10.9 us
  transfers between devices with their start and end apart: 23, of which 10 were waited for; matrix products, arithmetic and copies ran while one was open for 0% of the time, Pallas kernels for 33%

profile of v4, /device:TPU:1, one launch (start us, length us, event | category | flops | bytes accessed | tf_op | source)
XLA Modules:
  0.0 218.7 jit_solution(18283014254969764730)
XLA Ops:
  0.0 2.4 %constant_dynamic-slice_fusion = (bf16[8,128,256]{2,1,0:T(8,128)(2,1)}, bf16[8,128,256]{2,1,0:T(8,128)(2,1)}) fusion(bf16[32,128,256]{2,1,0:T(8,128)(2,1)} %bitcast.7, s32[]{:T(128)S(6)} %select_n.7, s32[]{:T(128)S(6)} %select_n.6), kind=kLoop, calls=%fused_computation.3 | loop fusion | bytes 2097160 | tf_op jit(solution)/shard_map/dynamic_slice | solution.py:210
  2.4 1.4 collective-permute-start
  3.8 3.2 %collective-permute-start.2 = (bf16[8,128,256]{2,1,0:T(8,128)(2,1)}, bf16[8,128,256]{2,1,0:T(8,128)(2,1)S(1)}, u32[]{:S(2)}, u32[]{:S(2)}) collective-permute-start(bf16[8,128,256]{2,1,0:T(8,128)(2,1)} %get-tuple-element.63), channel_id=1, source_target_pairs={{4,8},{8,4},{12,16},{16,12},{20,24},{24,20},{28,32},{32,28},{36,40... | collective-permute-start | bytes 1572872 | tf_op jit(solution)/shard_map/ppermute | solution.py:214
  7.0 0.1 copy.4
  7.1 0.1 pad_add_fusion.place
  7.2 0.0 copy-start
  7.2 2.5 %copy-done = bf16[32,5,128,128]{3,2,1,0:T(8,128)(2,1)S(1)} copy-done((bf16[32,5,128,128]{3,2,1,0:T(8,128)(2,1)S(1)}, bf16[32,5,128,128]{3,2,1,0:T(8,128)(2,1)}, u32[]{:S(2)}) %copy-start) | copy-done | bytes 5242904
  9.7 3.2 %filter_rest.4 = (f32[8,128,256]{2,1,0:T(8,128)S(1)}, f32[16,128,256]{2,1,0:T(8,128)S(1)}, bf16[8,128,256]{2,1,0:T(8,128)(2,1)S(1)}, bf16[16,128,256]{2,1,0:T(8,128)(2,1)S(1)}) custom-call(s32[32,5]{1,0:T(8,128)S(1)} %subtract_add_fusion.idx, s32[3]{0:T(128)S(1)} %pad_add_fusion.place, bf16[32,5,128,128]{3,2,1,0:T(8,128)(2,1)S(1)} %copy-done, ...), custom_call_target="tpu_custom_call" | custom-call | flops 1006632960 | bytes 12582912 | tf_op jit(solution)/shard_map/filter_rest/pallas_call | solution.py:179
  12.9 0.1 collective-permute-start.1
  13.0 1.5 collective-permute-done.2.refs_1_
  14.5 2.2 %filter_far.4 = (f32[8,128,256]{2,1,0:T(8,128)S(1)}, bf16[8,128,256]{2,1,0:T(8,128)(2,1)S(1)}) custom-call(s32[32,5]{1,0:T(8,128)S(1)} %subtract_add_fusion.idx, s32[3]{0:T(128)S(1)} %pad_add_fusion.place, bf16[32,5,128,128]{3,2,1,0:T(8,128)(2,1)S(1)} %copy-done, bf16[8,128,256]{2,1,0:T(8,128)(2,1)S(1)} %collective-permute-done.2.refs_1_, ...), custom_call_target="tpu_custom_call" | custom-call | flops 335544320 | bytes 4194304 | tf_op jit(solution)/shard_map/filter_far/pallas_call | solution.py:179
  16.7 3.2 %collective-permute-start.4 = (bf16[8,128,256]{2,1,0:T(8,128)(2,1)S(1)}, bf16[8,128,256]{2,1,0:T(8,128)(2,1)S(1)}, u32[]{:S(2)}, u32[]{:S(2)}) collective-permute-start(bf16[8,128,256]{2,1,0:T(8,128)(2,1)S(1)} %get-tuple-element.36.refs_5_.refs_2_), channel_id=1, source_target_pairs={{4,8},{8,4},{12,16},{16,12},{20,24},{24,20},{28,32},{32,28},{36,40... | collective-permute-start | bytes 1572872 | tf_op jit(solution)/shard_map/ppermute | solution.py:214
  19.9 0.0 collective-permute-done.1.refs_2_
  19.9 3.4 %filter_rest.5 = (f32[8,128,256]{2,1,0:T(8,128)S(1)}, f32[16,128,256]{2,1,0:T(8,128)S(1)}, bf16[8,128,256]{2,1,0:T(8,128)(2,1)S(1)}, bf16[16,128,256]{2,1,0:T(8,128)(2,1)S(1)}) custom-call(s32[32,5]{1,0:T(8,128)S(1)} %subtract_add_fusion.idx, s32[3]{0:T(128)S(1)} %pad_add_fusion.place, bf16[32,5,128,128]{3,2,1,0:T(8,128)(2,1)S(1)} %copy-done, ...), custom_call_target="tpu_custom_call" | custom-call | flops 1006632960 | bytes 12582912 | tf_op jit(solution)/shard_map/filter_rest/pallas_call | solution.py:179
  23.3 0.1 collective-permute-start.3
  23.4 3.9 %collective-permute-done.4.refs_1_ = bf16[8,128,256]{2,1,0:T(8,128)(2,1)S(1)} collective-permute-done((bf16[8,128,256]{2,1,0:T(8,128)(2,1)S(1)}, bf16[8,128,256]{2,1,0:T(8,128)(2,1)S(1)}, u32[]{:S(2)}, u32[]{:S(2)}) %collective-permute-start.4) | collective-permute-done | bytes 524320 | tf_op jit(solution)/shard_map/ppermute | solution.py:214
  27.2 2.2 %filter_far.5 = (f32[8,128,256]{2,1,0:T(8,128)S(1)}, bf16[8,128,256]{2,1,0:T(8,128)(2,1)S(1)}) custom-call(s32[32,5]{1,0:T(8,128)S(1)} %subtract_add_fusion.idx, s32[3]{0:T(128)S(1)} %pad_add_fusion.place, bf16[32,5,128,128]{3,2,1,0:T(8,128)(2,1)S(1)} %copy-done, bf16[8,128,256]{2,1,0:T(8,128)(2,1)S(1)} %collective-permute-done.4.refs_1_, ...), custom_call_target="tpu_custom_call" | custom-call | flops 335544320 | bytes 4194304 | tf_op jit(solution)/shard_map/filter_far/pallas_call | solution.py:179
  29.5 3.2 %collective-permute-start.6 = (bf16[8,128,256]{2,1,0:T(8,128)(2,1)S(1)}, bf16[8,128,256]{2,1,0:T(8,128)(2,1)S(1)}, u32[]{:S(2)}, u32[]{:S(2)}) collective-permute-start(bf16[8,128,256]{2,1,0:T(8,128)(2,1)S(1)} %get-tuple-element.42.refs_5_.refs_2_), channel_id=1, source_target_pairs={{4,8},{8,4},{12,16},{16,12},{20,24},{24,20},{28,32},{32,28},{36,40... | collective-permute-start | bytes 1572872 | tf_op jit(solution)/shard_map/ppermute | solution.py:214
  32.7 0.0 collective-permute-done.3.refs_2_
  32.7 3.3 %filter_rest.6 = (f32[8,128,256]{2,1,0:T(8,128)S(1)}, f32[16,128,256]{2,1,0:T(8,128)S(1)}, bf16[8,128,256]{2,1,0:T(8,128)(2,1)S(1)}, bf16[16,128,256]{2,1,0:T(8,128)(2,1)S(1)}) custom-call(s32[32,5]{1,0:T(8,128)S(1)} %subtract_add_fusion.idx, s32[3]{0:T(128)S(1)} %pad_add_fusion.place, bf16[32,5,128,128]{3,2,1,0:T(8,128)(2,1)S(1)} %copy-done, ...), custom_call_target="tpu_custom_call" | custom-call | flops 1006632960 | bytes 12582912 | tf_op jit(solution)/shard_map/filter_rest/pallas_call | solution.py:179
  36.0 0.1 collective-permute-start.5
  36.1 3.9 %collective-permute-done.6.refs_1_ = bf16[8,128,256]{2,1,0:T(8,128)(2,1)S(1)} collective-permute-done((bf16[8,128,256]{2,1,0:T(8,128)(2,1)S(1)}, bf16[8,128,256]{2,1,0:T(8,128)(2,1)S(1)}, u32[]{:S(2)}, u32[]{:S(2)}) %collective-permute-start.6) | collective-permute-done | bytes 524320 | tf_op jit(solution)/shard_map/ppermute | solution.py:214
  40.0 2.2 %filter_far.6 = (f32[8,128,256]{2,1,0:T(8,128)S(1)}, bf16[8,128,256]{2,1,0:T(8,128)(2,1)S(1)}) custom-call(s32[32,5]{1,0:T(8,128)S(1)} %subtract_add_fusion.idx, s32[3]{0:T(128)S(1)} %pad_add_fusion.place, bf16[32,5,128,128]{3,2,1,0:T(8,128)(2,1)S(1)} %copy-done, bf16[8,128,256]{2,1,0:T(8,128)(2,1)S(1)} %collective-permute-done.6.refs_1_, ...), custom_call_target="tpu_custom_call" | custom-call | flops 335544320 | bytes 4194304 | tf_op jit(solution)/shard_map/filter_far/pallas_call | solution.py:179
  42.2 3.2 %collective-permute-start.10 = (bf16[8,128,256]{2,1,0:T(8,128)(2,1)S(1)}, bf16[8,128,256]{2,1,0:T(8,128)(2,1)S(1)}, u32[]{:S(2)}, u32[]{:S(2)}) collective-permute-start(bf16[8,128,256]{2,1,0:T(8,128)(2,1)S(1)} %get-tuple-element.48.refs_5_.refs_2_), channel_id=1, source_target_pairs={{4,8},{8,4},{12,16},{16,12},{20,24},{24,20},{28,32},{32,28},{36,40... | collective-permute-start | bytes 1572872 | tf_op jit(solution)/shard_map/ppermute | solution.py:214
  45.4 3.8 %filter_rest.7 = (bf16[8,128,256]{2,1,0:T(8,128)(2,1)S(1)}, bf16[8,128,256]{2,1,0:T(8,128)(2,1)S(1)}, bf16[8,128,256]{2,1,0:T(8,128)(2,1)S(1)}, bf16[8,128,256]{2,1,0:T(8,128)(2,1)S(1)}) custom-call(s32[32,5]{1,0:T(8,128)S(1)} %subtract_add_fusion.idx, s32[3]{0:T(128)S(1)} %pad_add_fusion.place, bf16[32,5,128,128]{3,2,1,0:T(8,128)(2,1)S(1)} %copy-done, ...), custom_call_target="tpu_custom_call" | custom-call | flops 1006632960 | bytes 12582912 | tf_op jit(solution)/shard_map/filter_rest/pallas_call | solution.py:179
  49.2 1.3 collective-permute-start.7
  50.5 5.5 %collective-permute-start.8 = (bf16[8,128,256]{2,1,0:T(8,128)(2,1)S(1)}, bf16[8,128,256]{2,1,0:T(8,128)(2,1)S(1)}, u32[]{:S(2)}, u32[]{:S(2)}) collective-permute-start(bf16[8,128,256]{2,1,0:T(8,128)(2,1)S(1)} %get-tuple-element.53.refs_2_), channel_id=1, source_target_pairs={{0,2},{1,3},{3,1},{7,5},{6,4},{4,6},{8,10},{9,11},{11,9},{15,13},{... | collective-permute-start | bytes 1572872 | tf_op jit(solution)/shard_map/ppermute | solution.py:575
  56.1 1.9 collective-permute-start.9
  58.0 0.0 collective-permute-done.10.refs_1_
  58.0 2.2 %filter_far.7.refs_4_.refs_7_ = bf16[8,128,256]{2,1,0:T(8,128)(2,1)S(1)} custom-call(s32[32,5]{1,0:T(8,128)S(1)} %subtract_add_fusion.idx, s32[3]{0:T(128)S(1)} %pad_add_fusion.place, bf16[32,5,128,128]{3,2,1,0:T(8,128)(2,1)S(1)} %copy-done, bf16[8,128,256]{2,1,0:T(8,128)(2,1)S(1)} %collective-permute-done.10.refs_1_, ...), custom_call_target="tpu_custom_call" | custom-call | flops 335544320 | bytes 4194304 | tf_op jit(solution)/shard_map/filter_far/pallas_call | solution.py:179
  60.3 4.6 %collective-permute-start.11 = (bf16[8,128,256]{2,1,0:T(8,128)(2,1)S(1)}, bf16[8,128,256]{2,1,0:T(8,128)(2,1)S(1)}, u32[]{:S(2)}, u32[]{:S(2)}) collective-permute-start(bf16[8,128,256]{2,1,0:T(8,128)(2,1)S(1)} %filter_far.7.refs_4_.refs_7_), channel_id=1, source_target_pairs={{3,0},{4,7},{11,8},{12,15},{19,16},{20,23},{27,24},{28,31},{35,32}... | collective-permute-start | bytes 1572872 | tf_op jit(solution)/shard_map/ppermute | solution.py:575
  64.9 0.7 collective-permute-start.12
  65.6 0.0 collective-permute-done.7.refs_1_.refs_4_
  65.6 0.7 collective-permute-start.13
  66.3 12.9 %collective-permute-done.9.refs_3_.refs_6_ = bf16[8,128,256]{2,1,0:T(8,128)(2,1)S(1)} collective-permute-done((bf16[8,128,256]{2,1,0:T(8,128)(2,1)S(1)}, bf16[8,128,256]{2,1,0:T(8,128)(2,1)S(1)}, u32[]{:S(2)}, u32[]{:S(2)}) %collective-permute-start.9) | collective-permute-done | bytes 524320 | tf_op jit(solution)/shard_map/ppermute | solution.py:575
  79.3 3.3 %gram.1 = (f32[18,128,128]{2,1,0:T(8,128)S(1)}, f32[18,128,128]{2,1,0:T(8,128)S(1)}, bf16[3,8,128,256]{3,2,1,0:T(8,128)(2,1)S(1)}, bf16[3,8,128,256]{3,2,1,0:T(8,128)(2,1)S(1)}, bf16[3,8,128,256]{3,2,1,0:T(8,128)(2,1)S(1)}) custom-call(s32[3]{0:T(128)S(1)} %pad_add_fusion.place, bf16[8,128,256]{2,1,0:T(8,128)(2,1)S(1)} %get-tuple-element.51.refs_0_, ...), custom_call_target="tpu_custom_call" | custom-call | flops 1342177280 | bytes 8388608 | tf_op jit(solution)/shard_map/gram/pallas_call | solution.py:297
  82.7 0.0 copy-start.4
  82.8 0.9 collective-permute-start.17
  83.7 2.5 %collective-permute-done.17 = f32[18,128,128]{2,1,0:T(8,128)S(1)} collective-permute-done((f32[18,128,128]{2,1,0:T(8,128)S(1)}, f32[18,128,128]{2,1,0:T(8,128)S(1)}, u32[]{:S(2)}, u32[]{:S(2)}) %collective-permute-start.17) | collective-permute-done | bytes 1179680 | tf_op jit(solution)/shard_map/ppermute | solution.py:324
  86.2 0.2 add.32
  86.4 31.7 %all_to_all.10 = f32[16,144,128]{2,1,0:T(8,128)S(1)} all-to-all(f32[16,144,128]{2,1,0:T(8,128)S(1)} %bitcast.21), channel_id=1, replica_groups={{0,8,16,24,32,40,48,56,64,72,80,88,96,104,112,120},{4,12,20,28,36,44,52..., dimensions={0} | all-to-all | bytes 2359296 | tf_op jit(solution)/shard_map/all_to_all | solution.py:326
  118.1 0.1 reduce_sum.9
  118.2 2.1 collective-permute-start.20
  120.3 1.3 collective-permute-start.19
  121.5 0.1 collective-permute-done.20
  121.7 3.5 %collective-permute-done.18 = f32[144,128]{1,0:T(8,128)S(1)} collective-permute-done((f32[144,128]{1,0:T(8,128)S(1)}, f32[144,128]{1,0:T(8,128)S(1)}, u32[]{:S(2)}, u32[]{:S(2)}) %collective-permute-start.18) | collective-permute-done | bytes 73760 | tf_op jit(solution)/shard_map/ppermute | solution.py:328
  125.2 0.5 collective-permute-done.19
  125.8 1.2 broadcast_in_dim.2
  126.9 3.7 %all-to-all-start.1 = ((f32[16,144,128]{2,1,0:T(8,128)}), f32[16,144,128]{2,1,0:T(8,128)S(1)}, u32[]{:S(2)}, u32[]{:S(2)}) async-start(f32[16,144,128]{2,1,0:T(8,128)} %broadcast_in_dim.2), calls=%async_computation.1 | async-start | bytes 2359296 | tf_op jit(solution)/shard_map/all_to_all | solution.py:331
  130.6 2.0 collective-permute-start.14
  132.6 0.7 collective-permute-start.16
  133.3 13.3 %all-to-all-done.1 = f32[16,144,128]{2,1,0:T(8,128)S(1)} async-done(((f32[16,144,128]{2,1,0:T(8,128)}), f32[16,144,128]{2,1,0:T(8,128)S(1)}, u32[]{:S(2)}, u32[]{:S(2)}) %all-to-all-start.1) | async-done | bytes 1179680 | tf_op jit(solution)/shard_map/all_to_all | solution.py:331
  146.6 4.1 %collective-permute-start.21 = (f32[18,128,128]{2,1,0:T(8,128)S(1)}, f32[18,128,128]{2,1,0:T(8,128)S(1)}, u32[]{:S(2)}, u32[]{:S(2)}) collective-permute-start(f32[18,128,128]{2,1,0:T(8,128)S(1)} %bitcast.19), channel_id=1, source_target_pairs={{0,4},{4,0},{8,12},{12,8},{16,20},{20,16},{24,28},{28,24},{32,36},... | collective-permute-start | bytes 3538952 | tf_op jit(solution)/shard_map/ppermute | solution.py:332
  150.7 2.5 %collective-permute-done.21.other = f32[18,128,128]{2,1,0:T(8,128)S(1)} collective-permute-done((f32[18,128,128]{2,1,0:T(8,128)S(1)}, f32[18,128,128]{2,1,0:T(8,128)S(1)}, u32[]{:S(2)}, u32[]{:S(2)}) %collective-permute-start.21) | collective-permute-done | bytes 1179680 | tf_op jit(solution)/shard_map/ppermute | solution.py:332
  153.2 48.6 %factor.1 = (bf16[256,1024]{1,0:T(8,128)(2,1)S(1)}, bf16[256,1024]{1,0:T(8,128)(2,1)S(1)}) custom-call(s32[3]{0:T(128)S(1)} %pad_add_fusion.place, f32[18,128,128]{2,1,0:T(8,128)S(1)} %bitcast.20, f32[18,128,128]{2,1,0:T(8,128)S(1)} %collective-permute-done.21.other), custom_call_target="tpu_custom_call" | custom-call | flops 1000000 | bytes 4194304 | tf_op jit(solution)/shard_map/factor/pallas_call | solution.py:473
  201.8 1.0 copy-done.6
  202.8 1.0 copy-done.8
  203.8 1.0 copy-done.10
  204.9 1.0 copy-done.12
  205.9 1.0 copy-done.14
  207.0 1.0 copy-done.16
  208.0 1.0 copy-done.18
  209.0 1.0 copy-done.20
  210.1 8.5 %apply.1 = f32[4,8,128,256]{3,2,1,0:T(8,128)} custom-call(s32[3]{0:T(128)S(1)} %pad_add_fusion.place, bf16[8,128,256]{2,1,0:T(8,128)(2,1)S(1)} %get-tuple-element.51.refs_0_, bf16[8,128,256]{2,1,0:T(8,128)(2,1)S(1)} %get-tuple-element.52.refs_1_, bf16[8,128,256]{2,1,0:T(8,128)(2,1)S(1)} %copy-done.6, bf16[8,128,256]{2,1,0:T(8,128)(2,1)S(1)} %copy-done.8, ...), custom_call_target="tpu_custom_call" | custom-call | flops 4294967296 | bytes 14680064 | tf_op jit(solution)/shard_map/apply/pallas_call | solution.py:544
  (46 shorter events, 0.1 us)
Async XLA Ops:
  0.0 7.2 %copy-start.1 = (bf16[4096,256]{1,0:T(8,128)(2,1)S(1)}, bf16[4096,256]{1,0:T(8,128)(2,1)}, u32[]{:S(2)}) copy-start(bf16[4096,256]{1,0:T(8,128)(2,1)} %param.3) | copy-start | bytes 6291460
  0.0 7.0 %copy-start.21 = (s32[32,5]{0,1:T(8,128)S(1)}, s32[32,5]{0,1:T(8,128)}, u32[]{:S(2)}) copy-start(s32[32,5]{0,1:T(8,128)} %param.5) | copy-start | bytes 1924
  2.4 4.8 %collective-permute-start = (bf16[8,128,256]{2,1,0:T(8,128)(2,1)}, bf16[8,128,256]{2,1,0:T(8,128)(2,1)S(1)}, u32[]{:S(2)}, u32[]{:S(2)}) collective-permute-start(bf16[8,128,256]{2,1,0:T(8,128)(2,1)} %get-tuple-element.64), channel_id=1, source_target_pairs={{0,4},{4,0},{8,12},{12,8},{16,20},{20,16},{24,28},{28,24},{32,36},... | collective-permute-start | bytes 1572872 | tf_op jit(solution)/shard_map/ppermute | solution.py:215
  3.8 10.7 %collective-permute-start.2 = (bf16[8,128,256]{2,1,0:T(8,128)(2,1)}, bf16[8,128,256]{2,1,0:T(8,128)(2,1)S(1)}, u32[]{:S(2)}, u32[]{:S(2)}) collective-permute-start(bf16[8,128,256]{2,1,0:T(8,128)(2,1)} %get-tuple-element.63), channel_id=1, source_target_pairs={{4,8},{8,4},{12,16},{16,12},{20,24},{24,20},{28,32},{32,28},{36,40... | collective-permute-start | bytes 1572872 | tf_op jit(solution)/shard_map/ppermute | solution.py:214
  7.2 2.5 %copy-start = (bf16[32,5,128,128]{3,2,1,0:T(8,128)(2,1)S(1)}, bf16[32,5,128,128]{3,2,1,0:T(8,128)(2,1)}, u32[]{:S(2)}) copy-start(bf16[32,5,128,128]{3,2,1,0:T(8,128)(2,1)} %refs_0_.15) | copy-start | bytes 15728644
  12.9 7.0 %collective-permute-start.1 = (bf16[8,128,256]{2,1,0:T(8,128)(2,1)S(1)}, bf16[8,128,256]{2,1,0:T(8,128)(2,1)S(1)}, u32[]{:S(2)}, u32[]{:S(2)}) collective-permute-start(bf16[8,128,256]{2,1,0:T(8,128)(2,1)S(1)} %get-tuple-element.34.refs_3_), channel_id=1, source_target_pairs={{0,4},{4,0},{8,12},{12,8},{16,20},{20,16},{24,28},{28,24},{32,36},... | collective-permute-start | bytes 1572872 | tf_op jit(solution)/shard_map/ppermute | solution.py:215
  16.7 10.5 %collective-permute-start.4 = (bf16[8,128,256]{2,1,0:T(8,128)(2,1)S(1)}, bf16[8,128,256]{2,1,0:T(8,128)(2,1)S(1)}, u32[]{:S(2)}, u32[]{:S(2)}) collective-permute-start(bf16[8,128,256]{2,1,0:T(8,128)(2,1)S(1)} %get-tuple-element.36.refs_5_.refs_2_), channel_id=1, source_target_pairs={{4,8},{8,4},{12,16},{16,12},{20,24},{24,20},{28,32},{32,28},{36,40... | collective-permute-start | bytes 1572872 | tf_op jit(solution)/shard_map/ppermute | solution.py:214
  23.3 9.4 %collective-permute-start.3 = (bf16[8,128,256]{2,1,0:T(8,128)(2,1)S(1)}, bf16[8,128,256]{2,1,0:T(8,128)(2,1)S(1)}, u32[]{:S(2)}, u32[]{:S(2)}) collective-permute-start(bf16[8,128,256]{2,1,0:T(8,128)(2,1)S(1)} %get-tuple-element.39.refs_3_), channel_id=1, source_target_pairs={{0,4},{4,0},{8,12},{12,8},{16,20},{20,16},{24,28},{28,24},{32,36},... | collective-permute-start | bytes 1572872 | tf_op jit(solution)/shard_map/ppermute | solution.py:215
  29.5 10.5 %collective-permute-start.6 = (bf16[8,128,256]{2,1,0:T(8,128)(2,1)S(1)}, bf16[8,128,256]{2,1,0:T(8,128)(2,1)S(1)}, u32[]{:S(2)}, u32[]{:S(2)}) collective-permute-start(bf16[8,128,256]{2,1,0:T(8,128)(2,1)S(1)} %get-tuple-element.42.refs_5_.refs_2_), channel_id=1, source_target_pairs={{4,8},{8,4},{12,16},{16,12},{20,24},{24,20},{28,32},{32,28},{36,40... | collective-permute-start | bytes 1572872 | tf_op jit(solution)/shard_map/ppermute | solution.py:214
  36.0 9.4 %collective-permute-start.5 = (bf16[8,128,256]{2,1,0:T(8,128)(2,1)S(1)}, bf16[8,128,256]{2,1,0:T(8,128)(2,1)S(1)}, u32[]{:S(2)}, u32[]{:S(2)}) collective-permute-start(bf16[8,128,256]{2,1,0:T(8,128)(2,1)S(1)} %get-tuple-element.45.refs_3_), channel_id=1, source_target_pairs={{0,4},{4,0},{8,12},{12,8},{16,20},{20,16},{24,28},{28,24},{32,36},... | collective-permute-start | bytes 1572872 | tf_op jit(solution)/shard_map/ppermute | solution.py:215
  42.2 15.8 %collective-permute-start.10 = (bf16[8,128,256]{2,1,0:T(8,128)(2,1)S(1)}, bf16[8,128,256]{2,1,0:T(8,128)(2,1)S(1)}, u32[]{:S(2)}, u32[]{:S(2)}) collective-permute-start(bf16[8,128,256]{2,1,0:T(8,128)(2,1)S(1)} %get-tuple-element.48.refs_5_.refs_2_), channel_id=1, source_target_pairs={{4,8},{8,4},{12,16},{16,12},{20,24},{24,20},{28,32},{32,28},{36,40... | collective-permute-start | bytes 1572872 | tf_op jit(solution)/shard_map/ppermute | solution.py:214
  49.2 11.0 %copy-start.5 = (bf16[8,128,256]{2,1,0:T(8,128)(2,1)}, bf16[8,128,256]{2,1,0:T(8,128)(2,1)S(1)}, u32[]{:S(2)}) copy-start(bf16[8,128,256]{2,1,0:T(8,128)(2,1)S(1)} %get-tuple-element.53.refs_2_) | copy-start | bytes 1572868
  49.2 11.0 %copy-start.7 = (bf16[8,128,256]{2,1,0:T(8,128)(2,1)}, bf16[8,128,256]{2,1,0:T(8,128)(2,1)S(1)}, u32[]{:S(2)}) copy-start(bf16[8,128,256]{2,1,0:T(8,128)(2,1)S(1)} %get-tuple-element.54.refs_3_) | copy-start | bytes 1572868
  49.2 16.4 %collective-permute-start.7 = (bf16[8,128,256]{2,1,0:T(8,128)(2,1)S(1)}, bf16[8,128,256]{2,1,0:T(8,128)(2,1)S(1)}, u32[]{:S(2)}, u32[]{:S(2)}) collective-permute-start(bf16[8,128,256]{2,1,0:T(8,128)(2,1)S(1)} %get-tuple-element.52.refs_1_), channel_id=1, source_target_pairs={{0,1},{1,2},{2,3},{7,6},{6,5},{5,4},{8,9},{9,10},{10,11},{15,14},{... | collective-permute-start | bytes 1572872 | tf_op jit(solution)/shard_map/ppermute | solution.py:575
  50.5 15.8 %collective-permute-start.8 = (bf16[8,128,256]{2,1,0:T(8,128)(2,1)S(1)}, bf16[8,128,256]{2,1,0:T(8,128)(2,1)S(1)}, u32[]{:S(2)}, u32[]{:S(2)}) collective-permute-start(bf16[8,128,256]{2,1,0:T(8,128)(2,1)S(1)} %get-tuple-element.53.refs_2_), channel_id=1, source_target_pairs={{0,2},{1,3},{3,1},{7,5},{6,4},{4,6},{8,10},{9,11},{11,9},{15,13},{... | collective-permute-start | bytes 1572872 | tf_op jit(solution)/shard_map/ppermute | solution.py:575
  56.1 23.2 %collective-permute-start.9 = (bf16[8,128,256]{2,1,0:T(8,128)(2,1)S(1)}, bf16[8,128,256]{2,1,0:T(8,128)(2,1)S(1)}, u32[]{:S(2)}, u32[]{:S(2)}) collective-permute-start(bf16[8,128,256]{2,1,0:T(8,128)(2,1)S(1)} %get-tuple-element.54.refs_3_), channel_id=1, source_target_pairs={{0,3},{2,1},{3,2},{7,4},{5,6},{4,5},{8,11},{10,9},{11,10},{15,12},... | collective-permute-start | bytes 1572872 | tf_op jit(solution)/shard_map/ppermute | solution.py:575
  60.3 19.0 %collective-permute-start.11 = (bf16[8,128,256]{2,1,0:T(8,128)(2,1)S(1)}, bf16[8,128,256]{2,1,0:T(8,128)(2,1)S(1)}, u32[]{:S(2)}, u32[]{:S(2)}) collective-permute-start(bf16[8,128,256]{2,1,0:T(8,128)(2,1)S(1)} %filter_far.7.refs_4_.refs_7_), channel_id=1, source_target_pairs={{3,0},{4,7},{11,8},{12,15},{19,16},{20,23},{27,24},{28,31},{35,32}... | collective-permute-start | bytes 1572872 | tf_op jit(solution)/shard_map/ppermute | solution.py:575
  64.9 14.4 %collective-permute-start.12 = (bf16[8,128,256]{2,1,0:T(8,128)(2,1)S(1)}, bf16[8,128,256]{2,1,0:T(8,128)(2,1)S(1)}, u32[]{:S(2)}, u32[]{:S(2)}) collective-permute-start(bf16[8,128,256]{2,1,0:T(8,128)(2,1)S(1)} %filter_far.7.refs_4_.refs_7_), channel_id=1, source_target_pairs={{2,0},{5,7},{10,8},{13,15},{18,16},{21,23},{26,24},{29,31},{34,32}... | collective-permute-start | bytes 1572872 | tf_op jit(solution)/shard_map/ppermute | solution.py:575
  65.6 17.1 %copy-start.9 = (bf16[8,128,256]{2,1,0:T(8,128)(2,1)}, bf16[8,128,256]{2,1,0:T(8,128)(2,1)S(1)}, u32[]{:S(2)}) copy-start(bf16[8,128,256]{2,1,0:T(8,128)(2,1)S(1)} %collective-permute-done.7.refs_1_.refs_4_) | copy-start | bytes 1572868
  65.6 13.7 %collective-permute-start.13 = (bf16[8,128,256]{2,1,0:T(8,128)(2,1)S(1)}, bf16[8,128,256]{2,1,0:T(8,128)(2,1)S(1)}, u32[]{:S(2)}, u32[]{:S(2)}) collective-permute-start(bf16[8,128,256]{2,1,0:T(8,128)(2,1)S(1)} %filter_far.7.refs_4_.refs_7_), channel_id=1, source_target_pairs={{1,0},{6,7},{9,8},{14,15},{17,16},{22,23},{25,24},{30,31},{33,32},... | collective-permute-start | bytes 1572872 | tf_op jit(solution)/shard_map/ppermute | solution.py:575
  66.3 16.3 %copy-start.11 = (bf16[8,128,256]{2,1,0:T(8,128)(2,1)}, bf16[8,128,256]{2,1,0:T(8,128)(2,1)S(1)}, u32[]{:S(2)}) copy-start(bf16[8,128,256]{2,1,0:T(8,128)(2,1)S(1)} %collective-permute-done.8.refs_2_.refs_5_) | copy-start | bytes 1572868
  79.3 3.4 %copy-start.13 = (bf16[8,128,256]{2,1,0:T(8,128)(2,1)}, bf16[8,128,256]{2,1,0:T(8,128)(2,1)S(1)}, u32[]{:S(2)}) copy-start(bf16[8,128,256]{2,1,0:T(8,128)(2,1)S(1)} %collective-permute-done.9.refs_3_.refs_6_) | copy-start | bytes 1572868
  79.3 3.4 %copy-start.15 = (bf16[8,128,256]{2,1,0:T(8,128)(2,1)}, bf16[8,128,256]{2,1,0:T(8,128)(2,1)S(1)}, u32[]{:S(2)}) copy-start(bf16[8,128,256]{2,1,0:T(8,128)(2,1)S(1)} %collective-permute-done.11.refs_5_.refs_8_) | copy-start | bytes 1572868
  79.3 3.4 %copy-start.17 = (bf16[8,128,256]{2,1,0:T(8,128)(2,1)}, bf16[8,128,256]{2,1,0:T(8,128)(2,1)S(1)}, u32[]{:S(2)}) copy-start(bf16[8,128,256]{2,1,0:T(8,128)(2,1)S(1)} %collective-permute-done.12.refs_6_.refs_9_) | copy-start | bytes 1572868
  79.3 3.4 %copy-start.19 = (bf16[8,128,256]{2,1,0:T(8,128)(2,1)}, bf16[8,128,256]{2,1,0:T(8,128)(2,1)S(1)}, u32[]{:S(2)}) copy-start(bf16[8,128,256]{2,1,0:T(8,128)(2,1)S(1)} %collective-permute-done.13.refs_7_.refs_10_) | copy-start | bytes 1572868
  82.7 3.6 %copy-start.2 = (bf16[3,8,128,256]{3,2,1,0:T(8,128)(2,1)}, bf16[3,8,128,256]{3,2,1,0:T(8,128)(2,1)S(1)}, u32[]{:S(2)}) copy-start(bf16[3,8,128,256]{3,2,1,0:T(8,128)(2,1)S(1)} %get-tuple-element.58) | copy-start | bytes 4718596
  82.7 3.6 %copy-start.3 = (bf16[3,8,128,256]{3,2,1,0:T(8,128)(2,1)}, bf16[3,8,128,256]{3,2,1,0:T(8,128)(2,1)S(1)}, u32[]{:S(2)}) copy-start(bf16[3,8,128,256]{3,2,1,0:T(8,128)(2,1)S(1)} %get-tuple-element.57) | copy-start | bytes 4718596
  82.7 3.6 %copy-start.4 = (bf16[3,8,128,256]{3,2,1,0:T(8,128)(2,1)}, bf16[3,8,128,256]{3,2,1,0:T(8,128)(2,1)S(1)}, u32[]{:S(2)}) copy-start(bf16[3,8,128,256]{3,2,1,0:T(8,128)(2,1)S(1)} %get-tuple-element.56) | copy-start | bytes 4718596
  82.8 3.4 %collective-permute-start.17 = (f32[18,128,128]{2,1,0:T(8,128)S(1)}, f32[18,128,128]{2,1,0:T(8,128)S(1)}, u32[]{:S(2)}, u32[]{:S(2)}) collective-permute-start(f32[18,128,128]{2,1,0:T(8,128)S(1)} %get-tuple-element.60), channel_id=1, source_target_pairs={{0,4},{4,0},{8,12},{12,8},{16,20},{20,16},{24,28},{28,24},{32,36},... | collective-permute-start | bytes 3538952 | tf_op jit(solution)/shard_map/ppermute | solution.py:324
  118.2 3.5 %collective-permute-start.20 = (f32[144,128]{1,0:T(8,128)S(1)}, f32[144,128]{1,0:T(8,128)S(1)}, u32[]{:S(2)}, u32[]{:S(2)}) collective-permute-start(f32[144,128]{1,0:T(8,128)S(1)} %reduce_sum.9), channel_id=1, source_target_pairs={{0,3},{1,0},{2,1},{3,2},{4,7},{5,4},{6,5},{7,6},{8,11},{9,8},{10,9... | collective-permute-start | bytes 221192 | tf_op jit(solution)/shard_map/ppermute | solution.py:328
  120.3 4.9 %collective-permute-start.18 = (f32[144,128]{1,0:T(8,128)S(1)}, f32[144,128]{1,0:T(8,128)S(1)}, u32[]{:S(2)}, u32[]{:S(2)}) collective-permute-start(f32[144,128]{1,0:T(8,128)S(1)} %reduce_sum.9), channel_id=1, source_target_pairs={{0,1},{1,2},{2,3},{3,0},{4,5},{5,6},{6,7},{7,4},{8,9},{9,10},{10,1... | collective-permute-start | bytes 221192 | tf_op jit(solution)/shard_map/ppermute | solution.py:328
  120.3 5.5 %collective-permute-start.19 = (f32[144,128]{1,0:T(8,128)S(1)}, f32[144,128]{1,0:T(8,128)S(1)}, u32[]{:S(2)}, u32[]{:S(2)}) collective-permute-start(f32[144,128]{1,0:T(8,128)S(1)} %reduce_sum.9), channel_id=1, source_target_pairs={{0,2},{1,3},{2,0},{3,1},{4,6},{5,7},{6,4},{7,5},{8,10},{9,11},{10,... | collective-permute-start | bytes 221192 | tf_op jit(solution)/shard_map/ppermute | solution.py:328
  126.9 19.7 %all-to-all-start.1 = ((f32[16,144,128]{2,1,0:T(8,128)}), f32[16,144,128]{2,1,0:T(8,128)S(1)}, u32[]{:S(2)}, u32[]{:S(2)}) async-start(f32[16,144,128]{2,1,0:T(8,128)} %broadcast_in_dim.2), calls=%async_computation.1 | async-start | bytes 2359296 | tf_op jit(solution)/shard_map/all_to_all | solution.py:331
  130.6 71.1 %collective-permute-start.14 = (bf16[3,8,128,256]{3,2,1,0:T(8,128)(2,1)}, bf16[3,8,128,256]{3,2,1,0:T(8,128)(2,1)}, u32[]{:S(2)}, u32[]{:S(2)}) collective-permute-start(bf16[3,8,128,256]{3,2,1,0:T(8,128)(2,1)} %copy-done.4), channel_id=1, source_target_pairs={{0,1},{1,2},{2,3},{3,0},{7,6},{6,5},{5,4},{4,7},{8,9},{9,10},{10,1... | collective-permute-start | bytes 4718600 | tf_op jit(solution)/shard_map/ppermute | solution.py:575
  132.6 69.1 %collective-permute-start.15 = (bf16[3,8,128,256]{3,2,1,0:T(8,128)(2,1)}, bf16[3,8,128,256]{3,2,1,0:T(8,128)(2,1)}, u32[]{:S(2)}, u32[]{:S(2)}) collective-permute-start(bf16[3,8,128,256]{3,2,1,0:T(8,128)(2,1)} %copy-done.3), channel_id=1, source_target_pairs={{0,2},{1,3},{2,0},{3,1},{7,5},{6,4},{5,7},{4,6},{8,10},{9,11},{10,... | collective-permute-start | bytes 4718600 | tf_op jit(solution)/shard_map/ppermute | solution.py:575
  132.6 69.1 %collective-permute-start.16 = (bf16[3,8,128,256]{3,2,1,0:T(8,128)(2,1)}, bf16[3,8,128,256]{3,2,1,0:T(8,128)(2,1)}, u32[]{:S(2)}, u32[]{:S(2)}) collective-permute-start(bf16[3,8,128,256]{3,2,1,0:T(8,128)(2,1)} %copy-done.2), channel_id=1, source_target_pairs={{0,3},{1,0},{2,1},{3,2},{7,4},{6,7},{5,6},{4,5},{8,11},{9,8},{10,9... | collective-permute-start | bytes 4718600 | tf_op jit(solution)/shard_map/ppermute | solution.py:575
  146.6 6.5 %collective-permute-start.21 = (f32[18,128,128]{2,1,0:T(8,128)S(1)}, f32[18,128,128]{2,1,0:T(8,128)S(1)}, u32[]{:S(2)}, u32[]{:S(2)}) collective-permute-start(f32[18,128,128]{2,1,0:T(8,128)S(1)} %bitcast.19), channel_id=1, source_target_pairs={{0,4},{4,0},{8,12},{12,8},{16,20},{20,16},{24,28},{28,24},{32,36},... | collective-permute-start | bytes 3538952 | tf_op jit(solution)/shard_map/ppermute | solution.py:332
  201.7 1.0 copy-start.6
  202.8 1.0 copy-start.8
  203.8 1.0 copy-start.10
  204.9 1.0 copy-start.12
  205.9 1.0 copy-start.14
  207.0 1.0 copy-start.16
  208.0 1.0 copy-start.18
  209.0 1.0 copy-start.20

commit v5 on v3

--- a/solution.py
+++ b/solution.py
@@ -233,7 +233,7 @@
         near_out, far_out = rounded["near"], rounded["far"]
 
 
-PAIRS = [(a, b) for a in range(4) for b in range(a, 4)]
+PAIRS = [(i, j) for i in range(8) for j in range(i, 8)]
 HALF = len(PAIRS) // 2
 
 
@@ -253,9 +253,12 @@
     for a in range(4):
         left = f[a].reshape(depth, width).T
         for b in range(a, 4):
-            n = PAIRS.index((a, b))
-            tile = jnp.dot(left, f[b].reshape(depth, width), preferred_element_type=F32)
-            g[n // HALF, n % HALF] = tile * (1.0 / total_rows)
+            tile = jnp.dot(left, f[b].reshape(depth, width), preferred_element_type=F32) * (1.0 / total_rows)
+            for i in range(2):
+                for j in range(2):
+                    if 2 * a + i <= 2 * b + j:
+                        n = PAIRS.index((2 * a + i, 2 * b + j))
+                        g[n // HALF, n % HALF] = tile[i * SIZE : (i + 1) * SIZE, j * SIZE : (j + 1) * SIZE]
     copies.append(pltpu.make_async_copy(g.at[core], keep, out_sems.at[0]))
     copies.append(pltpu.make_async_copy(g.at[1 - core], send, out_sems.at[1]))
     for copy in copies[-2:]:
@@ -266,7 +269,7 @@
 
 def gram(total_rows, place, own, got):
     width = own.shape[-1]
-    half = jax.ShapeDtypeStruct((HALF, width, width), F32)
+    half = jax.ShapeDtypeStruct((HALF, SIZE, SIZE), F32)
     return pl.pallas_call(
         functools.partial(gram_kernel, total_rows),
         out_shape=[half, half] + [jax.ShapeDtypeStruct((3, 8, SIZE, width), BF)] * 3,
@@ -277,7 +280,7 @@
             out_specs=[ANY] * 5,
             scratch_shapes=[
                 pltpu.VMEM((4, 8, SIZE, width), BF),
-                pltpu.VMEM((2, HALF, width, width), F32),
+                pltpu.VMEM((2, HALF, SIZE, SIZE), F32),
                 pltpu.SemaphoreType.DMA((4,)),
                 pltpu.SemaphoreType.DMA((11,)),
             ],
@@ -377,9 +380,9 @@
     def copies(halves):
         return [
             pltpu.make_async_copy(
-                halves[m // HALF].at[m % HALF], w.at[pl.ds(256 * a, 256), pl.ds(256 * b, 256)], sems.at[m]
+                halves[m // HALF].at[m % HALF], w.at[pl.ds(SIZE * i, SIZE), pl.ds(SIZE * j, SIZE)], sems.at[m]
             )
-            for m, (a, b) in enumerate(PAIRS)
+            for m, (i, j) in enumerate(PAIRS)
         ]
 
     @pl.when(core == 0)
@@ -396,8 +399,8 @@
     left[...] = jnp.zeros(left.shape, BF)
     for copy in copies([mine, other]):
         copy.wait()
-    for a in range(1, 4):
-        w[pl.ds(256 * a, 256), pl.ds(0, 256 * a)] = jnp.zeros((256, 256 * a), F32)
+    for i in range(1, n):
+        w[pl.ds(SIZE * i, SIZE), pl.ds(0, SIZE * i)] = jnp.zeros((SIZE, SIZE * i), F32)
     w[pl.ds(n * SIZE, (n - 1) * SIZE), :] = jnp.zeros(((n - 1) * SIZE, n * SIZE), F32)
     following[...] = w[pl.ds(0, SIZE), pl.ds(0, SIZE)]
 
@@ -523,7 +526,7 @@
             out_specs=ANY,
             scratch_shapes=[pltpu.VMEM((2, 4, per, SIZE, width), F32), pltpu.SemaphoreType.DMA((2, 4))],
         ),
-        compiler_params=params(32),
+        compiler_params=params(60),
         cost_estimate=pl.CostEstimate(flops=4 * 1024 * 1024 * 256 * 4, bytes_accessed=14 * MIB, transcendentals=0),
         name="apply",
     )(place, *own, *got, *far, high, low)

time: 212 us -> 211 us (level)
  transfers between devices with their start and end apart: 20 -> 20, of which waited for: 12 -> 11; matrix products, arithmetic and copies ran while one was open for 0% -> 0% of each run, Pallas kernels for 32% -> 32%
where the time goes in v5:
time: 211 us; the launch traced here: 210 us
  Pallas kernels  83.4 us (40%)
  waiting for transfers between devices  49.5 us (23%)
  blocking collectives  36 us (17%)
  starting transfers between devices  33 us (16%)
  local copies, waits for them, and re-layouts  7.71 us (4%)
    pallas_call x1, Pallas kernels, factor(): pl.pallas_call(factor_kernel, out_shape=[jax.ShapeDtypeStruct((n * SIZE,...  48.4 us
    all_to_all x1, blocking collectives, sum_everywhere(): lax.all_to_all(parts, 'rows', 0, 0, axis_index_groups=groups, tiled=True)  36 us
    pallas_call x8, Pallas kernels, filter_call(): pl.pallas_call(functools.partial(kernel, step, last, source_at), out_shap...  22.2 us
    ppermute x6, waiting for transfers between devices, shards(): lax.ppermute(a, 'vecs', [(i, (i + s) % vecs) for i in range(vecs)])  14.7 us
    ppermute x4, waiting for transfers between devices, chebyshev(): far_halo = lax.ppermute(far_out, 'rows', between)  13.8 us
    ppermute x4, starting transfers between devices, chebyshev(): far_halo = lax.ppermute(far_out, 'rows', between)  12.7 us
    all_to_all x1, waiting for transfers between devices, sum_everywhere(): lax.all_to_all(spread_out, 'rows', 0, 0, axis_index_groups=groups, tiled=...  12.3 us
    pallas_call x1, Pallas kernels, apply(): pl.pallas_call(apply_kernel, out_shape=jax.ShapeDtypeStruct((4, 8, SIZE,...  9.54 us
  transfers between devices with their start and end apart: 20, of which 11 were waited for; matrix products, arithmetic and copies ran while one was open for 0% of the time, Pallas kernels for 32%

profile of v5, /device:TPU:1, one launch (start us, length us, event | category | flops | bytes accessed | tf_op | source)
XLA Modules:
  0.0 210.5 jit_solution(15448581187219130628)
XLA Ops:
  0.0 2.4 %constant_dynamic-slice_fusion = (bf16[8,128,256]{2,1,0:T(8,128)(2,1)}, bf16[8,128,256]{2,1,0:T(8,128)(2,1)}) fusion(bf16[32,128,256]{2,1,0:T(8,128)(2,1)} %bitcast.6, s32[]{:T(128)S(6)} %select_n.7, s32[]{:T(128)S(6)} %select_n.6), kind=kLoop, calls=%fused_computation.3 | loop fusion | bytes 2097160 | tf_op jit(solution)/shard_map/dynamic_slice | solution.py:215
  2.4 1.4 collective-permute-start.2
  3.9 3.2 %collective-permute-start = (bf16[8,128,256]{2,1,0:T(8,128)(2,1)}, bf16[8,128,256]{2,1,0:T(8,128)(2,1)S(1)}, u32[]{:S(2)}, u32[]{:S(2)}) collective-permute-start(bf16[8,128,256]{2,1,0:T(8,128)(2,1)} %get-tuple-element.68), channel_id=1, source_target_pairs={{4,8},{8,4},{12,16},{16,12},{20,24},{24,20},{28,32},{32,28},{36,40... | collective-permute-start | bytes 1572872 | tf_op jit(solution)/shard_map/ppermute | solution.py:218
  7.0 0.1 pad_add_fusion.place
  7.1 0.0 copy-done.14
  7.1 0.1 copy.4
  7.2 0.0 collective-permute-done.2.refs_2_
  7.2 0.0 copy-start
  7.2 2.5 %copy-done = bf16[32,5,128,128]{3,2,1,0:T(8,128)(2,1)S(1)} copy-done((bf16[32,5,128,128]{3,2,1,0:T(8,128)(2,1)S(1)}, bf16[32,5,128,128]{3,2,1,0:T(8,128)(2,1)}, u32[]{:S(2)}) %copy-start) | copy-done | bytes 5242904
  9.7 3.2 %filter_rest.4 = (f32[8,128,256]{2,1,0:T(8,128)S(1)}, f32[16,128,256]{2,1,0:T(8,128)S(1)}, bf16[8,128,256]{2,1,0:T(8,128)(2,1)S(1)}, bf16[16,128,256]{2,1,0:T(8,128)(2,1)S(1)}) custom-call(s32[32,5]{1,0:T(8,128)S(1)} %subtract_add_fusion.idx, s32[2]{0:T(128)S(1)} %pad_add_fusion.place, bf16[32,5,128,128]{3,2,1,0:T(8,128)(2,1)S(1)} %copy-done, ...), custom_call_target="tpu_custom_call" | custom-call | flops 1006632960 | bytes 12582912 | tf_op jit(solution)/shard_map/filter_rest/pallas_call | solution.py:183
  12.9 0.1 collective-permute-start.4
  13.0 1.6 collective-permute-done.refs_1_
  14.5 2.2 %filter_far.4 = (f32[8,128,256]{2,1,0:T(8,128)S(1)}, bf16[8,128,256]{2,1,0:T(8,128)(2,1)S(1)}) custom-call(s32[32,5]{1,0:T(8,128)S(1)} %subtract_add_fusion.idx, s32[2]{0:T(128)S(1)} %pad_add_fusion.place, bf16[32,5,128,128]{3,2,1,0:T(8,128)(2,1)S(1)} %copy-done, bf16[8,128,256]{2,1,0:T(8,128)(2,1)S(1)} %collective-permute-done.refs_1_, ...), custom_call_target="tpu_custom_call" | custom-call | flops 335544320 | bytes 4194304 | tf_op jit(solution)/shard_map/filter_far/pallas_call | solution.py:183
  16.7 3.2 %collective-permute-start.1 = (bf16[8,128,256]{2,1,0:T(8,128)(2,1)S(1)}, bf16[8,128,256]{2,1,0:T(8,128)(2,1)S(1)}, u32[]{:S(2)}, u32[]{:S(2)}) collective-permute-start(bf16[8,128,256]{2,1,0:T(8,128)(2,1)S(1)} %get-tuple-element.36.refs_2_.refs_5_), channel_id=1, source_target_pairs={{4,8},{8,4},{12,16},{16,12},{20,24},{24,20},{28,32},{32,28},{36,40... | collective-permute-start | bytes 1572872 | tf_op jit(solution)/shard_map/ppermute | solution.py:218
  19.9 0.0 collective-permute-done.4.refs_2_
  19.9 3.3 %filter_rest.5 = (f32[8,128,256]{2,1,0:T(8,128)S(1)}, f32[16,128,256]{2,1,0:T(8,128)S(1)}, bf16[8,128,256]{2,1,0:T(8,128)(2,1)S(1)}, bf16[16,128,256]{2,1,0:T(8,128)(2,1)S(1)}) custom-call(s32[32,5]{1,0:T(8,128)S(1)} %subtract_add_fusion.idx, s32[2]{0:T(128)S(1)} %pad_add_fusion.place, bf16[32,5,128,128]{3,2,1,0:T(8,128)(2,1)S(1)} %copy-done, ...), custom_call_target="tpu_custom_call" | custom-call | flops 1006632960 | bytes 12582912 | tf_op jit(solution)/shard_map/filter_rest/pallas_call | solution.py:183
  23.2 0.1 collective-permute-start.6
  23.3 3.9 %collective-permute-done.1.refs_1_ = bf16[8,128,256]{2,1,0:T(8,128)(2,1)S(1)} collective-permute-done((bf16[8,128,256]{2,1,0:T(8,128)(2,1)S(1)}, bf16[8,128,256]{2,1,0:T(8,128)(2,1)S(1)}, u32[]{:S(2)}, u32[]{:S(2)}) %collective-permute-start.1) | collective-permute-done | bytes 524320 | tf_op jit(solution)/shard_map/ppermute | solution.py:218
  27.2 2.2 %filter_far.5 = (f32[8,128,256]{2,1,0:T(8,128)S(1)}, bf16[8,128,256]{2,1,0:T(8,128)(2,1)S(1)}) custom-call(s32[32,5]{1,0:T(8,128)S(1)} %subtract_add_fusion.idx, s32[2]{0:T(128)S(1)} %pad_add_fusion.place, bf16[32,5,128,128]{3,2,1,0:T(8,128)(2,1)S(1)} %copy-done, bf16[8,128,256]{2,1,0:T(8,128)(2,1)S(1)} %collective-permute-done.1.refs_1_, ...), custom_call_target="tpu_custom_call" | custom-call | flops 335544320 | bytes 4194304 | tf_op jit(solution)/shard_map/filter_far/pallas_call | solution.py:183
  29.4 3.2 %collective-permute-start.3 = (bf16[8,128,256]{2,1,0:T(8,128)(2,1)S(1)}, bf16[8,128,256]{2,1,0:T(8,128)(2,1)S(1)}, u32[]{:S(2)}, u32[]{:S(2)}) collective-permute-start(bf16[8,128,256]{2,1,0:T(8,128)(2,1)S(1)} %get-tuple-element.39.refs_2_.refs_5_), channel_id=1, source_target_pairs={{4,8},{8,4},{12,16},{16,12},{20,24},{24,20},{28,32},{32,28},{36,40... | collective-permute-start | bytes 1572872 | tf_op jit(solution)/shard_map/ppermute | solution.py:218
  32.6 0.0 collective-permute-done.6.refs_2_
  32.6 3.3 %filter_rest.6 = (f32[8,128,256]{2,1,0:T(8,128)S(1)}, f32[16,128,256]{2,1,0:T(8,128)S(1)}, bf16[8,128,256]{2,1,0:T(8,128)(2,1)S(1)}, bf16[16,128,256]{2,1,0:T(8,128)(2,1)S(1)}) custom-call(s32[32,5]{1,0:T(8,128)S(1)} %subtract_add_fusion.idx, s32[2]{0:T(128)S(1)} %pad_add_fusion.place, bf16[32,5,128,128]{3,2,1,0:T(8,128)(2,1)S(1)} %copy-done, ...), custom_call_target="tpu_custom_call" | custom-call | flops 1006632960 | bytes 12582912 | tf_op jit(solution)/shard_map/filter_rest/pallas_call | solution.py:183
  35.9 0.1 collective-permute-start.7
  36.0 3.9 %collective-permute-done.3.refs_1_ = bf16[8,128,256]{2,1,0:T(8,128)(2,1)S(1)} collective-permute-done((bf16[8,128,256]{2,1,0:T(8,128)(2,1)S(1)}, bf16[8,128,256]{2,1,0:T(8,128)(2,1)S(1)}, u32[]{:S(2)}, u32[]{:S(2)}) %collective-permute-start.3) | collective-permute-done | bytes 524320 | tf_op jit(solution)/shard_map/ppermute | solution.py:218
  39.9 2.2 %filter_far.6 = (f32[8,128,256]{2,1,0:T(8,128)S(1)}, bf16[8,128,256]{2,1,0:T(8,128)(2,1)S(1)}) custom-call(s32[32,5]{1,0:T(8,128)S(1)} %subtract_add_fusion.idx, s32[2]{0:T(128)S(1)} %pad_add_fusion.place, bf16[32,5,128,128]{3,2,1,0:T(8,128)(2,1)S(1)} %copy-done, bf16[8,128,256]{2,1,0:T(8,128)(2,1)S(1)} %collective-permute-done.3.refs_1_, ...), custom_call_target="tpu_custom_call" | custom-call | flops 335544320 | bytes 4194304 | tf_op jit(solution)/shard_map/filter_far/pallas_call | solution.py:183
  42.2 3.2 %collective-permute-start.5 = (bf16[8,128,256]{2,1,0:T(8,128)(2,1)S(1)}, bf16[8,128,256]{2,1,0:T(8,128)(2,1)S(1)}, u32[]{:S(2)}, u32[]{:S(2)}) collective-permute-start(bf16[8,128,256]{2,1,0:T(8,128)(2,1)S(1)} %get-tuple-element.45.refs_5_.refs_2_), channel_id=1, source_target_pairs={{4,8},{8,4},{12,16},{16,12},{20,24},{24,20},{28,32},{32,28},{36,40... | collective-permute-start | bytes 1572872 | tf_op jit(solution)/shard_map/ppermute | solution.py:218
  45.3 0.0 collective-permute-done.7.refs_2_
  45.3 3.2 %filter_rest.7 = (bf16[8,128,256]{2,1,0:T(8,128)(2,1)S(1)}, bf16[16,128,256]{2,1,0:T(8,128)(2,1)S(1)}) custom-call(s32[32,5]{1,0:T(8,128)S(1)} %subtract_add_fusion.idx, s32[2]{0:T(128)S(1)} %pad_add_fusion.place, bf16[32,5,128,128]{3,2,1,0:T(8,128)(2,1)S(1)} %copy-done, bf16[32,5,128,128]{3,2,1,0:T(8,128)(2,1)S(1)} %copy-done, ...), custom_call_target="tpu_custom_call" | custom-call | flops 1006632960 | bytes 12582912 | tf_op jit(solution)/shard_map/filter_rest/pallas_call | solution.py:183
  48.6 4.4 %collective-permute-done.5.refs_1_ = bf16[8,128,256]{2,1,0:T(8,128)(2,1)S(1)} collective-permute-done((bf16[8,128,256]{2,1,0:T(8,128)(2,1)S(1)}, bf16[8,128,256]{2,1,0:T(8,128)(2,1)S(1)}, u32[]{:S(2)}, u32[]{:S(2)}) %collective-permute-start.5) | collective-permute-done | bytes 524320 | tf_op jit(solution)/shard_map/ppermute | solution.py:218
  53.0 2.7 %filter_far.7 = (bf16[8,128,256]{2,1,0:T(8,128)(2,1)S(1)}, bf16[8,128,256]{2,1,0:T(8,128)(2,1)S(1)}, bf16[8,128,256]{2,1,0:T(8,128)(2,1)S(1)}, bf16[8,128,256]{2,1,0:T(8,128)(2,1)S(1)}) custom-call(s32[32,5]{1,0:T(8,128)S(1)} %subtract_add_fusion.idx, s32[2]{0:T(128)S(1)} %pad_add_fusion.place, bf16[32,5,128,128]{3,2,1,0:T(8,128)(2,1)S(1)} %copy-done, ...), custom_call_target="tpu_custom_call" | custom-call | flops 335544320 | bytes 4194304 | tf_op jit(solution)/shard_map/filter_far/pallas_call | solution.py:183
  55.7 2.6 %collective-permute-start.10 = (bf16[8,128,256]{2,1,0:T(8,128)(2,1)S(1)}, bf16[8,128,256]{2,1,0:T(8,128)(2,1)S(1)}, u32[]{:S(2)}, u32[]{:S(2)}) collective-permute-start(bf16[8,128,256]{2,1,0:T(8,128)(2,1)S(1)} %get-tuple-element.59.refs_3_), channel_id=1, source_target_pairs={{0,3},{1,0},{2,1},{3,2},{4,7},{5,4},{6,5},{7,6},{8,11},{9,8},{10,9... | collective-permute-start | bytes 1572872 | tf_op jit(solution)/shard_map/ppermute | solution.py:545
  58.4 0.0 collective-permute-start.8
  58.4 1.7 collective-permute-start.9
  60.1 11.3 %collective-permute-done.10.got3.refs_6_ = bf16[8,128,256]{2,1,0:T(8,128)(2,1)S(1)} collective-permute-done((bf16[8,128,256]{2,1,0:T(8,128)(2,1)S(1)}, bf16[8,128,256]{2,1,0:T(8,128)(2,1)S(1)}, u32[]{:S(2)}, u32[]{:S(2)}) %collective-permute-start.10) | collective-permute-done | bytes 524320 | tf_op jit(solution)/shard_map/ppermute | solution.py:545
  71.4 3.4 %collective-permute-done.8.got1.refs_4_ = bf16[8,128,256]{2,1,0:T(8,128)(2,1)S(1)} collective-permute-done((bf16[8,128,256]{2,1,0:T(8,128)(2,1)S(1)}, bf16[8,128,256]{2,1,0:T(8,128)(2,1)S(1)}, u32[]{:S(2)}, u32[]{:S(2)}) %collective-permute-start.8) | collective-permute-done | bytes 524320 | tf_op jit(solution)/shard_map/ppermute | solution.py:545
  74.8 0.0 collective-permute-done.9.got2.refs_5_
  74.8 3.2 %gram.1 = (f32[18,128,128]{2,1,0:T(8,128)S(1)}, f32[18,128,128]{2,1,0:T(8,128)S(1)}, bf16[3,8,128,256]{3,2,1,0:T(8,128)(2,1)S(1)}, bf16[3,8,128,256]{3,2,1,0:T(8,128)(2,1)S(1)}, bf16[3,8,128,256]{3,2,1,0:T(8,128)(2,1)S(1)}) custom-call(s32[2]{0:T(128)S(1)} %pad_add_fusion.place, bf16[8,128,256]{2,1,0:T(8,128)(2,1)S(1)} %get-tuple-element.56.own.refs_0_, ...), custom_call_target="tpu_custom_call" | custom-call | flops 1342177280 | bytes 8388608 | tf_op jit(solution)/shard_map/gram/pallas_call | solution.py:273
  78.1 0.0 copy-start.4
  78.1 0.1 collective-permute-start.14
  78.2 2.8 %collective-permute-done.14 = f32[18,128,128]{2,1,0:T(8,128)S(1)} collective-permute-done((f32[18,128,128]{2,1,0:T(8,128)S(1)}, f32[18,128,128]{2,1,0:T(8,128)S(1)}, u32[]{:S(2)}, u32[]{:S(2)}) %collective-permute-start.14) | collective-permute-done | bytes 1179680 | tf_op jit(solution)/shard_map/ppermute | solution.py:300
  81.0 0.2 add.28
  81.2 36.0 %all_to_all.10 = f32[16,144,128]{2,1,0:T(8,128)S(1)} all-to-all(f32[16,144,128]{2,1,0:T(8,128)S(1)} %bitcast.20), channel_id=1, replica_groups={{0,8,16,24,32,40,48,56,64,72,80,88,96,104,112,120},{4,12,20,28,36,44,52..., dimensions={0} | all-to-all | bytes 2359296 | tf_op jit(solution)/shard_map/all_to_all | solution.py:302
  117.2 0.1 reduce_sum.9
  117.3 0.1 collective-permute-start.15
  117.4 0.8 collective-permute-start.16
  118.2 1.8 collective-permute-start.17
  120.1 2.5 %collective-permute-done.15 = f32[144,128]{1,0:T(8,128)S(1)} collective-permute-done((f32[144,128]{1,0:T(8,128)S(1)}, f32[144,128]{1,0:T(8,128)S(1)}, u32[]{:S(2)}, u32[]{:S(2)}) %collective-permute-start.15) | collective-permute-done | bytes 73760 | tf_op jit(solution)/shard_map/ppermute | solution.py:304
  122.6 0.0 collective-permute-done.16
  122.6 0.9 collective-permute-done.17
  123.5 1.1 broadcast_in_dim.2
  124.6 3.7 %all-to-all-start.1 = ((f32[16,144,128]{2,1,0:T(8,128)}), f32[16,144,128]{2,1,0:T(8,128)S(1)}, u32[]{:S(2)}, u32[]{:S(2)}) async-start(f32[16,144,128]{2,1,0:T(8,128)} %broadcast_in_dim.2), calls=%async_computation.1 | async-start | bytes 2359296 | tf_op jit(solution)/shard_map/all_to_all | solution.py:307
  128.3 1.2 collective-permute-start.11
  129.5 1.8 collective-permute-start.12
  131.3 0.7 collective-permute-start.13
  132.0 12.3 %all-to-all-done.1 = f32[16,144,128]{2,1,0:T(8,128)S(1)} async-done(((f32[16,144,128]{2,1,0:T(8,128)}), f32[16,144,128]{2,1,0:T(8,128)S(1)}, u32[]{:S(2)}, u32[]{:S(2)}) %all-to-all-start.1) | async-done | bytes 1179680 | tf_op jit(solution)/shard_map/all_to_all | solution.py:307
  144.3 4.0 %collective-permute-start.18 = (f32[18,128,128]{2,1,0:T(8,128)S(1)}, f32[18,128,128]{2,1,0:T(8,128)S(1)}, u32[]{:S(2)}, u32[]{:S(2)}) collective-permute-start(f32[18,128,128]{2,1,0:T(8,128)S(1)} %bitcast.18), channel_id=1, source_target_pairs={{0,4},{4,0},{8,12},{12,8},{16,20},{20,16},{24,28},{28,24},{32,36},... | collective-permute-start | bytes 3538952 | tf_op jit(solution)/shard_map/ppermute | solution.py:308
  148.3 2.5 %collective-permute-done.18.other = f32[18,128,128]{2,1,0:T(8,128)S(1)} collective-permute-done((f32[18,128,128]{2,1,0:T(8,128)S(1)}, f32[18,128,128]{2,1,0:T(8,128)S(1)}, u32[]{:S(2)}, u32[]{:S(2)}) %collective-permute-start.18) | collective-permute-done | bytes 1179680 | tf_op jit(solution)/shard_map/ppermute | solution.py:308
  150.8 48.4 %factor.1 = (bf16[1024,256]{1,0:T(8,128)(2,1)S(1)}, bf16[1024,256]{1,0:T(8,128)(2,1)S(1)}) custom-call(s32[2]{0:T(128)S(1)} %pad_add_fusion.place, f32[18,128,128]{2,1,0:T(8,128)S(1)} %bitcast.19, f32[18,128,128]{2,1,0:T(8,128)S(1)} %collective-permute-done.18.other), custom_call_target="tpu_custom_call" | custom-call | flops 1000000 | bytes 4194304 | tf_op jit(solution)/shard_map/factor/pallas_call | solution.py:450
  199.2 0.8 copy-done.12
  200.0 0.8 copy-done.13
  200.8 0.0 collective-permute-done.11.refs_7_
  200.8 0.0 collective-permute-done.12.refs_8_
  200.8 0.0 collective-permute-done.13.refs_9_
  200.8 9.5 %apply.1 = f32[4,8,128,256]{3,2,1,0:T(8,128)} custom-call(s32[2]{0:T(128)} %copy-done.2, bf16[8,128,256]{2,1,0:T(8,128)(2,1)} %copy-done.5, bf16[8,128,256]{2,1,0:T(8,128)(2,1)} %copy-done.6, bf16[8,128,256]{2,1,0:T(8,128)(2,1)} %copy-done.7, bf16[8,128,256]{2,1,0:T(8,128)(2,1)} %copy-done.8, bf16[8,128,256]{2,1,0:T(8,128)(2,1)} %copy-done.10, ...), custom_call_target="tpu_custom_call" | custom-call | flops 4294967296 | bytes 14680064 | tf_op jit(solution)/shard_map/apply/pallas_call | solution.py:519
  (26 shorter events, 0.1 us)
Async XLA Ops:
  0.0 7.2 %copy-start.1 = (bf16[4096,256]{1,0:T(8,128)(2,1)S(1)}, bf16[4096,256]{1,0:T(8,128)(2,1)}, u32[]{:S(2)}) copy-start(bf16[4096,256]{1,0:T(8,128)(2,1)} %param.3) | copy-start | bytes 6291460
  0.0 7.1 %copy-start.14 = (s32[32,5]{0,1:T(8,128)S(1)}, s32[32,5]{0,1:T(8,128)}, u32[]{:S(2)}) copy-start(s32[32,5]{0,1:T(8,128)} %param.5) | copy-start | bytes 1924
  2.4 4.8 %collective-permute-start.2 = (bf16[8,128,256]{2,1,0:T(8,128)(2,1)}, bf16[8,128,256]{2,1,0:T(8,128)(2,1)S(1)}, u32[]{:S(2)}, u32[]{:S(2)}) collective-permute-start(bf16[8,128,256]{2,1,0:T(8,128)(2,1)} %get-tuple-element.67), channel_id=1, source_target_pairs={{0,4},{4,0},{8,12},{12,8},{16,20},{20,16},{24,28},{28,24},{32,36},... | collective-permute-start | bytes 1572872 | tf_op jit(solution)/shard_map/ppermute | solution.py:219
  3.9 10.7 %collective-permute-start = (bf16[8,128,256]{2,1,0:T(8,128)(2,1)}, bf16[8,128,256]{2,1,0:T(8,128)(2,1)S(1)}, u32[]{:S(2)}, u32[]{:S(2)}) collective-permute-start(bf16[8,128,256]{2,1,0:T(8,128)(2,1)} %get-tuple-element.68), channel_id=1, source_target_pairs={{4,8},{8,4},{12,16},{16,12},{20,24},{24,20},{28,32},{32,28},{36,40... | collective-permute-start | bytes 1572872 | tf_op jit(solution)/shard_map/ppermute | solution.py:218
  7.1 143.7 %copy-start.2 = (s32[2]{0:T(128)}, s32[2]{0:T(128)S(1)}, u32[]{:S(2)}) copy-start(s32[2]{0:T(128)S(1)} %pad_add_fusion.place) | copy-start | bytes 28
  7.2 2.5 %copy-start = (bf16[32,5,128,128]{3,2,1,0:T(8,128)(2,1)S(1)}, bf16[32,5,128,128]{3,2,1,0:T(8,128)(2,1)}, u32[]{:S(2)}) copy-start(bf16[32,5,128,128]{3,2,1,0:T(8,128)(2,1)} %refs_0_.15) | copy-start | bytes 15728644
  12.9 7.0 %collective-permute-start.4 = (bf16[8,128,256]{2,1,0:T(8,128)(2,1)S(1)}, bf16[8,128,256]{2,1,0:T(8,128)(2,1)S(1)}, u32[]{:S(2)}, u32[]{:S(2)}) collective-permute-start(bf16[8,128,256]{2,1,0:T(8,128)(2,1)S(1)} %get-tuple-element.40.refs_3_), channel_id=1, source_target_pairs={{0,4},{4,0},{8,12},{12,8},{16,20},{20,16},{24,28},{28,24},{32,36},... | collective-permute-start | bytes 1572872 | tf_op jit(solution)/shard_map/ppermute | solution.py:219
  16.7 10.5 %collective-permute-start.1 = (bf16[8,128,256]{2,1,0:T(8,128)(2,1)S(1)}, bf16[8,128,256]{2,1,0:T(8,128)(2,1)S(1)}, u32[]{:S(2)}, u32[]{:S(2)}) collective-permute-start(bf16[8,128,256]{2,1,0:T(8,128)(2,1)S(1)} %get-tuple-element.36.refs_2_.refs_5_), channel_id=1, source_target_pairs={{4,8},{8,4},{12,16},{16,12},{20,24},{24,20},{28,32},{32,28},{36,40... | collective-permute-start | bytes 1572872 | tf_op jit(solution)/shard_map/ppermute | solution.py:218
  23.2 9.4 %collective-permute-start.6 = (bf16[8,128,256]{2,1,0:T(8,128)(2,1)S(1)}, bf16[8,128,256]{2,1,0:T(8,128)(2,1)S(1)}, u32[]{:S(2)}, u32[]{:S(2)}) collective-permute-start(bf16[8,128,256]{2,1,0:T(8,128)(2,1)S(1)} %get-tuple-element.46.refs_3_), channel_id=1, source_target_pairs={{0,4},{4,0},{8,12},{12,8},{16,20},{20,16},{24,28},{28,24},{32,36},... | collective-permute-start | bytes 1572872 | tf_op jit(solution)/shard_map/ppermute | solution.py:219
  29.4 10.5 %collective-permute-start.3 = (bf16[8,128,256]{2,1,0:T(8,128)(2,1)S(1)}, bf16[8,128,256]{2,1,0:T(8,128)(2,1)S(1)}, u32[]{:S(2)}, u32[]{:S(2)}) collective-permute-start(bf16[8,128,256]{2,1,0:T(8,128)(2,1)S(1)} %get-tuple-element.39.refs_2_.refs_5_), channel_id=1, source_target_pairs={{4,8},{8,4},{12,16},{16,12},{20,24},{24,20},{28,32},{32,28},{36,40... | collective-permute-start | bytes 1572872 | tf_op jit(solution)/shard_map/ppermute | solution.py:218
  35.9 9.4 %collective-permute-start.7 = (bf16[8,128,256]{2,1,0:T(8,128)(2,1)S(1)}, bf16[8,128,256]{2,1,0:T(8,128)(2,1)S(1)}, u32[]{:S(2)}, u32[]{:S(2)}) collective-permute-start(bf16[8,128,256]{2,1,0:T(8,128)(2,1)S(1)} %get-tuple-element.51.refs_3_), channel_id=1, source_target_pairs={{0,4},{4,0},{8,12},{12,8},{16,20},{20,16},{24,28},{28,24},{32,36},... | collective-permute-start | bytes 1572872 | tf_op jit(solution)/shard_map/ppermute | solution.py:219
  42.2 10.8 %collective-permute-start.5 = (bf16[8,128,256]{2,1,0:T(8,128)(2,1)S(1)}, bf16[8,128,256]{2,1,0:T(8,128)(2,1)S(1)}, u32[]{:S(2)}, u32[]{:S(2)}) collective-permute-start(bf16[8,128,256]{2,1,0:T(8,128)(2,1)S(1)} %get-tuple-element.45.refs_5_.refs_2_), channel_id=1, source_target_pairs={{4,8},{8,4},{12,16},{16,12},{20,24},{24,20},{28,32},{32,28},{36,40... | collective-permute-start | bytes 1572872 | tf_op jit(solution)/shard_map/ppermute | solution.py:218
  55.7 22.3 %copy-start.5 = (bf16[8,128,256]{2,1,0:T(8,128)(2,1)}, bf16[8,128,256]{2,1,0:T(8,128)(2,1)S(1)}, u32[]{:S(2)}) copy-start(bf16[8,128,256]{2,1,0:T(8,128)(2,1)S(1)} %get-tuple-element.56.own.refs_0_) | copy-start | bytes 1572868
  55.7 22.3 %copy-start.6 = (bf16[8,128,256]{2,1,0:T(8,128)(2,1)}, bf16[8,128,256]{2,1,0:T(8,128)(2,1)S(1)}, u32[]{:S(2)}) copy-start(bf16[8,128,256]{2,1,0:T(8,128)(2,1)S(1)} %get-tuple-element.57.refs_1_) | copy-start | bytes 1572868
  55.7 22.3 %copy-start.7 = (bf16[8,128,256]{2,1,0:T(8,128)(2,1)}, bf16[8,128,256]{2,1,0:T(8,128)(2,1)S(1)}, u32[]{:S(2)}) copy-start(bf16[8,128,256]{2,1,0:T(8,128)(2,1)S(1)} %get-tuple-element.58.refs_2_) | copy-start | bytes 1572868
  55.7 22.3 %copy-start.8 = (bf16[8,128,256]{2,1,0:T(8,128)(2,1)}, bf16[8,128,256]{2,1,0:T(8,128)(2,1)S(1)}, u32[]{:S(2)}) copy-start(bf16[8,128,256]{2,1,0:T(8,128)(2,1)S(1)} %get-tuple-element.59.refs_3_) | copy-start | bytes 1572868
  55.7 15.7 %collective-permute-start.10 = (bf16[8,128,256]{2,1,0:T(8,128)(2,1)S(1)}, bf16[8,128,256]{2,1,0:T(8,128)(2,1)S(1)}, u32[]{:S(2)}, u32[]{:S(2)}) collective-permute-start(bf16[8,128,256]{2,1,0:T(8,128)(2,1)S(1)} %get-tuple-element.59.refs_3_), channel_id=1, source_target_pairs={{0,3},{1,0},{2,1},{3,2},{4,7},{5,4},{6,5},{7,6},{8,11},{9,8},{10,9... | collective-permute-start | bytes 1572872 | tf_op jit(solution)/shard_map/ppermute | solution.py:545
  58.4 16.4 %collective-permute-start.8 = (bf16[8,128,256]{2,1,0:T(8,128)(2,1)S(1)}, bf16[8,128,256]{2,1,0:T(8,128)(2,1)S(1)}, u32[]{:S(2)}, u32[]{:S(2)}) collective-permute-start(bf16[8,128,256]{2,1,0:T(8,128)(2,1)S(1)} %get-tuple-element.57.refs_1_), channel_id=1, source_target_pairs={{0,1},{1,2},{2,3},{3,0},{4,5},{5,6},{6,7},{7,4},{8,9},{9,10},{10,1... | collective-permute-start | bytes 1572872 | tf_op jit(solution)/shard_map/ppermute | solution.py:545
  58.4 16.4 %collective-permute-start.9 = (bf16[8,128,256]{2,1,0:T(8,128)(2,1)S(1)}, bf16[8,128,256]{2,1,0:T(8,128)(2,1)S(1)}, u32[]{:S(2)}, u32[]{:S(2)}) collective-permute-start(bf16[8,128,256]{2,1,0:T(8,128)(2,1)S(1)} %get-tuple-element.58.refs_2_), channel_id=1, source_target_pairs={{0,2},{1,3},{2,0},{3,1},{4,6},{5,7},{6,4},{7,5},{8,10},{9,11},{10,... | collective-permute-start | bytes 1572872 | tf_op jit(solution)/shard_map/ppermute | solution.py:545
  71.4 6.7 %copy-start.9 = (bf16[8,128,256]{2,1,0:T(8,128)(2,1)}, bf16[8,128,256]{2,1,0:T(8,128)(2,1)S(1)}, u32[]{:S(2)}) copy-start(bf16[8,128,256]{2,1,0:T(8,128)(2,1)S(1)} %collective-permute-done.10.got3.refs_6_) | copy-start | bytes 1572868
  74.8 3.3 %copy-start.10 = (bf16[8,128,256]{2,1,0:T(8,128)(2,1)}, bf16[8,128,256]{2,1,0:T(8,128)(2,1)S(1)}, u32[]{:S(2)}) copy-start(bf16[8,128,256]{2,1,0:T(8,128)(2,1)S(1)} %collective-permute-done.8.got1.refs_4_) | copy-start | bytes 1572868
  74.8 3.3 %copy-start.11 = (bf16[8,128,256]{2,1,0:T(8,128)(2,1)}, bf16[8,128,256]{2,1,0:T(8,128)(2,1)S(1)}, u32[]{:S(2)}) copy-start(bf16[8,128,256]{2,1,0:T(8,128)(2,1)S(1)} %collective-permute-done.9.got2.refs_5_) | copy-start | bytes 1572868
  78.1 3.1 %copy-start.3 = (bf16[3,8,128,256]{3,2,1,0:T(8,128)(2,1)}, bf16[3,8,128,256]{3,2,1,0:T(8,128)(2,1)S(1)}, u32[]{:S(2)}) copy-start(bf16[3,8,128,256]{3,2,1,0:T(8,128)(2,1)S(1)} %get-tuple-element.61) | copy-start | bytes 4718596
  78.1 3.1 %copy-start.4 = (bf16[3,8,128,256]{3,2,1,0:T(8,128)(2,1)}, bf16[3,8,128,256]{3,2,1,0:T(8,128)(2,1)S(1)}, u32[]{:S(2)}) copy-start(bf16[3,8,128,256]{3,2,1,0:T(8,128)(2,1)S(1)} %get-tuple-element.60) | copy-start | bytes 4718596
  78.1 2.9 %collective-permute-start.14 = (f32[18,128,128]{2,1,0:T(8,128)S(1)}, f32[18,128,128]{2,1,0:T(8,128)S(1)}, u32[]{:S(2)}, u32[]{:S(2)}) collective-permute-start(f32[18,128,128]{2,1,0:T(8,128)S(1)} %get-tuple-element.64), channel_id=1, source_target_pairs={{0,4},{4,0},{8,12},{12,8},{16,20},{20,16},{24,28},{28,24},{32,36},... | collective-permute-start | bytes 3538952 | tf_op jit(solution)/shard_map/ppermute | solution.py:300
  117.3 5.3 %collective-permute-start.15 = (f32[144,128]{1,0:T(8,128)S(1)}, f32[144,128]{1,0:T(8,128)S(1)}, u32[]{:S(2)}, u32[]{:S(2)}) collective-permute-start(f32[144,128]{1,0:T(8,128)S(1)} %reduce_sum.9), channel_id=1, source_target_pairs={{0,1},{1,2},{2,3},{3,0},{4,5},{5,6},{6,7},{7,4},{8,9},{9,10},{10,1... | collective-permute-start | bytes 221192 | tf_op jit(solution)/shard_map/ppermute | solution.py:304
  117.4 5.2 %collective-permute-start.16 = (f32[144,128]{1,0:T(8,128)S(1)}, f32[144,128]{1,0:T(8,128)S(1)}, u32[]{:S(2)}, u32[]{:S(2)}) collective-permute-start(f32[144,128]{1,0:T(8,128)S(1)} %reduce_sum.9), channel_id=1, source_target_pairs={{0,2},{1,3},{2,0},{3,1},{4,6},{5,7},{6,4},{7,5},{8,10},{9,11},{10,... | collective-permute-start | bytes 221192 | tf_op jit(solution)/shard_map/ppermute | solution.py:304
  118.2 5.2 %collective-permute-start.17 = (f32[144,128]{1,0:T(8,128)S(1)}, f32[144,128]{1,0:T(8,128)S(1)}, u32[]{:S(2)}, u32[]{:S(2)}) collective-permute-start(f32[144,128]{1,0:T(8,128)S(1)} %reduce_sum.9), channel_id=1, source_target_pairs={{0,3},{1,0},{2,1},{3,2},{4,7},{5,4},{6,5},{7,6},{8,11},{9,8},{10,9... | collective-permute-start | bytes 221192 | tf_op jit(solution)/shard_map/ppermute | solution.py:304
  124.6 19.7 %all-to-all-start.1 = ((f32[16,144,128]{2,1,0:T(8,128)}), f32[16,144,128]{2,1,0:T(8,128)S(1)}, u32[]{:S(2)}, u32[]{:S(2)}) async-start(f32[16,144,128]{2,1,0:T(8,128)} %broadcast_in_dim.2), calls=%async_computation.1 | async-start | bytes 2359296 | tf_op jit(solution)/shard_map/all_to_all | solution.py:307
  128.3 72.5 %collective-permute-start.11 = (bf16[3,8,128,256]{3,2,1,0:T(8,128)(2,1)}, bf16[3,8,128,256]{3,2,1,0:T(8,128)(2,1)}, u32[]{:S(2)}, u32[]{:S(2)}) collective-permute-start(bf16[3,8,128,256]{3,2,1,0:T(8,128)(2,1)} %copy-done.4), channel_id=1, source_target_pairs={{0,1},{1,2},{2,3},{3,0},{4,5},{5,6},{6,7},{7,4},{8,9},{9,10},{10,1... | collective-permute-start | bytes 4718600 | tf_op jit(solution)/shard_map/ppermute | solution.py:545
  129.5 71.3 %collective-permute-start.12 = (bf16[3,8,128,256]{3,2,1,0:T(8,128)(2,1)}, bf16[3,8,128,256]{3,2,1,0:T(8,128)(2,1)}, u32[]{:S(2)}, u32[]{:S(2)}) collective-permute-start(bf16[3,8,128,256]{3,2,1,0:T(8,128)(2,1)} %copy-done.3), channel_id=1, source_target_pairs={{0,2},{1,3},{2,0},{3,1},{4,6},{5,7},{6,4},{7,5},{8,10},{9,11},{10,... | collective-permute-start | bytes 4718600 | tf_op jit(solution)/shard_map/ppermute | solution.py:545
  131.3 69.4 %collective-permute-start.13 = (bf16[3,8,128,256]{3,2,1,0:T(8,128)(2,1)S(1)}, bf16[3,8,128,256]{3,2,1,0:T(8,128)(2,1)}, u32[]{:S(2)}, u32[]{:S(2)}) collective-permute-start(bf16[3,8,128,256]{3,2,1,0:T(8,128)(2,1)S(1)} %get-tuple-element.62), channel_id=1, source_target_pairs={{0,3},{1,0},{2,1},{3,2},{4,7},{5,4},{6,5},{7,6},{8,11},{9,8},{10,9... | collective-permute-start | bytes 4718600 | tf_op jit(solution)/shard_map/ppermute | solution.py:545
  144.3 6.4 %collective-permute-start.18 = (f32[18,128,128]{2,1,0:T(8,128)S(1)}, f32[18,128,128]{2,1,0:T(8,128)S(1)}, u32[]{:S(2)}, u32[]{:S(2)}) collective-permute-start(f32[18,128,128]{2,1,0:T(8,128)S(1)} %bitcast.18), channel_id=1, source_target_pairs={{0,4},{4,0},{8,12},{12,8},{16,20},{20,16},{24,28},{28,24},{32,36},... | collective-permute-start | bytes 3538952 | tf_op jit(solution)/shard_map/ppermute | solution.py:308
  199.2 0.8 copy-start.12
  200.0 0.8 copy-start.13

commit v6 on v5

--- a/solution.py
+++ b/solution.py
@@ -46,151 +46,104 @@
     return newer - older.astype(F32) if step else newer
 
 
-def far_kernel(step, last, source_at, idx, place, *refs):
+def far_kernel(step, last, whole, idx, place, *refs):
     refs = list(refs)
     take = lambda n: [refs.pop(0) for _ in range(n)]
-    (blocks,) = take(1)
-    halo, far, mid = take(3)
-    (current,) = take(1)
+    blocks, halo, far, mid, current = take(5)
     older = take(1)[0] if step else None
     if last:
         near_new, mid_new = take(2)
         sends = take(4)
-        pad, sems, rounded, out_sems = take(4)
+        pad, rounded, out_sems = take(3)
     else:
-        fresh, rounded = take(2)
-        pad, sems = take(2)
-    g = pl.program_id(0)
-    per = blocks.shape[0]
+        fresh, rounded, pad = take(3)
     core = place[1]
-    far_at = 24 * core if source_at else 0
-    mid_at = 8 if source_at else 0
-
-    @pl.when(g == 0)
-    def _():
-        load_all(
-            [
-                (halo, pad.at[pl.ds(16 * core, 8)]),
-                (far.at[pl.ds(far_at, 8)], pad.at[pl.ds(8, 8)]),
-                (mid.at[pl.ds(mid_at + 8 * core, 8)], pad.at[pl.ds(16 * (1 - core), 8)]),
-            ],
-            sems,
-        )
-
-    for r in range(per):
-        product = row_product(idx, 24 * core + g * per + r, 24 * core, blocks, r, pad)
-        newer = recurrence(step, product, current[r], older[r] if step else None)
-        if last:
-            rounded[g * per + r] = newer.astype(BF)
-        else:
+    first = 24 * core
+    far_at = first if whole else 0
+    mid_at = (8 if whole else 0) + 8 * core
+    pad[pl.ds(16 * core, 8)] = halo[...]
+    pad[pl.ds(8, 8)] = far[pl.ds(far_at, 8)]
+    pad[pl.ds(16 * (1 - core), 8)] = mid[pl.ds(mid_at, 8)]
+    for r in range(8):
+        product = row_product(idx, first + r, first, blocks, first + r, pad)
+        newer = recurrence(step, product, current[far_at + r], older[(first if step == 1 else 0) + r] if step else None)
+        if not last:
             fresh[r] = newer
-            rounded[r] = newer.astype(BF)
+        rounded[r] = newer.astype(BF)
 
     if last:
-
-        @pl.when(g == pl.num_programs(0) - 1)
-        def _():
-            sources = {
-                0: [rounded, mid_new.at[pl.ds(0, 8)], mid_new.at[pl.ds(8, 8)], near_new],
-                1: [near_new, mid_new.at[pl.ds(0, 8)], mid_new.at[pl.ds(8, 8)], rounded],
-            }
-            for s in range(4):
-                for q in range(4):
-                    for c in range(2):
-
-                        @pl.when((lax.rem(place[0] + s, 4) == q) & (core == c))
-                        def _():
-                            pltpu.make_async_copy(sources[c][q], sends[s], out_sems.at[s]).start()
-
-            for s in range(4):
-                pltpu.make_async_copy(rounded, sends[s], out_sems.at[s]).wait()
-
-
-def rest_kernel(step, last, source_at, idx, place, *refs):
+        halves = [mid_new.at[pl.ds(0, 8)], mid_new.at[pl.ds(8, 8)]]
+        sources = {0: [rounded] + halves + [near_new], 1: [near_new] + halves + [rounded]}
+        for s in range(4):
+            for q in range(4):
+                for c in range(2):
+
+                    @pl.when((lax.rem(place[0] + s, 4) == q) & (core == c))
+                    def _():
+                        pltpu.make_async_copy(sources[c][q], sends[s], out_sems.at[s]).start()
+
+        for s in range(4):
+            pltpu.make_async_copy(rounded, sends[s], out_sems.at[s]).wait()
+
+
+def rest_kernel(step, last, whole, idx, place, *refs):
     refs = list(refs)
     take = lambda n: [refs.pop(0) for _ in range(n)]
-    blocks = take(2)
-    halo, near, mid, far = take(4)
+    blocks, halo, near, mid, far = take(5)
     current = take(2)
     older = take(2) if step else None
     fresh = None if last else take(2)
     rounded = take(2)
-    pad, sems = take(2)
-    g = pl.program_id(0)
+    (pad,) = take(1)
     core = place[1]
     near_at = 24 * (1 - core)
     far_at = 24 * core
-
-    @pl.when(g == 0)
-    def _():
-        load_all(
-            [
-                (halo, pad.at[pl.ds(40 * (1 - core), 8)]),
-                (near.at[pl.ds(near_at if source_at else 0, 8)], pad.at[pl.ds(8 + near_at, 8)]),
-                (mid.at[pl.ds(8 if source_at else 0, 16)], pad.at[pl.ds(16, 16)]),
-                (far.at[pl.ds(far_at if source_at else 0, 8)], pad.at[pl.ds(8 + far_at, 8)]),
-            ],
-            sems,
-        )
-
-    for n, first in enumerate((near_at, 8)):
-        per = blocks[n].shape[0]
-        for r in range(per):
-            product = row_product(idx, first + g * per + r, 0, blocks[n], r, pad)
-            newer = recurrence(step, product, current[n][r], older[n][r] if step else None)
+    pad[pl.ds(40 * (1 - core), 8)] = halo[...]
+    pad[pl.ds(8 + near_at, 8)] = near[pl.ds(near_at if whole else 0, 8)]
+    pad[pl.ds(16, 16)] = mid[pl.ds(8 if whole else 0, 16)]
+    pad[pl.ds(8 + far_at, 8)] = far[pl.ds(far_at if whole else 0, 8)]
+    for n, (first, count) in enumerate(((near_at, 8), (8, 16))):
+        for r in range(count):
+            product = row_product(idx, first + r, 0, blocks, first + r, pad)
+            now = current[n][(first if whole else 0) + r]
+            before = older[n][(first if step == 1 else 0) + r] if step else None
+            newer = recurrence(step, product, now, before)
             if not last:
                 fresh[n][r] = newer
             rounded[n][r] = newer.astype(BF)
 
 
-def filter_call(kernel, name, step, last, source_at, idx, place, parts, moved, halo, rounded, current, older, extra):
+VMEM = pl.BlockSpec(memory_space=pltpu.VMEM)
+
+
+def filter_call(kernel, name, step, last, whole, idx, place, blocks, window, groups, moved, halo, rounded, current, older, extra):
     width = halo.shape[-1]
-    nnz = parts["blocks"].shape[1]
-    blocks = parts["blocks"]
-    in_specs, operands, shapes, out_specs = [], [], [], []
-    groups = parts["groups"]
-    for key, count, per, first in groups:
-        in_specs.append(
-            pl.BlockSpec((per, nnz, SIZE, SIZE), lambda g, idx, place, per=per, first=first: (g + first(place[1]) // per, 0, 0, 0))
-        )
-        operands.append(blocks)
-    in_specs += [ANY] * (1 + len(moved))
-    operands += [halo] + [rounded[key] for key in moved]
-    for arrays in [current] + ([older] if step else []):
-        at = arrays.get("whole", False)
-        for key, count, per, first in groups:
-            index = (
-                (lambda g, idx, place, per=per, first=first: (g + first(place[1]) // per, 0, 0))
-                if at
-                else (lambda g, idx, place: (g, 0, 0))
-            )
-            in_specs.append(pl.BlockSpec((per, SIZE, width), index))
-            operands.append(arrays[key])
-    scratch = [pltpu.VMEM((parts["window"], SIZE, width), BF), pltpu.SemaphoreType.DMA((1 + len(moved),))]
-    for kind in (F32, BF):
-        if kind is F32 and last:
-            continue
-        for key, count, per, first in groups:
-            shapes.append(jax.ShapeDtypeStruct((count, SIZE, width), kind))
-            out_specs.append(pl.BlockSpec((per, SIZE, width), lambda g, idx, place: (g, 0, 0)))
+    nnz = blocks.shape[1]
+    keys = [key for key, _ in groups]
+    operands = [blocks, halo] + [rounded[key] for key in moved] + [current[key] for key in keys]
+    if step:
+        operands += [older[key] for key in keys]
+    operands += extra
+    kinds = [BF] if last else [F32, BF]
+    shapes = [jax.ShapeDtypeStruct((count, SIZE, width), kind) for kind in kinds for _, count in groups]
+    out_specs = [VMEM] * len(shapes)
+    scratch = [pltpu.VMEM((window, SIZE, width), BF)]
     if extra:
-        in_specs += [ANY] * len(extra)
-        operands += extra
         shapes = [jax.ShapeDtypeStruct((8, SIZE, width), BF)] * 4
         out_specs = [ANY] * 4
         scratch += [pltpu.VMEM((8, SIZE, width), BF), pltpu.SemaphoreType.DMA((4,))]
-    total = sum(count for _, count, _, _ in groups)
+    total = sum(count for _, count in groups)
     return pl.pallas_call(
-        functools.partial(kernel, step, last, source_at),
+        functools.partial(kernel, step, last, whole),
         out_shape=shapes,
         grid_spec=pltpu.PrefetchScalarGridSpec(
             num_scalar_prefetch=2,
-            grid=(4,),
-            in_specs=in_specs,
+            grid=(),
+            in_specs=[VMEM] * len(operands),
             out_specs=out_specs,
             scratch_shapes=scratch,
         ),
-        compiler_params=params(24),
+        compiler_params=params(30),
         cost_estimate=pl.CostEstimate(
             flops=total * nnz * 2 * SIZE * SIZE * width, bytes_accessed=total * MIB // 2, transcendentals=0
         ),
@@ -203,12 +156,7 @@
     core = place[1]
     within = [(i, i ^ 1) for i in range(rows)]
     between = [(i, i + 1 if i % 2 else i - 1) for i in range(1, rows - 1)]
-    far_group = ("far", 8, 2, lambda c: 24 * c)
-    near_group = ("near", 8, 2, lambda c: 24 * (1 - c))
-    mid_group = ("mid", 16, 4, lambda c: 8)
-    far_parts = dict(blocks=blocks, groups=[far_group], window=24)
-    rest_parts = dict(blocks=blocks, groups=[near_group, mid_group], window=48)
-    start = dict(near=vectors, mid=vectors, far=vectors, whole=True)
+    start = dict(near=vectors, mid=vectors, far=vectors)
     rounded = current = start
     older = None
     far_out = lax.dynamic_slice_in_dim(vectors, 24 * core, 8, 0)
@@ -219,11 +167,12 @@
         near_halo = lax.ppermute(near_out, "rows", within)
         common = (step, last, step == 0, idx, place)
         rest = filter_call(
-            rest_kernel, "filter_rest", *common, rest_parts, ["near", "mid", "far"], near_halo, rounded, current, older, None
+            rest_kernel, "filter_rest", *common, blocks, 48, [("near", 8), ("mid", 16)], ["near", "mid", "far"], near_halo,
+            rounded, current, older, [],
         )
-        extra = rest if last else None
         far = filter_call(
-            far_kernel, "filter_far", *common, far_parts, ["far", "mid"], far_halo, rounded, current, older, extra
+            far_kernel, "filter_far", *common, blocks, 24, [("far", 8)], ["far", "mid"], far_halo,
+            rounded, current, older, list(rest) if last else [],
         )
         if last:
             return far
@@ -493,15 +442,17 @@
         for copy in copies(slot, t - 2):
             copy.wait()
 
+    tall = []
     for s in range(4):
         if s == 0:
             panels = [own[0][...], got[2][...], got[1][...], got[0][...]]
         else:
             panels = [own[4 - s][...]] + [far[s - 1][r] for r in range(3)]
-        left = jnp.concatenate([p.reshape(per * SIZE, width) for p in panels], axis=1)
-        value = jnp.dot(left, high[...], preferred_element_type=F32)
-        value = value + jnp.dot(left, low[...], preferred_element_type=F32)
-        tiles[slot, s] = value.reshape(per, SIZE, width)
+        tall.append(jnp.concatenate([p.reshape(per * SIZE, width) for p in panels], axis=1))
+    left = jnp.concatenate(tall, axis=0)
+    value = jnp.dot(left, high[...], preferred_element_type=F32)
+    value = value + jnp.dot(left, low[...], preferred_element_type=F32)
+    tiles[slot] = value.reshape(4, per, SIZE, width)
     for copy in copies(slot, t):
         copy.start()
 

time: 211 us -> 208 us (0.986)
  Pallas kernels: 83.4 us -> 78.4 us
    pallas_call x8, Pallas kernels: 22.2 us -> 17 us  [filter_call(): pl.pallas_call(functools.partial(kernel, step, last, whole), out_shape=sh...]
    ppermute x4, waiting for transfers between devices: 13.8 us -> 16.4 us  [chebyshev(): far_halo = lax.ppermute(far_out, 'rows', between)]
  transfers between devices with their start and end apart: 20 -> 20, of which waited for: 11 -> 12; matrix products, arithmetic and copies ran while one was open for 0% -> 0% of each run, Pallas kernels for 32% -> 31%
where the time goes in v6:
time: 208 us
  Pallas kernels  78.4 us (38%)
  waiting for transfers between devices  50.8 us (24%)
  blocking collectives  36.7 us (18%)
  starting transfers between devices  33.2 us (16%)
  local copies, waits for them, and re-layouts  7.71 us (4%)
    pallas_call x1, Pallas kernels, factor(): pl.pallas_call(factor_kernel, out_shape=[jax.ShapeDtypeStruct((n * SIZE,...  48.6 us
    all_to_all x1, blocking collectives, sum_everywhere(): lax.all_to_all(parts, 'rows', 0, 0, axis_index_groups=groups, tiled=True)  36.7 us
    pallas_call x8, Pallas kernels, filter_call(): pl.pallas_call(functools.partial(kernel, step, last, whole), out_shape=sh...  17 us
    ppermute x4, waiting for transfers between devices, chebyshev(): far_halo = lax.ppermute(far_out, 'rows', between)  16.4 us
    ppermute x6, waiting for transfers between devices, shards(): lax.ppermute(a, 'vecs', [(i, (i + s) % vecs) for i in range(vecs)])  13.4 us
    ppermute x4, starting transfers between devices, chebyshev(): far_halo = lax.ppermute(far_out, 'rows', between)  12.7 us
    all_to_all x1, waiting for transfers between devices, sum_everywhere(): lax.all_to_all(spread_out, 'rows', 0, 0, axis_index_groups=groups, tiled=...  12.3 us
    pallas_call x1, Pallas kernels, apply(): pl.pallas_call(apply_kernel, out_shape=jax.ShapeDtypeStruct((4, 8, SIZE,...  9.55 us
  transfers between devices with their start and end apart: 20, of which 12 were waited for; matrix products, arithmetic and copies ran while one was open for 0% of the time, Pallas kernels for 31%

profile of v6, /device:TPU:1, one launch (start us, length us, event | category | flops | bytes accessed | tf_op | source)
XLA Modules:
  0.0 207.8 jit_solution(12763511690856765542)
XLA Ops:
  0.0 2.4 %constant_dynamic-slice_fusion = (bf16[8,128,256]{2,1,0:T(8,128)(2,1)}, bf16[8,128,256]{2,1,0:T(8,128)(2,1)}) fusion(bf16[32,128,256]{2,1,0:T(8,128)(2,1)} %bitcast.6, s32[]{:T(128)S(6)} %select_n.7, s32[]{:T(128)S(6)} %select_n.6), kind=kLoop, calls=%fused_computation.3 | loop fusion | bytes 2097160 | tf_op jit(solution)/shard_map/dynamic_slice | solution.py:163
  2.4 1.4 collective-permute-start.2
  3.9 3.2 %collective-permute-start = (bf16[8,128,256]{2,1,0:T(8,128)(2,1)}, bf16[8,128,256]{2,1,0:T(8,128)(2,1)S(1)}, u32[]{:S(2)}, u32[]{:S(2)}) collective-permute-start(bf16[8,128,256]{2,1,0:T(8,128)(2,1)} %get-tuple-element.68), channel_id=1, source_target_pairs={{4,8},{8,4},{12,16},{16,12},{20,24},{24,20},{28,32},{32,28},{36,40... | collective-permute-start | bytes 1572872 | tf_op jit(solution)/shard_map/ppermute | solution.py:166
  7.0 0.1 pad_add_fusion.place
  7.1 0.1 copy.4
  7.2 0.0 collective-permute-done.2.refs_1_
  7.2 0.0 copy-start
  7.2 2.5 %copy-done = bf16[32,5,128,128]{3,2,1,0:T(8,128)(2,1)S(1)} copy-done((bf16[32,5,128,128]{3,2,1,0:T(8,128)(2,1)S(1)}, bf16[32,5,128,128]{3,2,1,0:T(8,128)(2,1)}, u32[]{:S(2)}) %copy-start) | copy-done | bytes 5242904
  9.7 2.5 %filter_rest.4 = (f32[8,128,256]{2,1,0:T(8,128)S(1)}, f32[16,128,256]{2,1,0:T(8,128)S(1)}, bf16[8,128,256]{2,1,0:T(8,128)(2,1)S(1)}, bf16[16,128,256]{2,1,0:T(8,128)(2,1)S(1)}) custom-call(s32[32,5]{1,0:T(8,128)S(1)} %subtract_add_fusion.idx, s32[2]{0:T(128)S(1)} %pad_add_fusion.place, bf16[32,5,128,128]{3,2,1,0:T(8,128)(2,1)S(1)} %copy-done, ...), custom_call_target="tpu_custom_call" | custom-call | flops 1006632960 | bytes 12582912 | tf_op jit(solution)/shard_map/filter_rest/pallas_call | solution.py:136
  12.2 0.1 collective-permute-start.4
  12.3 2.2 %collective-permute-done.refs_1_ = bf16[8,128,256]{2,1,0:T(8,128)(2,1)S(1)} collective-permute-done((bf16[8,128,256]{2,1,0:T(8,128)(2,1)}, bf16[8,128,256]{2,1,0:T(8,128)(2,1)S(1)}, u32[]{:S(2)}, u32[]{:S(2)}) %collective-permute-start) | collective-permute-done | bytes 524320 | tf_op jit(solution)/shard_map/ppermute | solution.py:166
  14.5 1.5 filter_far.4
  16.1 3.2 %collective-permute-start.1 = (bf16[8,128,256]{2,1,0:T(8,128)(2,1)S(1)}, bf16[8,128,256]{2,1,0:T(8,128)(2,1)S(1)}, u32[]{:S(2)}, u32[]{:S(2)}) collective-permute-start(bf16[8,128,256]{2,1,0:T(8,128)(2,1)S(1)} %get-tuple-element.36.refs_2_.refs_4_), channel_id=1, source_target_pairs={{4,8},{8,4},{12,16},{16,12},{20,24},{24,20},{28,32},{32,28},{36,40... | collective-permute-start | bytes 1572872 | tf_op jit(solution)/shard_map/ppermute | solution.py:166
  19.3 0.0 collective-permute-done.4.refs_1_
  19.3 2.6 %filter_rest.5 = (f32[8,128,256]{2,1,0:T(8,128)S(1)}, f32[16,128,256]{2,1,0:T(8,128)S(1)}, bf16[8,128,256]{2,1,0:T(8,128)(2,1)S(1)}, bf16[16,128,256]{2,1,0:T(8,128)(2,1)S(1)}) custom-call(s32[32,5]{1,0:T(8,128)S(1)} %subtract_add_fusion.idx, s32[2]{0:T(128)S(1)} %pad_add_fusion.place, bf16[32,5,128,128]{3,2,1,0:T(8,128)(2,1)S(1)} %copy-done, ...), custom_call_target="tpu_custom_call" | custom-call | flops 1006632960 | bytes 12582912 | tf_op jit(solution)/shard_map/filter_rest/pallas_call | solution.py:136
  21.9 0.1 collective-permute-start.6
  22.0 4.6 %collective-permute-done.1.refs_1_ = bf16[8,128,256]{2,1,0:T(8,128)(2,1)S(1)} collective-permute-done((bf16[8,128,256]{2,1,0:T(8,128)(2,1)S(1)}, bf16[8,128,256]{2,1,0:T(8,128)(2,1)S(1)}, u32[]{:S(2)}, u32[]{:S(2)}) %collective-permute-start.1) | collective-permute-done | bytes 524320 | tf_op jit(solution)/shard_map/ppermute | solution.py:166
  26.6 1.5 filter_far.5
  28.1 3.2 %collective-permute-start.3 = (bf16[8,128,256]{2,1,0:T(8,128)(2,1)S(1)}, bf16[8,128,256]{2,1,0:T(8,128)(2,1)S(1)}, u32[]{:S(2)}, u32[]{:S(2)}) collective-permute-start(bf16[8,128,256]{2,1,0:T(8,128)(2,1)S(1)} %get-tuple-element.39.refs_2_.refs_4_), channel_id=1, source_target_pairs={{4,8},{8,4},{12,16},{16,12},{20,24},{24,20},{28,32},{32,28},{36,40... | collective-permute-start | bytes 1572872 | tf_op jit(solution)/shard_map/ppermute | solution.py:166
  31.3 0.0 collective-permute-done.6.refs_1_
  31.3 2.6 %filter_rest.6 = (f32[8,128,256]{2,1,0:T(8,128)S(1)}, f32[16,128,256]{2,1,0:T(8,128)S(1)}, bf16[8,128,256]{2,1,0:T(8,128)(2,1)S(1)}, bf16[16,128,256]{2,1,0:T(8,128)(2,1)S(1)}) custom-call(s32[32,5]{1,0:T(8,128)S(1)} %subtract_add_fusion.idx, s32[2]{0:T(128)S(1)} %pad_add_fusion.place, bf16[32,5,128,128]{3,2,1,0:T(8,128)(2,1)S(1)} %copy-done, ...), custom_call_target="tpu_custom_call" | custom-call | flops 1006632960 | bytes 12582912 | tf_op jit(solution)/shard_map/filter_rest/pallas_call | solution.py:136
  34.0 0.1 collective-permute-start.7
  34.1 4.6 %collective-permute-done.3.refs_1_ = bf16[8,128,256]{2,1,0:T(8,128)(2,1)S(1)} collective-permute-done((bf16[8,128,256]{2,1,0:T(8,128)(2,1)S(1)}, bf16[8,128,256]{2,1,0:T(8,128)(2,1)S(1)}, u32[]{:S(2)}, u32[]{:S(2)}) %collective-permute-start.3) | collective-permute-done | bytes 524320 | tf_op jit(solution)/shard_map/ppermute | solution.py:166
  38.6 1.5 filter_far.6
  40.2 3.2 %collective-permute-start.5 = (bf16[8,128,256]{2,1,0:T(8,128)(2,1)S(1)}, bf16[8,128,256]{2,1,0:T(8,128)(2,1)S(1)}, u32[]{:S(2)}, u32[]{:S(2)}) collective-permute-start(bf16[8,128,256]{2,1,0:T(8,128)(2,1)S(1)} %get-tuple-element.45.refs_4_.refs_2_), channel_id=1, source_target_pairs={{4,8},{8,4},{12,16},{16,12},{20,24},{24,20},{28,32},{32,28},{36,40... | collective-permute-start | bytes 1572872 | tf_op jit(solution)/shard_map/ppermute | solution.py:166
  43.4 0.0 collective-permute-done.7.refs_1_
  43.4 2.6 %filter_rest.7 = (bf16[8,128,256]{2,1,0:T(8,128)(2,1)S(1)}, bf16[16,128,256]{2,1,0:T(8,128)(2,1)S(1)}) custom-call(s32[32,5]{1,0:T(8,128)S(1)} %subtract_add_fusion.idx, s32[2]{0:T(128)S(1)} %pad_add_fusion.place, bf16[32,5,128,128]{3,2,1,0:T(8,128)(2,1)S(1)} %copy-done, bf16[8,128,256]{2,1,0:T(8,128)(2,1)S(1)} %collective-permute-done.7.refs_1_, ...), custom_call_target="tpu_custom_call" | custom-call | flops 1006632960 | bytes 12582912 | tf_op jit(solution)/shard_map/filter_rest/pallas_call | solution.py:136
  45.9 5.0 %collective-permute-done.5.refs_1_ = bf16[8,128,256]{2,1,0:T(8,128)(2,1)S(1)} collective-permute-done((bf16[8,128,256]{2,1,0:T(8,128)(2,1)S(1)}, bf16[8,128,256]{2,1,0:T(8,128)(2,1)S(1)}, u32[]{:S(2)}, u32[]{:S(2)}) %collective-permute-start.5) | collective-permute-done | bytes 524320 | tf_op jit(solution)/shard_map/ppermute | solution.py:166
  51.0 2.1 filter_far.7
  53.1 2.8 %collective-permute-start.10 = (bf16[8,128,256]{2,1,0:T(8,128)(2,1)S(1)}, bf16[8,128,256]{2,1,0:T(8,128)(2,1)S(1)}, u32[]{:S(2)}, u32[]{:S(2)}) collective-permute-start(bf16[8,128,256]{2,1,0:T(8,128)(2,1)S(1)} %get-tuple-element.59.refs_3_), channel_id=1, source_target_pairs={{0,3},{1,0},{2,1},{3,2},{4,7},{5,4},{6,5},{7,6},{8,11},{9,8},{10,9... | collective-permute-start | bytes 1572872 | tf_op jit(solution)/shard_map/ppermute | solution.py:496
  55.9 0.0 collective-permute-start.8
  55.9 1.7 collective-permute-start.9
  57.6 10.0 %collective-permute-done.10.got3.refs_6_ = bf16[8,128,256]{2,1,0:T(8,128)(2,1)S(1)} collective-permute-done((bf16[8,128,256]{2,1,0:T(8,128)(2,1)S(1)}, bf16[8,128,256]{2,1,0:T(8,128)(2,1)S(1)}, u32[]{:S(2)}, u32[]{:S(2)}) %collective-permute-start.10) | collective-permute-done | bytes 524320 | tf_op jit(solution)/shard_map/ppermute | solution.py:496
  67.7 3.4 %collective-permute-done.8.got1.refs_4_ = bf16[8,128,256]{2,1,0:T(8,128)(2,1)S(1)} collective-permute-done((bf16[8,128,256]{2,1,0:T(8,128)(2,1)S(1)}, bf16[8,128,256]{2,1,0:T(8,128)(2,1)S(1)}, u32[]{:S(2)}, u32[]{:S(2)}) %collective-permute-start.8) | collective-permute-done | bytes 524320 | tf_op jit(solution)/shard_map/ppermute | solution.py:496
  71.1 0.0 collective-permute-done.9.got2.refs_5_
  71.1 3.2 %gram.1 = (f32[18,128,128]{2,1,0:T(8,128)S(1)}, f32[18,128,128]{2,1,0:T(8,128)S(1)}, bf16[3,8,128,256]{3,2,1,0:T(8,128)(2,1)S(1)}, bf16[3,8,128,256]{3,2,1,0:T(8,128)(2,1)S(1)}, bf16[3,8,128,256]{3,2,1,0:T(8,128)(2,1)S(1)}) custom-call(s32[2]{0:T(128)S(1)} %pad_add_fusion.place, bf16[8,128,256]{2,1,0:T(8,128)(2,1)S(1)} %get-tuple-element.56.own.refs_0_, ...), custom_call_target="tpu_custom_call" | custom-call | flops 1342177280 | bytes 8388608 | tf_op jit(solution)/shard_map/gram/pallas_call | solution.py:222
  74.4 0.0 copy-start.4
  74.4 0.1 collective-permute-start.14
  74.5 2.8 %collective-permute-done.14 = f32[18,128,128]{2,1,0:T(8,128)S(1)} collective-permute-done((f32[18,128,128]{2,1,0:T(8,128)S(1)}, f32[18,128,128]{2,1,0:T(8,128)S(1)}, u32[]{:S(2)}, u32[]{:S(2)}) %collective-permute-start.14) | collective-permute-done | bytes 1179680 | tf_op jit(solution)/shard_map/ppermute | solution.py:249
  77.3 0.2 add.28
  77.5 36.7 %all_to_all.10 = f32[16,144,128]{2,1,0:T(8,128)S(1)} all-to-all(f32[16,144,128]{2,1,0:T(8,128)S(1)} %bitcast.20), channel_id=1, replica_groups={{0,8,16,24,32,40,48,56,64,72,80,88,96,104,112,120},{4,12,20,28,36,44,52..., dimensions={0} | all-to-all | bytes 2359296 | tf_op jit(solution)/shard_map/all_to_all | solution.py:251
  114.2 0.1 reduce_sum.9
  114.3 0.1 collective-permute-start.15
  114.4 1.0 collective-permute-start.16
  115.4 1.7 collective-permute-start.17
  117.1 2.1 %collective-permute-done.15 = f32[144,128]{1,0:T(8,128)S(1)} collective-permute-done((f32[144,128]{1,0:T(8,128)S(1)}, f32[144,128]{1,0:T(8,128)S(1)}, u32[]{:S(2)}, u32[]{:S(2)}) %collective-permute-start.15) | collective-permute-done | bytes 73760 | tf_op jit(solution)/shard_map/ppermute | solution.py:253
  119.2 0.7 collective-permute-done.16
  119.9 0.6 collective-permute-done.17
  120.5 1.1 broadcast_in_dim.2
  121.6 3.7 %all-to-all-start.1 = ((f32[16,144,128]{2,1,0:T(8,128)}), f32[16,144,128]{2,1,0:T(8,128)S(1)}, u32[]{:S(2)}, u32[]{:S(2)}) async-start(f32[16,144,128]{2,1,0:T(8,128)} %broadcast_in_dim.2), calls=%async_computation.1 | async-start | bytes 2359296 | tf_op jit(solution)/shard_map/all_to_all | solution.py:256
  125.3 1.2 collective-permute-start.11
  126.5 1.8 collective-permute-start.12
  128.3 0.7 collective-permute-start.13
  129.0 12.3 %all-to-all-done.1 = f32[16,144,128]{2,1,0:T(8,128)S(1)} async-done(((f32[16,144,128]{2,1,0:T(8,128)}), f32[16,144,128]{2,1,0:T(8,128)S(1)}, u32[]{:S(2)}, u32[]{:S(2)}) %all-to-all-start.1) | async-done | bytes 1179680 | tf_op jit(solution)/shard_map/all_to_all | solution.py:256
  141.3 4.0 %collective-permute-start.18 = (f32[18,128,128]{2,1,0:T(8,128)S(1)}, f32[18,128,128]{2,1,0:T(8,128)S(1)}, u32[]{:S(2)}, u32[]{:S(2)}) collective-permute-start(f32[18,128,128]{2,1,0:T(8,128)S(1)} %bitcast.18), channel_id=1, source_target_pairs={{0,4},{4,0},{8,12},{12,8},{16,20},{20,16},{24,28},{28,24},{32,36},... | collective-permute-start | bytes 3538952 | tf_op jit(solution)/shard_map/ppermute | solution.py:257
  145.3 2.5 %collective-permute-done.18.other = f32[18,128,128]{2,1,0:T(8,128)S(1)} collective-permute-done((f32[18,128,128]{2,1,0:T(8,128)S(1)}, f32[18,128,128]{2,1,0:T(8,128)S(1)}, u32[]{:S(2)}, u32[]{:S(2)}) %collective-permute-start.18) | collective-permute-done | bytes 1179680 | tf_op jit(solution)/shard_map/ppermute | solution.py:257
  147.8 0.0 copy-done.2
  147.8 48.6 %factor.1 = (bf16[1024,256]{1,0:T(8,128)(2,1)S(1)}, bf16[1024,256]{1,0:T(8,128)(2,1)S(1)}) custom-call(s32[2]{0:T(128)S(1)} %pad_add_fusion.place, f32[18,128,128]{2,1,0:T(8,128)S(1)} %bitcast.19, f32[18,128,128]{2,1,0:T(8,128)S(1)} %collective-permute-done.18.other), custom_call_target="tpu_custom_call" | custom-call | flops 1000000 | bytes 4194304 | tf_op jit(solution)/shard_map/factor/pallas_call | solution.py:399
  196.4 0.8 copy-done.12
  197.2 0.8 copy-done.13
  198.0 0.0 collective-permute-done.11.refs_7_
  198.0 0.0 collective-permute-done.12.refs_8_
  198.0 0.0 collective-permute-done.13.refs_9_
  198.0 9.5 %apply.1 = f32[4,8,128,256]{3,2,1,0:T(8,128)} custom-call(s32[2]{0:T(128)} %copy-done.2, bf16[8,128,256]{2,1,0:T(8,128)(2,1)} %copy-done.5, bf16[8,128,256]{2,1,0:T(8,128)(2,1)} %copy-done.6, bf16[8,128,256]{2,1,0:T(8,128)(2,1)} %copy-done.7, bf16[8,128,256]{2,1,0:T(8,128)(2,1)} %copy-done.8, bf16[8,128,256]{2,1,0:T(8,128)(2,1)} %copy-done.10, ...), custom_call_target="tpu_custom_call" | custom-call | flops 4294967296 | bytes 14680064 | tf_op jit(solution)/shard_map/apply/pallas_call | solution.py:470
  (26 shorter events, 0.1 us)
Async XLA Ops:
  0.0 7.2 %copy-start.1 = (bf16[4096,256]{1,0:T(8,128)(2,1)S(1)}, bf16[4096,256]{1,0:T(8,128)(2,1)}, u32[]{:S(2)}) copy-start(bf16[4096,256]{1,0:T(8,128)(2,1)} %param.3) | copy-start | bytes 6291460
  0.0 7.1 %copy-start.14 = (s32[32,5]{0,1:T(8,128)S(1)}, s32[32,5]{0,1:T(8,128)}, u32[]{:S(2)}) copy-start(s32[32,5]{0,1:T(8,128)} %param.5) | copy-start | bytes 1924
  2.4 4.8 %collective-permute-start.2 = (bf16[8,128,256]{2,1,0:T(8,128)(2,1)}, bf16[8,128,256]{2,1,0:T(8,128)(2,1)S(1)}, u32[]{:S(2)}, u32[]{:S(2)}) collective-permute-start(bf16[8,128,256]{2,1,0:T(8,128)(2,1)} %get-tuple-element.67), channel_id=1, source_target_pairs={{0,4},{4,0},{8,12},{12,8},{16,20},{20,16},{24,28},{28,24},{32,36},... | collective-permute-start | bytes 1572872 | tf_op jit(solution)/shard_map/ppermute | solution.py:167
  3.9 10.7 %collective-permute-start = (bf16[8,128,256]{2,1,0:T(8,128)(2,1)}, bf16[8,128,256]{2,1,0:T(8,128)(2,1)S(1)}, u32[]{:S(2)}, u32[]{:S(2)}) collective-permute-start(bf16[8,128,256]{2,1,0:T(8,128)(2,1)} %get-tuple-element.68), channel_id=1, source_target_pairs={{4,8},{8,4},{12,16},{16,12},{20,24},{24,20},{28,32},{32,28},{36,40... | collective-permute-start | bytes 1572872 | tf_op jit(solution)/shard_map/ppermute | solution.py:166
  7.1 140.7 %copy-start.2 = (s32[2]{0:T(128)}, s32[2]{0:T(128)S(1)}, u32[]{:S(2)}) copy-start(s32[2]{0:T(128)S(1)} %pad_add_fusion.place) | copy-start | bytes 28
  7.2 2.5 %copy-start = (bf16[32,5,128,128]{3,2,1,0:T(8,128)(2,1)S(1)}, bf16[32,5,128,128]{3,2,1,0:T(8,128)(2,1)}, u32[]{:S(2)}) copy-start(bf16[32,5,128,128]{3,2,1,0:T(8,128)(2,1)} %refs_0_.15) | copy-start | bytes 15728644
  12.2 7.0 %collective-permute-start.4 = (bf16[8,128,256]{2,1,0:T(8,128)(2,1)S(1)}, bf16[8,128,256]{2,1,0:T(8,128)(2,1)S(1)}, u32[]{:S(2)}, u32[]{:S(2)}) collective-permute-start(bf16[8,128,256]{2,1,0:T(8,128)(2,1)S(1)} %get-tuple-element.40.refs_2_), channel_id=1, source_target_pairs={{0,4},{4,0},{8,12},{12,8},{16,20},{20,16},{24,28},{28,24},{32,36},... | collective-permute-start | bytes 1572872 | tf_op jit(solution)/shard_map/ppermute | solution.py:167
  16.1 10.5 %collective-permute-start.1 = (bf16[8,128,256]{2,1,0:T(8,128)(2,1)S(1)}, bf16[8,128,256]{2,1,0:T(8,128)(2,1)S(1)}, u32[]{:S(2)}, u32[]{:S(2)}) collective-permute-start(bf16[8,128,256]{2,1,0:T(8,128)(2,1)S(1)} %get-tuple-element.36.refs_2_.refs_4_), channel_id=1, source_target_pairs={{4,8},{8,4},{12,16},{16,12},{20,24},{24,20},{28,32},{32,28},{36,40... | collective-permute-start | bytes 1572872 | tf_op jit(solution)/shard_map/ppermute | solution.py:166
  21.9 9.4 %collective-permute-start.6 = (bf16[8,128,256]{2,1,0:T(8,128)(2,1)S(1)}, bf16[8,128,256]{2,1,0:T(8,128)(2,1)S(1)}, u32[]{:S(2)}, u32[]{:S(2)}) collective-permute-start(bf16[8,128,256]{2,1,0:T(8,128)(2,1)S(1)} %get-tuple-element.46.refs_2_), channel_id=1, source_target_pairs={{0,4},{4,0},{8,12},{12,8},{16,20},{20,16},{24,28},{28,24},{32,36},... | collective-permute-start | bytes 1572872 | tf_op jit(solution)/shard_map/ppermute | solution.py:167
  28.1 10.5 %collective-permute-start.3 = (bf16[8,128,256]{2,1,0:T(8,128)(2,1)S(1)}, bf16[8,128,256]{2,1,0:T(8,128)(2,1)S(1)}, u32[]{:S(2)}, u32[]{:S(2)}) collective-permute-start(bf16[8,128,256]{2,1,0:T(8,128)(2,1)S(1)} %get-tuple-element.39.refs_2_.refs_4_), channel_id=1, source_target_pairs={{4,8},{8,4},{12,16},{16,12},{20,24},{24,20},{28,32},{32,28},{36,40... | collective-permute-start | bytes 1572872 | tf_op jit(solution)/shard_map/ppermute | solution.py:166
  34.0 9.4 %collective-permute-start.7 = (bf16[8,128,256]{2,1,0:T(8,128)(2,1)S(1)}, bf16[8,128,256]{2,1,0:T(8,128)(2,1)S(1)}, u32[]{:S(2)}, u32[]{:S(2)}) collective-permute-start(bf16[8,128,256]{2,1,0:T(8,128)(2,1)S(1)} %get-tuple-element.51.refs_2_), channel_id=1, source_target_pairs={{0,4},{4,0},{8,12},{12,8},{16,20},{20,16},{24,28},{28,24},{32,36},... | collective-permute-start | bytes 1572872 | tf_op jit(solution)/shard_map/ppermute | solution.py:167
  40.2 10.8 %collective-permute-start.5 = (bf16[8,128,256]{2,1,0:T(8,128)(2,1)S(1)}, bf16[8,128,256]{2,1,0:T(8,128)(2,1)S(1)}, u32[]{:S(2)}, u32[]{:S(2)}) collective-permute-start(bf16[8,128,256]{2,1,0:T(8,128)(2,1)S(1)} %get-tuple-element.45.refs_4_.refs_2_), channel_id=1, source_target_pairs={{4,8},{8,4},{12,16},{16,12},{20,24},{24,20},{28,32},{32,28},{36,40... | collective-permute-start | bytes 1572872 | tf_op jit(solution)/shard_map/ppermute | solution.py:166
  53.1 21.3 %copy-start.5 = (bf16[8,128,256]{2,1,0:T(8,128)(2,1)}, bf16[8,128,256]{2,1,0:T(8,128)(2,1)S(1)}, u32[]{:S(2)}) copy-start(bf16[8,128,256]{2,1,0:T(8,128)(2,1)S(1)} %get-tuple-element.56.own.refs_0_) | copy-start | bytes 1572868
  53.1 21.3 %copy-start.6 = (bf16[8,128,256]{2,1,0:T(8,128)(2,1)}, bf16[8,128,256]{2,1,0:T(8,128)(2,1)S(1)}, u32[]{:S(2)}) copy-start(bf16[8,128,256]{2,1,0:T(8,128)(2,1)S(1)} %get-tuple-element.57.refs_1_) | copy-start | bytes 1572868
  53.1 21.3 %copy-start.7 = (bf16[8,128,256]{2,1,0:T(8,128)(2,1)}, bf16[8,128,256]{2,1,0:T(8,128)(2,1)S(1)}, u32[]{:S(2)}) copy-start(bf16[8,128,256]{2,1,0:T(8,128)(2,1)S(1)} %get-tuple-element.58.refs_2_) | copy-start | bytes 1572868
  53.1 21.3 %copy-start.8 = (bf16[8,128,256]{2,1,0:T(8,128)(2,1)}, bf16[8,128,256]{2,1,0:T(8,128)(2,1)S(1)}, u32[]{:S(2)}) copy-start(bf16[8,128,256]{2,1,0:T(8,128)(2,1)S(1)} %get-tuple-element.59.refs_3_) | copy-start | bytes 1572868
  53.1 14.6 %collective-permute-start.10 = (bf16[8,128,256]{2,1,0:T(8,128)(2,1)S(1)}, bf16[8,128,256]{2,1,0:T(8,128)(2,1)S(1)}, u32[]{:S(2)}, u32[]{:S(2)}) collective-permute-start(bf16[8,128,256]{2,1,0:T(8,128)(2,1)S(1)} %get-tuple-element.59.refs_3_), channel_id=1, source_target_pairs={{0,3},{1,0},{2,1},{3,2},{4,7},{5,4},{6,5},{7,6},{8,11},{9,8},{10,9... | collective-permute-start | bytes 1572872 | tf_op jit(solution)/shard_map/ppermute | solution.py:496
  55.9 15.2 %collective-permute-start.8 = (bf16[8,128,256]{2,1,0:T(8,128)(2,1)S(1)}, bf16[8,128,256]{2,1,0:T(8,128)(2,1)S(1)}, u32[]{:S(2)}, u32[]{:S(2)}) collective-permute-start(bf16[8,128,256]{2,1,0:T(8,128)(2,1)S(1)} %get-tuple-element.57.refs_1_), channel_id=1, source_target_pairs={{0,1},{1,2},{2,3},{3,0},{4,5},{5,6},{6,7},{7,4},{8,9},{9,10},{10,1... | collective-permute-start | bytes 1572872 | tf_op jit(solution)/shard_map/ppermute | solution.py:496
  55.9 15.2 %collective-permute-start.9 = (bf16[8,128,256]{2,1,0:T(8,128)(2,1)S(1)}, bf16[8,128,256]{2,1,0:T(8,128)(2,1)S(1)}, u32[]{:S(2)}, u32[]{:S(2)}) collective-permute-start(bf16[8,128,256]{2,1,0:T(8,128)(2,1)S(1)} %get-tuple-element.58.refs_2_), channel_id=1, source_target_pairs={{0,2},{1,3},{2,0},{3,1},{4,6},{5,7},{6,4},{7,5},{8,10},{9,11},{10,... | collective-permute-start | bytes 1572872 | tf_op jit(solution)/shard_map/ppermute | solution.py:496
  67.7 6.7 %copy-start.9 = (bf16[8,128,256]{2,1,0:T(8,128)(2,1)}, bf16[8,128,256]{2,1,0:T(8,128)(2,1)S(1)}, u32[]{:S(2)}) copy-start(bf16[8,128,256]{2,1,0:T(8,128)(2,1)S(1)} %collective-permute-done.10.got3.refs_6_) | copy-start | bytes 1572868
  71.1 3.3 %copy-start.10 = (bf16[8,128,256]{2,1,0:T(8,128)(2,1)}, bf16[8,128,256]{2,1,0:T(8,128)(2,1)S(1)}, u32[]{:S(2)}) copy-start(bf16[8,128,256]{2,1,0:T(8,128)(2,1)S(1)} %collective-permute-done.8.got1.refs_4_) | copy-start | bytes 1572868
  71.1 3.3 %copy-start.11 = (bf16[8,128,256]{2,1,0:T(8,128)(2,1)}, bf16[8,128,256]{2,1,0:T(8,128)(2,1)S(1)}, u32[]{:S(2)}) copy-start(bf16[8,128,256]{2,1,0:T(8,128)(2,1)S(1)} %collective-permute-done.9.got2.refs_5_) | copy-start | bytes 1572868
  74.4 3.1 %copy-start.3 = (bf16[3,8,128,256]{3,2,1,0:T(8,128)(2,1)}, bf16[3,8,128,256]{3,2,1,0:T(8,128)(2,1)S(1)}, u32[]{:S(2)}) copy-start(bf16[3,8,128,256]{3,2,1,0:T(8,128)(2,1)S(1)} %get-tuple-element.61) | copy-start | bytes 4718596
  74.4 3.1 %copy-start.4 = (bf16[3,8,128,256]{3,2,1,0:T(8,128)(2,1)}, bf16[3,8,128,256]{3,2,1,0:T(8,128)(2,1)S(1)}, u32[]{:S(2)}) copy-start(bf16[3,8,128,256]{3,2,1,0:T(8,128)(2,1)S(1)} %get-tuple-element.60) | copy-start | bytes 4718596
  74.4 2.9 %collective-permute-start.14 = (f32[18,128,128]{2,1,0:T(8,128)S(1)}, f32[18,128,128]{2,1,0:T(8,128)S(1)}, u32[]{:S(2)}, u32[]{:S(2)}) collective-permute-start(f32[18,128,128]{2,1,0:T(8,128)S(1)} %get-tuple-element.64), channel_id=1, source_target_pairs={{0,4},{4,0},{8,12},{12,8},{16,20},{20,16},{24,28},{28,24},{32,36},... | collective-permute-start | bytes 3538952 | tf_op jit(solution)/shard_map/ppermute | solution.py:249
  114.3 4.9 %collective-permute-start.15 = (f32[144,128]{1,0:T(8,128)S(1)}, f32[144,128]{1,0:T(8,128)S(1)}, u32[]{:S(2)}, u32[]{:S(2)}) collective-permute-start(f32[144,128]{1,0:T(8,128)S(1)} %reduce_sum.9), channel_id=1, source_target_pairs={{0,1},{1,2},{2,3},{3,0},{4,5},{5,6},{6,7},{7,4},{8,9},{9,10},{10,1... | collective-permute-start | bytes 221192 | tf_op jit(solution)/shard_map/ppermute | solution.py:253
  114.4 5.5 %collective-permute-start.16 = (f32[144,128]{1,0:T(8,128)S(1)}, f32[144,128]{1,0:T(8,128)S(1)}, u32[]{:S(2)}, u32[]{:S(2)}) collective-permute-start(f32[144,128]{1,0:T(8,128)S(1)} %reduce_sum.9), channel_id=1, source_target_pairs={{0,2},{1,3},{2,0},{3,1},{4,6},{5,7},{6,4},{7,5},{8,10},{9,11},{10,... | collective-permute-start | bytes 221192 | tf_op jit(solution)/shard_map/ppermute | solution.py:253
  115.4 5.1 %collective-permute-start.17 = (f32[144,128]{1,0:T(8,128)S(1)}, f32[144,128]{1,0:T(8,128)S(1)}, u32[]{:S(2)}, u32[]{:S(2)}) collective-permute-start(f32[144,128]{1,0:T(8,128)S(1)} %reduce_sum.9), channel_id=1, source_target_pairs={{0,3},{1,0},{2,1},{3,2},{4,7},{5,4},{6,5},{7,6},{8,11},{9,8},{10,9... | collective-permute-start | bytes 221192 | tf_op jit(solution)/shard_map/ppermute | solution.py:253
  121.6 19.7 %all-to-all-start.1 = ((f32[16,144,128]{2,1,0:T(8,128)}), f32[16,144,128]{2,1,0:T(8,128)S(1)}, u32[]{:S(2)}, u32[]{:S(2)}) async-start(f32[16,144,128]{2,1,0:T(8,128)} %broadcast_in_dim.2), calls=%async_computation.1 | async-start | bytes 2359296 | tf_op jit(solution)/shard_map/all_to_all | solution.py:256
  125.3 72.7 %collective-permute-start.11 = (bf16[3,8,128,256]{3,2,1,0:T(8,128)(2,1)}, bf16[3,8,128,256]{3,2,1,0:T(8,128)(2,1)}, u32[]{:S(2)}, u32[]{:S(2)}) collective-permute-start(bf16[3,8,128,256]{3,2,1,0:T(8,128)(2,1)} %copy-done.4), channel_id=1, source_target_pairs={{0,1},{1,2},{2,3},{3,0},{4,5},{5,6},{6,7},{7,4},{8,9},{9,10},{10,1... | collective-permute-start | bytes 4718600 | tf_op jit(solution)/shard_map/ppermute | solution.py:496
  126.5 71.5 %collective-permute-start.12 = (bf16[3,8,128,256]{3,2,1,0:T(8,128)(2,1)}, bf16[3,8,128,256]{3,2,1,0:T(8,128)(2,1)}, u32[]{:S(2)}, u32[]{:S(2)}) collective-permute-start(bf16[3,8,128,256]{3,2,1,0:T(8,128)(2,1)} %copy-done.3), channel_id=1, source_target_pairs={{0,2},{1,3},{2,0},{3,1},{4,6},{5,7},{6,4},{7,5},{8,10},{9,11},{10,... | collective-permute-start | bytes 4718600 | tf_op jit(solution)/shard_map/ppermute | solution.py:496
  128.3 69.7 %collective-permute-start.13 = (bf16[3,8,128,256]{3,2,1,0:T(8,128)(2,1)S(1)}, bf16[3,8,128,256]{3,2,1,0:T(8,128)(2,1)}, u32[]{:S(2)}, u32[]{:S(2)}) collective-permute-start(bf16[3,8,128,256]{3,2,1,0:T(8,128)(2,1)S(1)} %get-tuple-element.62), channel_id=1, source_target_pairs={{0,3},{1,0},{2,1},{3,2},{4,7},{5,4},{6,5},{7,6},{8,11},{9,8},{10,9... | collective-permute-start | bytes 4718600 | tf_op jit(solution)/shard_map/ppermute | solution.py:496
  141.3 6.5 %collective-permute-start.18 = (f32[18,128,128]{2,1,0:T(8,128)S(1)}, f32[18,128,128]{2,1,0:T(8,128)S(1)}, u32[]{:S(2)}, u32[]{:S(2)}) collective-permute-start(f32[18,128,128]{2,1,0:T(8,128)S(1)} %bitcast.18), channel_id=1, source_target_pairs={{0,4},{4,0},{8,12},{12,8},{16,20},{20,16},{24,28},{28,24},{32,36},... | collective-permute-start | bytes 3538952 | tf_op jit(solution)/shard_map/ppermute | solution.py:257
  196.4 0.8 copy-start.12
  197.2 0.8 copy-start.13

commit v7 on v6

--- a/solution.py
+++ b/solution.py
@@ -143,7 +143,7 @@
             out_specs=out_specs,
             scratch_shapes=scratch,
         ),
-        compiler_params=params(30),
+        compiler_params=params(16),
         cost_estimate=pl.CostEstimate(
             flops=total * nnz * 2 * SIZE * SIZE * width, bytes_accessed=total * MIB // 2, transcendentals=0
         ),
@@ -186,13 +186,18 @@
 HALF = len(PAIRS) // 2
 
 
-def gram_kernel(total_rows, place, own, got1, got2, got3, keep, send, next1, next2, next3, f, g, sems, out_sems):
+def gram_kernel(total_rows, place, own, got1, got2, got3, keep, send, first1, first3, next1, next2, next3, f, g, sems, out_sems):
     pieces = [own, got1, got2, got3]
     x, core = place[0], place[1]
     load_all([(pieces[s], f.at[lax.rem(x + 4 - s, 4)]) for s in range(4)], sems)
+    places = {
+        1: [first1, next1.at[0], next1.at[1]],
+        2: [next2.at[0], next2.at[1], next2.at[2]],
+        3: [first3, next3.at[0], next3.at[1]],
+    }
     copies = [
-        pltpu.make_async_copy(f.at[lax.rem(x + s + r, 4)], out.at[r - 1], out_sems.at[3 * s + r - 2])
-        for s, out in ((1, next1), (2, next2), (3, next3))
+        pltpu.make_async_copy(f.at[lax.rem(x + s + r, 4)], places[s][r - 1], out_sems.at[3 * s + r - 2])
+        for s in (1, 2, 3)
         for r in (1, 2, 3)
     ]
     for copy in copies:
@@ -221,12 +226,14 @@
     half = jax.ShapeDtypeStruct((HALF, SIZE, SIZE), F32)
     return pl.pallas_call(
         functools.partial(gram_kernel, total_rows),
-        out_shape=[half, half] + [jax.ShapeDtypeStruct((3, 8, SIZE, width), BF)] * 3,
+        out_shape=[half, half]
+        + [jax.ShapeDtypeStruct((8, SIZE, width), BF)] * 2
+        + [jax.ShapeDtypeStruct((n, 8, SIZE, width), BF) for n in (2, 3, 2)],
         grid_spec=pltpu.PrefetchScalarGridSpec(
             num_scalar_prefetch=1,
             grid=(),
             in_specs=[ANY] * 4,
-            out_specs=[ANY] * 5,
+            out_specs=[ANY] * 7,
             scratch_shapes=[
                 pltpu.VMEM((4, 8, SIZE, width), BF),
                 pltpu.VMEM((2, HALF, SIZE, SIZE), F32),
@@ -234,13 +241,13 @@
                 pltpu.SemaphoreType.DMA((11,)),
             ],
         ),
-        compiler_params=params(24),
+        compiler_params=params(16),
         cost_estimate=pl.CostEstimate(flops=10 * 2 * 1024 * 256 * 256, bytes_accessed=8 * MIB, transcendentals=0),
         name="gram",
     )(place, own, *got)
 
 
-def sum_everywhere(keep, send):
+def sum_everywhere(keep, send, first):
     rows = lax.axis_size("rows")
     vecs = lax.axis_size("vecs")
     swap = [(i, i ^ 1) for i in range(rows)]
@@ -250,11 +257,12 @@
     parts = mine.reshape(count, -1, mine.shape[-1])
     parts = lax.all_to_all(parts, "rows", 0, 0, axis_index_groups=groups, tiled=True)
     part = jnp.sum(parts, axis=0)
+    part, *first = lax.optimization_barrier((part, *first))
     others = [lax.ppermute(part, "vecs", [(i, (i + s) % vecs) for i in range(vecs)]) for s in range(1, vecs)]
     part = part + sum(others)
     spread_out = jnp.broadcast_to(part[None], (count,) + part.shape)
     mine = lax.all_to_all(spread_out, "rows", 0, 0, axis_index_groups=groups, tiled=True).reshape(keep.shape)
-    return mine, lax.ppermute(mine, "rows", swap), part
+    return mine, lax.ppermute(mine, "rows", swap), first
 
 
 def recip(x):
@@ -320,9 +328,11 @@
     return high, mid, (rest - mid.astype(F32)).astype(BF)
 
 
-def factor_kernel(place, mine, other, high_ref, low_ref, w, diag, following, left, right, sems):
+def factor_kernel(place, mine, other, *refs):
+    arrays, (high_ref, low_ref, held, w, diag, following, left, right, sems, held_sems) = refs[:9], refs[9:]
     n = 8
     x, core = place[0], place[1]
+    bring = [pltpu.make_async_copy(array, held.at[m], held_sems.at[m]) for m, array in enumerate(arrays)]
     at = lambda i: pl.ds(pl.multiple_of(i * SIZE, SIZE), SIZE)
     exact = functools.partial(jnp.dot, preferred_element_type=F32, precision=EXACT)
 
@@ -344,6 +354,8 @@
         for copy in copies([other, mine]):
             copy.start()
 
+    for copy in bring:
+        copy.start()
     diag[...] = jnp.zeros(diag.shape, F32)
     left[...] = jnp.zeros(left.shape, BF)
     for copy in copies([mine, other]):
@@ -382,6 +394,8 @@
     end = pl.ds((n - 1) * SIZE, SIZE)
     w[end, :] = exact(diag[...], w[end, :])
     w[end, end] = diag[...]
+    for copy in bring:
+        copy.wait()
     for r in range(2):
         row = 2 * x + r
         for c in range(n):
@@ -393,17 +407,18 @@
             low_ref[pl.ds(SIZE * c, SIZE), pl.ds(SIZE * r, SIZE)] = (value - high.astype(F32)).astype(BF)
 
 
-def factor(place, mine, other):
+def factor(place, mine, other, arrays):
     n = 8
     vmem = pl.BlockSpec(memory_space=pltpu.VMEM)
     return pl.pallas_call(
         factor_kernel,
-        out_shape=[jax.ShapeDtypeStruct((n * SIZE, 2 * SIZE), BF)] * 2,
+        out_shape=[jax.ShapeDtypeStruct((n * SIZE, 2 * SIZE), BF)] * 2
+        + [jax.ShapeDtypeStruct((len(arrays),) + arrays[0].shape, BF)],
         grid_spec=pltpu.PrefetchScalarGridSpec(
             num_scalar_prefetch=1,
             grid=(),
-            in_specs=[ANY] * 2,
-            out_specs=[vmem] * 2,
+            in_specs=[ANY] * (2 + len(arrays)),
+            out_specs=[vmem] * 3,
             scratch_shapes=[
                 pltpu.VMEM(((2 * n - 1) * SIZE, n * SIZE), F32),
                 pltpu.VMEM((SIZE, SIZE), F32),
@@ -411,76 +426,86 @@
                 pltpu.VMEM(((2 * n - 1) * SIZE, 6 * SIZE), BF),
                 pltpu.VMEM((6 * SIZE, n * SIZE), BF),
                 pltpu.SemaphoreType.DMA((len(PAIRS),)),
+                pltpu.SemaphoreType.DMA((len(arrays),)),
             ],
         ),
-        compiler_params=params(32),
+        compiler_params=params(24),
         cost_estimate=pl.CostEstimate(flops=1_000_000, bytes_accessed=4 * MIB, transcendentals=0),
         name="factor",
-    )(place, mine, other)
+    )(place, mine, other, *arrays)
 
 
 def apply_kernel(place, *refs):
-    own, got, far = refs[0:4], refs[4:7], refs[7:10]
-    high, low, out, tiles, sems = refs[10:]
+    held, far1, far2_at, far3, high, low, out, far2, tiles, in_sems, sems = refs
+    far = [far1, far2, far3]
+    own = [held.at[n] for n in range(4)]
+    got = [held.at[n] for n in range(4, 7)]
+    near = [held.at[n] for n in range(7, 9)]
     x = place[0]
-    t = pl.program_id(0)
-    steps = pl.num_programs(0)
-    per = own[0].shape[0]
-    width = own[0].shape[-1]
-    slot = lax.rem(t, 2)
-
-    def copies(slot, t):
+    count = held.shape[1]
+    per = tiles.shape[2]
+    width = held.shape[-1]
+
+    def copies(t):
         return [
             pltpu.make_async_copy(
-                tiles.at[slot, s], out.at[lax.rem(x + 4 - s, 4), pl.ds(t * per, per)], sems.at[slot, s]
+                tiles.at[t % 2, s], out.at[lax.rem(x + 4 - s, 4), pl.ds(t * per, per)], sems.at[t % 2, s]
             )
             for s in range(4)
         ]
 
-    @pl.when(t >= 2)
-    def _():
-        for copy in copies(slot, t - 2):
+    def load(t):
+        part = pl.ds(t * per, per)
+        return pltpu.make_async_copy(far2_at.at[:, part], far2.at[:, part], in_sems.at[t])
+
+    for t in range(count // per):
+        load(t).start()
+    for t in range(count // per):
+        if t >= 2:
+            for copy in copies(t - 2):
+                copy.wait()
+        rows = slice(t * per, (t + 1) * per)
+        for s in (0, 1, 3, 2):
+            if s == 2:
+                load(t).wait()
+            if s == 0:
+                panels = [own[0][rows], got[2][rows], got[1][rows], got[0][rows]]
+            elif s == 2:
+                panels = [own[2][rows]] + [far[1][r, rows] for r in range(3)]
+            else:
+                panels = [own[4 - s][rows], near[s // 2][rows]] + [far[s - 1][r, rows] for r in range(2)]
+            left = jnp.concatenate([p.reshape(per * SIZE, width) for p in panels], axis=1)
+            value = jnp.dot(left, high[...], preferred_element_type=F32)
+            value = value + jnp.dot(left, low[...], preferred_element_type=F32)
+            tiles[t % 2, s] = value.reshape(per, SIZE, width)
+        for copy in copies(t):
+            copy.start()
+    for t in range(count // per - 2, count // per):
+        for copy in copies(t):
             copy.wait()
 
-    tall = []
-    for s in range(4):
-        if s == 0:
-            panels = [own[0][...], got[2][...], got[1][...], got[0][...]]
-        else:
-            panels = [own[4 - s][...]] + [far[s - 1][r] for r in range(3)]
-        tall.append(jnp.concatenate([p.reshape(per * SIZE, width) for p in panels], axis=1))
-    left = jnp.concatenate(tall, axis=0)
-    value = jnp.dot(left, high[...], preferred_element_type=F32)
-    value = value + jnp.dot(left, low[...], preferred_element_type=F32)
-    tiles[slot] = value.reshape(4, per, SIZE, width)
-    for copy in copies(slot, t):
-        copy.start()
-
-    @pl.when(t == steps - 1)
-    def _():
-        for copy in copies(1 - slot, t - 1) + copies(slot, t):
-            copy.wait()
-
-
-def apply(place, own, got, far, high, low):
-    width = own[0].shape[-1]
-    per = 2
-    whole = pl.BlockSpec(high.shape, lambda t, *_: (0, 0))
-    rows = pl.BlockSpec((per, SIZE, width), lambda t, *_: (t, 0, 0))
+
+def apply(place, held, far, high, low):
+    width = held.shape[-1]
     return pl.pallas_call(
         apply_kernel,
         out_shape=jax.ShapeDtypeStruct((4, 8, SIZE, width), F32),
         grid_spec=pltpu.PrefetchScalarGridSpec(
             num_scalar_prefetch=1,
-            grid=(8 // per,),
-            in_specs=[rows] * 7 + [pl.BlockSpec((3, per, SIZE, width), lambda t, *_: (0, t, 0, 0))] * 3 + [whole, whole],
+            grid=(),
+            in_specs=[VMEM, VMEM, ANY, VMEM, VMEM, VMEM],
             out_specs=ANY,
-            scratch_shapes=[pltpu.VMEM((2, 4, per, SIZE, width), F32), pltpu.SemaphoreType.DMA((2, 4))],
+            scratch_shapes=[
+                pltpu.VMEM(far[1].shape, BF),
+                pltpu.VMEM((2, 4, 2, SIZE, width), F32),
+                pltpu.SemaphoreType.DMA((4,)),
+                pltpu.SemaphoreType.DMA((2, 4)),
+            ],
         ),
-        compiler_params=params(60),
+        compiler_params=params(24),
         cost_estimate=pl.CostEstimate(flops=4 * 1024 * 1024 * 256 * 4, bytes_accessed=14 * MIB, transcendentals=0),
         name="apply",
-    )(place, *own, *got, *far, high, low)
+    )(place, held, *far, high, low)
 
 
 def shards(vectors, blocks, columns):
@@ -495,11 +520,12 @@
     own = chebyshev(vectors.reshape(block_rows, SIZE, width), blocks, idx, place)
     shift = lambda a, s: lax.ppermute(a, "vecs", [(i, (i + s) % vecs) for i in range(vecs)])
     got = [shift(own[s], s) for s in range(1, vecs)]
-    keep, send, *following = gram(total_rows, place, own[0], got)
-    mine, other, part = sum_everywhere(keep, send)
+    keep, send, first1, first3, *following = gram(total_rows, place, own[0], got)
+    near = [shift(first1, 1), shift(first3, 3)]
+    mine, other, near = sum_everywhere(keep, send, near)
     far = [shift(following[s - 1], s) for s in range(1, vecs)]
-    inverse_high, inverse_low = factor(place, mine, other)
-    return apply(place, own, got, far, inverse_high, inverse_low).reshape(vectors.shape)
+    inverse_high, inverse_low, held = factor(place, mine, other, [*own, *got, *near])
+    return apply(place, held, far, inverse_high, inverse_low).reshape(vectors.shape)
 
 
 def solution(mesh):

time: 208 us -> 217 us (1.043)
  blocking collectives: 36.7 us -> 0 us
  starting transfers between devices: 33.2 us -> 55.4 us
  waiting for transfers between devices: 50.8 us -> 67.1 us
  local copies, waits for them, and re-layouts: 7.71 us -> 12.3 us
  other arithmetic: 0.32 us -> 2.65 us
    all_to_all x1 -> x0, blocking collectives: 36.7 us -> none  [sum_everywhere(): lax.all_to_all(parts, 'rows', 0, 0, axis_index_groups=groups, tiled=True)]
    all_to_all x0 -> x1, starting transfers between devices: none -> 18.9 us  [sum_everywhere(): lax.all_to_all(parts, 'rows', 0, 0, axis_index_groups=groups, tiled=True)]
    all_to_all x0 -> x1, waiting for transfers between devices: none -> 15.7 us  [sum_everywhere(): lax.all_to_all(parts, 'rows', 0, 0, axis_index_groups=groups, tiled=True)]
    unnamed x31 -> x35, local copies, waits for them, and re-layouts: 4.19 us -> 8.76 us
    all_to_all x1, waiting for transfers between devices: 12.3 us -> 15.6 us  [sum_everywhere(): lax.all_to_all(spread_out, 'rows', 0, 0, axis_index_groups=groups, tiled=...]
    ppermute x6 -> x8, starting transfers between devices: 8.28 us -> 10.8 us  [shards(): lax.ppermute(a, 'vecs', [(i, (i + s) % vecs) for i in range(vecs)])]
    ppermute x1, waiting for transfers between devices: 2.47 us -> 0.01 us  [sum_everywhere(): return (mine, lax.ppermute(mine, 'rows', swap), first)]
    ppermute x6 -> x8, waiting for transfers between devices: 13.4 us -> 13.5 us  [shards(): lax.ppermute(a, 'vecs', [(i, (i + s) % vecs) for i in range(vecs)])]
  transfers between devices with their start and end apart: 20 -> 23, of which waited for: 12 -> 11; matrix products, arithmetic and copies ran while one was open for 0% -> 1% of each run, Pallas kernels for 31% -> 30%
where the time goes in v7:
time: 217 us; the launch traced here: 216 us
  Pallas kernels  77.9 us (36%)
  waiting for transfers between devices  67.1 us (31%)
  starting transfers between devices  55.4 us (26%)
  local copies, waits for them, and re-layouts  12.3 us (6%)
  other arithmetic  2.65 us (1%)
    pallas_call x1, Pallas kernels, factor(): pl.pallas_call(factor_kernel, out_shape=[jax.ShapeDtypeStruct((n * SIZE,...  49.1 us
    all_to_all x1, starting transfers between devices, sum_everywhere(): lax.all_to_all(parts, 'rows', 0, 0, axis_index_groups=groups, tiled=True)  18.9 us
    pallas_call x8, Pallas kernels, filter_call(): pl.pallas_call(functools.partial(kernel, step, last, whole), out_shape=sh...  17 us
    ppermute x4, waiting for transfers between devices, chebyshev(): far_halo = lax.ppermute(far_out, 'rows', between)  16.4 us
    all_to_all x1, waiting for transfers between devices, sum_everywhere(): lax.all_to_all(parts, 'rows', 0, 0, axis_index_groups=groups, tiled=True)  15.7 us
    all_to_all x1, waiting for transfers between devices, sum_everywhere(): lax.all_to_all(spread_out, 'rows', 0, 0, axis_index_groups=groups, tiled=...  15.6 us
    ppermute x8, waiting for transfers between devices, shards(): lax.ppermute(a, 'vecs', [(i, (i + s) % vecs) for i in range(vecs)])  13.5 us
    ppermute x4, starting transfers between devices, chebyshev(): far_halo = lax.ppermute(far_out, 'rows', between)  12.7 us
  transfers between devices with their start and end apart: 23, of which 11 were waited for; matrix products, arithmetic and copies ran while one was open for 1% of the time, Pallas kernels for 30%

profile of v7, /device:TPU:1, one launch (start us, length us, event | category | flops | bytes accessed | tf_op | source)
XLA Modules:
  0.0 215.9 jit_solution(2917694241687505881)
XLA Ops:
  0.0 2.4 %constant_dynamic-slice_fusion = (bf16[8,128,256]{2,1,0:T(8,128)(2,1)}, bf16[8,128,256]{2,1,0:T(8,128)(2,1)}) fusion(bf16[32,128,256]{2,1,0:T(8,128)(2,1)} %bitcast.6, s32[]{:T(128)S(6)} %select_n.7, s32[]{:T(128)S(6)} %select_n.6), kind=kLoop, calls=%fused_computation.3 | loop fusion | bytes 2097160 | tf_op jit(solution)/shard_map/dynamic_slice | solution.py:163
  2.4 1.4 collective-permute-start.2
  3.9 3.2 %collective-permute-start = (bf16[8,128,256]{2,1,0:T(8,128)(2,1)}, bf16[8,128,256]{2,1,0:T(8,128)(2,1)S(1)}, u32[]{:S(2)}, u32[]{:S(2)}) collective-permute-start(bf16[8,128,256]{2,1,0:T(8,128)(2,1)} %get-tuple-element.80), channel_id=1, source_target_pairs={{4,8},{8,4},{12,16},{16,12},{20,24},{24,20},{28,32},{32,28},{36,40... | collective-permute-start | bytes 1572872 | tf_op jit(solution)/shard_map/ppermute | solution.py:166
  7.0 0.1 pad_add_fusion.place
  7.1 0.1 copy.4
  7.2 0.0 copy-start
  7.2 2.5 %copy-done = bf16[32,5,128,128]{3,2,1,0:T(8,128)(2,1)S(1)} copy-done((bf16[32,5,128,128]{3,2,1,0:T(8,128)(2,1)S(1)}, bf16[32,5,128,128]{3,2,1,0:T(8,128)(2,1)}, u32[]{:S(2)}) %copy-start) | copy-done | bytes 5242904
  9.7 2.5 %filter_rest.4 = (f32[8,128,256]{2,1,0:T(8,128)S(1)}, f32[16,128,256]{2,1,0:T(8,128)S(1)}, bf16[8,128,256]{2,1,0:T(8,128)(2,1)S(1)}, bf16[16,128,256]{2,1,0:T(8,128)(2,1)S(1)}) custom-call(s32[32,5]{1,0:T(8,128)S(1)} %subtract_add_fusion.idx, s32[2]{0:T(128)S(1)} %pad_add_fusion.place, bf16[32,5,128,128]{3,2,1,0:T(8,128)(2,1)S(1)} %copy-done, ...), custom_call_target="tpu_custom_call" | custom-call | flops 1006632960 | bytes 12582912 | tf_op jit(solution)/shard_map/filter_rest/pallas_call | solution.py:136
  12.2 0.1 collective-permute-start.4
  12.3 2.2 %collective-permute-done.refs_1_ = bf16[8,128,256]{2,1,0:T(8,128)(2,1)S(1)} collective-permute-done((bf16[8,128,256]{2,1,0:T(8,128)(2,1)}, bf16[8,128,256]{2,1,0:T(8,128)(2,1)S(1)}, u32[]{:S(2)}, u32[]{:S(2)}) %collective-permute-start) | collective-permute-done | bytes 524320 | tf_op jit(solution)/shard_map/ppermute | solution.py:166
  14.6 1.5 filter_far.4
  16.1 3.2 %collective-permute-start.1 = (bf16[8,128,256]{2,1,0:T(8,128)(2,1)S(1)}, bf16[8,128,256]{2,1,0:T(8,128)(2,1)S(1)}, u32[]{:S(2)}, u32[]{:S(2)}) collective-permute-start(bf16[8,128,256]{2,1,0:T(8,128)(2,1)S(1)} %get-tuple-element.42.refs_2_.refs_4_), channel_id=1, source_target_pairs={{4,8},{8,4},{12,16},{16,12},{20,24},{24,20},{28,32},{32,28},{36,40... | collective-permute-start | bytes 1572872 | tf_op jit(solution)/shard_map/ppermute | solution.py:166
  19.3 2.6 %filter_rest.5 = (f32[8,128,256]{2,1,0:T(8,128)S(1)}, f32[16,128,256]{2,1,0:T(8,128)S(1)}, bf16[8,128,256]{2,1,0:T(8,128)(2,1)S(1)}, bf16[16,128,256]{2,1,0:T(8,128)(2,1)S(1)}) custom-call(s32[32,5]{1,0:T(8,128)S(1)} %subtract_add_fusion.idx, s32[2]{0:T(128)S(1)} %pad_add_fusion.place, bf16[32,5,128,128]{3,2,1,0:T(8,128)(2,1)S(1)} %copy-done, ...), custom_call_target="tpu_custom_call" | custom-call | flops 1006632960 | bytes 12582912 | tf_op jit(solution)/shard_map/filter_rest/pallas_call | solution.py:136
  21.9 0.1 collective-permute-start.6
  22.0 4.6 %collective-permute-done.1.refs_1_ = bf16[8,128,256]{2,1,0:T(8,128)(2,1)S(1)} collective-permute-done((bf16[8,128,256]{2,1,0:T(8,128)(2,1)S(1)}, bf16[8,128,256]{2,1,0:T(8,128)(2,1)S(1)}, u32[]{:S(2)}, u32[]{:S(2)}) %collective-permute-start.1) | collective-permute-done | bytes 524320 | tf_op jit(solution)/shard_map/ppermute | solution.py:166
  26.6 1.5 filter_far.5
  28.1 3.2 %collective-permute-start.3 = (bf16[8,128,256]{2,1,0:T(8,128)(2,1)S(1)}, bf16[8,128,256]{2,1,0:T(8,128)(2,1)S(1)}, u32[]{:S(2)}, u32[]{:S(2)}) collective-permute-start(bf16[8,128,256]{2,1,0:T(8,128)(2,1)S(1)} %get-tuple-element.45.refs_2_.refs_4_), channel_id=1, source_target_pairs={{4,8},{8,4},{12,16},{16,12},{20,24},{24,20},{28,32},{32,28},{36,40... | collective-permute-start | bytes 1572872 | tf_op jit(solution)/shard_map/ppermute | solution.py:166
  31.3 0.0 collective-permute-done.6.refs_1_
  31.3 2.6 %filter_rest.6 = (f32[8,128,256]{2,1,0:T(8,128)S(1)}, f32[16,128,256]{2,1,0:T(8,128)S(1)}, bf16[8,128,256]{2,1,0:T(8,128)(2,1)S(1)}, bf16[16,128,256]{2,1,0:T(8,128)(2,1)S(1)}) custom-call(s32[32,5]{1,0:T(8,128)S(1)} %subtract_add_fusion.idx, s32[2]{0:T(128)S(1)} %pad_add_fusion.place, bf16[32,5,128,128]{3,2,1,0:T(8,128)(2,1)S(1)} %copy-done, ...), custom_call_target="tpu_custom_call" | custom-call | flops 1006632960 | bytes 12582912 | tf_op jit(solution)/shard_map/filter_rest/pallas_call | solution.py:136
  34.0 0.1 collective-permute-start.7
  34.1 4.6 %collective-permute-done.3.refs_1_ = bf16[8,128,256]{2,1,0:T(8,128)(2,1)S(1)} collective-permute-done((bf16[8,128,256]{2,1,0:T(8,128)(2,1)S(1)}, bf16[8,128,256]{2,1,0:T(8,128)(2,1)S(1)}, u32[]{:S(2)}, u32[]{:S(2)}) %collective-permute-start.3) | collective-permute-done | bytes 524320 | tf_op jit(solution)/shard_map/ppermute | solution.py:166
  38.6 1.5 filter_far.6
  40.2 3.2 %collective-permute-start.5 = (bf16[8,128,256]{2,1,0:T(8,128)(2,1)S(1)}, bf16[8,128,256]{2,1,0:T(8,128)(2,1)S(1)}, u32[]{:S(2)}, u32[]{:S(2)}) collective-permute-start(bf16[8,128,256]{2,1,0:T(8,128)(2,1)S(1)} %get-tuple-element.51.refs_4_.refs_2_), channel_id=1, source_target_pairs={{4,8},{8,4},{12,16},{16,12},{20,24},{24,20},{28,32},{32,28},{36,40... | collective-permute-start | bytes 1572872 | tf_op jit(solution)/shard_map/ppermute | solution.py:166
  43.4 0.0 collective-permute-done.7.refs_1_
  43.4 2.6 %filter_rest.7 = (bf16[8,128,256]{2,1,0:T(8,128)(2,1)S(1)}, bf16[16,128,256]{2,1,0:T(8,128)(2,1)S(1)}) custom-call(s32[32,5]{1,0:T(8,128)S(1)} %subtract_add_fusion.idx, s32[2]{0:T(128)S(1)} %pad_add_fusion.place, bf16[32,5,128,128]{3,2,1,0:T(8,128)(2,1)S(1)} %copy-done, bf16[8,128,256]{2,1,0:T(8,128)(2,1)S(1)} %collective-permute-done.7.refs_1_, ...), custom_call_target="tpu_custom_call" | custom-call | flops 1006632960 | bytes 12582912 | tf_op jit(solution)/shard_map/filter_rest/pallas_call | solution.py:136
  45.9 5.0 %collective-permute-done.5.refs_1_ = bf16[8,128,256]{2,1,0:T(8,128)(2,1)S(1)} collective-permute-done((bf16[8,128,256]{2,1,0:T(8,128)(2,1)S(1)}, bf16[8,128,256]{2,1,0:T(8,128)(2,1)S(1)}, u32[]{:S(2)}, u32[]{:S(2)}) %collective-permute-start.5) | collective-permute-done | bytes 524320 | tf_op jit(solution)/shard_map/ppermute | solution.py:166
  51.0 2.1 filter_far.7
  53.1 2.8 %collective-permute-start.10 = (bf16[8,128,256]{2,1,0:T(8,128)(2,1)S(1)}, bf16[8,128,256]{2,1,0:T(8,128)(2,1)S(1)}, u32[]{:S(2)}, u32[]{:S(2)}) collective-permute-start(bf16[8,128,256]{2,1,0:T(8,128)(2,1)S(1)} %get-tuple-element.65.refs_3_), channel_id=1, source_target_pairs={{0,3},{1,0},{2,1},{3,2},{4,7},{5,4},{6,5},{7,6},{8,11},{9,8},{10,9... | collective-permute-start | bytes 1572872 | tf_op jit(solution)/shard_map/ppermute | solution.py:521
  55.9 0.0 collective-permute-start.8
  55.9 1.7 collective-permute-start.9
  57.6 10.1 %collective-permute-done.10.got3.refs_6_ = bf16[8,128,256]{2,1,0:T(8,128)(2,1)S(1)} collective-permute-done((bf16[8,128,256]{2,1,0:T(8,128)(2,1)S(1)}, bf16[8,128,256]{2,1,0:T(8,128)(2,1)S(1)}, u32[]{:S(2)}, u32[]{:S(2)}) %collective-permute-start.10) | collective-permute-done | bytes 524320 | tf_op jit(solution)/shard_map/ppermute | solution.py:521
  67.6 3.4 %collective-permute-done.8.got1.refs_4_ = bf16[8,128,256]{2,1,0:T(8,128)(2,1)S(1)} collective-permute-done((bf16[8,128,256]{2,1,0:T(8,128)(2,1)S(1)}, bf16[8,128,256]{2,1,0:T(8,128)(2,1)S(1)}, u32[]{:S(2)}, u32[]{:S(2)}) %collective-permute-start.8) | collective-permute-done | bytes 524320 | tf_op jit(solution)/shard_map/ppermute | solution.py:521
  71.0 3.2 %gram.1 = (f32[18,128,128]{2,1,0:T(8,128)S(1)}, f32[18,128,128]{2,1,0:T(8,128)S(1)}, bf16[8,128,256]{2,1,0:T(8,128)(2,1)}, bf16[8,128,256]{2,1,0:T(8,128)(2,1)S(...) custom-call(s32[2]{0:T(128)S(1)} %pad_add_fusion.place, ...), custom_call_target="tpu_custom_call" | custom-call | flops 1342177280 | bytes 8388608 | tf_op jit(solution)/shard_map/gram/pallas_call | solution.py:227
  74.3 0.9 copy-done.14
  75.2 2.8 %collective-permute-done.11 = f32[18,128,128]{2,1,0:T(8,128)S(1)} collective-permute-done((f32[18,128,128]{2,1,0:T(8,128)S(1)}, f32[18,128,128]{2,1,0:T(8,128)S(1)}, u32[]{:S(2)}, u32[]{:S(2)}) %collective-permute-start.11) | collective-permute-done | bytes 1179680 | tf_op jit(solution)/shard_map/ppermute | solution.py:256
  78.1 1.2 add.28
  79.3 18.9 %all-to-all-start = ((f32[16,144,128]{2,1,0:T(8,128)}), f32[16,144,128]{2,1,0:T(8,128)}, u32[]{:S(2)}, u32[]{:S(2)}) async-start(f32[16,144,128]{2,1,0:T(8,128)} %bitcast.3), calls=%async_computation | async-start | bytes 2359296 | tf_op jit(solution)/shard_map/all_to_all | solution.py:258
  98.2 0.1 collective-permute-start.12
  98.2 2.7 %collective-permute-start.13 = (bf16[8,128,256]{2,1,0:T(8,128)(2,1)}, bf16[8,128,256]{2,1,0:T(8,128)(2,1)S(1)}, u32[]{:S(2)}, u32[]{:S(2)}) collective-permute-start(bf16[8,128,256]{2,1,0:T(8,128)(2,1)} %copy-done.15), channel_id=1, source_target_pairs={{0,3},{1,0},{2,1},{3,2},{4,7},{5,4},{6,5},{7,6},{8,11},{9,8},{10,9... | collective-permute-start | bytes 1572872 | tf_op jit(solution)/shard_map/ppermute | solution.py:521
  100.9 15.7 %all-to-all-done = f32[16,144,128]{2,1,0:T(8,128)} async-done(((f32[16,144,128]{2,1,0:T(8,128)}), f32[16,144,128]{2,1,0:T(8,128)}, u32[]{:S(2)}, u32[]{:S(2)}) %all-to-all-start) | async-done | bytes 1179680 | tf_op jit(solution)/shard_map/all_to_all | solution.py:258
  116.6 1.3 reduce_sum.9
  117.9 0.0 collective-permute-done.12.refs_7_
  117.9 0.0 collective-permute-done.13.refs_8_
  117.9 0.1 collective-permute-start.14
  118.0 0.7 collective-permute-start.15
  118.7 2.0 collective-permute-start.16
  120.7 2.5 %collective-permute-done.14 = f32[144,128]{1,0:T(8,128)S(1)} collective-permute-done((f32[144,128]{1,0:T(8,128)S(1)}, f32[144,128]{1,0:T(8,128)S(1)}, u32[]{:S(2)}, u32[]{:S(2)}) %collective-permute-start.14) | collective-permute-done | bytes 73760 | tf_op jit(solution)/shard_map/ppermute | solution.py:261
  123.2 0.6 collective-permute-done.16
  123.8 1.1 broadcast_in_dim.2
  124.9 5.2 %all-to-all-start.1 = ((f32[16,144,128]{2,1,0:T(8,128)}), f32[16,144,128]{2,1,0:T(8,128)S(1)}, u32[]{:S(2)}, u32[]{:S(2)}) async-start(f32[16,144,128]{2,1,0:T(8,128)} %broadcast_in_dim.2), calls=%async_computation.1 | async-start | bytes 2359296 | tf_op jit(solution)/shard_map/all_to_all | solution.py:264
  130.2 0.8 collective-permute-start.19
  131.0 15.6 %all-to-all-done.1 = f32[16,144,128]{2,1,0:T(8,128)S(1)} async-done(((f32[16,144,128]{2,1,0:T(8,128)}), f32[16,144,128]{2,1,0:T(8,128)S(1)}, u32[]{:S(2)}, u32[]{:S(2)}) %all-to-all-start.1) | async-done | bytes 1179680 | tf_op jit(solution)/shard_map/all_to_all | solution.py:264
  146.6 3.4 %collective-permute-start.17 = (f32[18,128,128]{2,1,0:T(8,128)S(1)}, f32[18,128,128]{2,1,0:T(8,128)S(1)}, u32[]{:S(2)}, u32[]{:S(2)}) collective-permute-start(f32[18,128,128]{2,1,0:T(8,128)S(1)} %bitcast.18), channel_id=1, source_target_pairs={{0,4},{4,0},{8,12},{12,8},{16,20},{20,16},{24,28},{28,24},{32,36},... | collective-permute-start | bytes 3538952 | tf_op jit(solution)/shard_map/ppermute | solution.py:265
  150.0 0.6 collective-permute-start.18
  150.7 2.1 collective-permute-start.20
  152.7 0.0 collective-permute-done.17.other
  152.7 1.0 copy-done.3
  153.8 1.0 copy-done.5
  154.8 1.0 copy-done.7
  155.9 1.0 copy-done.9
  156.9 1.0 copy-done.11
  157.9 49.1 %factor.1 = (bf16[1024,256]{1,0:T(8,128)(2,1)S(1)}, bf16[1024,256]{1,0:T(8,128)(2,1)S(1)}, bf16[9,8,128,256]{3,2,1,0:T(8,128)(2,1)S(1)}) custom-call(s32[2]{0:T(128)S(1)} %pad_add_fusion.place, f32[18,128,128]{2,1,0:T(8,128)S(1)} %bitcast.19, f32[18,128,128]{2,1,0:T(8,128)S(1)} %collective-permute-done.17.other, ...), custom_call_target="tpu_custom_call" | custom-call | flops 1000000 | bytes 4194304 | tf_op jit(solution)/shard_map/factor/pallas_call | solution.py:413
  207.0 0.0 collective-permute-done.18.refs_1_
  207.0 8.7 %apply.1 = f32[4,8,128,256]{3,2,1,0:T(8,128)} custom-call(s32[2]{0:T(128)S(1)} %pad_add_fusion.place, bf16[9,8,128,256]{3,2,1,0:T(8,128)(2,1)S(1)} %get-tuple-element.73.refs_0_, bf16[2,8,128,256]{3,2,1,0:T(8,128)(2,1)S(1)} %collective-permute-done.18.refs_1_, bf16[3,8,128,256]{3,2,1,0:T(8,128)(2,1)} %collective-permute-done.19.refs_2_, ...), custom_call_target="tpu_custom_call" | custom-call | flops 4294967296 | bytes 14680064 | tf_op jit(solution)/shard_map/apply/pallas_call | solution.py:490
  (35 shorter events, 0.1 us)
Async XLA Ops:
  0.0 7.2 %copy-start.1 = (bf16[4096,256]{1,0:T(8,128)(2,1)S(1)}, bf16[4096,256]{1,0:T(8,128)(2,1)}, u32[]{:S(2)}) copy-start(bf16[4096,256]{1,0:T(8,128)(2,1)} %param.3) | copy-start | bytes 6291460
  0.0 7.1 %copy-start.16 = (s32[32,5]{0,1:T(8,128)S(1)}, s32[32,5]{0,1:T(8,128)}, u32[]{:S(2)}) copy-start(s32[32,5]{0,1:T(8,128)} %param.5) | copy-start | bytes 1924
  2.4 4.8 %collective-permute-start.2 = (bf16[8,128,256]{2,1,0:T(8,128)(2,1)}, bf16[8,128,256]{2,1,0:T(8,128)(2,1)S(1)}, u32[]{:S(2)}, u32[]{:S(2)}) collective-permute-start(bf16[8,128,256]{2,1,0:T(8,128)(2,1)} %get-tuple-element.79), channel_id=1, source_target_pairs={{0,4},{4,0},{8,12},{12,8},{16,20},{20,16},{24,28},{28,24},{32,36},... | collective-permute-start | bytes 1572872 | tf_op jit(solution)/shard_map/ppermute | solution.py:167
  3.9 10.7 %collective-permute-start = (bf16[8,128,256]{2,1,0:T(8,128)(2,1)}, bf16[8,128,256]{2,1,0:T(8,128)(2,1)S(1)}, u32[]{:S(2)}, u32[]{:S(2)}) collective-permute-start(bf16[8,128,256]{2,1,0:T(8,128)(2,1)} %get-tuple-element.80), channel_id=1, source_target_pairs={{4,8},{8,4},{12,16},{16,12},{20,24},{24,20},{28,32},{32,28},{36,40... | collective-permute-start | bytes 1572872 | tf_op jit(solution)/shard_map/ppermute | solution.py:166
  7.2 2.5 %copy-start = (bf16[32,5,128,128]{3,2,1,0:T(8,128)(2,1)S(1)}, bf16[32,5,128,128]{3,2,1,0:T(8,128)(2,1)}, u32[]{:S(2)}) copy-start(bf16[32,5,128,128]{3,2,1,0:T(8,128)(2,1)} %refs_0_.15) | copy-start | bytes 15728644
  12.2 7.0 %collective-permute-start.4 = (bf16[8,128,256]{2,1,0:T(8,128)(2,1)S(1)}, bf16[8,128,256]{2,1,0:T(8,128)(2,1)S(1)}, u32[]{:S(2)}, u32[]{:S(2)}) collective-permute-start(bf16[8,128,256]{2,1,0:T(8,128)(2,1)S(1)} %get-tuple-element.46.refs_2_), channel_id=1, source_target_pairs={{0,4},{4,0},{8,12},{12,8},{16,20},{20,16},{24,28},{28,24},{32,36},... | collective-permute-start | bytes 1572872 | tf_op jit(solution)/shard_map/ppermute | solution.py:167
  16.1 10.5 %collective-permute-start.1 = (bf16[8,128,256]{2,1,0:T(8,128)(2,1)S(1)}, bf16[8,128,256]{2,1,0:T(8,128)(2,1)S(1)}, u32[]{:S(2)}, u32[]{:S(2)}) collective-permute-start(bf16[8,128,256]{2,1,0:T(8,128)(2,1)S(1)} %get-tuple-element.42.refs_2_.refs_4_), channel_id=1, source_target_pairs={{4,8},{8,4},{12,16},{16,12},{20,24},{24,20},{28,32},{32,28},{36,40... | collective-permute-start | bytes 1572872 | tf_op jit(solution)/shard_map/ppermute | solution.py:166
  21.9 9.4 %collective-permute-start.6 = (bf16[8,128,256]{2,1,0:T(8,128)(2,1)S(1)}, bf16[8,128,256]{2,1,0:T(8,128)(2,1)S(1)}, u32[]{:S(2)}, u32[]{:S(2)}) collective-permute-start(bf16[8,128,256]{2,1,0:T(8,128)(2,1)S(1)} %get-tuple-element.52.refs_2_), channel_id=1, source_target_pairs={{0,4},{4,0},{8,12},{12,8},{16,20},{20,16},{24,28},{28,24},{32,36},... | collective-permute-start | bytes 1572872 | tf_op jit(solution)/shard_map/ppermute | solution.py:167
  28.1 10.5 %collective-permute-start.3 = (bf16[8,128,256]{2,1,0:T(8,128)(2,1)S(1)}, bf16[8,128,256]{2,1,0:T(8,128)(2,1)S(1)}, u32[]{:S(2)}, u32[]{:S(2)}) collective-permute-start(bf16[8,128,256]{2,1,0:T(8,128)(2,1)S(1)} %get-tuple-element.45.refs_2_.refs_4_), channel_id=1, source_target_pairs={{4,8},{8,4},{12,16},{16,12},{20,24},{24,20},{28,32},{32,28},{36,40... | collective-permute-start | bytes 1572872 | tf_op jit(solution)/shard_map/ppermute | solution.py:166
  34.0 9.4 %collective-permute-start.7 = (bf16[8,128,256]{2,1,0:T(8,128)(2,1)S(1)}, bf16[8,128,256]{2,1,0:T(8,128)(2,1)S(1)}, u32[]{:S(2)}, u32[]{:S(2)}) collective-permute-start(bf16[8,128,256]{2,1,0:T(8,128)(2,1)S(1)} %get-tuple-element.57.refs_2_), channel_id=1, source_target_pairs={{0,4},{4,0},{8,12},{12,8},{16,20},{20,16},{24,28},{28,24},{32,36},... | collective-permute-start | bytes 1572872 | tf_op jit(solution)/shard_map/ppermute | solution.py:167
  40.2 10.8 %collective-permute-start.5 = (bf16[8,128,256]{2,1,0:T(8,128)(2,1)S(1)}, bf16[8,128,256]{2,1,0:T(8,128)(2,1)S(1)}, u32[]{:S(2)}, u32[]{:S(2)}) collective-permute-start(bf16[8,128,256]{2,1,0:T(8,128)(2,1)S(1)} %get-tuple-element.51.refs_4_.refs_2_), channel_id=1, source_target_pairs={{4,8},{8,4},{12,16},{16,12},{20,24},{24,20},{28,32},{32,28},{36,40... | collective-permute-start | bytes 1572872 | tf_op jit(solution)/shard_map/ppermute | solution.py:166
  53.1 14.6 %collective-permute-start.10 = (bf16[8,128,256]{2,1,0:T(8,128)(2,1)S(1)}, bf16[8,128,256]{2,1,0:T(8,128)(2,1)S(1)}, u32[]{:S(2)}, u32[]{:S(2)}) collective-permute-start(bf16[8,128,256]{2,1,0:T(8,128)(2,1)S(1)} %get-tuple-element.65.refs_3_), channel_id=1, source_target_pairs={{0,3},{1,0},{2,1},{3,2},{4,7},{5,4},{6,5},{7,6},{8,11},{9,8},{10,9... | collective-permute-start | bytes 1572872 | tf_op jit(solution)/shard_map/ppermute | solution.py:521
  55.9 15.2 %collective-permute-start.8 = (bf16[8,128,256]{2,1,0:T(8,128)(2,1)S(1)}, bf16[8,128,256]{2,1,0:T(8,128)(2,1)S(1)}, u32[]{:S(2)}, u32[]{:S(2)}) collective-permute-start(bf16[8,128,256]{2,1,0:T(8,128)(2,1)S(1)} %get-tuple-element.63.refs_1_), channel_id=1, source_target_pairs={{0,1},{1,2},{2,3},{3,0},{4,5},{5,6},{6,7},{7,4},{8,9},{9,10},{10,1... | collective-permute-start | bytes 1572872 | tf_op jit(solution)/shard_map/ppermute | solution.py:521
  55.9 15.2 %collective-permute-start.9 = (bf16[8,128,256]{2,1,0:T(8,128)(2,1)S(1)}, bf16[8,128,256]{2,1,0:T(8,128)(2,1)S(1)}, u32[]{:S(2)}, u32[]{:S(2)}) collective-permute-start(bf16[8,128,256]{2,1,0:T(8,128)(2,1)S(1)} %get-tuple-element.64.refs_2_), channel_id=1, source_target_pairs={{0,2},{1,3},{2,0},{3,1},{4,6},{5,7},{6,4},{7,5},{8,10},{9,11},{10,... | collective-permute-start | bytes 1572872 | tf_op jit(solution)/shard_map/ppermute | solution.py:521
  67.6 6.6 %copy-start.2 = (bf16[8,128,256]{2,1,0:T(8,128)(2,1)}, bf16[8,128,256]{2,1,0:T(8,128)(2,1)S(1)}, u32[]{:S(2)}) copy-start(bf16[8,128,256]{2,1,0:T(8,128)(2,1)S(1)} %collective-permute-done.10.got3.refs_6_) | copy-start | bytes 1572868
  71.0 3.2 %copy-start.4 = (bf16[8,128,256]{2,1,0:T(8,128)(2,1)}, bf16[8,128,256]{2,1,0:T(8,128)(2,1)S(1)}, u32[]{:S(2)}) copy-start(bf16[8,128,256]{2,1,0:T(8,128)(2,1)S(1)} %collective-permute-done.8.got1.refs_4_) | copy-start | bytes 1572868
  71.0 3.2 %copy-start.6 = (bf16[8,128,256]{2,1,0:T(8,128)(2,1)}, bf16[8,128,256]{2,1,0:T(8,128)(2,1)S(1)}, u32[]{:S(2)}) copy-start(bf16[8,128,256]{2,1,0:T(8,128)(2,1)S(1)} %collective-permute-done.9.got2.refs_5_) | copy-start | bytes 1572868
  74.3 1.0 copy-start.14
  75.2 4.1 %copy-start.12 = (bf16[3,8,128,256]{3,2,1,0:T(8,128)(2,1)}, bf16[3,8,128,256]{3,2,1,0:T(8,128)(2,1)S(1)}, u32[]{:S(2)}) copy-start(bf16[3,8,128,256]{3,2,1,0:T(8,128)(2,1)S(1)} %get-tuple-element.75) | copy-start | bytes 4718596
  75.2 4.1 %copy-start.13 = (bf16[2,8,128,256]{3,2,1,0:T(8,128)(2,1)}, bf16[2,8,128,256]{3,2,1,0:T(8,128)(2,1)S(1)}, u32[]{:S(2)}) copy-start(bf16[2,8,128,256]{3,2,1,0:T(8,128)(2,1)S(1)} %get-tuple-element.76) | copy-start | bytes 3145732
  75.2 4.1 %copy-start.15 = (bf16[8,128,256]{2,1,0:T(8,128)(2,1)}, bf16[8,128,256]{2,1,0:T(8,128)(2,1)S(1)}, u32[]{:S(2)}) copy-start(bf16[8,128,256]{2,1,0:T(8,128)(2,1)S(1)} %get-tuple-element.69) | copy-start | bytes 1572868
  75.2 2.8 %collective-permute-start.11 = (f32[18,128,128]{2,1,0:T(8,128)S(1)}, f32[18,128,128]{2,1,0:T(8,128)S(1)}, u32[]{:S(2)}, u32[]{:S(2)}) collective-permute-start(f32[18,128,128]{2,1,0:T(8,128)S(1)} %get-tuple-element.67), channel_id=1, source_target_pairs={{0,4},{4,0},{8,12},{12,8},{16,20},{20,16},{24,28},{28,24},{32,36},... | collective-permute-start | bytes 3538952 | tf_op jit(solution)/shard_map/ppermute | solution.py:256
  79.3 37.3 %all-to-all-start = ((f32[16,144,128]{2,1,0:T(8,128)}), f32[16,144,128]{2,1,0:T(8,128)}, u32[]{:S(2)}, u32[]{:S(2)}) async-start(f32[16,144,128]{2,1,0:T(8,128)} %bitcast.3), calls=%async_computation | async-start | bytes 2359296 | tf_op jit(solution)/shard_map/all_to_all | solution.py:258
  98.2 19.8 %collective-permute-start.12 = (bf16[8,128,256]{2,1,0:T(8,128)(2,1)}, bf16[8,128,256]{2,1,0:T(8,128)(2,1)S(1)}, u32[]{:S(2)}, u32[]{:S(2)}) collective-permute-start(bf16[8,128,256]{2,1,0:T(8,128)(2,1)} %get-tuple-element.68), channel_id=1, source_target_pairs={{0,1},{1,2},{2,3},{3,0},{4,5},{5,6},{6,7},{7,4},{8,9},{9,10},{10,1... | collective-permute-start | bytes 1572872 | tf_op jit(solution)/shard_map/ppermute | solution.py:521
  98.2 19.7 %collective-permute-start.13 = (bf16[8,128,256]{2,1,0:T(8,128)(2,1)}, bf16[8,128,256]{2,1,0:T(8,128)(2,1)S(1)}, u32[]{:S(2)}, u32[]{:S(2)}) collective-permute-start(bf16[8,128,256]{2,1,0:T(8,128)(2,1)} %copy-done.15), channel_id=1, source_target_pairs={{0,3},{1,0},{2,1},{3,2},{4,7},{5,4},{6,5},{7,6},{8,11},{9,8},{10,9... | collective-permute-start | bytes 1572872 | tf_op jit(solution)/shard_map/ppermute | solution.py:521
  117.9 7.0 %copy-start.8 = (bf16[8,128,256]{2,1,0:T(8,128)(2,1)}, bf16[8,128,256]{2,1,0:T(8,128)(2,1)S(1)}, u32[]{:S(2)}) copy-start(bf16[8,128,256]{2,1,0:T(8,128)(2,1)S(1)} %collective-permute-done.12.refs_7_) | copy-start | bytes 1572868
  117.9 7.0 %copy-start.10 = (bf16[8,128,256]{2,1,0:T(8,128)(2,1)}, bf16[8,128,256]{2,1,0:T(8,128)(2,1)S(1)}, u32[]{:S(2)}) copy-start(bf16[8,128,256]{2,1,0:T(8,128)(2,1)S(1)} %collective-permute-done.13.refs_8_) | copy-start | bytes 1572868
  117.9 5.3 %collective-permute-start.14 = (f32[144,128]{1,0:T(8,128)S(1)}, f32[144,128]{1,0:T(8,128)S(1)}, u32[]{:S(2)}, u32[]{:S(2)}) collective-permute-start(f32[144,128]{1,0:T(8,128)S(1)} %reduce_sum.9), channel_id=1, source_target_pairs={{0,1},{1,2},{2,3},{3,0},{4,5},{5,6},{6,7},{7,4},{8,9},{9,10},{10,1... | collective-permute-start | bytes 221192 | tf_op jit(solution)/shard_map/ppermute | solution.py:261
  118.0 5.2 %collective-permute-start.15 = (f32[144,128]{1,0:T(8,128)S(1)}, f32[144,128]{1,0:T(8,128)S(1)}, u32[]{:S(2)}, u32[]{:S(2)}) collective-permute-start(f32[144,128]{1,0:T(8,128)S(1)} %reduce_sum.9), channel_id=1, source_target_pairs={{0,2},{1,3},{2,0},{3,1},{4,6},{5,7},{6,4},{7,5},{8,10},{9,11},{10,... | collective-permute-start | bytes 221192 | tf_op jit(solution)/shard_map/ppermute | solution.py:261
  118.7 5.1 %collective-permute-start.16 = (f32[144,128]{1,0:T(8,128)S(1)}, f32[144,128]{1,0:T(8,128)S(1)}, u32[]{:S(2)}, u32[]{:S(2)}) collective-permute-start(f32[144,128]{1,0:T(8,128)S(1)} %reduce_sum.9), channel_id=1, source_target_pairs={{0,3},{1,0},{2,1},{3,2},{4,7},{5,4},{6,5},{7,6},{8,11},{9,8},{10,9... | collective-permute-start | bytes 221192 | tf_op jit(solution)/shard_map/ppermute | solution.py:261
  124.9 21.7 %all-to-all-start.1 = ((f32[16,144,128]{2,1,0:T(8,128)}), f32[16,144,128]{2,1,0:T(8,128)S(1)}, u32[]{:S(2)}, u32[]{:S(2)}) async-start(f32[16,144,128]{2,1,0:T(8,128)} %broadcast_in_dim.2), calls=%async_computation.1 | async-start | bytes 2359296 | tf_op jit(solution)/shard_map/all_to_all | solution.py:264
  130.2 76.8 %collective-permute-start.19 = (bf16[3,8,128,256]{3,2,1,0:T(8,128)(2,1)}, bf16[3,8,128,256]{3,2,1,0:T(8,128)(2,1)}, u32[]{:S(2)}, u32[]{:S(2)}) collective-permute-start(bf16[3,8,128,256]{3,2,1,0:T(8,128)(2,1)} %copy-done.12), channel_id=1, source_target_pairs={{0,2},{1,3},{2,0},{3,1},{4,6},{5,7},{6,4},{7,5},{8,10},{9,11},{10,... | collective-permute-start | bytes 4718600 | tf_op jit(solution)/shard_map/ppermute | solution.py:521
  146.6 6.1 %collective-permute-start.17 = (f32[18,128,128]{2,1,0:T(8,128)S(1)}, f32[18,128,128]{2,1,0:T(8,128)S(1)}, u32[]{:S(2)}, u32[]{:S(2)}) collective-permute-start(f32[18,128,128]{2,1,0:T(8,128)S(1)} %bitcast.18), channel_id=1, source_target_pairs={{0,4},{4,0},{8,12},{12,8},{16,20},{20,16},{24,28},{28,24},{32,36},... | collective-permute-start | bytes 3538952 | tf_op jit(solution)/shard_map/ppermute | solution.py:265
  150.0 57.0 %collective-permute-start.18 = (bf16[2,8,128,256]{3,2,1,0:T(8,128)(2,1)}, bf16[2,8,128,256]{3,2,1,0:T(8,128)(2,1)S(1)}, u32[]{:S(2)}, u32[]{:S(2)}) collective-permute-start(bf16[2,8,128,256]{3,2,1,0:T(8,128)(2,1)} %copy-done.14), channel_id=1, source_target_pairs={{0,1},{1,2},{2,3},{3,0},{4,5},{5,6},{6,7},{7,4},{8,9},{9,10},{10,1... | collective-permute-start | bytes 3145736 | tf_op jit(solution)/shard_map/ppermute | solution.py:521
  150.7 56.4 %collective-permute-start.20 = (bf16[2,8,128,256]{3,2,1,0:T(8,128)(2,1)}, bf16[2,8,128,256]{3,2,1,0:T(8,128)(2,1)S(1)}, u32[]{:S(2)}, u32[]{:S(2)}) collective-permute-start(bf16[2,8,128,256]{3,2,1,0:T(8,128)(2,1)} %copy-done.13), channel_id=1, source_target_pairs={{0,3},{1,0},{2,1},{3,2},{4,7},{5,4},{6,5},{7,6},{8,11},{9,8},{10,9... | collective-permute-start | bytes 3145736 | tf_op jit(solution)/shard_map/ppermute | solution.py:521
  152.7 1.0 copy-start.3
  153.8 1.0 copy-start.5
  154.8 1.0 copy-start.7
  155.9 1.0 copy-start.9
  156.9 1.0 copy-start.11

commit v8 on v6

--- a/solution.py
+++ b/solution.py
@@ -251,10 +251,9 @@
     parts = lax.all_to_all(parts, "rows", 0, 0, axis_index_groups=groups, tiled=True)
     part = jnp.sum(parts, axis=0)
     others = [lax.ppermute(part, "vecs", [(i, (i + s) % vecs) for i in range(vecs)]) for s in range(1, vecs)]
-    part = part + sum(others)
-    spread_out = jnp.broadcast_to(part[None], (count,) + part.shape)
+    spread_out = sum(jnp.broadcast_to(p[None], (count,) + p.shape) for p in [part] + others)
     mine = lax.all_to_all(spread_out, "rows", 0, 0, axis_index_groups=groups, tiled=True).reshape(keep.shape)
-    return mine, lax.ppermute(mine, "rows", swap), part
+    return mine, lax.ppermute(mine, "rows", swap)
 
 
 def recip(x):
@@ -464,7 +463,7 @@
 
 def apply(place, own, got, far, high, low):
     width = own[0].shape[-1]
-    per = 2
+    per = 4
     whole = pl.BlockSpec(high.shape, lambda t, *_: (0, 0))
     rows = pl.BlockSpec((per, SIZE, width), lambda t, *_: (t, 0, 0))
     return pl.pallas_call(
@@ -496,7 +495,7 @@
     shift = lambda a, s: lax.ppermute(a, "vecs", [(i, (i + s) % vecs) for i in range(vecs)])
     got = [shift(own[s], s) for s in range(1, vecs)]
     keep, send, *following = gram(total_rows, place, own[0], got)
-    mine, other, part = sum_everywhere(keep, send)
+    mine, other = sum_everywhere(keep, send)
     far = [shift(following[s - 1], s) for s in range(1, vecs)]
     inverse_high, inverse_low = factor(place, mine, other)
     return apply(place, own, got, far, inverse_high, inverse_low).reshape(vectors.shape)

time: 208 us -> 208 us (level)
  no operation moved by 1% of the time
where the time goes in v8:
time: 208 us
  Pallas kernels  78.2 us (38%)
  waiting for transfers between devices  50.8 us (24%)
  blocking collectives  36.7 us (18%)
  starting transfers between devices  33.2 us (16%)
  local copies, waits for them, and re-layouts  7.71 us (4%)
    pallas_call x1, Pallas kernels, factor(): pl.pallas_call(factor_kernel, out_shape=[jax.ShapeDtypeStruct((n * SIZE,...  48.6 us
    all_to_all x1, blocking collectives, sum_everywhere(): lax.all_to_all(parts, 'rows', 0, 0, axis_index_groups=groups, tiled=True)  36.7 us
    pallas_call x8, Pallas kernels, filter_call(): pl.pallas_call(functools.partial(kernel, step, last, whole), out_shape=sh...  17 us
    ppermute x4, waiting for transfers between devices, chebyshev(): far_halo = lax.ppermute(far_out, 'rows', between)  16.4 us
    ppermute x6, waiting for transfers between devices, shards(): lax.ppermute(a, 'vecs', [(i, (i + s) % vecs) for i in range(vecs)])  13.4 us
    ppermute x4, starting transfers between devices, chebyshev(): far_halo = lax.ppermute(far_out, 'rows', between)  12.7 us
    all_to_all x1, waiting for transfers between devices, sum_everywhere(): lax.all_to_all(spread_out, 'rows', 0, 0, axis_index_groups=groups, tiled=...  12.3 us
    pallas_call x1, Pallas kernels, apply(): pl.pallas_call(apply_kernel, out_shape=jax.ShapeDtypeStruct((4, 8, SIZE,...  9.3 us
  transfers between devices with their start and end apart: 20, of which 12 were waited for; matrix products, arithmetic and copies ran while one was open for 0% of the time, Pallas kernels for 31%

profile of v8, /device:TPU:1, one launch (start us, length us, event | category | flops | bytes accessed | tf_op | source)
XLA Modules:
  0.0 207.5 jit_solution(1515221266792578291)
XLA Ops:
  0.0 2.4 %constant_dynamic-slice_fusion = (bf16[8,128,256]{2,1,0:T(8,128)(2,1)}, bf16[8,128,256]{2,1,0:T(8,128)(2,1)}) fusion(bf16[32,128,256]{2,1,0:T(8,128)(2,1)} %bitcast.6, s32[]{:T(128)S(6)} %select_n.7, s32[]{:T(128)S(6)} %select_n.6), kind=kLoop, calls=%fused_computation.3 | loop fusion | bytes 2097160 | tf_op jit(solution)/shard_map/dynamic_slice | solution.py:163
  2.4 1.4 collective-permute-start.2
  3.9 3.2 %collective-permute-start = (bf16[8,128,256]{2,1,0:T(8,128)(2,1)}, bf16[8,128,256]{2,1,0:T(8,128)(2,1)S(1)}, u32[]{:S(2)}, u32[]{:S(2)}) collective-permute-start(bf16[8,128,256]{2,1,0:T(8,128)(2,1)} %get-tuple-element.68), channel_id=1, source_target_pairs={{4,8},{8,4},{12,16},{16,12},{20,24},{24,20},{28,32},{32,28},{36,40... | collective-permute-start | bytes 1572872 | tf_op jit(solution)/shard_map/ppermute | solution.py:166
  7.0 0.1 pad_add_fusion.place
  7.1 0.1 copy.4
  7.2 0.0 collective-permute-done.2.refs_1_
  7.2 0.0 copy-done.1
  7.2 0.0 copy-start
  7.2 2.5 %copy-done = bf16[32,5,128,128]{3,2,1,0:T(8,128)(2,1)S(1)} copy-done((bf16[32,5,128,128]{3,2,1,0:T(8,128)(2,1)S(1)}, bf16[32,5,128,128]{3,2,1,0:T(8,128)(2,1)}, u32[]{:S(2)}) %copy-start) | copy-done | bytes 5242904
  9.7 2.5 %filter_rest.4 = (f32[8,128,256]{2,1,0:T(8,128)S(1)}, f32[16,128,256]{2,1,0:T(8,128)S(1)}, bf16[8,128,256]{2,1,0:T(8,128)(2,1)S(1)}, bf16[16,128,256]{2,1,0:T(8,128)(2,1)S(1)}) custom-call(s32[32,5]{1,0:T(8,128)S(1)} %subtract_add_fusion.idx, s32[2]{0:T(128)S(1)} %pad_add_fusion.place, bf16[32,5,128,128]{3,2,1,0:T(8,128)(2,1)S(1)} %copy-done, ...), custom_call_target="tpu_custom_call" | custom-call | flops 1006632960 | bytes 12582912 | tf_op jit(solution)/shard_map/filter_rest/pallas_call | solution.py:136
  12.2 0.1 collective-permute-start.4
  12.3 2.2 %collective-permute-done.refs_1_ = bf16[8,128,256]{2,1,0:T(8,128)(2,1)S(1)} collective-permute-done((bf16[8,128,256]{2,1,0:T(8,128)(2,1)}, bf16[8,128,256]{2,1,0:T(8,128)(2,1)S(1)}, u32[]{:S(2)}, u32[]{:S(2)}) %collective-permute-start) | collective-permute-done | bytes 524320 | tf_op jit(solution)/shard_map/ppermute | solution.py:166
  14.5 1.5 filter_far.4
  16.1 3.2 %collective-permute-start.1 = (bf16[8,128,256]{2,1,0:T(8,128)(2,1)S(1)}, bf16[8,128,256]{2,1,0:T(8,128)(2,1)S(1)}, u32[]{:S(2)}, u32[]{:S(2)}) collective-permute-start(bf16[8,128,256]{2,1,0:T(8,128)(2,1)S(1)} %get-tuple-element.36.refs_2_.refs_4_), channel_id=1, source_target_pairs={{4,8},{8,4},{12,16},{16,12},{20,24},{24,20},{28,32},{32,28},{36,40... | collective-permute-start | bytes 1572872 | tf_op jit(solution)/shard_map/ppermute | solution.py:166
  19.3 0.0 collective-permute-done.4.refs_1_
  19.3 2.6 %filter_rest.5 = (f32[8,128,256]{2,1,0:T(8,128)S(1)}, f32[16,128,256]{2,1,0:T(8,128)S(1)}, bf16[8,128,256]{2,1,0:T(8,128)(2,1)S(1)}, bf16[16,128,256]{2,1,0:T(8,128)(2,1)S(1)}) custom-call(s32[32,5]{1,0:T(8,128)S(1)} %subtract_add_fusion.idx, s32[2]{0:T(128)S(1)} %pad_add_fusion.place, bf16[32,5,128,128]{3,2,1,0:T(8,128)(2,1)S(1)} %copy-done, ...), custom_call_target="tpu_custom_call" | custom-call | flops 1006632960 | bytes 12582912 | tf_op jit(solution)/shard_map/filter_rest/pallas_call | solution.py:136
  21.9 0.1 collective-permute-start.6
  22.0 4.6 %collective-permute-done.1.refs_1_ = bf16[8,128,256]{2,1,0:T(8,128)(2,1)S(1)} collective-permute-done((bf16[8,128,256]{2,1,0:T(8,128)(2,1)S(1)}, bf16[8,128,256]{2,1,0:T(8,128)(2,1)S(1)}, u32[]{:S(2)}, u32[]{:S(2)}) %collective-permute-start.1) | collective-permute-done | bytes 524320 | tf_op jit(solution)/shard_map/ppermute | solution.py:166
  26.6 1.5 filter_far.5
  28.1 3.2 %collective-permute-start.3 = (bf16[8,128,256]{2,1,0:T(8,128)(2,1)S(1)}, bf16[8,128,256]{2,1,0:T(8,128)(2,1)S(1)}, u32[]{:S(2)}, u32[]{:S(2)}) collective-permute-start(bf16[8,128,256]{2,1,0:T(8,128)(2,1)S(1)} %get-tuple-element.39.refs_2_.refs_4_), channel_id=1, source_target_pairs={{4,8},{8,4},{12,16},{16,12},{20,24},{24,20},{28,32},{32,28},{36,40... | collective-permute-start | bytes 1572872 | tf_op jit(solution)/shard_map/ppermute | solution.py:166
  31.3 0.0 collective-permute-done.6.refs_1_
  31.3 2.6 %filter_rest.6 = (f32[8,128,256]{2,1,0:T(8,128)S(1)}, f32[16,128,256]{2,1,0:T(8,128)S(1)}, bf16[8,128,256]{2,1,0:T(8,128)(2,1)S(1)}, bf16[16,128,256]{2,1,0:T(8,128)(2,1)S(1)}) custom-call(s32[32,5]{1,0:T(8,128)S(1)} %subtract_add_fusion.idx, s32[2]{0:T(128)S(1)} %pad_add_fusion.place, bf16[32,5,128,128]{3,2,1,0:T(8,128)(2,1)S(1)} %copy-done, ...), custom_call_target="tpu_custom_call" | custom-call | flops 1006632960 | bytes 12582912 | tf_op jit(solution)/shard_map/filter_rest/pallas_call | solution.py:136
  34.0 0.1 collective-permute-start.7
  34.1 4.6 %collective-permute-done.3.refs_1_ = bf16[8,128,256]{2,1,0:T(8,128)(2,1)S(1)} collective-permute-done((bf16[8,128,256]{2,1,0:T(8,128)(2,1)S(1)}, bf16[8,128,256]{2,1,0:T(8,128)(2,1)S(1)}, u32[]{:S(2)}, u32[]{:S(2)}) %collective-permute-start.3) | collective-permute-done | bytes 524320 | tf_op jit(solution)/shard_map/ppermute | solution.py:166
  38.6 1.5 filter_far.6
  40.2 3.2 %collective-permute-start.5 = (bf16[8,128,256]{2,1,0:T(8,128)(2,1)S(1)}, bf16[8,128,256]{2,1,0:T(8,128)(2,1)S(1)}, u32[]{:S(2)}, u32[]{:S(2)}) collective-permute-start(bf16[8,128,256]{2,1,0:T(8,128)(2,1)S(1)} %get-tuple-element.45.refs_4_.refs_2_), channel_id=1, source_target_pairs={{4,8},{8,4},{12,16},{16,12},{20,24},{24,20},{28,32},{32,28},{36,40... | collective-permute-start | bytes 1572872 | tf_op jit(solution)/shard_map/ppermute | solution.py:166
  43.4 0.0 collective-permute-done.7.refs_1_
  43.4 2.6 %filter_rest.7 = (bf16[8,128,256]{2,1,0:T(8,128)(2,1)S(1)}, bf16[16,128,256]{2,1,0:T(8,128)(2,1)S(1)}) custom-call(s32[32,5]{1,0:T(8,128)S(1)} %subtract_add_fusion.idx, s32[2]{0:T(128)S(1)} %pad_add_fusion.place, bf16[32,5,128,128]{3,2,1,0:T(8,128)(2,1)S(1)} %copy-done, bf16[8,128,256]{2,1,0:T(8,128)(2,1)S(1)} %collective-permute-done.7.refs_1_, ...), custom_call_target="tpu_custom_call" | custom-call | flops 1006632960 | bytes 12582912 | tf_op jit(solution)/shard_map/filter_rest/pallas_call | solution.py:136
  45.9 5.0 %collective-permute-done.5.refs_1_ = bf16[8,128,256]{2,1,0:T(8,128)(2,1)S(1)} collective-permute-done((bf16[8,128,256]{2,1,0:T(8,128)(2,1)S(1)}, bf16[8,128,256]{2,1,0:T(8,128)(2,1)S(1)}, u32[]{:S(2)}, u32[]{:S(2)}) %collective-permute-start.5) | collective-permute-done | bytes 524320 | tf_op jit(solution)/shard_map/ppermute | solution.py:166
  51.0 2.1 filter_far.7
  53.1 2.8 %collective-permute-start.10 = (bf16[8,128,256]{2,1,0:T(8,128)(2,1)S(1)}, bf16[8,128,256]{2,1,0:T(8,128)(2,1)S(1)}, u32[]{:S(2)}, u32[]{:S(2)}) collective-permute-start(bf16[8,128,256]{2,1,0:T(8,128)(2,1)S(1)} %get-tuple-element.59.refs_3_), channel_id=1, source_target_pairs={{0,3},{1,0},{2,1},{3,2},{4,7},{5,4},{6,5},{7,6},{8,11},{9,8},{10,9... | collective-permute-start | bytes 1572872 | tf_op jit(solution)/shard_map/ppermute | solution.py:495
  55.9 0.0 collective-permute-start.8
  55.9 1.7 collective-permute-start.9
  57.6 10.0 %collective-permute-done.10.got3.refs_6_ = bf16[8,128,256]{2,1,0:T(8,128)(2,1)S(1)} collective-permute-done((bf16[8,128,256]{2,1,0:T(8,128)(2,1)S(1)}, bf16[8,128,256]{2,1,0:T(8,128)(2,1)S(1)}, u32[]{:S(2)}, u32[]{:S(2)}) %collective-permute-start.10) | collective-permute-done | bytes 524320 | tf_op jit(solution)/shard_map/ppermute | solution.py:495
  67.7 3.4 %collective-permute-done.8.got1.refs_4_ = bf16[8,128,256]{2,1,0:T(8,128)(2,1)S(1)} collective-permute-done((bf16[8,128,256]{2,1,0:T(8,128)(2,1)S(1)}, bf16[8,128,256]{2,1,0:T(8,128)(2,1)S(1)}, u32[]{:S(2)}, u32[]{:S(2)}) %collective-permute-start.8) | collective-permute-done | bytes 524320 | tf_op jit(solution)/shard_map/ppermute | solution.py:495
  71.1 0.0 collective-permute-done.9.got2.refs_5_
  71.1 3.2 %gram.1 = (f32[18,128,128]{2,1,0:T(8,128)S(1)}, f32[18,128,128]{2,1,0:T(8,128)S(1)}, bf16[3,8,128,256]{3,2,1,0:T(8,128)(2,1)S(1)}, bf16[3,8,128,256]{3,2,1,0:T(8,128)(2,1)S(1)}, bf16[3,8,128,256]{3,2,1,0:T(8,128)(2,1)S(1)}) custom-call(s32[2]{0:T(128)S(1)} %pad_add_fusion.place, bf16[8,128,256]{2,1,0:T(8,128)(2,1)S(1)} %get-tuple-element.56.own.refs_0_, ...), custom_call_target="tpu_custom_call" | custom-call | flops 1342177280 | bytes 8388608 | tf_op jit(solution)/shard_map/gram/pallas_call | solution.py:222
  74.4 0.0 copy-start.4
  74.4 0.1 collective-permute-start.14
  74.5 2.8 %collective-permute-done.14 = f32[18,128,128]{2,1,0:T(8,128)S(1)} collective-permute-done((f32[18,128,128]{2,1,0:T(8,128)S(1)}, f32[18,128,128]{2,1,0:T(8,128)S(1)}, u32[]{:S(2)}, u32[]{:S(2)}) %collective-permute-start.14) | collective-permute-done | bytes 1179680 | tf_op jit(solution)/shard_map/ppermute | solution.py:249
  77.3 0.2 add.31
  77.5 36.7 %all_to_all.10 = f32[16,144,128]{2,1,0:T(8,128)S(1)} all-to-all(f32[16,144,128]{2,1,0:T(8,128)S(1)} %bitcast.20), channel_id=1, replica_groups={{0,8,16,24,32,40,48,56,64,72,80,88,96,104,112,120},{4,12,20,28,36,44,52..., dimensions={0} | all-to-all | bytes 2359296 | tf_op jit(solution)/shard_map/all_to_all | solution.py:251
  114.2 0.1 reduce_sum.9
  114.3 0.1 collective-permute-start.15
  114.4 1.0 collective-permute-start.16
  115.4 1.7 collective-permute-start.17
  117.1 2.1 %collective-permute-done.15 = f32[144,128]{1,0:T(8,128)S(1)} collective-permute-done((f32[144,128]{1,0:T(8,128)S(1)}, f32[144,128]{1,0:T(8,128)S(1)}, u32[]{:S(2)}, u32[]{:S(2)}) %collective-permute-start.15) | collective-permute-done | bytes 73760 | tf_op jit(solution)/shard_map/ppermute | solution.py:253
  119.2 0.7 collective-permute-done.16
  119.9 0.6 collective-permute-done.17
  120.5 1.1 broadcast_in_dim.2
  121.6 3.7 %all-to-all-start.1 = ((f32[16,144,128]{2,1,0:T(8,128)}), f32[16,144,128]{2,1,0:T(8,128)S(1)}, u32[]{:S(2)}, u32[]{:S(2)}) async-start(f32[16,144,128]{2,1,0:T(8,128)} %broadcast_in_dim.2), calls=%async_computation.1 | async-start | bytes 2359296 | tf_op jit(solution)/shard_map/all_to_all | solution.py:255
  125.3 1.2 collective-permute-start.11
  126.5 1.8 collective-permute-start.12
  128.3 0.7 collective-permute-start.13
  129.0 12.3 %all-to-all-done.1 = f32[16,144,128]{2,1,0:T(8,128)S(1)} async-done(((f32[16,144,128]{2,1,0:T(8,128)}), f32[16,144,128]{2,1,0:T(8,128)S(1)}, u32[]{:S(2)}, u32[]{:S(2)}) %all-to-all-start.1) | async-done | bytes 1179680 | tf_op jit(solution)/shard_map/all_to_all | solution.py:255
  141.3 4.0 %collective-permute-start.18 = (f32[18,128,128]{2,1,0:T(8,128)S(1)}, f32[18,128,128]{2,1,0:T(8,128)S(1)}, u32[]{:S(2)}, u32[]{:S(2)}) collective-permute-start(f32[18,128,128]{2,1,0:T(8,128)S(1)} %bitcast.18), channel_id=1, source_target_pairs={{0,4},{4,0},{8,12},{12,8},{16,20},{20,16},{24,28},{28,24},{32,36},... | collective-permute-start | bytes 3538952 | tf_op jit(solution)/shard_map/ppermute | solution.py:256
  145.3 2.5 %collective-permute-done.18.other = f32[18,128,128]{2,1,0:T(8,128)S(1)} collective-permute-done((f32[18,128,128]{2,1,0:T(8,128)S(1)}, f32[18,128,128]{2,1,0:T(8,128)S(1)}, u32[]{:S(2)}, u32[]{:S(2)}) %collective-permute-start.18) | collective-permute-done | bytes 1179680 | tf_op jit(solution)/shard_map/ppermute | solution.py:256
  147.8 48.6 %factor.1 = (bf16[1024,256]{1,0:T(8,128)(2,1)S(1)}, bf16[1024,256]{1,0:T(8,128)(2,1)S(1)}) custom-call(s32[2]{0:T(128)S(1)} %pad_add_fusion.place, f32[18,128,128]{2,1,0:T(8,128)S(1)} %bitcast.19, f32[18,128,128]{2,1,0:T(8,128)S(1)} %collective-permute-done.18.other), custom_call_target="tpu_custom_call" | custom-call | flops 1000000 | bytes 4194304 | tf_op jit(solution)/shard_map/factor/pallas_call | solution.py:398
  196.4 0.8 copy-done.12
  197.2 0.8 copy-done.13
  198.0 0.0 collective-permute-done.11.refs_7_
  198.0 0.0 collective-permute-done.12.refs_8_
  198.0 0.0 collective-permute-done.13.refs_9_
  198.0 9.3 %apply.1 = f32[4,8,128,256]{3,2,1,0:T(8,128)} custom-call(s32[2]{0:T(128)} %copy-done.2, bf16[8,128,256]{2,1,0:T(8,128)(2,1)} %copy-done.5, bf16[8,128,256]{2,1,0:T(8,128)(2,1)} %copy-done.6, bf16[8,128,256]{2,1,0:T(8,128)(2,1)} %copy-done.7, bf16[8,128,256]{2,1,0:T(8,128)(2,1)} %copy-done.8, bf16[8,128,256]{2,1,0:T(8,128)(2,1)} %copy-done.10, ...), custom_call_target="tpu_custom_call" | custom-call | flops 4294967296 | bytes 14680064 | tf_op jit(solution)/shard_map/apply/pallas_call | solution.py:469
  (26 shorter events, 0.1 us)
Async XLA Ops:
  0.0 7.2 %copy-start.1 = (bf16[4096,256]{1,0:T(8,128)(2,1)S(1)}, bf16[4096,256]{1,0:T(8,128)(2,1)}, u32[]{:S(2)}) copy-start(bf16[4096,256]{1,0:T(8,128)(2,1)} %param.3) | copy-start | bytes 6291460
  0.0 7.1 %copy-start.14 = (s32[32,5]{0,1:T(8,128)S(1)}, s32[32,5]{0,1:T(8,128)}, u32[]{:S(2)}) copy-start(s32[32,5]{0,1:T(8,128)} %param.5) | copy-start | bytes 1924
  2.4 4.8 %collective-permute-start.2 = (bf16[8,128,256]{2,1,0:T(8,128)(2,1)}, bf16[8,128,256]{2,1,0:T(8,128)(2,1)S(1)}, u32[]{:S(2)}, u32[]{:S(2)}) collective-permute-start(bf16[8,128,256]{2,1,0:T(8,128)(2,1)} %get-tuple-element.67), channel_id=1, source_target_pairs={{0,4},{4,0},{8,12},{12,8},{16,20},{20,16},{24,28},{28,24},{32,36},... | collective-permute-start | bytes 1572872 | tf_op jit(solution)/shard_map/ppermute | solution.py:167
  3.9 10.7 %collective-permute-start = (bf16[8,128,256]{2,1,0:T(8,128)(2,1)}, bf16[8,128,256]{2,1,0:T(8,128)(2,1)S(1)}, u32[]{:S(2)}, u32[]{:S(2)}) collective-permute-start(bf16[8,128,256]{2,1,0:T(8,128)(2,1)} %get-tuple-element.68), channel_id=1, source_target_pairs={{4,8},{8,4},{12,16},{16,12},{20,24},{24,20},{28,32},{32,28},{36,40... | collective-permute-start | bytes 1572872 | tf_op jit(solution)/shard_map/ppermute | solution.py:166
  7.1 140.7 %copy-start.2 = (s32[2]{0:T(128)}, s32[2]{0:T(128)S(1)}, u32[]{:S(2)}) copy-start(s32[2]{0:T(128)S(1)} %pad_add_fusion.place) | copy-start | bytes 28
  7.2 2.5 %copy-start = (bf16[32,5,128,128]{3,2,1,0:T(8,128)(2,1)S(1)}, bf16[32,5,128,128]{3,2,1,0:T(8,128)(2,1)}, u32[]{:S(2)}) copy-start(bf16[32,5,128,128]{3,2,1,0:T(8,128)(2,1)} %refs_0_.15) | copy-start | bytes 15728644
  12.2 7.0 %collective-permute-start.4 = (bf16[8,128,256]{2,1,0:T(8,128)(2,1)S(1)}, bf16[8,128,256]{2,1,0:T(8,128)(2,1)S(1)}, u32[]{:S(2)}, u32[]{:S(2)}) collective-permute-start(bf16[8,128,256]{2,1,0:T(8,128)(2,1)S(1)} %get-tuple-element.40.refs_2_), channel_id=1, source_target_pairs={{0,4},{4,0},{8,12},{12,8},{16,20},{20,16},{24,28},{28,24},{32,36},... | collective-permute-start | bytes 1572872 | tf_op jit(solution)/shard_map/ppermute | solution.py:167
  16.1 10.5 %collective-permute-start.1 = (bf16[8,128,256]{2,1,0:T(8,128)(2,1)S(1)}, bf16[8,128,256]{2,1,0:T(8,128)(2,1)S(1)}, u32[]{:S(2)}, u32[]{:S(2)}) collective-permute-start(bf16[8,128,256]{2,1,0:T(8,128)(2,1)S(1)} %get-tuple-element.36.refs_2_.refs_4_), channel_id=1, source_target_pairs={{4,8},{8,4},{12,16},{16,12},{20,24},{24,20},{28,32},{32,28},{36,40... | collective-permute-start | bytes 1572872 | tf_op jit(solution)/shard_map/ppermute | solution.py:166
  21.9 9.4 %collective-permute-start.6 = (bf16[8,128,256]{2,1,0:T(8,128)(2,1)S(1)}, bf16[8,128,256]{2,1,0:T(8,128)(2,1)S(1)}, u32[]{:S(2)}, u32[]{:S(2)}) collective-permute-start(bf16[8,128,256]{2,1,0:T(8,128)(2,1)S(1)} %get-tuple-element.46.refs_2_), channel_id=1, source_target_pairs={{0,4},{4,0},{8,12},{12,8},{16,20},{20,16},{24,28},{28,24},{32,36},... | collective-permute-start | bytes 1572872 | tf_op jit(solution)/shard_map/ppermute | solution.py:167
  28.1 10.5 %collective-permute-start.3 = (bf16[8,128,256]{2,1,0:T(8,128)(2,1)S(1)}, bf16[8,128,256]{2,1,0:T(8,128)(2,1)S(1)}, u32[]{:S(2)}, u32[]{:S(2)}) collective-permute-start(bf16[8,128,256]{2,1,0:T(8,128)(2,1)S(1)} %get-tuple-element.39.refs_2_.refs_4_), channel_id=1, source_target_pairs={{4,8},{8,4},{12,16},{16,12},{20,24},{24,20},{28,32},{32,28},{36,40... | collective-permute-start | bytes 1572872 | tf_op jit(solution)/shard_map/ppermute | solution.py:166
  34.0 9.4 %collective-permute-start.7 = (bf16[8,128,256]{2,1,0:T(8,128)(2,1)S(1)}, bf16[8,128,256]{2,1,0:T(8,128)(2,1)S(1)}, u32[]{:S(2)}, u32[]{:S(2)}) collective-permute-start(bf16[8,128,256]{2,1,0:T(8,128)(2,1)S(1)} %get-tuple-element.51.refs_2_), channel_id=1, source_target_pairs={{0,4},{4,0},{8,12},{12,8},{16,20},{20,16},{24,28},{28,24},{32,36},... | collective-permute-start | bytes 1572872 | tf_op jit(solution)/shard_map/ppermute | solution.py:167
  40.2 10.8 %collective-permute-start.5 = (bf16[8,128,256]{2,1,0:T(8,128)(2,1)S(1)}, bf16[8,128,256]{2,1,0:T(8,128)(2,1)S(1)}, u32[]{:S(2)}, u32[]{:S(2)}) collective-permute-start(bf16[8,128,256]{2,1,0:T(8,128)(2,1)S(1)} %get-tuple-element.45.refs_4_.refs_2_), channel_id=1, source_target_pairs={{4,8},{8,4},{12,16},{16,12},{20,24},{24,20},{28,32},{32,28},{36,40... | collective-permute-start | bytes 1572872 | tf_op jit(solution)/shard_map/ppermute | solution.py:166
  53.1 21.3 %copy-start.5 = (bf16[8,128,256]{2,1,0:T(8,128)(2,1)}, bf16[8,128,256]{2,1,0:T(8,128)(2,1)S(1)}, u32[]{:S(2)}) copy-start(bf16[8,128,256]{2,1,0:T(8,128)(2,1)S(1)} %get-tuple-element.56.own.refs_0_) | copy-start | bytes 1572868
  53.1 21.3 %copy-start.6 = (bf16[8,128,256]{2,1,0:T(8,128)(2,1)}, bf16[8,128,256]{2,1,0:T(8,128)(2,1)S(1)}, u32[]{:S(2)}) copy-start(bf16[8,128,256]{2,1,0:T(8,128)(2,1)S(1)} %get-tuple-element.57.refs_1_) | copy-start | bytes 1572868
  53.1 21.3 %copy-start.7 = (bf16[8,128,256]{2,1,0:T(8,128)(2,1)}, bf16[8,128,256]{2,1,0:T(8,128)(2,1)S(1)}, u32[]{:S(2)}) copy-start(bf16[8,128,256]{2,1,0:T(8,128)(2,1)S(1)} %get-tuple-element.58.refs_2_) | copy-start | bytes 1572868
  53.1 21.3 %copy-start.8 = (bf16[8,128,256]{2,1,0:T(8,128)(2,1)}, bf16[8,128,256]{2,1,0:T(8,128)(2,1)S(1)}, u32[]{:S(2)}) copy-start(bf16[8,128,256]{2,1,0:T(8,128)(2,1)S(1)} %get-tuple-element.59.refs_3_) | copy-start | bytes 1572868
  53.1 14.6 %collective-permute-start.10 = (bf16[8,128,256]{2,1,0:T(8,128)(2,1)S(1)}, bf16[8,128,256]{2,1,0:T(8,128)(2,1)S(1)}, u32[]{:S(2)}, u32[]{:S(2)}) collective-permute-start(bf16[8,128,256]{2,1,0:T(8,128)(2,1)S(1)} %get-tuple-element.59.refs_3_), channel_id=1, source_target_pairs={{0,3},{1,0},{2,1},{3,2},{4,7},{5,4},{6,5},{7,6},{8,11},{9,8},{10,9... | collective-permute-start | bytes 1572872 | tf_op jit(solution)/shard_map/ppermute | solution.py:495
  55.9 15.2 %collective-permute-start.8 = (bf16[8,128,256]{2,1,0:T(8,128)(2,1)S(1)}, bf16[8,128,256]{2,1,0:T(8,128)(2,1)S(1)}, u32[]{:S(2)}, u32[]{:S(2)}) collective-permute-start(bf16[8,128,256]{2,1,0:T(8,128)(2,1)S(1)} %get-tuple-element.57.refs_1_), channel_id=1, source_target_pairs={{0,1},{1,2},{2,3},{3,0},{4,5},{5,6},{6,7},{7,4},{8,9},{9,10},{10,1... | collective-permute-start | bytes 1572872 | tf_op jit(solution)/shard_map/ppermute | solution.py:495
  55.9 15.2 %collective-permute-start.9 = (bf16[8,128,256]{2,1,0:T(8,128)(2,1)S(1)}, bf16[8,128,256]{2,1,0:T(8,128)(2,1)S(1)}, u32[]{:S(2)}, u32[]{:S(2)}) collective-permute-start(bf16[8,128,256]{2,1,0:T(8,128)(2,1)S(1)} %get-tuple-element.58.refs_2_), channel_id=1, source_target_pairs={{0,2},{1,3},{2,0},{3,1},{4,6},{5,7},{6,4},{7,5},{8,10},{9,11},{10,... | collective-permute-start | bytes 1572872 | tf_op jit(solution)/shard_map/ppermute | solution.py:495
  67.7 6.7 %copy-start.9 = (bf16[8,128,256]{2,1,0:T(8,128)(2,1)}, bf16[8,128,256]{2,1,0:T(8,128)(2,1)S(1)}, u32[]{:S(2)}) copy-start(bf16[8,128,256]{2,1,0:T(8,128)(2,1)S(1)} %collective-permute-done.10.got3.refs_6_) | copy-start | bytes 1572868
  71.1 3.3 %copy-start.10 = (bf16[8,128,256]{2,1,0:T(8,128)(2,1)}, bf16[8,128,256]{2,1,0:T(8,128)(2,1)S(1)}, u32[]{:S(2)}) copy-start(bf16[8,128,256]{2,1,0:T(8,128)(2,1)S(1)} %collective-permute-done.8.got1.refs_4_) | copy-start | bytes 1572868
  71.1 3.3 %copy-start.11 = (bf16[8,128,256]{2,1,0:T(8,128)(2,1)}, bf16[8,128,256]{2,1,0:T(8,128)(2,1)S(1)}, u32[]{:S(2)}) copy-start(bf16[8,128,256]{2,1,0:T(8,128)(2,1)S(1)} %collective-permute-done.9.got2.refs_5_) | copy-start | bytes 1572868
  74.4 3.1 %copy-start.3 = (bf16[3,8,128,256]{3,2,1,0:T(8,128)(2,1)}, bf16[3,8,128,256]{3,2,1,0:T(8,128)(2,1)S(1)}, u32[]{:S(2)}) copy-start(bf16[3,8,128,256]{3,2,1,0:T(8,128)(2,1)S(1)} %get-tuple-element.61) | copy-start | bytes 4718596
  74.4 3.1 %copy-start.4 = (bf16[3,8,128,256]{3,2,1,0:T(8,128)(2,1)}, bf16[3,8,128,256]{3,2,1,0:T(8,128)(2,1)S(1)}, u32[]{:S(2)}) copy-start(bf16[3,8,128,256]{3,2,1,0:T(8,128)(2,1)S(1)} %get-tuple-element.60) | copy-start | bytes 4718596
  74.4 2.9 %collective-permute-start.14 = (f32[18,128,128]{2,1,0:T(8,128)S(1)}, f32[18,128,128]{2,1,0:T(8,128)S(1)}, u32[]{:S(2)}, u32[]{:S(2)}) collective-permute-start(f32[18,128,128]{2,1,0:T(8,128)S(1)} %get-tuple-element.64), channel_id=1, source_target_pairs={{0,4},{4,0},{8,12},{12,8},{16,20},{20,16},{24,28},{28,24},{32,36},... | collective-permute-start | bytes 3538952 | tf_op jit(solution)/shard_map/ppermute | solution.py:249
  114.3 4.9 %collective-permute-start.15 = (f32[144,128]{1,0:T(8,128)S(1)}, f32[144,128]{1,0:T(8,128)S(1)}, u32[]{:S(2)}, u32[]{:S(2)}) collective-permute-start(f32[144,128]{1,0:T(8,128)S(1)} %reduce_sum.9), channel_id=1, source_target_pairs={{0,1},{1,2},{2,3},{3,0},{4,5},{5,6},{6,7},{7,4},{8,9},{9,10},{10,1... | collective-permute-start | bytes 221192 | tf_op jit(solution)/shard_map/ppermute | solution.py:253
  114.4 5.5 %collective-permute-start.16 = (f32[144,128]{1,0:T(8,128)S(1)}, f32[144,128]{1,0:T(8,128)S(1)}, u32[]{:S(2)}, u32[]{:S(2)}) collective-permute-start(f32[144,128]{1,0:T(8,128)S(1)} %reduce_sum.9), channel_id=1, source_target_pairs={{0,2},{1,3},{2,0},{3,1},{4,6},{5,7},{6,4},{7,5},{8,10},{9,11},{10,... | collective-permute-start | bytes 221192 | tf_op jit(solution)/shard_map/ppermute | solution.py:253
  115.4 5.1 %collective-permute-start.17 = (f32[144,128]{1,0:T(8,128)S(1)}, f32[144,128]{1,0:T(8,128)S(1)}, u32[]{:S(2)}, u32[]{:S(2)}) collective-permute-start(f32[144,128]{1,0:T(8,128)S(1)} %reduce_sum.9), channel_id=1, source_target_pairs={{0,3},{1,0},{2,1},{3,2},{4,7},{5,4},{6,5},{7,6},{8,11},{9,8},{10,9... | collective-permute-start | bytes 221192 | tf_op jit(solution)/shard_map/ppermute | solution.py:253
  121.6 19.7 %all-to-all-start.1 = ((f32[16,144,128]{2,1,0:T(8,128)}), f32[16,144,128]{2,1,0:T(8,128)S(1)}, u32[]{:S(2)}, u32[]{:S(2)}) async-start(f32[16,144,128]{2,1,0:T(8,128)} %broadcast_in_dim.2), calls=%async_computation.1 | async-start | bytes 2359296 | tf_op jit(solution)/shard_map/all_to_all | solution.py:255
  125.3 72.7 %collective-permute-start.11 = (bf16[3,8,128,256]{3,2,1,0:T(8,128)(2,1)}, bf16[3,8,128,256]{3,2,1,0:T(8,128)(2,1)}, u32[]{:S(2)}, u32[]{:S(2)}) collective-permute-start(bf16[3,8,128,256]{3,2,1,0:T(8,128)(2,1)} %copy-done.4), channel_id=1, source_target_pairs={{0,1},{1,2},{2,3},{3,0},{4,5},{5,6},{6,7},{7,4},{8,9},{9,10},{10,1... | collective-permute-start | bytes 4718600 | tf_op jit(solution)/shard_map/ppermute | solution.py:495
  126.5 71.5 %collective-permute-start.12 = (bf16[3,8,128,256]{3,2,1,0:T(8,128)(2,1)}, bf16[3,8,128,256]{3,2,1,0:T(8,128)(2,1)}, u32[]{:S(2)}, u32[]{:S(2)}) collective-permute-start(bf16[3,8,128,256]{3,2,1,0:T(8,128)(2,1)} %copy-done.3), channel_id=1, source_target_pairs={{0,2},{1,3},{2,0},{3,1},{4,6},{5,7},{6,4},{7,5},{8,10},{9,11},{10,... | collective-permute-start | bytes 4718600 | tf_op jit(solution)/shard_map/ppermute | solution.py:495
  128.3 69.7 %collective-permute-start.13 = (bf16[3,8,128,256]{3,2,1,0:T(8,128)(2,1)S(1)}, bf16[3,8,128,256]{3,2,1,0:T(8,128)(2,1)}, u32[]{:S(2)}, u32[]{:S(2)}) collective-permute-start(bf16[3,8,128,256]{3,2,1,0:T(8,128)(2,1)S(1)} %get-tuple-element.62), channel_id=1, source_target_pairs={{0,3},{1,0},{2,1},{3,2},{4,7},{5,4},{6,5},{7,6},{8,11},{9,8},{10,9... | collective-permute-start | bytes 4718600 | tf_op jit(solution)/shard_map/ppermute | solution.py:495
  141.3 6.5 %collective-permute-start.18 = (f32[18,128,128]{2,1,0:T(8,128)S(1)}, f32[18,128,128]{2,1,0:T(8,128)S(1)}, u32[]{:S(2)}, u32[]{:S(2)}) collective-permute-start(f32[18,128,128]{2,1,0:T(8,128)S(1)} %bitcast.18), channel_id=1, source_target_pairs={{0,4},{4,0},{8,12},{12,8},{16,20},{20,16},{24,28},{28,24},{32,36},... | collective-permute-start | bytes 3538952 | tf_op jit(solution)/shard_map/ppermute | solution.py:256
  196.4 0.8 copy-start.12
  197.2 0.8 copy-start.13
